TPU v7x, 512 devices: a whole 4x4x16 slice. The times are simulated.
512 devices in a mesh: pb: 32 (over z_lo, y), ta: 8 (over x, core), row: 2 (over z_hi).
Axes of the slice: x: 4, y: 4, z: 16 (z_hi: 2, z_lo: 8; z = z_hi * 8 + z_lo), core: 2. Of those that a mesh axis runs over, the one named last changes fastest.
Arguments:
- query_features: bfloat16 [16384, 4096], P('pb', 'ta'), may hold values from -6 to 6
- inverse_gram: bfloat16 [4096, 4096], P('pb', 'ta'), may hold values from -0.03125 to 2.03125
- training_features: bfloat16 [8192, 4096], P(('row', 'ta'), 'pb'), parts along dimension 0, may hold values from -0.09375 to 0.09375
- residual_weight: float32 [8192], P(('row', 'ta')), parts along dimension 0, may hold values from 0.05 to 0.95
Outputs:
- scores: float32 [16384, 8192], P('pb', ('row', 'ta')), parts along dimension 1
There are 2 independent parts, one for each index of `row`. A program takes and returns all parts, laid end to end along the dimension named above; an argument that names none is the same for every part. Nothing has to cross between parts.
All inputs are finite; a program needn't handle non-finite values.
Results may differ from a plain program's by a relative error of at most 0.0029.
Values may be sent and summed in bfloat16 or wider, within the bound.
No kernel may reach another device: no remote copies, remote signals or barrier semaphores. Data moves between devices by JAX's collectives and lax.ppermute only.
A program may use at most 64 MiB of HBM per device.

v0:
```python
import jax
import jax.numpy as jnp
from jax import lax
from jax.sharding import PartitionSpec as P


def local(query_features, inverse_gram, training_features, residual_weight):
    whole_query = lax.all_gather(query_features, "ta", axis=1, tiled=True)
    columns = whole_query
    panel_sum = jnp.dot(
        columns,
        lax.all_gather(inverse_gram, "pb", axis=0, tiled=True),
        preferred_element_type=jnp.float32,
    )
    preconditioned = panel_sum.astype(jnp.bfloat16)
    whole_pre = lax.all_gather(preconditioned, "ta", axis=1, tiled=True)
    columns = whole_pre
    raw = lax.dot_general(
        columns,
        lax.all_gather(training_features, "pb", axis=1, tiled=True),
        (((1,), (1,)), ((), ())),
        preferred_element_type=jnp.float32,
    )
    return raw * residual_weight[None, :]


def solution(mesh):
    placed = (P("pb", "ta"), P("pb", "ta"), P(("row", "ta"), "pb"), P(("row", "ta")))
    return jax.shard_map(
        local, mesh=mesh, in_specs=placed, out_specs=P("pb", ("row", "ta")), check_vma=False
    )
```

profile of v0, /device:TPU:6, one launch (start us, length us, event | category | flops | bytes accessed | tf_op | source)
XLA Modules:
  0.0 522.5 jit_solution(15471313217204520551)
XLA Ops:
  6.5 0.0 all-gather.5.cloned.1.call-start
  6.5 0.7 all-gather.5.cloned.1.call-update
  7.3 0.0 all-gather.7.cloned.1.call-start
  7.3 0.7 all-gather.7.cloned.1.call-update
  8.0 0.0 all-gather.11.cloned.1.call-start
  8.1 0.7 all-gather.11.cloned.1.call-update
  8.7 0.0 copy-start
  8.8 0.0 all-gather.9.cloned.1.call-start
  8.8 43.0 %all-gather.5.cloned.1.call-done = bf16[512,4096]{1,0:T(8,128)(2,1)} async-done(((bf16[512,512]{1,0:T(8,128)(2,1)}), bf16[512,4096]{1,0:T(8,128)(2,1)}) %all-gather.5.cloned.1.call-update) | async-done | bytes 4194320 | tf_op jit(solution)/shard_map/all_gather | solution.py:8
  51.8 232.0 %all-gather.7.cloned.1.call-done = bf16[4096,512]{1,0:T(8,128)(2,1)} async-done(((bf16[128,512]{1,0:T(8,128)(2,1)}), bf16[4096,512]{1,0:T(8,128)(2,1)}) %all-gather.7.cloned.1.call-update) | async-done | bytes 4194320 | tf_op jit(solution)/shard_map/all_gather | solution.py:12
  283.8 6.6 %convolution_convert_fusion = bf16[512,512]{1,0:T(8,128)(2,1)} fusion(bf16[512,4096]{1,0:T(8,128)(2,1)} %all-gather.5.cloned.1.call-done, bf16[4096,512]{1,0:T(8,128)(2,1)} %all-gather.7.cloned.1.call-done), kind=kOutput, calls=%fused_computation.1 | convolution fusion | flops 2147745792 | bytes 8912896 | tf_op jit(solution)/shard_map/dot_general | solution.py:10
  290.4 0.0 all-gather.9.cloned.1.call-update
  290.4 184.3 %all-gather.11.cloned.1.call-done = bf16[512,4096]{1,0:T(8,128)(2,1)} async-done(((bf16[512,128]{1,0:T(8,128)(2,1)}), bf16[512,4096]{1,0:T(8,128)(2,1)}) %all-gather.11.cloned.1.call-update) | async-done | bytes 4194320 | tf_op jit(solution)/shard_map/all_gather | solution.py:20
  474.7 34.5 %all-gather.9.cloned.1.call-done = bf16[512,4096]{1,0:T(8,128)(2,1)} async-done(((bf16[512,512]{1,0:T(8,128)(2,1)}), bf16[512,4096]{1,0:T(8,128)(2,1)}) %all-gather.9.cloned.1.call-update) | async-done | bytes 4194320 | tf_op jit(solution)/shard_map/all_gather | solution.py:16
  509.2 0.0 copy-done
  509.2 6.8 %convolution_multiply_fusion = f32[512,512]{1,0:T(8,128)} fusion(bf16[512,4096]{1,0:T(8,128)(2,1)} %all-gather.9.cloned.1.call-done, bf16[512,4096]{1,0:T(8,128)(2,1)} %all-gather.11.cloned.1.call-done, f32[512]{0:T(512)S(1)} %copy-done), kind=kOutput, calls=%fused_computation | convolution fusion | flops 2147745792 | bytes 9439232 | tf_op jit(solution)/shard_map/dot_general | solution.py:18
Async XLA Ops:
  6.5 45.3 %all-gather.5.cloned.1.call-start = ((), (), s32[]{:S(2)}) async-start(), calls=%async_computation | async-start | bytes 4718592 | tf_op jit(solution)/shard_map/all_gather | solution.py:8
  7.3 276.6 %all-gather.7.cloned.1.call-start = ((), (), s32[]{:S(2)}) async-start(), calls=%async_computation.1 | async-start | bytes 4325376 | tf_op jit(solution)/shard_map/all_gather | solution.py:12
  8.0 466.7 %all-gather.11.cloned.1.call-start = ((), (), s32[]{:S(2)}) async-start(), calls=%async_computation.3 | async-start | bytes 4325376 | tf_op jit(solution)/shard_map/all_gather | solution.py:20
  8.7 500.4 %copy-start = (f32[512]{0:T(512)S(1)}, f32[512]{0:T(512)}, u32[]{:S(2)}) copy-start(f32[512]{0:T(512)} %param.7) | copy-start | bytes 6148
  8.8 500.4 %all-gather.9.cloned.1.call-start = ((), (), s32[]{:S(2)}) async-start(), calls=%async_computation.2 | async-start | bytes 4718592 | tf_op jit(solution)/shard_map/all_gather | solution.py:16
Sparse Core Ops, SparseCore 0:
  9.5 42.3 all-gather.4
  53.9 229.8 all-gather.6
  285.8 188.8 all-gather.10
  476.7 32.4 all-gather.8
where the time goes:
time: 526 us; the launch traced here: 523 us
  waiting for transfers between devices  496 us (94%)
  matrix products  13.4 us (3%)
  between operations  13.1 us (2%)
    all_gather x1, waiting for transfers between devices, local(): lax.all_gather(inverse_gram, 'pb', axis=0, tiled=True)  232 us
    all_gather x1, waiting for transfers between devices, local(): lax.all_gather(training_features, 'pb', axis=1, tiled=True)  184 us
    all_gather x1, waiting for transfers between devices, local(): whole_query = lax.all_gather(query_features, 'ta', axis=1, tiled=True)  43 us
    all_gather x1, waiting for transfers between devices, local(): whole_pre = lax.all_gather(preconditioned, 'ta', axis=1, tiled=True)  34.5 us
  transfers between devices with their start and end apart: 4, of which 4 were waited for; matrix products, arithmetic and copies ran while one was open for 1% of the time, Pallas kernels for 0%

commit v1 on v0

v1 whole, which is shorter than its diff:
```python
import jax
import jax.numpy as jnp
from jax import lax
from jax.experimental import pallas as pl
from jax.experimental.pallas import tpu as pltpu
from jax.sharding import Mesh, PartitionSpec as P

NT_DIMS = (((1,), (1,)), ((), ()))
RELATIVE = (0, 4, 2, 6, 1, 5, 3, 7)


def product_kernel(slots, place, left_ref, right_ref, out_ref, total):
    step = pl.program_id(0)

    @pl.when(step == 0)
    def _():
        total[...] = jnp.zeros_like(total)

    total[...] += lax.dot_general(
        left_ref[0], right_ref[0], NT_DIMS, preferred_element_type=jnp.float32
    )

    @pl.when(step == pl.num_programs(0) - 1)
    def _():
        out_ref[...] = total[...].astype(out_ref.dtype)


def kernel_matrix(slots, inverse_gram, training):
    n, t, depth = training.shape
    rows = inverse_gram.shape[1]
    return pl.pallas_call(
        lambda s, *refs: product_kernel(s, None, *refs),
        out_shape=jax.ShapeDtypeStruct((rows, t), jnp.bfloat16),
        grid_spec=pltpu.PrefetchScalarGridSpec(
            num_scalar_prefetch=1,
            grid=(n,),
            in_specs=[
                pl.BlockSpec((1, rows, depth), lambda s, slots: (slots[s], 0, 0)),
                pl.BlockSpec((1, t, depth), lambda s, slots: (s, 0, 0)),
            ],
            out_specs=pl.BlockSpec((rows, t), lambda s, slots: (0, 0)),
            scratch_shapes=[pltpu.VMEM((rows, t), jnp.float32)],
        ),
        compiler_params=pltpu.CompilerParams(vmem_limit_bytes=24 * 1024 * 1024),
        cost_estimate=pl.CostEstimate(
            flops=2 * n * rows * t * depth, bytes_accessed=2 * n * depth * (rows + t), transcendentals=0
        ),
        name="kernel_matrix",
    )(slots, inverse_gram, training)


def score_columns(slots, place, query, parts, weight, out, columns):
    n, rows, depth = query.shape
    t = parts[0].shape[2]
    each = n // len(parts)

    def kernel(slots, place, query_ref, *refs):
        part_refs, weight_ref, out_ref, total = refs[: len(parts)], refs[len(parts)], refs[-2], refs[-1]
        step = pl.program_id(0)

        @pl.when(step == 0)
        def _():
            total[...] = jnp.zeros_like(total)

        for k, part_ref in enumerate(part_refs):

            @pl.when(step // each == k)
            def _():
                total[...] += jnp.dot(query_ref[0], part_ref[0], preferred_element_type=jnp.float32)

        @pl.when(step == n - 1)
        def _():
            out_ref[...] = total[...] * weight_ref[...]

    operands = [slots, place, query, *parts, weight] + ([] if out is None else [out])
    in_specs = [
        pl.BlockSpec((1, rows, depth), lambda s, slots, place: (slots[s], 0, 0)),
        *[
            pl.BlockSpec((1, depth, t), lambda s, slots, place, k=k: (jnp.clip(s - k * each, 0, each - 1), 0, 0))
            for k in range(len(parts))
        ],
        pl.BlockSpec((1, t), lambda s, slots, place: (0, place[0])),
    ]
    if out is not None:
        in_specs.append(pl.BlockSpec(memory_space=pl.ANY))
    return pl.pallas_call(
        kernel,
        out_shape=jax.ShapeDtypeStruct((rows, columns), jnp.float32),
        grid_spec=pltpu.PrefetchScalarGridSpec(
            num_scalar_prefetch=2,
            grid=(n,),
            in_specs=in_specs,
            out_specs=pl.BlockSpec((rows, t), lambda s, slots, place: (0, place[0])),
            scratch_shapes=[pltpu.VMEM((rows, t), jnp.float32)],
        ),
        input_output_aliases={} if out is None else {len(operands) - 1: 0},
        compiler_params=pltpu.CompilerParams(vmem_limit_bytes=24 * 1024 * 1024),
        cost_estimate=pl.CostEstimate(
            flops=2 * n * rows * t * depth, bytes_accessed=2 * n * depth * (rows + t), transcendentals=0
        ),
        name="score_columns",
    )(*operands)


def gather_z(block):
    held = block[None]
    for distance in (4, 2, 1):
        other = lax.ppermute(held, "z", [(i, i ^ distance) for i in range(8)])
        held = jnp.concatenate([held, other], axis=0)
    return held


def local(query_features, inverse_gram, training_features, residual_weight):
    z, y = lax.axis_index("z"), lax.axis_index("y")
    slots = z ^ jnp.array(RELATIVE, jnp.int32)
    ny = 4

    training = lax.all_to_all(training_features, "y", split_axis=0, concat_axis=1, tiled=True)
    rows = lax.all_gather(inverse_gram, "y", axis=0, tiled=True)
    whole_rows = lax.all_gather(rows, ("x", "core"), axis=0)
    whole_query = lax.all_gather(query_features, ("x", "core"), axis=0)

    whole_training = gather_z(training)
    block = kernel_matrix(slots, whole_rows, whole_training)
    own = gather_z(block)

    up = [(i, (i + 1) % ny) for i in range(ny)]
    down = [(i, (i - 1) % ny) for i in range(ny)]
    below = lax.ppermute(own, "y", up)
    above = lax.ppermute(own, "y", down)
    far_first = lax.ppermute(below[:4], "y", up)
    far_second = lax.ppermute(above[4:], "y", down)

    weight = residual_weight[None, :]
    columns = residual_weight.shape[0]
    out = None
    for distance, parts in ((0, [own]), (ny - 1, [below]), (1, [above]), (2, [far_first, far_second])):
        place = ((y + distance) % ny).astype(jnp.int32)[None]
        out = score_columns(slots, place, whole_query, parts, weight, out, columns)
    return out


def solution(mesh):
    fine = Mesh(mesh.devices.reshape(8, 4, 4, 2, 2), ("z", "y", "x", "core", "row"))
    pb, ta = ("z", "y"), ("x", "core")
    placed = (P(pb, ta), P(pb, ta), P(("row", *ta), pb), P(("row", *ta)))
    return jax.shard_map(
        local, mesh=fine, in_specs=placed, out_specs=P(pb, ("row", *ta)), check_vma=False
    )
```

time: 526 us -> 193 us (0.37)
  waiting for transfers between devices: 496 us -> 84.4 us
  starting transfers between devices: 0.12 us -> 39.1 us
  blocking collectives: 0 us -> 24.3 us
  Pallas kernels: 0 us -> 21.3 us
  matrix products: 13.4 us -> 0 us
  local copies, waits for them, and re-layouts: 0.01 us -> 6.21 us
    all_gather x4 -> x2, waiting for transfers between devices: 494 us -> 0.04 us  [the longest x1 0.02 us: local(): whole_query = lax.all_gather(query_features, ('x', 'core'), axis=0)]
    ppermute x0 -> x10, waiting for transfers between devices: none -> 83.7 us  [the longest x6 64.3 us: gather_z(): other = lax.ppermute(held, 'z', [(i, i ^ distance) for i in range(8)])]
    ppermute x0 -> x10, starting transfers between devices: none -> 39 us  [the longest x6 24.9 us: gather_z(): other = lax.ppermute(held, 'z', [(i, i ^ distance) for i in range(8)])]
    pallas_call x0 -> x5, Pallas kernels: none -> 21.3 us  [the longest x4 18.2 us: score_columns(): pl.pallas_call(kernel, out_shape=jax.ShapeDtypeStruct((rows, columns), jn...]
    all_gather x0 -> x1, blocking collectives: none -> 15.1 us  [local(): rows = lax.all_gather(inverse_gram, 'y', axis=0, tiled=True)]
    dot_general x2 -> x0, matrix products: 13.4 us -> none  [the longest x1 6.8 us: local(): lax.dot_general(columns, lax.all_gather(training_features, 'pb', axis=1,...]
    all_to_all x0 -> x1, blocking collectives: none -> 9.28 us  [local(): lax.all_to_all(training_features, 'y', split_axis=0, concat_axis=1, tiled...]
  transfers between devices with their start and end apart: 4 -> 12, of which waited for: 4 -> 7; matrix products, arithmetic and copies ran while one was open for 1% -> 2% of each run, Pallas kernels for 0% -> 8%
where the time goes in v1:
time: 193 us; the launch traced here: 190 us
  waiting for transfers between devices  84.4 us (44%)
  starting transfers between devices  39.1 us (20%)
  blocking collectives  24.3 us (13%)
  Pallas kernels  21.3 us (11%)
  between operations  13.6 us (7%)
  local copies, waits for them, and re-layouts  6.21 us (3%)
    ppermute x6, waiting for transfers between devices, gather_z(): other = lax.ppermute(held, 'z', [(i, i ^ distance) for i in range(8)])  64.3 us
    ppermute x6, starting transfers between devices, gather_z(): other = lax.ppermute(held, 'z', [(i, i ^ distance) for i in range(8)])  24.9 us
    ppermute x1, waiting for transfers between devices, local(): below = lax.ppermute(own, 'y', up)  19.4 us
    pallas_call x4, Pallas kernels, score_columns(): pl.pallas_call(kernel, out_shape=jax.ShapeDtypeStruct((rows, columns), jn...  18.2 us
    all_gather x1, blocking collectives, local(): rows = lax.all_gather(inverse_gram, 'y', axis=0, tiled=True)  15.1 us
    all_to_all x1, blocking collectives, local(): lax.all_to_all(training_features, 'y', split_axis=0, concat_axis=1, tiled...  9.28 us
    ppermute x1, starting transfers between devices, local(): far_second = lax.ppermute(above[4:], 'y', down)  5.12 us
    ppermute x1, starting transfers between devices, local(): above = lax.ppermute(own, 'y', down)  4.58 us
  transfers between devices with their start and end apart: 12, of which 7 were waited for; matrix products, arithmetic and copies ran while one was open for 2% of the time, Pallas kernels for 8%

profile of v1, /device:TPU:6, one launch (start us, length us, event | category | flops | bytes accessed | tf_op | source)
XLA Modules:
  0.0 190.0 jit_solution(12302833615177426031)
XLA Ops:
  6.5 0.0 all-gather.7.cloned.1.call-start
  6.5 15.1 %all_gather.17 = bf16[512,512]{1,0:T(8,128)(2,1)} all-gather(bf16[128,512]{1,0:T(8,128)(2,1)} %param.6), channel_id=1, replica_groups=mesh['z'=8,'y'=4,'x'=4,'core'=2,'row'=2] {'y'}, dimensions={0}, use_global_device_ids=true | all-gather | bytes 655360 | tf_op jit(solution)/shard_map/all_gather | solution.py:119
  21.6 0.0 all-gather.7.cloned.1.call-update
  21.6 0.0 all-gather.5.cloned.1.call-start
  21.7 0.7 all-gather.5.cloned.1.call-update
  22.4 9.3 %all_to_all.16 = bf16[4,128,128]{2,1,0:T(8,128)(2,1)S(1)} all-to-all(bf16[4,128,128]{2,1,0:T(8,128)(2,1)} %bitcast.24), channel_id=1, replica_groups=mesh['z'=8,'y'=4,'x'=4,'core'=2,'row'=2] {'y'}, dimensions={0} | all-to-all | bytes 262144 | tf_op jit(solution)/shard_map/all_to_all | solution.py:118
  31.7 0.1 copy.10
  31.8 0.1 broadcast_in_dim.22
  31.8 9.1 %collective-permute-start = (bf16[1,128,512]{2,1,0:T(8,128)(2,1)S(1)}, bf16[1,128,512]{2,1,0:T(8,128)(2,1)S(1)}, u32[]{:S(2)}, u32[]{:S(2)}) collective-permute-start(bf16[1,128,512]{2,1,0:T(8,128)(2,1)S(1)} %broadcast_in_dim.22), channel_id=1, source_target_pairs={{0,256},{64,320},{128,384},{192,448},{256,0},{320,64},{384,128},{4... | collective-permute-start | bytes 393224 | tf_op jit(solution)/shard_map/ppermute | solution.py:108
  40.9 8.3 %collective-permute-done = bf16[1,128,512]{2,1,0:T(8,128)(2,1)S(1)} collective-permute-done((bf16[1,128,512]{2,1,0:T(8,128)(2,1)S(1)}, bf16[1,128,512]{2,1,0:T(8,128)(2,1)S(1)}, u32[]{:S(2)}, u32[]{:S(2)}) %collective-permute-start) | collective-permute-done | bytes 131104 | tf_op jit(solution)/shard_map/ppermute | solution.py:108
  49.2 1.9 %collective-permute-start.1 = (bf16[2,128,512]{2,1,0:T(8,128)(2,1)S(1)}, bf16[2,128,512]{2,1,0:T(8,128)(2,1)S(1)}, u32[]{:S(2)}, u32[]{:S(2)}) collective-permute-start(bf16[2,128,512]{2,1,0:T(8,128)(2,1)S(1)} %pad_maximum_fusion.4), channel_id=1, source_target_pairs={{0,128},{64,192},{128,0},{192,64},{256,384},{320,448},{384,256},{4... | collective-permute-start | bytes 786440 | tf_op jit(solution)/shard_map/ppermute | solution.py:108
  51.1 10.9 %collective-permute-done.1 = bf16[2,128,512]{2,1,0:T(8,128)(2,1)S(1)} collective-permute-done((bf16[2,128,512]{2,1,0:T(8,128)(2,1)S(1)}, bf16[2,128,512]{2,1,0:T(8,128)(2,1)S(1)}, u32[]{:S(2)}, u32[]{:S(2)}) %collective-permute-start.1) | collective-permute-done | bytes 262176 | tf_op jit(solution)/shard_map/ppermute | solution.py:108
  62.0 0.1 pad_maximum_fusion.2
  62.1 1.9 %collective-permute-start.2 = (bf16[4,128,512]{2,1,0:T(8,128)(2,1)S(1)}, bf16[4,128,512]{2,1,0:T(8,128)(2,1)S(1)}, u32[]{:S(2)}, u32[]{:S(2)}) collective-permute-start(bf16[4,128,512]{2,1,0:T(8,128)(2,1)S(1)} %pad_maximum_fusion.2), channel_id=1, source_target_pairs={{0,64},{64,0},{128,192},{192,128},{256,320},{320,256},{384,448},{4... | collective-permute-start | bytes 1572872 | tf_op jit(solution)/shard_map/ppermute | solution.py:108
  64.0 0.7 broadcast_xor_fusion.s.slots
  64.7 11.0 %collective-permute-done.2 = bf16[4,128,512]{2,1,0:T(8,128)(2,1)S(1)} collective-permute-done((bf16[4,128,512]{2,1,0:T(8,128)(2,1)S(1)}, bf16[4,128,512]{2,1,0:T(8,128)(2,1)S(1)}, u32[]{:S(2)}, u32[]{:S(2)}) %collective-permute-start.2) | collective-permute-done | bytes 524320 | tf_op jit(solution)/shard_map/ppermute | solution.py:108
  75.7 0.1 pad_maximum_fusion.refs_1_
  75.8 0.0 all-gather.7.cloned.1.call-done
  75.8 0.0 copy-start.2
  75.8 2.2 %copy-done.2 = bf16[4096,512]{1,0:T(8,128)(2,1)S(1)} copy-done((bf16[4096,512]{1,0:T(8,128)(2,1)S(1)}, bf16[4096,512]{1,0:T(8,128)(2,1)}, u32[]{:S(2)}) %copy-start.2) | copy-done | bytes 4194328
  78.0 3.0 %kernel_matrix.1 = bf16[512,128]{1,0:T(8,128)(2,1)S(1)} custom-call(s32[8]{0:T(128)S(1)} %broadcast_xor_fusion.s.slots, bf16[8,512,512]{2,1,0:T(8,128)(2,1)S(1)} %bitcast.14, bf16[8,128,512]{2,1,0:T(8,128)(2,1)S(1)} %pad_maximum_fusion.refs_1_), custom_call_target="tpu_custom_call" | custom-call | flops 536870912 | bytes 5242880 | tf_op jit(solution)/shard_map/kernel_matrix/pallas_call | solution.py:31
  81.0 0.0 copy-start.3
  81.0 8.2 %collective-permute-start.3 = (bf16[1,512,128]{2,1,0:T(8,128)(2,1)S(1)}, bf16[1,512,128]{2,1,0:T(8,128)(2,1)S(1)}, u32[]{:S(2)}, u32[]{:S(2)}) collective-permute-start(bf16[1,512,128]{2,1,0:T(8,128)(2,1)S(1)} %bitcast.15), channel_id=1, source_target_pairs={{0,256},{64,320},{128,384},{192,448},{256,0},{320,64},{384,128},{4... | collective-permute-start | bytes 393224 | tf_op jit(solution)/shard_map/ppermute | solution.py:108
  89.2 11.0 %collective-permute-done.3 = bf16[1,512,128]{2,1,0:T(8,128)(2,1)S(1)} collective-permute-done((bf16[1,512,128]{2,1,0:T(8,128)(2,1)S(1)}, bf16[1,512,128]{2,1,0:T(8,128)(2,1)S(1)}, u32[]{:S(2)}, u32[]{:S(2)}) %collective-permute-start.3) | collective-permute-done | bytes 131104 | tf_op jit(solution)/shard_map/ppermute | solution.py:108
  100.3 1.9 %collective-permute-start.4 = (bf16[2,512,128]{2,1,0:T(8,128)(2,1)S(1)}, bf16[2,512,128]{2,1,0:T(8,128)(2,1)S(1)}, u32[]{:S(2)}, u32[]{:S(2)}) collective-permute-start(bf16[2,512,128]{2,1,0:T(8,128)(2,1)S(1)} %pad_maximum_fusion.5), channel_id=1, source_target_pairs={{0,128},{64,192},{128,0},{192,64},{256,384},{320,448},{384,256},{4... | collective-permute-start | bytes 786440 | tf_op jit(solution)/shard_map/ppermute | solution.py:108
  102.2 11.3 %collective-permute-done.4 = bf16[2,512,128]{2,1,0:T(8,128)(2,1)S(1)} collective-permute-done((bf16[2,512,128]{2,1,0:T(8,128)(2,1)S(1)}, bf16[2,512,128]{2,1,0:T(8,128)(2,1)S(1)}, u32[]{:S(2)}, u32[]{:S(2)}) %collective-permute-start.4) | collective-permute-done | bytes 262176 | tf_op jit(solution)/shard_map/ppermute | solution.py:108
  113.4 0.1 pad_maximum_fusion.3
  113.5 1.9 %collective-permute-start.5 = (bf16[4,512,128]{2,1,0:T(8,128)(2,1)S(1)}, bf16[4,512,128]{2,1,0:T(8,128)(2,1)S(1)}, u32[]{:S(2)}, u32[]{:S(2)}) collective-permute-start(bf16[4,512,128]{2,1,0:T(8,128)(2,1)S(1)} %pad_maximum_fusion.3), channel_id=1, source_target_pairs={{0,64},{64,0},{128,192},{192,128},{256,320},{320,256},{384,448},{4... | collective-permute-start | bytes 1572872 | tf_op jit(solution)/shard_map/ppermute | solution.py:108
  115.4 11.9 %collective-permute-done.5 = bf16[4,512,128]{2,1,0:T(8,128)(2,1)S(1)} collective-permute-done((bf16[4,512,128]{2,1,0:T(8,128)(2,1)S(1)}, bf16[4,512,128]{2,1,0:T(8,128)(2,1)S(1)}, u32[]{:S(2)}, u32[]{:S(2)}) %collective-permute-start.5) | collective-permute-done | bytes 524320 | tf_op jit(solution)/shard_map/ppermute | solution.py:108
  127.4 0.1 pad_maximum_fusion.1.refs_0_
  127.5 2.5 %collective-permute-start.6 = (bf16[8,512,128]{2,1,0:T(8,128)(2,1)S(1)}, bf16[8,512,128]{2,1,0:T(8,128)(2,1)S(1)}, u32[]{:S(2)}, u32[]{:S(2)}) collective-permute-start(bf16[8,512,128]{2,1,0:T(8,128)(2,1)S(1)} %pad_maximum_fusion.1.refs_0_), channel_id=1, source_target_pairs={{0,16},{16,32},{32,48},{48,0},{1,17},{17,33},{33,49},{49,1},{2,18}... | collective-permute-start | bytes 3145736 | tf_op jit(solution)/shard_map/ppermute | solution.py:129
  130.0 4.6 %collective-permute-start.8 = (bf16[8,512,128]{2,1,0:T(8,128)(2,1)S(1)}, bf16[8,512,128]{2,1,0:T(8,128)(2,1)S(1)}, u32[]{:S(2)}, u32[]{:S(2)}) collective-permute-start(bf16[8,512,128]{2,1,0:T(8,128)(2,1)S(1)} %pad_maximum_fusion.1.refs_0_), channel_id=1, source_target_pairs={{0,48},{16,0},{32,16},{48,32},{1,49},{17,1},{33,17},{49,33},{2,50}... | collective-permute-start | bytes 3145736 | tf_op jit(solution)/shard_map/ppermute | solution.py:130
  134.5 19.4 %collective-permute-done.6.refs_0_ = bf16[8,512,128]{2,1,0:T(8,128)(2,1)S(1)} collective-permute-done((bf16[8,512,128]{2,1,0:T(8,128)(2,1)S(1)}, bf16[8,512,128]{2,1,0:T(8,128)(2,1)S(1)}, u32[]{:S(2)}, u32[]{:S(2)}) %collective-permute-start.6) | collective-permute-done | bytes 1048608 | tf_op jit(solution)/shard_map/ppermute | solution.py:129
  153.9 0.8 slice.8
  154.7 1.9 %collective-permute-start.7 = (bf16[4,512,128]{2,1,0:T(8,128)(2,1)}, bf16[4,512,128]{2,1,0:T(8,128)(2,1)}, u32[]{:S(2)}, u32[]{:S(2)}) collective-permute-start(bf16[4,512,128]{2,1,0:T(8,128)(2,1)} %slice.8), channel_id=1, source_target_pairs={{0,16},{16,32},{32,48},{48,0},{1,17},{17,33},{33,49},{49,1},{2,18}... | collective-permute-start | bytes 1572872 | tf_op jit(solution)/shard_map/ppermute | solution.py:131
  156.7 0.0 collective-permute-done.8.refs_0_
  156.7 0.8 slice.9
  157.5 5.1 %collective-permute-start.9 = (bf16[4,512,128]{2,1,0:T(8,128)(2,1)}, bf16[4,512,128]{2,1,0:T(8,128)(2,1)}, u32[]{:S(2)}, u32[]{:S(2)}) collective-permute-start(bf16[4,512,128]{2,1,0:T(8,128)(2,1)} %slice.9), channel_id=1, source_target_pairs={{0,48},{16,0},{32,16},{48,32},{1,49},{17,1},{33,17},{49,33},{2,50}... | collective-permute-start | bytes 1572872 | tf_op jit(solution)/shard_map/ppermute | solution.py:132
  162.7 0.0 all-gather.5.cloned.1.call-done
  162.7 0.0 copy-done.3
  162.7 0.0 copy-start
  162.7 2.2 %copy-done = bf16[4096,512]{1,0:T(8,128)(2,1)S(1)} copy-done((bf16[4096,512]{1,0:T(8,128)(2,1)S(1)}, bf16[4096,512]{1,0:T(8,128)(2,1)}, u32[]{:S(2)}) %copy-start) | copy-done | bytes 4194328
  164.9 0.0 copy-start.1
  164.9 3.9 %score_columns.4.refs_2_ = f32[512,512]{1,0:T(8,128)} custom-call(s32[8]{0:T(128)S(1)} %broadcast_xor_fusion.s.slots, s32[1]{0:T(128)} %bitcast.9.place, bf16[8,512,512]{2,1,0:T(8,128)(2,1)S(1)} %bitcast.10, bf16[8,512,128]{2,1,0:T(8,128)(2,1)S(1)} %pad_maximum_fusion.1.refs_0_, f32[1,512]{1,0:T(1,128)S(1)} %bitcast.19), custom_call_target="tpu_custom_call" | custom-call | flops 536870912 | bytes 5242880 | tf_op jit(solution)/shard_map/score_columns/pallas_call | solution.py:86
  168.8 0.0 copy-done.1
  168.8 3.9 %score_columns.5.refs_2_ = f32[512,512]{1,0:T(8,128)} custom-call(s32[8]{0:T(128)S(1)} %broadcast_xor_fusion.s.slots, s32[1]{0:T(128)} %bitcast.8.place, bf16[8,512,512]{2,1,0:T(8,128)(2,1)S(1)} %bitcast.11, bf16[8,512,128]{2,1,0:T(8,128)(2,1)S(1)} %collective-permute-done.6.refs_0_, f32[1,512]{1,0:T(1,128)S(1)} %bitcast.20, ...), custom_call_target="tpu_custom_call", output_to_operand_aliasing={{}: (5, {})} | custom-call | flops 536870912 | bytes 5242880 | tf_op jit(solution)/shard_map/score_columns/pallas_call | solution.py:86
  172.7 3.9 %score_columns.6.refs_3_ = f32[512,512]{1,0:T(8,128)} custom-call(s32[8]{0:T(128)S(1)} %broadcast_xor_fusion.s.slots, s32[1]{0:T(128)} %bitcast.7.place, bf16[8,512,512]{2,1,0:T(8,128)(2,1)S(1)} %bitcast.12, bf16[8,512,128]{2,1,0:T(8,128)(2,1)S(1)} %collective-permute-done.8.refs_0_, f32[1,512]{1,0:T(1,128)S(1)} %bitcast.21, ...), custom_call_target="tpu_custom_call", output_to_operand_aliasing={{}: (5, {})} | custom-call | flops 536870912 | bytes 5242880 | tf_op jit(solution)/shard_map/score_columns/pallas_call | solution.py:86
  176.5 0.0 collective-permute-done.7.refs_0_
  176.5 0.0 collective-permute-done.9.refs_1_
  176.5 6.6 %score_columns.7 = f32[512,512]{1,0:T(8,128)} custom-call(s32[8]{0:T(128)S(1)} %broadcast_xor_fusion.s.slots, s32[1]{0:T(128)} %bitcast.place, bf16[8,512,512]{2,1,0:T(8,128)(2,1)S(1)} %bitcast.13, bf16[4,512,128]{2,1,0:T(8,128)(2,1)} %collective-permute-done.7.refs_0_, ...), custom_call_target="tpu_custom_call", output_to_operand_aliasing={{}: (6, {})} | custom-call | flops 536870912 | bytes 5242880 | tf_op jit(solution)/shard_map/score_columns/pallas_call | solution.py:86
  (2 shorter events, 0.1 us)
Async XLA Ops:
  6.5 69.3 %all-gather.7.cloned.1.call-start = ((), (), s32[]{:S(2)}) async-start(), calls=%async_computation.2 | async-start | bytes 4718592 | tf_op jit(solution)/shard_map/all_gather | solution.py:120
  21.6 141.1 %all-gather.5.cloned.1.call-start = ((), (), s32[]{:S(2)}) async-start(), calls=%async_computation.1 | async-start | bytes 4718592 | tf_op jit(solution)/shard_map/all_gather | solution.py:121
  31.8 17.4 %collective-permute-start = (bf16[1,128,512]{2,1,0:T(8,128)(2,1)S(1)}, bf16[1,128,512]{2,1,0:T(8,128)(2,1)S(1)}, u32[]{:S(2)}, u32[]{:S(2)}) collective-permute-start(bf16[1,128,512]{2,1,0:T(8,128)(2,1)S(1)} %broadcast_in_dim.22), channel_id=1, source_target_pairs={{0,256},{64,320},{128,384},{192,448},{256,0},{320,64},{384,128},{4... | collective-permute-start | bytes 393224 | tf_op jit(solution)/shard_map/ppermute | solution.py:108
  49.2 12.8 %collective-permute-start.1 = (bf16[2,128,512]{2,1,0:T(8,128)(2,1)S(1)}, bf16[2,128,512]{2,1,0:T(8,128)(2,1)S(1)}, u32[]{:S(2)}, u32[]{:S(2)}) collective-permute-start(bf16[2,128,512]{2,1,0:T(8,128)(2,1)S(1)} %pad_maximum_fusion.4), channel_id=1, source_target_pairs={{0,128},{64,192},{128,0},{192,64},{256,384},{320,448},{384,256},{4... | collective-permute-start | bytes 786440 | tf_op jit(solution)/shard_map/ppermute | solution.py:108
  62.1 13.6 %collective-permute-start.2 = (bf16[4,128,512]{2,1,0:T(8,128)(2,1)S(1)}, bf16[4,128,512]{2,1,0:T(8,128)(2,1)S(1)}, u32[]{:S(2)}, u32[]{:S(2)}) collective-permute-start(bf16[4,128,512]{2,1,0:T(8,128)(2,1)S(1)} %pad_maximum_fusion.2), channel_id=1, source_target_pairs={{0,64},{64,0},{128,192},{192,128},{256,320},{320,256},{384,448},{4... | collective-permute-start | bytes 1572872 | tf_op jit(solution)/shard_map/ppermute | solution.py:108
  75.8 2.2 %copy-start.2 = (bf16[4096,512]{1,0:T(8,128)(2,1)S(1)}, bf16[4096,512]{1,0:T(8,128)(2,1)}, u32[]{:S(2)}) copy-start(bf16[4096,512]{1,0:T(8,128)(2,1)} %all-gather.7.cloned.1.call-done) | copy-start | bytes 12582916
  81.0 81.7 %copy-start.3 = (f32[512]{0:T(512)S(1)}, f32[512]{0:T(512)}, u32[]{:S(2)}) copy-start(f32[512]{0:T(512)} %param.8) | copy-start | bytes 6148
  81.0 19.2 %collective-permute-start.3 = (bf16[1,512,128]{2,1,0:T(8,128)(2,1)S(1)}, bf16[1,512,128]{2,1,0:T(8,128)(2,1)S(1)}, u32[]{:S(2)}, u32[]{:S(2)}) collective-permute-start(bf16[1,512,128]{2,1,0:T(8,128)(2,1)S(1)} %bitcast.15), channel_id=1, source_target_pairs={{0,256},{64,320},{128,384},{192,448},{256,0},{320,64},{384,128},{4... | collective-permute-start | bytes 393224 | tf_op jit(solution)/shard_map/ppermute | solution.py:108
  100.3 13.2 %collective-permute-start.4 = (bf16[2,512,128]{2,1,0:T(8,128)(2,1)S(1)}, bf16[2,512,128]{2,1,0:T(8,128)(2,1)S(1)}, u32[]{:S(2)}, u32[]{:S(2)}) collective-permute-start(bf16[2,512,128]{2,1,0:T(8,128)(2,1)S(1)} %pad_maximum_fusion.5), channel_id=1, source_target_pairs={{0,128},{64,192},{128,0},{192,64},{256,384},{320,448},{384,256},{4... | collective-permute-start | bytes 786440 | tf_op jit(solution)/shard_map/ppermute | solution.py:108
  113.5 13.9 %collective-permute-start.5 = (bf16[4,512,128]{2,1,0:T(8,128)(2,1)S(1)}, bf16[4,512,128]{2,1,0:T(8,128)(2,1)S(1)}, u32[]{:S(2)}, u32[]{:S(2)}) collective-permute-start(bf16[4,512,128]{2,1,0:T(8,128)(2,1)S(1)} %pad_maximum_fusion.3), channel_id=1, source_target_pairs={{0,64},{64,0},{128,192},{192,128},{256,320},{320,256},{384,448},{4... | collective-permute-start | bytes 1572872 | tf_op jit(solution)/shard_map/ppermute | solution.py:108
  127.5 26.4 %collective-permute-start.6 = (bf16[8,512,128]{2,1,0:T(8,128)(2,1)S(1)}, bf16[8,512,128]{2,1,0:T(8,128)(2,1)S(1)}, u32[]{:S(2)}, u32[]{:S(2)}) collective-permute-start(bf16[8,512,128]{2,1,0:T(8,128)(2,1)S(1)} %pad_maximum_fusion.1.refs_0_), channel_id=1, source_target_pairs={{0,16},{16,32},{32,48},{48,0},{1,17},{17,33},{33,49},{49,1},{2,18}... | collective-permute-start | bytes 3145736 | tf_op jit(solution)/shard_map/ppermute | solution.py:129
  130.0 26.7 %collective-permute-start.8 = (bf16[8,512,128]{2,1,0:T(8,128)(2,1)S(1)}, bf16[8,512,128]{2,1,0:T(8,128)(2,1)S(1)}, u32[]{:S(2)}, u32[]{:S(2)}) collective-permute-start(bf16[8,512,128]{2,1,0:T(8,128)(2,1)S(1)} %pad_maximum_fusion.1.refs_0_), channel_id=1, source_target_pairs={{0,48},{16,0},{32,16},{48,32},{1,49},{17,1},{33,17},{49,33},{2,50}... | collective-permute-start | bytes 3145736 | tf_op jit(solution)/shard_map/ppermute | solution.py:130
  154.7 21.8 %collective-permute-start.7 = (bf16[4,512,128]{2,1,0:T(8,128)(2,1)}, bf16[4,512,128]{2,1,0:T(8,128)(2,1)}, u32[]{:S(2)}, u32[]{:S(2)}) collective-permute-start(bf16[4,512,128]{2,1,0:T(8,128)(2,1)} %slice.8), channel_id=1, source_target_pairs={{0,16},{16,32},{32,48},{48,0},{1,17},{17,33},{33,49},{49,1},{2,18}... | collective-permute-start | bytes 1572872 | tf_op jit(solution)/shard_map/ppermute | solution.py:131
  157.5 19.0 %collective-permute-start.9 = (bf16[4,512,128]{2,1,0:T(8,128)(2,1)}, bf16[4,512,128]{2,1,0:T(8,128)(2,1)}, u32[]{:S(2)}, u32[]{:S(2)}) collective-permute-start(bf16[4,512,128]{2,1,0:T(8,128)(2,1)} %slice.9), channel_id=1, source_target_pairs={{0,48},{16,0},{32,16},{48,32},{1,49},{17,1},{33,17},{49,33},{2,50}... | collective-permute-start | bytes 1572872 | tf_op jit(solution)/shard_map/ppermute | solution.py:132
  162.7 2.2 %copy-start = (bf16[4096,512]{1,0:T(8,128)(2,1)S(1)}, bf16[4096,512]{1,0:T(8,128)(2,1)}, u32[]{:S(2)}) copy-start(bf16[4096,512]{1,0:T(8,128)(2,1)} %all-gather.5.cloned.1.call-done) | copy-start | bytes 12582916
  164.9 3.9 %copy-start.1 = (bf16[4096,512]{1,0:T(8,128)(2,1)S(1)}, bf16[4096,512]{1,0:T(8,128)(2,1)}, u32[]{:S(2)}) copy-start(bf16[4096,512]{1,0:T(8,128)(2,1)} %all-gather.5.cloned.1.call-done) | copy-start | bytes 12582916
Sparse Core Ops, SparseCore 0:
  21.7 40.7 all-gather.6
  64.7 39.7 all-gather.4

commit v2 on v1

v2 whole, which is shorter than its diff:
```python
import jax
import jax.numpy as jnp
from jax import lax
from jax.experimental import pallas as pl
from jax.experimental.pallas import tpu as pltpu
from jax.sharding import Mesh, PartitionSpec as P

NZ, NY, CHUNKS = 8, 4, 2
NT_DIMS = (((1,), (1,)), ((), ()))
RELATIVE = (0, 4, 2, 6, 1, 5, 3, 7)
VMEM_LIMIT = 24 * 1024 * 1024


def kernel_matrix(slots, inverse_gram, training):
    n, t, depth = training.shape
    rows = inverse_gram.shape[1]

    def kernel(slots, gram_ref, training_ref, out_ref, total):
        step = pl.program_id(0)

        @pl.when(step == 0)
        def _():
            total[...] = jnp.zeros_like(total)

        total[...] += lax.dot_general(training_ref[0], gram_ref[0], NT_DIMS, preferred_element_type=jnp.float32)

        @pl.when(step == n - 1)
        def _():
            out_ref[...] = total[...].astype(out_ref.dtype)

    return pl.pallas_call(
        kernel,
        out_shape=jax.ShapeDtypeStruct((t, rows), jnp.bfloat16),
        grid_spec=pltpu.PrefetchScalarGridSpec(
            num_scalar_prefetch=1,
            grid=(n,),
            in_specs=[
                pl.BlockSpec((1, rows, depth), lambda s, slots: (slots[s], 0, 0)),
                pl.BlockSpec((1, t, depth), lambda s, slots: (s, 0, 0)),
            ],
            out_specs=pl.BlockSpec((t, rows), lambda s, slots: (0, 0)),
            scratch_shapes=[pltpu.VMEM((t, rows), jnp.float32)],
        ),
        compiler_params=pltpu.CompilerParams(vmem_limit_bytes=VMEM_LIMIT),
        cost_estimate=pl.CostEstimate(
            flops=2 * n * rows * t * depth, bytes_accessed=2 * n * depth * (rows + t), transcendentals=0
        ),
        name="kernel_matrix",
    )(slots, inverse_gram, training)


def score_columns(slots, place, query, blocks, weight, out, chunk, columns):
    n, rows, depth = query.shape
    ny, _, t, _ = blocks.shape
    width = ny * t

    def kernel(slots, place, query_ref, blocks_ref, weight_ref, *refs):
        out_ref, total = refs[-2:]
        step = pl.program_id(0)

        @pl.when(step == 0)
        def _():
            total[...] = jnp.zeros_like(total)

        ordered = jnp.concatenate([blocks_ref[lax.rem(p - place[0] + ny, ny), 0] for p in range(ny)], axis=0)
        total[...] += lax.dot_general(query_ref[0], ordered, NT_DIMS, preferred_element_type=jnp.float32)

        @pl.when(step == n - 1)
        def _():
            out_ref[...] = total[...] * weight_ref[...]

    operands = [slots, place, query, blocks, weight] + ([] if out is None else [out])
    in_specs = [
        pl.BlockSpec((1, rows, depth), lambda s, slots, place: (slots[s], 0, 0)),
        pl.BlockSpec((ny, 1, t, depth), lambda s, slots, place: (0, s, 0, 0)),
        pl.BlockSpec((1, width), lambda s, slots, place: (0, chunk)),
    ]
    if out is not None:
        in_specs.append(pl.BlockSpec(memory_space=pl.ANY))
    return pl.pallas_call(
        kernel,
        out_shape=jax.ShapeDtypeStruct((rows, columns), jnp.float32),
        grid_spec=pltpu.PrefetchScalarGridSpec(
            num_scalar_prefetch=2,
            grid=(n,),
            in_specs=in_specs,
            out_specs=pl.BlockSpec((rows, width), lambda s, slots, place: (0, chunk)),
            scratch_shapes=[pltpu.VMEM((rows, width), jnp.float32)],
        ),
        input_output_aliases={} if out is None else {len(operands) - 1: 0},
        compiler_params=pltpu.CompilerParams(vmem_limit_bytes=VMEM_LIMIT),
        cost_estimate=pl.CostEstimate(
            flops=2 * n * rows * width * depth, bytes_accessed=2 * n * depth * (rows + width), transcendentals=0
        ),
        name="score_columns",
    )(*operands)


def exchange(held, distance):
    other = lax.ppermute(held, "z", [(i, i ^ distance) for i in range(NZ)])
    return jnp.concatenate([held, other], axis=0)


def gather_y(own):
    up = [(i, (i + 1) % NY) for i in range(NY)]
    down = [(i, (i - 1) % NY) for i in range(NY)]
    half = own.shape[0] // 2
    below = lax.ppermute(own, "y", up)
    above = lax.ppermute(own, "y", down)
    far = jnp.concatenate(
        [lax.ppermute(below[:half], "y", up), lax.ppermute(above[half:], "y", down)], axis=0
    )
    return jnp.stack([own, above, far, below])


def local(query_features, inverse_gram, training_features, residual_weight):
    slots = lax.axis_index("z") ^ jnp.array(RELATIVE, jnp.int32)
    place = lax.axis_index("y").astype(jnp.int32)[None]
    columns, lanes = training_features.shape
    rows, depth = inverse_gram.shape
    t = columns // (CHUNKS * NY)

    gram_tiles = inverse_gram.reshape(rows, NY, lanes).transpose(1, 0, 2).reshape(NY * rows, lanes)
    pieces = training_features.reshape(CHUNKS, NY, t, lanes).transpose(1, 0, 2, 3).reshape(NY, CHUNKS * t, lanes)
    sent = jnp.concatenate([pieces, jnp.broadcast_to(gram_tiles, (NY, *gram_tiles.shape))], axis=1)
    got = lax.all_to_all(sent, "y", split_axis=0, concat_axis=0, tiled=True)
    training = got[:, : CHUNKS * t].reshape(NY, CHUNKS, t, lanes).transpose(1, 2, 0, 3).reshape(CHUNKS, t, NY * lanes)
    gram_rows = got[:, CHUNKS * t :].reshape(NY, NY, rows, lanes).transpose(0, 2, 1, 3).reshape(NY * rows, depth)

    gram = lax.all_gather(gram_rows, ("x", "core"), axis=0)
    query = lax.all_gather(query_features, ("x", "core"), axis=0)

    weight = residual_weight[None, :]
    held = [training[c][None] for c in range(CHUNKS)]
    for distance in (4, 2, 1):
        held = [exchange(h, distance) for h in held]
    held = [kernel_matrix(slots, gram, h)[None] for h in held]
    for distance in (4, 2, 1):
        held = [exchange(h, distance) for h in held]
    out = None
    for c, h in enumerate(held):
        out = score_columns(slots, place, query, gather_y(h), weight, out, c, columns)
    return out


def solution(mesh):
    fine = Mesh(mesh.devices.reshape(NZ, NY, 4, 2, 2), ("z", "y", "x", "core", "row"))
    pb, ta = ("z", "y"), ("x", "core")
    placed = (P(pb, ta), P(pb, ta), P(("row", *ta), pb), P(("row", *ta)))
    return jax.shard_map(
        local, mesh=fine, in_specs=placed, out_specs=P(pb, ("row", *ta)), check_vma=False
    )
```

time: 193 us -> 180 us (0.933)
  waiting for transfers between devices: 84.4 us -> 32.8 us
  starting transfers between devices: 39.1 us -> 84.9 us
  blocking collectives: 24.3 us -> 15.1 us
  Pallas kernels: 21.3 us -> 14.6 us
  local copies, waits for them, and re-layouts: 6.21 us -> 11.5 us
  other arithmetic: 1.03 us -> 5.76 us
    ppermute x10 -> x20, waiting for transfers between devices: 83.7 us -> 31.3 us  [the longest x12 18.2 us: exchange(): other = lax.ppermute(held, 'z', [(i, i ^ distance) for i in range(NZ)])]
    ppermute x10 -> x20, starting transfers between devices: 39 us -> 84.8 us  [the longest x12 55.9 us: exchange(): other = lax.ppermute(held, 'z', [(i, i ^ distance) for i in range(NZ)])]
    all_gather x1 -> x0, blocking collectives: 15.1 us -> none  [local(): rows = lax.all_gather(inverse_gram, 'y', axis=0, tiled=True)]
    pallas_call x4 -> x2, Pallas kernels: 18.2 us -> 8.8 us  [score_columns(): pl.pallas_call(kernel, out_shape=jax.ShapeDtypeStruct((rows, columns), jn...]
    all_to_all x1, blocking collectives: 9.28 us -> 15.1 us  [local(): got = lax.all_to_all(sent, 'y', split_axis=0, concat_axis=0, tiled=True)]
    another operation x0 -> x6, other arithmetic: none -> 5.43 us  [gather_y(): return jnp.stack([own, above, far, below])]
    unnamed x8 -> x23, local copies, waits for them, and re-layouts: 4.37 us -> 8.61 us
    pallas_call x1 -> x2, Pallas kernels: 3.03 us -> 5.76 us  [kernel_matrix(): pl.pallas_call(kernel, out_shape=jax.ShapeDtypeStruct((t, rows), jnp.bflo...]
  transfers between devices with their start and end apart: 12 -> 22, of which waited for: 7 -> 13; matrix products, arithmetic and copies ran while one was open for 2% -> 3% of each run, Pallas kernels for 8% -> 3%
where the time goes in v2:
time: 180 us; the launch traced here: 179 us
  starting transfers between devices  84.9 us (47%)
  waiting for transfers between devices  32.8 us (18%)
  blocking collectives  15.1 us (8%)
  Pallas kernels  14.6 us (8%)
  between operations  13.9 us (8%)
  local copies, waits for them, and re-layouts  11.5 us (6%)
  other arithmetic  5.76 us (3%)
    ppermute x12, starting transfers between devices, exchange(): other = lax.ppermute(held, 'z', [(i, i ^ distance) for i in range(NZ)])  55.9 us
    ppermute x12, waiting for transfers between devices, exchange(): other = lax.ppermute(held, 'z', [(i, i ^ distance) for i in range(NZ)])  18.2 us
    all_to_all x1, blocking collectives, local(): got = lax.all_to_all(sent, 'y', split_axis=0, concat_axis=0, tiled=True)  15.1 us
    ppermute x2, starting transfers between devices, gather_y(): lax.ppermute(above[half:], 'y', down)  11.2 us
    ppermute x2, starting transfers between devices, gather_y(): above = lax.ppermute(own, 'y', down)  10 us
    pallas_call x2, Pallas kernels, score_columns(): pl.pallas_call(kernel, out_shape=jax.ShapeDtypeStruct((rows, columns), jn...  8.8 us
    unnamed x23, local copies, waits for them, and re-layouts  8.61 us
    ppermute x2, waiting for transfers between devices, gather_y(): lax.ppermute(below[:half], 'y', up)  6.63 us
  transfers between devices with their start and end apart: 22, of which 13 were waited for; matrix products, arithmetic and copies ran while one was open for 3% of the time, Pallas kernels for 3%

profile of v2, /device:TPU:6, one launch (start us, length us, event | category | flops | bytes accessed | tf_op | source)
XLA Modules:
  0.0 178.5 jit_solution(4123844210171390920)
XLA Ops:
  6.5 1.0 copy.19
  7.6 0.1 copy.20
  7.7 0.9 copy.18
  8.6 0.1 broadcast_in_dim.16
  8.8 15.1 %all_to_all.5 = bf16[4,640,128]{2,1,0:T(8,128)(2,1)S(1)} all-to-all(bf16[4,640,128]{2,1,0:T(8,128)(2,1)S(1)} %pad_maximum_fusion.2), channel_id=1, replica_groups=mesh['z'=8,'y'=4,'x'=4,'core'=2,'row'=2] {'y'}, dimensions={0} | all-to-all | bytes 1310720 | tf_op jit(solution)/shard_map/all_to_all | solution.py:126
  23.9 0.4 copy.21
  24.4 1.0 all_gather_reshape.3
  25.4 0.0 all-gather.4.cloned.1.call-update
  25.4 0.0 all-gather.6.cloned.1.call-start
  25.4 0.7 all-gather.6.cloned.1.call-update
  26.1 0.1 copy.24
  26.4 9.1 %collective-permute-start = (bf16[1,64,512]{2,1,0:T(8,128)(2,1)S(1)}, bf16[1,64,512]{2,1,0:T(8,128)(2,1)S(1)}, u32[]{:S(2)}, u32[]{:S(2)}) collective-permute-start(bf16[1,64,512]{2,1,0:T(8,128)(2,1)S(1)} %slice.33), channel_id=1, source_target_pairs={{0,256},{64,320},{128,384},{192,448},{256,0},{320,64},{384,128},{4... | collective-permute-start | bytes 196616 | tf_op jit(solution)/shard_map/ppermute | solution.py:100
  35.5 1.9 %collective-permute-start.10 = (bf16[1,64,512]{2,1,0:T(8,128)(2,1)S(1)}, bf16[1,64,512]{2,1,0:T(8,128)(2,1)S(1)}, u32[]{:S(2)}, u32[]{:S(2)}) collective-permute-start(bf16[1,64,512]{2,1,0:T(8,128)(2,1)S(1)} %slice.37), channel_id=1, source_target_pairs={{0,256},{64,320},{128,384},{192,448},{256,0},{320,64},{384,128},{4... | collective-permute-start | bytes 196616 | tf_op jit(solution)/shard_map/ppermute | solution.py:100
  37.4 0.3 collective-permute-done
  37.7 8.5 %collective-permute-start.1 = (bf16[2,64,512]{2,1,0:T(8,128)(2,1)S(1)}, bf16[2,64,512]{2,1,0:T(8,128)(2,1)S(1)}, u32[]{:S(2)}, u32[]{:S(2)}) collective-permute-start(bf16[2,64,512]{2,1,0:T(8,128)(2,1)S(1)} %pad_maximum_fusion.11), channel_id=1, source_target_pairs={{0,128},{64,192},{128,0},{192,64},{256,384},{320,448},{384,256},{4... | collective-permute-start | bytes 393224 | tf_op jit(solution)/shard_map/ppermute | solution.py:100
  46.3 2.2 %collective-permute-done.10 = bf16[1,64,512]{2,1,0:T(8,128)(2,1)S(1)} collective-permute-done((bf16[1,64,512]{2,1,0:T(8,128)(2,1)S(1)}, bf16[1,64,512]{2,1,0:T(8,128)(2,1)S(1)}, u32[]{:S(2)}, u32[]{:S(2)}) %collective-permute-start.10) | collective-permute-done | bytes 65568 | tf_op jit(solution)/shard_map/ppermute | solution.py:100
  48.5 2.3 %collective-permute-start.11 = (bf16[2,64,512]{2,1,0:T(8,128)(2,1)S(1)}, bf16[2,64,512]{2,1,0:T(8,128)(2,1)S(1)}, u32[]{:S(2)}, u32[]{:S(2)}) collective-permute-start(bf16[2,64,512]{2,1,0:T(8,128)(2,1)S(1)} %pad_maximum_fusion.13), channel_id=1, source_target_pairs={{0,128},{64,192},{128,0},{192,64},{256,384},{320,448},{384,256},{4... | collective-permute-start | bytes 393224 | tf_op jit(solution)/shard_map/ppermute | solution.py:100
  50.8 0.0 collective-permute-done.1
  50.9 7.0 %collective-permute-start.2 = (bf16[4,64,512]{2,1,0:T(8,128)(2,1)S(1)}, bf16[4,64,512]{2,1,0:T(8,128)(2,1)S(1)}, u32[]{:S(2)}, u32[]{:S(2)}) collective-permute-start(bf16[4,64,512]{2,1,0:T(8,128)(2,1)S(1)} %pad_maximum_fusion.7), channel_id=1, source_target_pairs={{0,64},{64,0},{128,192},{192,128},{256,320},{320,256},{384,448},{4... | collective-permute-start | bytes 786440 | tf_op jit(solution)/shard_map/ppermute | solution.py:100
  57.9 0.6 collective-permute-done.11
  58.5 2.1 %collective-permute-start.12 = (bf16[4,64,512]{2,1,0:T(8,128)(2,1)S(1)}, bf16[4,64,512]{2,1,0:T(8,128)(2,1)S(1)}, u32[]{:S(2)}, u32[]{:S(2)}) collective-permute-start(bf16[4,64,512]{2,1,0:T(8,128)(2,1)S(1)} %pad_maximum_fusion.9), channel_id=1, source_target_pairs={{0,64},{64,0},{128,192},{192,128},{256,320},{320,256},{384,448},{4... | collective-permute-start | bytes 786440 | tf_op jit(solution)/shard_map/ppermute | solution.py:100
  60.6 4.4 %collective-permute-done.2 = bf16[4,64,512]{2,1,0:T(8,128)(2,1)S(1)} collective-permute-done((bf16[4,64,512]{2,1,0:T(8,128)(2,1)S(1)}, bf16[4,64,512]{2,1,0:T(8,128)(2,1)S(1)}, u32[]{:S(2)}, u32[]{:S(2)}) %collective-permute-start.2) | collective-permute-done | bytes 262176 | tf_op jit(solution)/shard_map/ppermute | solution.py:100
  65.0 0.1 pad_maximum_fusion.3.training_ref
  65.0 0.8 all-gather.4.cloned.1.call-done.gram_ref
  65.8 2.2 %copy-done.1 = bf16[8,512,512]{2,1,0:T(8,128)(2,1)S(1)} copy-done((bf16[8,512,512]{2,1,0:T(8,128)(2,1)S(1)}, bf16[8,512,512]{2,1,0:T(8,128)(2,1)}, u32[]{:S(2)}) %copy-start.1) | copy-done | bytes 4194328
  68.0 2.9 %kernel_matrix.2 = bf16[64,512]{1,0:T(8,128)(2,1)S(1)} custom-call(s32[8]{0:T(128)S(1)} %broadcast_xor_fusion.slots, bf16[8,512,512]{2,1,0:T(8,128)(2,1)S(1)} %copy-done.1, bf16[8,64,512]{2,1,0:T(8,128)(2,1)S(1)} %pad_maximum_fusion.3.training_ref), custom_call_target="tpu_custom_call" | custom-call | flops 268435456 | bytes 4718592 | tf_op jit(solution)/shard_map/kernel_matrix/pallas_call | solution.py:31
  70.9 7.6 %collective-permute-start.3 = (bf16[1,64,512]{2,1,0:T(8,128)(2,1)S(1)}, bf16[1,64,512]{2,1,0:T(8,128)(2,1)S(1)}, u32[]{:S(2)}, u32[]{:S(2)}) collective-permute-start(bf16[1,64,512]{2,1,0:T(8,128)(2,1)S(1)} %bitcast.38), channel_id=1, source_target_pairs={{0,256},{64,320},{128,384},{192,448},{256,0},{320,64},{384,128},{4... | collective-permute-start | bytes 196616 | tf_op jit(solution)/shard_map/ppermute | solution.py:100
  78.6 0.1 pad_maximum_fusion.5.training_ref
  78.6 2.9 %kernel_matrix.3 = bf16[64,512]{1,0:T(8,128)(2,1)S(1)} custom-call(s32[8]{0:T(128)S(1)} %broadcast_xor_fusion.slots, bf16[8,512,512]{2,1,0:T(8,128)(2,1)S(1)} %copy-done.1, bf16[8,64,512]{2,1,0:T(8,128)(2,1)S(1)} %pad_maximum_fusion.5.training_ref), custom_call_target="tpu_custom_call" | custom-call | flops 268435456 | bytes 4718592 | tf_op jit(solution)/shard_map/kernel_matrix/pallas_call | solution.py:31
  81.5 2.1 %collective-permute-start.13 = (bf16[1,64,512]{2,1,0:T(8,128)(2,1)S(1)}, bf16[1,64,512]{2,1,0:T(8,128)(2,1)S(1)}, u32[]{:S(2)}, u32[]{:S(2)}) collective-permute-start(bf16[1,64,512]{2,1,0:T(8,128)(2,1)S(1)} %bitcast.34), channel_id=1, source_target_pairs={{0,256},{64,320},{128,384},{192,448},{256,0},{320,64},{384,128},{4... | collective-permute-start | bytes 196616 | tf_op jit(solution)/shard_map/ppermute | solution.py:100
  83.6 1.6 collective-permute-done.3
  85.3 2.9 %collective-permute-start.4 = (bf16[2,64,512]{2,1,0:T(8,128)(2,1)S(1)}, bf16[2,64,512]{2,1,0:T(8,128)(2,1)S(1)}, u32[]{:S(2)}, u32[]{:S(2)}) collective-permute-start(bf16[2,64,512]{2,1,0:T(8,128)(2,1)S(1)} %pad_maximum_fusion.12), channel_id=1, source_target_pairs={{0,128},{64,192},{128,0},{192,64},{256,384},{320,448},{384,256},{4... | collective-permute-start | bytes 393224 | tf_op jit(solution)/shard_map/ppermute | solution.py:100
  88.2 7.3 %collective-permute-done.13 = bf16[1,64,512]{2,1,0:T(8,128)(2,1)S(1)} collective-permute-done((bf16[1,64,512]{2,1,0:T(8,128)(2,1)S(1)}, bf16[1,64,512]{2,1,0:T(8,128)(2,1)S(1)}, u32[]{:S(2)}, u32[]{:S(2)}) %collective-permute-start.13) | collective-permute-done | bytes 65568 | tf_op jit(solution)/shard_map/ppermute | solution.py:100
  95.5 1.9 %collective-permute-start.14 = (bf16[2,64,512]{2,1,0:T(8,128)(2,1)S(1)}, bf16[2,64,512]{2,1,0:T(8,128)(2,1)S(1)}, u32[]{:S(2)}, u32[]{:S(2)}) collective-permute-start(bf16[2,64,512]{2,1,0:T(8,128)(2,1)S(1)} %pad_maximum_fusion.14), channel_id=1, source_target_pairs={{0,128},{64,192},{128,0},{192,64},{256,384},{320,448},{384,256},{4... | collective-permute-start | bytes 393224 | tf_op jit(solution)/shard_map/ppermute | solution.py:100
  97.5 5.2 %collective-permute-start.5 = (bf16[4,64,512]{2,1,0:T(8,128)(2,1)S(1)}, bf16[4,64,512]{2,1,0:T(8,128)(2,1)S(1)}, u32[]{:S(2)}, u32[]{:S(2)}) collective-permute-start(bf16[4,64,512]{2,1,0:T(8,128)(2,1)S(1)} %pad_maximum_fusion.8), channel_id=1, source_target_pairs={{0,64},{64,0},{128,192},{192,128},{256,320},{320,256},{384,448},{4... | collective-permute-start | bytes 786440 | tf_op jit(solution)/shard_map/ppermute | solution.py:100
  102.7 0.7 collective-permute-done.14
  103.4 5.3 %collective-permute-start.15 = (bf16[4,64,512]{2,1,0:T(8,128)(2,1)S(1)}, bf16[4,64,512]{2,1,0:T(8,128)(2,1)S(1)}, u32[]{:S(2)}, u32[]{:S(2)}) collective-permute-start(bf16[4,64,512]{2,1,0:T(8,128)(2,1)S(1)} %pad_maximum_fusion.10), channel_id=1, source_target_pairs={{0,64},{64,0},{128,192},{192,128},{256,320},{320,256},{384,448},{4... | collective-permute-start | bytes 786440 | tf_op jit(solution)/shard_map/ppermute | solution.py:100
  108.7 1.1 collective-permute-done.5
  109.8 0.1 fusion.1
  109.9 4.9 %collective-permute-start.6 = (bf16[8,64,512]{2,1,0:T(8,128)(2,1)S(1)}, bf16[8,64,512]{2,1,0:T(8,128)(2,1)S(1)}, u32[]{:S(2)}, u32[]{:S(2)}) collective-permute-start(bf16[8,64,512]{2,1,0:T(8,128)(2,1)S(1)} %get-tuple-element.8), channel_id=1, source_target_pairs={{0,48},{16,0},{32,16},{48,32},{1,49},{17,1},{33,17},{49,33},{2,50}... | collective-permute-start | bytes 1572872 | tf_op jit(solution)/shard_map/ppermute | solution.py:109
  114.8 1.9 %collective-permute-start.7 = (bf16[8,64,512]{2,1,0:T(8,128)(2,1)S(1)}, bf16[8,64,512]{2,1,0:T(8,128)(2,1)S(1)}, u32[]{:S(2)}, u32[]{:S(2)}) collective-permute-start(bf16[8,64,512]{2,1,0:T(8,128)(2,1)S(1)} %get-tuple-element.8), channel_id=1, source_target_pairs={{0,16},{16,32},{32,48},{48,0},{1,17},{17,33},{33,49},{49,1},{2,18}... | collective-permute-start | bytes 1572872 | tf_op jit(solution)/shard_map/ppermute | solution.py:108
  116.7 0.1 fusion
  116.8 5.1 %collective-permute-start.16 = (bf16[8,64,512]{2,1,0:T(8,128)(2,1)S(1)}, bf16[8,64,512]{2,1,0:T(8,128)(2,1)S(1)}, u32[]{:S(2)}, u32[]{:S(2)}) collective-permute-start(bf16[8,64,512]{2,1,0:T(8,128)(2,1)S(1)} %get-tuple-element.6), channel_id=1, source_target_pairs={{0,48},{16,0},{32,16},{48,32},{1,49},{17,1},{33,17},{49,33},{2,50}... | collective-permute-start | bytes 1572872 | tf_op jit(solution)/shard_map/ppermute | solution.py:109
  121.9 1.9 %collective-permute-start.17 = (bf16[8,64,512]{2,1,0:T(8,128)(2,1)S(1)}, bf16[8,64,512]{2,1,0:T(8,128)(2,1)S(1)}, u32[]{:S(2)}, u32[]{:S(2)}) collective-permute-start(bf16[8,64,512]{2,1,0:T(8,128)(2,1)S(1)} %get-tuple-element.6), channel_id=1, source_target_pairs={{0,16},{16,32},{32,48},{48,0},{1,17},{17,33},{33,49},{49,1},{2,18}... | collective-permute-start | bytes 1572872 | tf_op jit(solution)/shard_map/ppermute | solution.py:108
  123.9 3.3 %collective-permute-done.6 = bf16[8,64,512]{2,1,0:T(8,128)(2,1)S(1)} collective-permute-done((bf16[8,64,512]{2,1,0:T(8,128)(2,1)S(1)}, bf16[8,64,512]{2,1,0:T(8,128)(2,1)S(1)}, u32[]{:S(2)}, u32[]{:S(2)}) %collective-permute-start.6) | collective-permute-done | bytes 524320 | tf_op jit(solution)/shard_map/ppermute | solution.py:109
  127.2 5.6 %collective-permute-start.9 = (bf16[4,64,512]{2,1,0:T(8,128)(2,1)S(1)}, bf16[4,64,512]{2,1,0:T(8,128)(2,1)S(1)}, u32[]{:S(2)}, u32[]{:S(2)}) collective-permute-start(bf16[4,64,512]{2,1,0:T(8,128)(2,1)S(1)} %slice.44), channel_id=1, source_target_pairs={{0,48},{16,0},{32,16},{48,32},{1,49},{17,1},{33,17},{49,33},{2,50}... | collective-permute-start | bytes 786440 | tf_op jit(solution)/shard_map/ppermute | solution.py:111
  132.8 0.0 copy-start.5
  132.8 1.9 %collective-permute-start.8 = (bf16[4,64,512]{2,1,0:T(8,128)(2,1)S(1)}, bf16[4,64,512]{2,1,0:T(8,128)(2,1)}, u32[]{:S(2)}, u32[]{:S(2)}) collective-permute-start(bf16[4,64,512]{2,1,0:T(8,128)(2,1)S(1)} %slice.43), channel_id=1, source_target_pairs={{0,16},{16,32},{32,48},{48,0},{1,17},{17,33},{33,49},{49,1},{2,18}... | collective-permute-start | bytes 786440 | tf_op jit(solution)/shard_map/ppermute | solution.py:111
  134.7 3.2 %collective-permute-done.16 = bf16[8,64,512]{2,1,0:T(8,128)(2,1)S(1)} collective-permute-done((bf16[8,64,512]{2,1,0:T(8,128)(2,1)S(1)}, bf16[8,64,512]{2,1,0:T(8,128)(2,1)S(1)}, u32[]{:S(2)}, u32[]{:S(2)}) %collective-permute-start.16) | collective-permute-done | bytes 524320 | tf_op jit(solution)/shard_map/ppermute | solution.py:109
  137.9 0.8 copy-done.6
  138.7 5.6 %collective-permute-start.19 = (bf16[4,64,512]{2,1,0:T(8,128)(2,1)S(1)}, bf16[4,64,512]{2,1,0:T(8,128)(2,1)}, u32[]{:S(2)}, u32[]{:S(2)}) collective-permute-start(bf16[4,64,512]{2,1,0:T(8,128)(2,1)S(1)} %slice.47), channel_id=1, source_target_pairs={{0,48},{16,0},{32,16},{48,32},{1,49},{17,1},{33,17},{49,33},{2,50}... | collective-permute-start | bytes 786440 | tf_op jit(solution)/shard_map/ppermute | solution.py:111
  144.4 0.8 copy-done.8
  145.2 1.9 %collective-permute-start.18 = (bf16[4,64,512]{2,1,0:T(8,128)(2,1)S(1)}, bf16[4,64,512]{2,1,0:T(8,128)(2,1)}, u32[]{:S(2)}, u32[]{:S(2)}) collective-permute-start(bf16[4,64,512]{2,1,0:T(8,128)(2,1)S(1)} %slice.46), channel_id=1, source_target_pairs={{0,16},{16,32},{32,48},{48,0},{1,17},{17,33},{33,49},{49,1},{2,18}... | collective-permute-start | bytes 786440 | tf_op jit(solution)/shard_map/ppermute | solution.py:111
  147.1 0.4 collective-permute-done.8
  147.5 1.0 maximum_bitcast_fusion
  148.5 6.2 %collective-permute-done.18 = bf16[4,64,512]{2,1,0:T(8,128)(2,1)} collective-permute-done((bf16[4,64,512]{2,1,0:T(8,128)(2,1)S(1)}, bf16[4,64,512]{2,1,0:T(8,128)(2,1)}, u32[]{:S(2)}, u32[]{:S(2)}) %collective-permute-start.18) | collective-permute-done | bytes 262176 | tf_op jit(solution)/shard_map/ppermute | solution.py:111
  154.8 1.1 maximum_bitcast_fusion.1
  155.9 1.5 pad_maximum_fusion.blocks_ref
  157.4 0.0 copy-start.3
  157.5 1.7 pad_maximum_fusion.1.blocks_ref
  159.1 2.2 %copy-done = bf16[4096,512]{1,0:T(8,128)(2,1)S(1)} copy-done((bf16[4096,512]{1,0:T(8,128)(2,1)S(1)}, bf16[4096,512]{1,0:T(8,128)(2,1)}, u32[]{:S(2)}) %copy-start) | copy-done | bytes 4194328
  161.3 1.6 copy-done.2
  162.9 4.4 %score_columns.2.refs_0_ = f32[512,512]{1,0:T(8,128)} custom-call(s32[8]{0:T(128)S(1)} %broadcast_xor_fusion.slots, s32[1]{0:T(128)} %bitcast.place, bf16[8,512,512]{2,1,0:T(8,128)(2,1)S(1)} %bitcast.32, bf16[4,8,64,512]{3,2,1,0:T(8,128)(2,1)S(1)} %copy-done.2, f32[1,512]{1,0:T(1,128)S(1)} %bitcast.42), custom_call_target="tpu_custom_call" | custom-call | flops 1073741824 | bytes 6291456 | tf_op jit(solution)/shard_map/score_columns/pallas_call | solution.py:80
  167.3 4.4 %score_columns.3 = f32[512,512]{1,0:T(8,128)} custom-call(s32[8]{0:T(128)S(1)} %broadcast_xor_fusion.slots, s32[1]{0:T(128)} %bitcast.place, bf16[8,512,512]{2,1,0:T(8,128)(2,1)S(1)} %bitcast.33, bf16[4,8,64,512]{3,2,1,0:T(8,128)(2,1)S(1)} %pad_maximum_fusion.blocks_ref, f32[1,512]{1,0:T(1,128)S(1)} %bitcast.43, ...), custom_call_target="tpu_custom_call", output_to_operand_aliasing={{}: (5, {})} | custom-call | flops 1073741824 | bytes 6291456 | tf_op jit(solution)/shard_map/score_columns/pallas_call | solution.py:80
  (43 shorter events, 0.5 us)
Async XLA Ops:
  6.5 59.3 %all-gather.4.cloned.1.call-start = ((), (), s32[]{:S(2)}) async-start(), calls=%async_computation.1 | async-start | bytes 4718592 | tf_op jit(solution)/shard_map/all_gather | solution.py:130
  25.3 35.2 %copy-start.10 = (s32[8]{0:T(128)S(1)}, s32[8]{0:T(128)}, u32[]{:S(2)}) copy-start(s32[8]{0:T(128)} %constant.14.clone) | copy-start | bytes 100
  25.4 133.7 %all-gather.6.cloned.1.call-start = ((), (), s32[]{:S(2)}) async-start(), calls=%async_computation.2 | async-start | bytes 4718592 | tf_op jit(solution)/shard_map/all_gather | solution.py:131
  26.4 11.4 %collective-permute-start = (bf16[1,64,512]{2,1,0:T(8,128)(2,1)S(1)}, bf16[1,64,512]{2,1,0:T(8,128)(2,1)S(1)}, u32[]{:S(2)}, u32[]{:S(2)}) collective-permute-start(bf16[1,64,512]{2,1,0:T(8,128)(2,1)S(1)} %slice.33), channel_id=1, source_target_pairs={{0,256},{64,320},{128,384},{192,448},{256,0},{320,64},{384,128},{4... | collective-permute-start | bytes 196616 | tf_op jit(solution)/shard_map/ppermute | solution.py:100
  35.5 13.0 %collective-permute-start.10 = (bf16[1,64,512]{2,1,0:T(8,128)(2,1)S(1)}, bf16[1,64,512]{2,1,0:T(8,128)(2,1)S(1)}, u32[]{:S(2)}, u32[]{:S(2)}) collective-permute-start(bf16[1,64,512]{2,1,0:T(8,128)(2,1)S(1)} %slice.37), channel_id=1, source_target_pairs={{0,256},{64,320},{128,384},{192,448},{256,0},{320,64},{384,128},{4... | collective-permute-start | bytes 196616 | tf_op jit(solution)/shard_map/ppermute | solution.py:100
  37.7 13.1 %collective-permute-start.1 = (bf16[2,64,512]{2,1,0:T(8,128)(2,1)S(1)}, bf16[2,64,512]{2,1,0:T(8,128)(2,1)S(1)}, u32[]{:S(2)}, u32[]{:S(2)}) collective-permute-start(bf16[2,64,512]{2,1,0:T(8,128)(2,1)S(1)} %pad_maximum_fusion.11), channel_id=1, source_target_pairs={{0,128},{64,192},{128,0},{192,64},{256,384},{320,448},{384,256},{4... | collective-permute-start | bytes 393224 | tf_op jit(solution)/shard_map/ppermute | solution.py:100
  48.5 10.0 %collective-permute-start.11 = (bf16[2,64,512]{2,1,0:T(8,128)(2,1)S(1)}, bf16[2,64,512]{2,1,0:T(8,128)(2,1)S(1)}, u32[]{:S(2)}, u32[]{:S(2)}) collective-permute-start(bf16[2,64,512]{2,1,0:T(8,128)(2,1)S(1)} %pad_maximum_fusion.13), channel_id=1, source_target_pairs={{0,128},{64,192},{128,0},{192,64},{256,384},{320,448},{384,256},{4... | collective-permute-start | bytes 393224 | tf_op jit(solution)/shard_map/ppermute | solution.py:100
  50.9 14.1 %collective-permute-start.2 = (bf16[4,64,512]{2,1,0:T(8,128)(2,1)S(1)}, bf16[4,64,512]{2,1,0:T(8,128)(2,1)S(1)}, u32[]{:S(2)}, u32[]{:S(2)}) collective-permute-start(bf16[4,64,512]{2,1,0:T(8,128)(2,1)S(1)} %pad_maximum_fusion.7), channel_id=1, source_target_pairs={{0,64},{64,0},{128,192},{192,128},{256,320},{320,256},{384,448},{4... | collective-permute-start | bytes 786440 | tf_op jit(solution)/shard_map/ppermute | solution.py:100
  58.5 20.1 %collective-permute-start.12 = (bf16[4,64,512]{2,1,0:T(8,128)(2,1)S(1)}, bf16[4,64,512]{2,1,0:T(8,128)(2,1)S(1)}, u32[]{:S(2)}, u32[]{:S(2)}) collective-permute-start(bf16[4,64,512]{2,1,0:T(8,128)(2,1)S(1)} %pad_maximum_fusion.9), channel_id=1, source_target_pairs={{0,64},{64,0},{128,192},{192,128},{256,320},{320,256},{384,448},{4... | collective-permute-start | bytes 786440 | tf_op jit(solution)/shard_map/ppermute | solution.py:100
  65.8 2.2 %copy-start.1 = (bf16[8,512,512]{2,1,0:T(8,128)(2,1)S(1)}, bf16[8,512,512]{2,1,0:T(8,128)(2,1)}, u32[]{:S(2)}) copy-start(bf16[8,512,512]{2,1,0:T(8,128)(2,1)} %all-gather.4.cloned.1.call-done.gram_ref) | copy-start | bytes 12582916
  70.9 14.4 %collective-permute-start.3 = (bf16[1,64,512]{2,1,0:T(8,128)(2,1)S(1)}, bf16[1,64,512]{2,1,0:T(8,128)(2,1)S(1)}, u32[]{:S(2)}, u32[]{:S(2)}) collective-permute-start(bf16[1,64,512]{2,1,0:T(8,128)(2,1)S(1)} %bitcast.38), channel_id=1, source_target_pairs={{0,256},{64,320},{128,384},{192,448},{256,0},{320,64},{384,128},{4... | collective-permute-start | bytes 196616 | tf_op jit(solution)/shard_map/ppermute | solution.py:100
  81.5 14.0 %collective-permute-start.13 = (bf16[1,64,512]{2,1,0:T(8,128)(2,1)S(1)}, bf16[1,64,512]{2,1,0:T(8,128)(2,1)S(1)}, u32[]{:S(2)}, u32[]{:S(2)}) collective-permute-start(bf16[1,64,512]{2,1,0:T(8,128)(2,1)S(1)} %bitcast.34), channel_id=1, source_target_pairs={{0,256},{64,320},{128,384},{192,448},{256,0},{320,64},{384,128},{4... | collective-permute-start | bytes 196616 | tf_op jit(solution)/shard_map/ppermute | solution.py:100
  85.3 12.1 %collective-permute-start.4 = (bf16[2,64,512]{2,1,0:T(8,128)(2,1)S(1)}, bf16[2,64,512]{2,1,0:T(8,128)(2,1)S(1)}, u32[]{:S(2)}, u32[]{:S(2)}) collective-permute-start(bf16[2,64,512]{2,1,0:T(8,128)(2,1)S(1)} %pad_maximum_fusion.12), channel_id=1, source_target_pairs={{0,128},{64,192},{128,0},{192,64},{256,384},{320,448},{384,256},{4... | collective-permute-start | bytes 393224 | tf_op jit(solution)/shard_map/ppermute | solution.py:100
  95.5 7.9 %collective-permute-start.14 = (bf16[2,64,512]{2,1,0:T(8,128)(2,1)S(1)}, bf16[2,64,512]{2,1,0:T(8,128)(2,1)S(1)}, u32[]{:S(2)}, u32[]{:S(2)}) collective-permute-start(bf16[2,64,512]{2,1,0:T(8,128)(2,1)S(1)} %pad_maximum_fusion.14), channel_id=1, source_target_pairs={{0,128},{64,192},{128,0},{192,64},{256,384},{320,448},{384,256},{4... | collective-permute-start | bytes 393224 | tf_op jit(solution)/shard_map/ppermute | solution.py:100
  97.5 12.3 %collective-permute-start.5 = (bf16[4,64,512]{2,1,0:T(8,128)(2,1)S(1)}, bf16[4,64,512]{2,1,0:T(8,128)(2,1)S(1)}, u32[]{:S(2)}, u32[]{:S(2)}) collective-permute-start(bf16[4,64,512]{2,1,0:T(8,128)(2,1)S(1)} %pad_maximum_fusion.8), channel_id=1, source_target_pairs={{0,64},{64,0},{128,192},{192,128},{256,320},{320,256},{384,448},{4... | collective-permute-start | bytes 786440 | tf_op jit(solution)/shard_map/ppermute | solution.py:100
  103.4 13.3 %collective-permute-start.15 = (bf16[4,64,512]{2,1,0:T(8,128)(2,1)S(1)}, bf16[4,64,512]{2,1,0:T(8,128)(2,1)S(1)}, u32[]{:S(2)}, u32[]{:S(2)}) collective-permute-start(bf16[4,64,512]{2,1,0:T(8,128)(2,1)S(1)} %pad_maximum_fusion.10), channel_id=1, source_target_pairs={{0,64},{64,0},{128,192},{192,128},{256,320},{320,256},{384,448},{4... | collective-permute-start | bytes 786440 | tf_op jit(solution)/shard_map/ppermute | solution.py:100
  109.9 17.2 %collective-permute-start.6 = (bf16[8,64,512]{2,1,0:T(8,128)(2,1)S(1)}, bf16[8,64,512]{2,1,0:T(8,128)(2,1)S(1)}, u32[]{:S(2)}, u32[]{:S(2)}) collective-permute-start(bf16[8,64,512]{2,1,0:T(8,128)(2,1)S(1)} %get-tuple-element.8), channel_id=1, source_target_pairs={{0,48},{16,0},{32,16},{48,32},{1,49},{17,1},{33,17},{49,33},{2,50}... | collective-permute-start | bytes 1572872 | tf_op jit(solution)/shard_map/ppermute | solution.py:109
  114.8 18.0 %collective-permute-start.7 = (bf16[8,64,512]{2,1,0:T(8,128)(2,1)S(1)}, bf16[8,64,512]{2,1,0:T(8,128)(2,1)S(1)}, u32[]{:S(2)}, u32[]{:S(2)}) collective-permute-start(bf16[8,64,512]{2,1,0:T(8,128)(2,1)S(1)} %get-tuple-element.8), channel_id=1, source_target_pairs={{0,16},{16,32},{32,48},{48,0},{1,17},{17,33},{33,49},{49,1},{2,18}... | collective-permute-start | bytes 1572872 | tf_op jit(solution)/shard_map/ppermute | solution.py:108
  116.8 21.1 %collective-permute-start.16 = (bf16[8,64,512]{2,1,0:T(8,128)(2,1)S(1)}, bf16[8,64,512]{2,1,0:T(8,128)(2,1)S(1)}, u32[]{:S(2)}, u32[]{:S(2)}) collective-permute-start(bf16[8,64,512]{2,1,0:T(8,128)(2,1)S(1)} %get-tuple-element.6), channel_id=1, source_target_pairs={{0,48},{16,0},{32,16},{48,32},{1,49},{17,1},{33,17},{49,33},{2,50}... | collective-permute-start | bytes 1572872 | tf_op jit(solution)/shard_map/ppermute | solution.py:109
  121.9 22.4 %collective-permute-start.17 = (bf16[8,64,512]{2,1,0:T(8,128)(2,1)S(1)}, bf16[8,64,512]{2,1,0:T(8,128)(2,1)S(1)}, u32[]{:S(2)}, u32[]{:S(2)}) collective-permute-start(bf16[8,64,512]{2,1,0:T(8,128)(2,1)S(1)} %get-tuple-element.6), channel_id=1, source_target_pairs={{0,16},{16,32},{32,48},{48,0},{1,17},{17,33},{33,49},{49,1},{2,18}... | collective-permute-start | bytes 1572872 | tf_op jit(solution)/shard_map/ppermute | solution.py:108
  127.1 28.7 %copy-start.4 = (bf16[8,64,512]{2,1,0:T(8,128)(2,1)}, bf16[8,64,512]{2,1,0:T(8,128)(2,1)S(1)}, u32[]{:S(2)}) copy-start(bf16[8,64,512]{2,1,0:T(8,128)(2,1)S(1)} %collective-permute-done.6) | copy-start | bytes 1572868
  127.2 20.0 %collective-permute-start.9 = (bf16[4,64,512]{2,1,0:T(8,128)(2,1)S(1)}, bf16[4,64,512]{2,1,0:T(8,128)(2,1)S(1)}, u32[]{:S(2)}, u32[]{:S(2)}) collective-permute-start(bf16[4,64,512]{2,1,0:T(8,128)(2,1)S(1)} %slice.44), channel_id=1, source_target_pairs={{0,48},{16,0},{32,16},{48,32},{1,49},{17,1},{33,17},{49,33},{2,50}... | collective-permute-start | bytes 786440 | tf_op jit(solution)/shard_map/ppermute | solution.py:111
  132.8 23.1 %copy-start.5 = (bf16[8,64,512]{2,1,0:T(8,128)(2,1)}, bf16[8,64,512]{2,1,0:T(8,128)(2,1)S(1)}, u32[]{:S(2)}) copy-start(bf16[8,64,512]{2,1,0:T(8,128)(2,1)S(1)} %collective-permute-done.7) | copy-start | bytes 1572868
  132.8 14.7 %collective-permute-start.8 = (bf16[4,64,512]{2,1,0:T(8,128)(2,1)S(1)}, bf16[4,64,512]{2,1,0:T(8,128)(2,1)}, u32[]{:S(2)}, u32[]{:S(2)}) collective-permute-start(bf16[4,64,512]{2,1,0:T(8,128)(2,1)S(1)} %slice.43), channel_id=1, source_target_pairs={{0,16},{16,32},{32,48},{48,0},{1,17},{17,33},{33,49},{49,1},{2,18}... | collective-permute-start | bytes 786440 | tf_op jit(solution)/shard_map/ppermute | solution.py:111
  137.9 0.8 copy-start.6
  138.7 9.8 %collective-permute-start.19 = (bf16[4,64,512]{2,1,0:T(8,128)(2,1)S(1)}, bf16[4,64,512]{2,1,0:T(8,128)(2,1)}, u32[]{:S(2)}, u32[]{:S(2)}) collective-permute-start(bf16[4,64,512]{2,1,0:T(8,128)(2,1)S(1)} %slice.47), channel_id=1, source_target_pairs={{0,48},{16,0},{32,16},{48,32},{1,49},{17,1},{33,17},{49,33},{2,50}... | collective-permute-start | bytes 786440 | tf_op jit(solution)/shard_map/ppermute | solution.py:111
  144.4 0.8 copy-start.8
  145.2 9.6 %collective-permute-start.18 = (bf16[4,64,512]{2,1,0:T(8,128)(2,1)S(1)}, bf16[4,64,512]{2,1,0:T(8,128)(2,1)}, u32[]{:S(2)}, u32[]{:S(2)}) collective-permute-start(bf16[4,64,512]{2,1,0:T(8,128)(2,1)S(1)} %slice.46), channel_id=1, source_target_pairs={{0,16},{16,32},{32,48},{48,0},{1,17},{17,33},{33,49},{49,1},{2,18}... | collective-permute-start | bytes 786440 | tf_op jit(solution)/shard_map/ppermute | solution.py:111
  155.9 1.6 copy-start.7
  155.9 1.6 copy-start.9
  157.4 1.7 copy-start.3
  159.1 2.2 %copy-start = (bf16[4096,512]{1,0:T(8,128)(2,1)S(1)}, bf16[4096,512]{1,0:T(8,128)(2,1)}, u32[]{:S(2)}) copy-start(bf16[4096,512]{1,0:T(8,128)(2,1)} %all-gather.6.cloned.1.call-done) | copy-start | bytes 12582916
  161.3 1.6 copy-start.2
Sparse Core Ops, SparseCore 0:
  25.5 40.2 all-gather.3
  68.0 39.7 all-gather.5

commit v3 on v0

v3 whole, which is shorter than its diff:
```python
import jax
import jax.numpy as jnp
from jax import lax
from jax.experimental import pallas as pl
from jax.experimental.pallas import tpu as pltpu
from jax.sharding import Mesh, PartitionSpec as P

NZ, NY, CHUNKS = 8, 4, 2
NT_DIMS = (((1,), (1,)), ((), ()))
RELATIVE = (0, 4, 2, 6, 1, 5, 3, 7)
VMEM_LIMIT = 57 * 1024 * 1024


def kernel_matrix(slots, gram, training):
    n, t, depth = training.shape
    rows = gram.shape[1]

    def kernel(slots, gram_ref, training_ref, out_ref, held, arrived):
        copies = [pltpu.make_async_copy(gram_ref.at[slots[s]], held.at[s], arrived.at[s]) for s in range(n)]
        for copy in copies:
            copy.start()
        total = jnp.zeros((t, rows), jnp.float32)
        for s, copy in enumerate(copies):
            copy.wait()
            total += lax.dot_general(training_ref[s], held[s], NT_DIMS, preferred_element_type=jnp.float32)
        out_ref[...] = total.astype(out_ref.dtype)

    return pl.pallas_call(
        kernel,
        out_shape=jax.ShapeDtypeStruct((t, rows), jnp.bfloat16),
        in_specs=[
            pl.BlockSpec(memory_space=pltpu.SMEM),
            pl.BlockSpec(memory_space=pltpu.HBM),
            pl.BlockSpec(memory_space=pltpu.VMEM),
        ],
        out_specs=pl.BlockSpec(memory_space=pltpu.VMEM),
        scratch_shapes=[pltpu.VMEM((n, rows, depth), jnp.bfloat16), pltpu.SemaphoreType.DMA((n,))],
        compiler_params=pltpu.CompilerParams(vmem_limit_bytes=VMEM_LIMIT),
        cost_estimate=pl.CostEstimate(
            flops=2 * n * rows * t * depth, bytes_accessed=2 * n * depth * (rows + t), transcendentals=0
        ),
        name="kernel_matrix",
    )(slots, gram, training)


def score_columns(slots, place, query, blocks, weight, out, chunk):
    n, rows, depth = query.shape
    t = blocks[0][0].shape[1]
    width = NY * t
    columns = weight.shape[1]
    parts = [(d, part) for d, cut in enumerate(blocks) for part in cut]

    def kernel(slots, place, query_ref, weight_ref, *refs):
        part_refs = refs[: len(parts)]
        out_ref, held, ordered, total, query_sems, part_sems = refs[-6:]
        part_copies, first = [], 0
        for k, ((d, part), ref) in enumerate(zip(parts, part_refs)):
            size = part.shape[0]
            target = ordered.at[pl.ds(first, size), lax.rem(place[0] + d, NY)]
            part_copies.append(pltpu.make_async_copy(ref, target, part_sems.at[k]))
            first = (first + size) % n
        copies = [pltpu.make_async_copy(query_ref.at[slots[s]], held.at[s], query_sems.at[s]) for s in range(n)]
        for copy in part_copies + copies:
            copy.start()
        for copy in part_copies:
            copy.wait()
        for s, copy in enumerate(copies):
            copy.wait()
            product = lax.dot_general(
                held[s], ordered[s].reshape(width, depth), NT_DIMS, preferred_element_type=jnp.float32
            )
            if s == 0:
                total[...] = product
            elif s < n - 1:
                total[...] += product
            else:
                out_ref[...] = (total[...] + product) * weight_ref[...]

    operands = [slots, place, query, weight, *(part for _, part in parts)] + ([] if out is None else [out])
    in_specs = [
        pl.BlockSpec(memory_space=pltpu.SMEM),
        pl.BlockSpec(memory_space=pltpu.SMEM),
        pl.BlockSpec(memory_space=pltpu.HBM),
        pl.BlockSpec((1, width), lambda _: (0, chunk)),
    ] + [pl.BlockSpec(memory_space=pl.ANY)] * (len(operands) - 4)
    return pl.pallas_call(
        kernel,
        out_shape=jax.ShapeDtypeStruct((rows, columns), jnp.float32),
        grid=(1,),
        in_specs=in_specs,
        out_specs=pl.BlockSpec((rows, width), lambda _: (0, chunk)),
        scratch_shapes=[
            pltpu.VMEM((n, rows, depth), jnp.bfloat16),
            pltpu.VMEM((n, NY, t, depth), jnp.bfloat16),
            pltpu.VMEM((rows, width), jnp.float32),
            pltpu.SemaphoreType.DMA((n,)),
            pltpu.SemaphoreType.DMA((len(parts),)),
        ],
        input_output_aliases={} if out is None else {len(operands) - 1: 0},
        compiler_params=pltpu.CompilerParams(vmem_limit_bytes=VMEM_LIMIT),
        cost_estimate=pl.CostEstimate(
            flops=2 * n * rows * width * depth, bytes_accessed=2 * n * depth * (rows + width), transcendentals=0
        ),
        name="score_columns",
    )(*operands)


def after(array, *earlier):
    return lax.optimization_barrier((array, earlier))[0]


def exchange(held, distance):
    other = lax.ppermute(held, "z", [(i, i ^ distance) for i in range(NZ)])
    return jnp.concatenate([held, other], axis=0)


UP = [(i, (i + 1) % NY) for i in range(NY)]
DOWN = [(i, (i - 1) % NY) for i in range(NY)]


def local(query_features, inverse_gram, training_features, residual_weight):
    slots = lax.axis_index("z") ^ jnp.array(RELATIVE, jnp.int32)
    place = lax.axis_index("y").astype(jnp.int32)[None]
    columns, lanes = training_features.shape
    rows, depth = inverse_gram.shape
    t = columns // (CHUNKS * NY)

    gram_tiles = inverse_gram.reshape(rows, NY, lanes).transpose(1, 0, 2).reshape(NY * rows, lanes)
    pieces = training_features.reshape(CHUNKS, NY, t, lanes).transpose(1, 0, 2, 3).reshape(NY, CHUNKS * t, lanes)
    sent = jnp.concatenate([pieces, jnp.broadcast_to(gram_tiles, (NY, *gram_tiles.shape))], axis=1)
    got = lax.all_to_all(sent, "y", split_axis=0, concat_axis=0, tiled=True)
    training = got[:, : CHUNKS * t].reshape(NY, CHUNKS, t, lanes).transpose(1, 2, 0, 3).reshape(CHUNKS, t, NY * lanes)
    gram_rows = got[:, CHUNKS * t :].reshape(NY, NY, rows, lanes).transpose(0, 2, 1, 3).reshape(NY * rows, depth)

    gram = lax.all_gather(gram_rows, ("x", "core"), axis=0)
    query = lax.all_gather(after(query_features, gram_rows), ("x", "core"), axis=0)
    weight = residual_weight[None, :]

    a, b = training[0][None], training[1][None]
    for distance in (4, 2, 1):
        a, b = exchange(a, distance), exchange(b, distance)
    a, b = kernel_matrix(slots, gram, a)[None], kernel_matrix(slots, gram, b)[None]

    a = exchange(exchange(a, 4), 2)
    b = after(b, a)
    a = exchange(a, 1)
    b = exchange(b, 4)
    half = NZ // 2
    below, above = lax.ppermute(a, "y", UP), lax.ppermute(a, "y", DOWN)
    b = exchange(b, 2)
    b = exchange(b, 1)
    far = lax.ppermute(below[:half], "y", UP), lax.ppermute(above[half:], "y", DOWN)
    b = after(b, below, above)
    below_b, above_b = lax.ppermute(b, "y", UP), lax.ppermute(b, "y", DOWN)
    out = score_columns(slots, place, query, ((a,), (above,), far, (below,)), weight, None, 0)
    first, second = after(below_b[:half], out), after(above_b[half:], out)
    far_b = lax.ppermute(first, "y", UP), lax.ppermute(second, "y", DOWN)
    return score_columns(slots, place, query, ((b,), (above_b,), far_b, (below_b,)), weight, out, 1)


def solution(mesh):
    fine = Mesh(mesh.devices.reshape(NZ, NY, 4, 2, 2), ("z", "y", "x", "core", "row"))
    pb, ta = ("z", "y"), ("x", "core")
    placed = (P(pb, ta), P(pb, ta), P(("row", *ta), pb), P(("row", *ta)))
    return jax.shard_map(
        local, mesh=fine, in_specs=placed, out_specs=P(pb, ("row", *ta)), check_vma=False
    )
```

time: 526 us -> 200 us (0.38)
  waiting for transfers between devices: 496 us -> 41.2 us
  starting transfers between devices: 0.12 us -> 91.8 us
  Pallas kernels: 0 us -> 23.2 us
  blocking collectives: 0 us -> 15.1 us
  matrix products: 13.4 us -> 0 us
  local copies, waits for them, and re-layouts: 0.01 us -> 6.05 us
    all_gather x4 -> x2, waiting for transfers between devices: 494 us -> 1.66 us  [the longest x1 1.64 us: local(): gram = lax.all_gather(gram_rows, ('x', 'core'), axis=0)]
    ppermute x0 -> x20, starting transfers between devices: none -> 91.7 us  [the longest x12 63.5 us: exchange(): other = lax.ppermute(held, 'z', [(i, i ^ distance) for i in range(NZ)])]
    ppermute x0 -> x20, waiting for transfers between devices: none -> 38.8 us  [the longest x12 25 us: exchange(): other = lax.ppermute(held, 'z', [(i, i ^ distance) for i in range(NZ)])]
    pallas_call x0 -> x4, Pallas kernels: none -> 23.2 us  [the longest x2 14.3 us: score_columns(): pl.pallas_call(kernel, out_shape=jax.ShapeDtypeStruct((rows, columns), jn...]
    all_to_all x0 -> x1, blocking collectives: none -> 15.1 us  [local(): got = lax.all_to_all(sent, 'y', split_axis=0, concat_axis=0, tiled=True)]
    dot_general x2 -> x0, matrix products: 13.4 us -> none  [the longest x1 6.8 us: local(): lax.dot_general(columns, lax.all_gather(training_features, 'pb', axis=1,...]
  transfers between devices with their start and end apart: 4 -> 22, of which waited for: 4 -> 13; matrix products, arithmetic and copies ran while one was open for 1% -> 3% of each run, Pallas kernels for 0% -> 8%
where the time goes in v3:
time: 200 us; the launch traced here: 196 us
  starting transfers between devices  91.8 us (46%)
  waiting for transfers between devices  41.2 us (21%)
  Pallas kernels  23.2 us (12%)
  blocking collectives  15.1 us (8%)
  between operations  13.9 us (7%)
  local copies, waits for them, and re-layouts  6.05 us (3%)
  other arithmetic  5.09 us (3%)
    ppermute x12, starting transfers between devices, exchange(): other = lax.ppermute(held, 'z', [(i, i ^ distance) for i in range(NZ)])  63.5 us
    ppermute x12, waiting for transfers between devices, exchange(): other = lax.ppermute(held, 'z', [(i, i ^ distance) for i in range(NZ)])  25 us
    all_to_all x1, blocking collectives, local(): got = lax.all_to_all(sent, 'y', split_axis=0, concat_axis=0, tiled=True)  15.1 us
    pallas_call x2, Pallas kernels, score_columns(): pl.pallas_call(kernel, out_shape=jax.ShapeDtypeStruct((rows, columns), jn...  14.3 us
    pallas_call x2, Pallas kernels, kernel_matrix(): pl.pallas_call(kernel, out_shape=jax.ShapeDtypeStruct((t, rows), jnp.bflo...  8.91 us
    ppermute x2, starting transfers between devices, local(): far_b = (lax.ppermute(first, 'y', UP), lax.ppermute(second, 'y', DOWN))  7.05 us
    ppermute x2, starting transfers between devices, local(): below, above = (lax.ppermute(a, 'y', UP), lax.ppermute(a, 'y', DOWN))  7.05 us
    ppermute x2, starting transfers between devices, local(): below_b, above_b = (lax.ppermute(b, 'y', UP), lax.ppermute(b, 'y', DOWN))  7.04 us
  transfers between devices with their start and end apart: 22, of which 13 were waited for; matrix products, arithmetic and copies ran while one was open for 3% of the time, Pallas kernels for 8%

profile of v3, /device:TPU:6, one launch (start us, length us, event | category | flops | bytes accessed | tf_op | source)
XLA Modules:
  0.0 196.4 jit_solution(1498119439230437092)
XLA Ops:
  6.5 1.0 copy.19
  7.6 0.1 copy.20
  7.7 0.9 copy.18
  8.6 0.1 broadcast_in_dim.17
  8.8 15.1 %all_to_all.5 = bf16[4,640,128]{2,1,0:T(8,128)(2,1)S(1)} all-to-all(bf16[4,640,128]{2,1,0:T(8,128)(2,1)S(1)} %pad_maximum_fusion), channel_id=1, replica_groups=mesh['z'=8,'y'=4,'x'=4,'core'=2,'row'=2] {'y'}, dimensions={0} | all-to-all | bytes 1310720 | tf_op jit(solution)/shard_map/all_to_all | solution.py:131
  23.9 0.4 copy.21
  24.4 1.0 all_gather_reshape.3
  25.3 0.0 all-gather.4.cloned.1.call-update
  25.4 0.0 copy-start.11
  25.4 0.0 all-gather.6.cloned.1.call-start
  25.4 0.7 all-gather.6.cloned.1.call-update
  26.2 0.1 copy.24
  26.4 9.1 %collective-permute-start.3 = (bf16[1,64,512]{2,1,0:T(8,128)(2,1)S(1)}, bf16[1,64,512]{2,1,0:T(8,128)(2,1)S(1)}, u32[]{:S(2)}, u32[]{:S(2)}) collective-permute-start(bf16[1,64,512]{2,1,0:T(8,128)(2,1)S(1)} %slice.35), channel_id=1, source_target_pairs={{0,256},{64,320},{128,384},{192,448},{256,0},{320,64},{384,128},{4... | collective-permute-start | bytes 196616 | tf_op jit(solution)/shard_map/ppermute | solution.py:113
  35.5 2.3 %collective-permute-done.3 = bf16[1,64,512]{2,1,0:T(8,128)(2,1)S(1)} collective-permute-done((bf16[1,64,512]{2,1,0:T(8,128)(2,1)S(1)}, bf16[1,64,512]{2,1,0:T(8,128)(2,1)S(1)}, u32[]{:S(2)}, u32[]{:S(2)}) %collective-permute-start.3) | collective-permute-done | bytes 65568 | tf_op jit(solution)/shard_map/ppermute | solution.py:113
  37.7 5.3 %collective-permute-start.4 = (bf16[2,64,512]{2,1,0:T(8,128)(2,1)S(1)}, bf16[2,64,512]{2,1,0:T(8,128)(2,1)S(1)}, u32[]{:S(2)}, u32[]{:S(2)}) collective-permute-start(bf16[2,64,512]{2,1,0:T(8,128)(2,1)S(1)} %pad_maximum_fusion.10), channel_id=1, source_target_pairs={{0,128},{64,192},{128,0},{192,64},{256,384},{320,448},{384,256},{4... | collective-permute-start | bytes 393224 | tf_op jit(solution)/shard_map/ppermute | solution.py:113
  43.1 8.2 %collective-permute-start = (bf16[1,64,512]{2,1,0:T(8,128)(2,1)S(1)}, bf16[1,64,512]{2,1,0:T(8,128)(2,1)S(1)}, u32[]{:S(2)}, u32[]{:S(2)}) collective-permute-start(bf16[1,64,512]{2,1,0:T(8,128)(2,1)S(1)} %slice.33), channel_id=1, source_target_pairs={{0,256},{64,320},{128,384},{192,448},{256,0},{320,64},{384,128},{4... | collective-permute-start | bytes 196616 | tf_op jit(solution)/shard_map/ppermute | solution.py:113
  51.3 0.0 collective-permute-done.4
  51.3 4.6 %collective-permute-start.5 = (bf16[4,64,512]{2,1,0:T(8,128)(2,1)S(1)}, bf16[4,64,512]{2,1,0:T(8,128)(2,1)S(1)}, u32[]{:S(2)}, u32[]{:S(2)}) collective-permute-start(bf16[4,64,512]{2,1,0:T(8,128)(2,1)S(1)} %pad_maximum_fusion.6), channel_id=1, source_target_pairs={{0,64},{64,0},{128,192},{192,128},{256,320},{320,256},{384,448},{4... | collective-permute-start | bytes 786440 | tf_op jit(solution)/shard_map/ppermute | solution.py:113
  55.9 0.5 broadcast_xor_fusion.slots
  56.4 0.0 collective-permute-done
  56.4 2.9 %collective-permute-start.1 = (bf16[2,64,512]{2,1,0:T(8,128)(2,1)S(1)}, bf16[2,64,512]{2,1,0:T(8,128)(2,1)S(1)}, u32[]{:S(2)}, u32[]{:S(2)}) collective-permute-start(bf16[2,64,512]{2,1,0:T(8,128)(2,1)S(1)} %pad_maximum_fusion.9), channel_id=1, source_target_pairs={{0,128},{64,192},{128,0},{192,64},{256,384},{320,448},{384,256},{4... | collective-permute-start | bytes 393224 | tf_op jit(solution)/shard_map/ppermute | solution.py:113
  59.3 4.0 %collective-permute-done.5 = bf16[4,64,512]{2,1,0:T(8,128)(2,1)S(1)} collective-permute-done((bf16[4,64,512]{2,1,0:T(8,128)(2,1)S(1)}, bf16[4,64,512]{2,1,0:T(8,128)(2,1)S(1)}, u32[]{:S(2)}, u32[]{:S(2)}) %collective-permute-start.5) | collective-permute-done | bytes 262176 | tf_op jit(solution)/shard_map/ppermute | solution.py:113
  63.3 0.9 pad_maximum_fusion.2.training_ref
  64.2 1.6 all-gather.4.cloned.1.call-done.gram_ref
  65.8 4.4 %kernel_matrix.3 = bf16[64,512]{1,0:T(8,128)(2,1)} custom-call(s32[8]{0:T(128)} %broadcast_xor_fusion.slots, bf16[8,512,512]{2,1,0:T(8,128)(2,1)} %all-gather.4.cloned.1.call-done.gram_ref, bf16[8,64,512]{2,1,0:T(8,128)(2,1)} %pad_maximum_fusion.2.training_ref), custom_call_target="tpu_custom_call" | custom-call | flops 268435456 | bytes 4718592 | tf_op jit(solution)/shard_map/kernel_matrix/pallas_call | solution.py:28
  70.3 7.6 %collective-permute-start.6 = (bf16[1,64,512]{2,1,0:T(8,128)(2,1)}, bf16[1,64,512]{2,1,0:T(8,128)(2,1)S(1)}, u32[]{:S(2)}, u32[]{:S(2)}) collective-permute-start(bf16[1,64,512]{2,1,0:T(8,128)(2,1)} %bitcast.23), channel_id=1, source_target_pairs={{0,256},{64,320},{128,384},{192,448},{256,0},{320,64},{384,128},{4... | collective-permute-start | bytes 196616 | tf_op jit(solution)/shard_map/ppermute | solution.py:113
  78.0 3.5 %collective-permute-start.2 = (bf16[4,64,512]{2,1,0:T(8,128)(2,1)S(1)}, bf16[4,64,512]{2,1,0:T(8,128)(2,1)S(1)}, u32[]{:S(2)}, u32[]{:S(2)}) collective-permute-start(bf16[4,64,512]{2,1,0:T(8,128)(2,1)S(1)} %pad_maximum_fusion.5), channel_id=1, source_target_pairs={{0,64},{64,0},{128,192},{192,128},{256,320},{320,256},{384,448},{4... | collective-permute-start | bytes 786440 | tf_op jit(solution)/shard_map/ppermute | solution.py:113
  81.4 3.5 %collective-permute-done.6 = bf16[1,64,512]{2,1,0:T(8,128)(2,1)S(1)} collective-permute-done((bf16[1,64,512]{2,1,0:T(8,128)(2,1)}, bf16[1,64,512]{2,1,0:T(8,128)(2,1)S(1)}, u32[]{:S(2)}, u32[]{:S(2)}) %collective-permute-start.6) | collective-permute-done | bytes 65568 | tf_op jit(solution)/shard_map/ppermute | solution.py:113
  85.0 0.9 pad_maximum_fusion.11
  85.8 2.2 %collective-permute-start.7 = (bf16[2,64,512]{2,1,0:T(8,128)(2,1)S(1)}, bf16[2,64,512]{2,1,0:T(8,128)(2,1)S(1)}, u32[]{:S(2)}, u32[]{:S(2)}) collective-permute-start(bf16[2,64,512]{2,1,0:T(8,128)(2,1)S(1)} %pad_maximum_fusion.11), channel_id=1, source_target_pairs={{0,128},{64,192},{128,0},{192,64},{256,384},{320,448},{384,256},{4... | collective-permute-start | bytes 393224 | tf_op jit(solution)/shard_map/ppermute | solution.py:113
  88.0 7.1 %collective-permute-done.7 = bf16[2,64,512]{2,1,0:T(8,128)(2,1)S(1)} collective-permute-done((bf16[2,64,512]{2,1,0:T(8,128)(2,1)S(1)}, bf16[2,64,512]{2,1,0:T(8,128)(2,1)S(1)}, u32[]{:S(2)}, u32[]{:S(2)}) %collective-permute-start.7) | collective-permute-done | bytes 131104 | tf_op jit(solution)/shard_map/ppermute | solution.py:113
  95.2 0.9 pad_maximum_fusion.7
  96.0 1.9 collective-permute-start.11
  98.0 0.8 pad_maximum_fusion.1.training_ref
  98.8 4.5 %kernel_matrix.2 = bf16[64,512]{1,0:T(8,128)(2,1)} custom-call(s32[8]{0:T(128)} %broadcast_xor_fusion.slots, bf16[8,512,512]{2,1,0:T(8,128)(2,1)} %all-gather.4.cloned.1.call-done.gram_ref, bf16[8,64,512]{2,1,0:T(8,128)(2,1)} %pad_maximum_fusion.1.training_ref), custom_call_target="tpu_custom_call" | custom-call | flops 268435456 | bytes 4718592 | tf_op jit(solution)/shard_map/kernel_matrix/pallas_call | solution.py:28
  103.3 8.3 %collective-permute-start.8 = (bf16[1,64,512]{2,1,0:T(8,128)(2,1)}, bf16[1,64,512]{2,1,0:T(8,128)(2,1)S(1)}, u32[]{:S(2)}, u32[]{:S(2)}) collective-permute-start(bf16[1,64,512]{2,1,0:T(8,128)(2,1)} %bitcast.27), channel_id=1, source_target_pairs={{0,256},{64,320},{128,384},{192,448},{256,0},{320,64},{384,128},{4... | collective-permute-start | bytes 196616 | tf_op jit(solution)/shard_map/ppermute | solution.py:113
  111.6 2.6 %collective-permute-done.8 = bf16[1,64,512]{2,1,0:T(8,128)(2,1)S(1)} collective-permute-done((bf16[1,64,512]{2,1,0:T(8,128)(2,1)}, bf16[1,64,512]{2,1,0:T(8,128)(2,1)S(1)}, u32[]{:S(2)}, u32[]{:S(2)}) %collective-permute-start.8) | collective-permute-done | bytes 65568 | tf_op jit(solution)/shard_map/ppermute | solution.py:113
  114.3 0.9 pad_maximum_fusion.12
  115.1 6.2 %collective-permute-start.9 = (bf16[2,64,512]{2,1,0:T(8,128)(2,1)S(1)}, bf16[2,64,512]{2,1,0:T(8,128)(2,1)S(1)}, u32[]{:S(2)}, u32[]{:S(2)}) collective-permute-start(bf16[2,64,512]{2,1,0:T(8,128)(2,1)S(1)} %pad_maximum_fusion.12), channel_id=1, source_target_pairs={{0,128},{64,192},{128,0},{192,64},{256,384},{320,448},{384,256},{4... | collective-permute-start | bytes 393224 | tf_op jit(solution)/shard_map/ppermute | solution.py:113
  121.3 0.1 pad_maximum_fusion.4.refs_0_
  121.4 3.4 %collective-permute-start.12 = (bf16[8,64,512]{2,1,0:T(8,128)(2,1)S(1)}, bf16[8,64,512]{2,1,0:T(8,128)(2,1)S(1)}, u32[]{:S(2)}, u32[]{:S(2)}) collective-permute-start(bf16[8,64,512]{2,1,0:T(8,128)(2,1)S(1)} %pad_maximum_fusion.4.refs_0_), channel_id=1, source_target_pairs={{0,16},{16,32},{32,48},{48,0},{1,17},{17,33},{33,49},{49,1},{2,18}... | collective-permute-start | bytes 1572872 | tf_op jit(solution)/shard_map/ppermute | solution.py:149
  124.8 3.7 %collective-permute-start.13 = (bf16[8,64,512]{2,1,0:T(8,128)(2,1)S(1)}, bf16[8,64,512]{2,1,0:T(8,128)(2,1)S(1)}, u32[]{:S(2)}, u32[]{:S(2)}) collective-permute-start(bf16[8,64,512]{2,1,0:T(8,128)(2,1)S(1)} %pad_maximum_fusion.4.refs_0_), channel_id=1, source_target_pairs={{0,48},{16,0},{32,16},{48,32},{1,49},{17,1},{33,17},{49,33},{2,50}... | collective-permute-start | bytes 1572872 | tf_op jit(solution)/shard_map/ppermute | solution.py:149
  128.5 3.9 %collective-permute-start.10 = (bf16[4,64,512]{2,1,0:T(8,128)(2,1)S(1)}, bf16[4,64,512]{2,1,0:T(8,128)(2,1)S(1)}, u32[]{:S(2)}, u32[]{:S(2)}) collective-permute-start(bf16[4,64,512]{2,1,0:T(8,128)(2,1)S(1)} %pad_maximum_fusion.8), channel_id=1, source_target_pairs={{0,64},{64,0},{128,192},{192,128},{256,320},{320,256},{384,448},{4... | collective-permute-start | bytes 786440 | tf_op jit(solution)/shard_map/ppermute | solution.py:113
  132.4 5.4 %collective-permute-done.10 = bf16[4,64,512]{2,1,0:T(8,128)(2,1)S(1)} collective-permute-done((bf16[4,64,512]{2,1,0:T(8,128)(2,1)S(1)}, bf16[4,64,512]{2,1,0:T(8,128)(2,1)S(1)}, u32[]{:S(2)}, u32[]{:S(2)}) %collective-permute-start.10) | collective-permute-done | bytes 262176 | tf_op jit(solution)/shard_map/ppermute | solution.py:113
  137.8 0.1 pad_maximum_fusion.3.refs_0_
  137.8 0.2 collective-permute-done.12.refs_4_
  138.0 1.9 collective-permute-done.13.refs_1_
  139.9 3.4 %collective-permute-start.15 = (bf16[8,64,512]{2,1,0:T(8,128)(2,1)S(1)}, bf16[8,64,512]{2,1,0:T(8,128)(2,1)S(1)}, u32[]{:S(2)}, u32[]{:S(2)}) collective-permute-start(bf16[8,64,512]{2,1,0:T(8,128)(2,1)S(1)} %pad_maximum_fusion.3.refs_0_), channel_id=1, source_target_pairs={{0,16},{16,32},{32,48},{48,0},{1,17},{17,33},{33,49},{49,1},{2,18}... | collective-permute-start | bytes 1572872 | tf_op jit(solution)/shard_map/ppermute | solution.py:154
  143.3 3.7 %collective-permute-start.14 = (bf16[8,64,512]{2,1,0:T(8,128)(2,1)S(1)}, bf16[8,64,512]{2,1,0:T(8,128)(2,1)S(1)}, u32[]{:S(2)}, u32[]{:S(2)}) collective-permute-start(bf16[8,64,512]{2,1,0:T(8,128)(2,1)S(1)} %pad_maximum_fusion.3.refs_0_), channel_id=1, source_target_pairs={{0,48},{16,0},{32,16},{48,32},{1,49},{17,1},{33,17},{49,33},{2,50}... | collective-permute-start | bytes 1572872 | tf_op jit(solution)/shard_map/ppermute | solution.py:154
  147.0 0.7 slice.45
  147.7 2.2 %collective-permute-start.16 = (bf16[4,64,512]{2,1,0:T(8,128)(2,1)}, bf16[4,64,512]{2,1,0:T(8,128)(2,1)S(1)}, u32[]{:S(2)}, u32[]{:S(2)}) collective-permute-start(bf16[4,64,512]{2,1,0:T(8,128)(2,1)} %slice.45), channel_id=1, source_target_pairs={{0,16},{16,32},{32,48},{48,0},{1,17},{17,33},{33,49},{49,1},{2,18}... | collective-permute-start | bytes 786440 | tf_op jit(solution)/shard_map/ppermute | solution.py:152
  149.9 0.7 slice.46
  150.6 4.9 %collective-permute-start.17 = (bf16[4,64,512]{2,1,0:T(8,128)(2,1)}, bf16[4,64,512]{2,1,0:T(8,128)(2,1)}, u32[]{:S(2)}, u32[]{:S(2)}) collective-permute-start(bf16[4,64,512]{2,1,0:T(8,128)(2,1)} %slice.46), channel_id=1, source_target_pairs={{0,48},{16,0},{32,16},{48,32},{1,49},{17,1},{33,17},{49,33},{2,50}... | collective-permute-start | bytes 786440 | tf_op jit(solution)/shard_map/ppermute | solution.py:152
  155.5 0.0 all-gather.6.cloned.1.call-done
  155.5 5.5 %collective-permute-done.16.refs_2_ = bf16[4,64,512]{2,1,0:T(8,128)(2,1)S(1)} collective-permute-done((bf16[4,64,512]{2,1,0:T(8,128)(2,1)}, bf16[4,64,512]{2,1,0:T(8,128)(2,1)S(1)}, u32[]{:S(2)}, u32[]{:S(2)}) %collective-permute-start.16) | collective-permute-done | bytes 262176 | tf_op jit(solution)/shard_map/ppermute | solution.py:152
  161.0 2.0 %collective-permute-done.17.refs_3_ = bf16[4,64,512]{2,1,0:T(8,128)(2,1)} collective-permute-done((bf16[4,64,512]{2,1,0:T(8,128)(2,1)}, bf16[4,64,512]{2,1,0:T(8,128)(2,1)}, u32[]{:S(2)}, u32[]{:S(2)}) %collective-permute-start.17) | collective-permute-done | bytes 262176 | tf_op jit(solution)/shard_map/ppermute | solution.py:152
  163.0 7.2 %score_columns.2.refs_5_ = f32[512,512]{1,0:T(8,128)} custom-call(s32[8]{0:T(128)} %broadcast_xor_fusion.slots, s32[1]{0:T(128)} %bitcast.place, bf16[8,512,512]{2,1,0:T(8,128)(2,1)} %bitcast.20, f32[1,512]{1,0:T(1,128)} %bitcast.37, bf16[8,64,512]{2,1,0:T(8,128)(2,1)} %copy-done.1, bf16[8,64,512]{2,1,0:T(8,128)(2,1)} %copy-done.4, ...), custom_call_target="tpu_custom_call" | custom-call | flops 1073741824 | bytes 6291456 | tf_op jit(solution)/shard_map/score_columns/pallas_call | solution.py:86
  170.2 0.0 collective-permute-done.15.refs_4_
  170.2 3.1 %collective-permute-start.18 = (bf16[4,64,512]{2,1,0:T(8,128)(2,1)S(1)}, bf16[4,64,512]{2,1,0:T(8,128)(2,1)S(1)}, u32[]{:S(2)}, u32[]{:S(2)}) collective-permute-start(bf16[4,64,512]{2,1,0:T(8,128)(2,1)S(1)} %slice.44), channel_id=1, source_target_pairs={{0,16},{16,32},{32,48},{48,0},{1,17},{17,33},{33,49},{49,1},{2,18}... | collective-permute-start | bytes 786440 | tf_op jit(solution)/shard_map/ppermute | solution.py:157
  173.4 4.0 %collective-permute-start.19 = (bf16[4,64,512]{2,1,0:T(8,128)(2,1)S(1)}, bf16[4,64,512]{2,1,0:T(8,128)(2,1)S(1)}, u32[]{:S(2)}, u32[]{:S(2)}) collective-permute-start(bf16[4,64,512]{2,1,0:T(8,128)(2,1)S(1)} %slice.47), channel_id=1, source_target_pairs={{0,48},{16,0},{32,16},{48,32},{1,49},{17,1},{33,17},{49,33},{2,50}... | collective-permute-start | bytes 786440 | tf_op jit(solution)/shard_map/ppermute | solution.py:157
  177.3 2.4 %collective-permute-done.18.refs_2_ = bf16[4,64,512]{2,1,0:T(8,128)(2,1)S(1)} collective-permute-done((bf16[4,64,512]{2,1,0:T(8,128)(2,1)S(1)}, bf16[4,64,512]{2,1,0:T(8,128)(2,1)S(1)}, u32[]{:S(2)}, u32[]{:S(2)}) %collective-permute-start.18) | collective-permute-done | bytes 262176 | tf_op jit(solution)/shard_map/ppermute | solution.py:157
  179.7 1.9 collective-permute-done.19.refs_3_
  181.7 0.7 copy-done.10
  182.4 7.1 %score_columns.3 = f32[512,512]{1,0:T(8,128)} custom-call(s32[8]{0:T(128)} %broadcast_xor_fusion.slots, s32[1]{0:T(128)} %bitcast.place, bf16[8,512,512]{2,1,0:T(8,128)(2,1)} %bitcast.21, f32[1,512]{1,0:T(1,128)} %bitcast.38, bf16[8,64,512]{2,1,0:T(8,128)(2,1)} %copy-done, bf16[8,64,512]{2,1,0:T(8,128)(2,1)} %copy-done.5, ...), custom_call_target="tpu_custom_call", output_to_operand_aliasing={{}: (9, {})} | custom-call | flops 1073741824 | bytes 6291456 | tf_op jit(solution)/shard_map/score_columns/pallas_call | solution.py:86
  (41 shorter events, 0.4 us)
Async XLA Ops:
  6.5 59.3 %all-gather.4.cloned.1.call-start = ((), (), s32[]{:S(2)}) async-start(), calls=%async_computation.1 | async-start | bytes 4718592 | tf_op jit(solution)/shard_map/all_gather | solution.py:135
  25.4 30.5 %copy-start.11 = (s32[8]{0:T(128)S(1)}, s32[8]{0:T(128)}, u32[]{:S(2)}) copy-start(s32[8]{0:T(128)} %constant.14.clone) | copy-start | bytes 100
  25.4 130.1 %all-gather.6.cloned.1.call-start = ((), (), s32[]{:S(2)}) async-start(), calls=%async_computation.2 | async-start | bytes 4718592 | tf_op jit(solution)/shard_map/all_gather | solution.py:136
  26.4 11.4 %collective-permute-start.3 = (bf16[1,64,512]{2,1,0:T(8,128)(2,1)S(1)}, bf16[1,64,512]{2,1,0:T(8,128)(2,1)S(1)}, u32[]{:S(2)}, u32[]{:S(2)}) collective-permute-start(bf16[1,64,512]{2,1,0:T(8,128)(2,1)S(1)} %slice.35), channel_id=1, source_target_pairs={{0,256},{64,320},{128,384},{192,448},{256,0},{320,64},{384,128},{4... | collective-permute-start | bytes 196616 | tf_op jit(solution)/shard_map/ppermute | solution.py:113
  37.7 13.5 %collective-permute-start.4 = (bf16[2,64,512]{2,1,0:T(8,128)(2,1)S(1)}, bf16[2,64,512]{2,1,0:T(8,128)(2,1)S(1)}, u32[]{:S(2)}, u32[]{:S(2)}) collective-permute-start(bf16[2,64,512]{2,1,0:T(8,128)(2,1)S(1)} %pad_maximum_fusion.10), channel_id=1, source_target_pairs={{0,128},{64,192},{128,0},{192,64},{256,384},{320,448},{384,256},{4... | collective-permute-start | bytes 393224 | tf_op jit(solution)/shard_map/ppermute | solution.py:113
  43.1 13.4 %collective-permute-start = (bf16[1,64,512]{2,1,0:T(8,128)(2,1)S(1)}, bf16[1,64,512]{2,1,0:T(8,128)(2,1)S(1)}, u32[]{:S(2)}, u32[]{:S(2)}) collective-permute-start(bf16[1,64,512]{2,1,0:T(8,128)(2,1)S(1)} %slice.33), channel_id=1, source_target_pairs={{0,256},{64,320},{128,384},{192,448},{256,0},{320,64},{384,128},{4... | collective-permute-start | bytes 196616 | tf_op jit(solution)/shard_map/ppermute | solution.py:113
  51.3 12.0 %collective-permute-start.5 = (bf16[4,64,512]{2,1,0:T(8,128)(2,1)S(1)}, bf16[4,64,512]{2,1,0:T(8,128)(2,1)S(1)}, u32[]{:S(2)}, u32[]{:S(2)}) collective-permute-start(bf16[4,64,512]{2,1,0:T(8,128)(2,1)S(1)} %pad_maximum_fusion.6), channel_id=1, source_target_pairs={{0,64},{64,0},{128,192},{192,128},{256,320},{320,256},{384,448},{4... | collective-permute-start | bytes 786440 | tf_op jit(solution)/shard_map/ppermute | solution.py:113
  56.4 21.5 %collective-permute-start.1 = (bf16[2,64,512]{2,1,0:T(8,128)(2,1)S(1)}, bf16[2,64,512]{2,1,0:T(8,128)(2,1)S(1)}, u32[]{:S(2)}, u32[]{:S(2)}) collective-permute-start(bf16[2,64,512]{2,1,0:T(8,128)(2,1)S(1)} %pad_maximum_fusion.9), channel_id=1, source_target_pairs={{0,128},{64,192},{128,0},{192,64},{256,384},{320,448},{384,256},{4... | collective-permute-start | bytes 393224 | tf_op jit(solution)/shard_map/ppermute | solution.py:113
  70.3 14.7 %collective-permute-start.6 = (bf16[1,64,512]{2,1,0:T(8,128)(2,1)}, bf16[1,64,512]{2,1,0:T(8,128)(2,1)S(1)}, u32[]{:S(2)}, u32[]{:S(2)}) collective-permute-start(bf16[1,64,512]{2,1,0:T(8,128)(2,1)} %bitcast.23), channel_id=1, source_target_pairs={{0,256},{64,320},{128,384},{192,448},{256,0},{320,64},{384,128},{4... | collective-permute-start | bytes 196616 | tf_op jit(solution)/shard_map/ppermute | solution.py:113
  78.0 20.0 %collective-permute-start.2 = (bf16[4,64,512]{2,1,0:T(8,128)(2,1)S(1)}, bf16[4,64,512]{2,1,0:T(8,128)(2,1)S(1)}, u32[]{:S(2)}, u32[]{:S(2)}) collective-permute-start(bf16[4,64,512]{2,1,0:T(8,128)(2,1)S(1)} %pad_maximum_fusion.5), channel_id=1, source_target_pairs={{0,64},{64,0},{128,192},{192,128},{256,320},{320,256},{384,448},{4... | collective-permute-start | bytes 786440 | tf_op jit(solution)/shard_map/ppermute | solution.py:113
  85.8 9.3 %collective-permute-start.7 = (bf16[2,64,512]{2,1,0:T(8,128)(2,1)S(1)}, bf16[2,64,512]{2,1,0:T(8,128)(2,1)S(1)}, u32[]{:S(2)}, u32[]{:S(2)}) collective-permute-start(bf16[2,64,512]{2,1,0:T(8,128)(2,1)S(1)} %pad_maximum_fusion.11), channel_id=1, source_target_pairs={{0,128},{64,192},{128,0},{192,64},{256,384},{320,448},{384,256},{4... | collective-permute-start | bytes 393224 | tf_op jit(solution)/shard_map/ppermute | solution.py:113
  96.0 25.3 %collective-permute-start.11 = (bf16[4,64,512]{2,1,0:T(8,128)(2,1)S(1)}, bf16[4,64,512]{2,1,0:T(8,128)(2,1)S(1)}, u32[]{:S(2)}, u32[]{:S(2)}) collective-permute-start(bf16[4,64,512]{2,1,0:T(8,128)(2,1)S(1)} %pad_maximum_fusion.7), channel_id=1, source_target_pairs={{0,64},{64,0},{128,192},{192,128},{256,320},{320,256},{384,448},{4... | collective-permute-start | bytes 786440 | tf_op jit(solution)/shard_map/ppermute | solution.py:113
  98.8 22.5 %copy-start.6 = (bf16[64,512]{1,0:T(8,128)(2,1)S(1)}, bf16[64,512]{1,0:T(8,128)(2,1)}, u32[]{:S(2)}) copy-start(bf16[64,512]{1,0:T(8,128)(2,1)} %kernel_matrix.3) | copy-start | bytes 196612
  103.3 25.1 %copy-start.7 = (bf16[64,512]{1,0:T(8,128)(2,1)S(1)}, bf16[64,512]{1,0:T(8,128)(2,1)}, u32[]{:S(2)}) copy-start(bf16[64,512]{1,0:T(8,128)(2,1)} %kernel_matrix.2) | copy-start | bytes 196612
  103.3 10.9 %collective-permute-start.8 = (bf16[1,64,512]{2,1,0:T(8,128)(2,1)}, bf16[1,64,512]{2,1,0:T(8,128)(2,1)S(1)}, u32[]{:S(2)}, u32[]{:S(2)}) collective-permute-start(bf16[1,64,512]{2,1,0:T(8,128)(2,1)} %bitcast.27), channel_id=1, source_target_pairs={{0,256},{64,320},{128,384},{192,448},{256,0},{320,64},{384,128},{4... | collective-permute-start | bytes 196616 | tf_op jit(solution)/shard_map/ppermute | solution.py:113
  115.1 13.3 %collective-permute-start.9 = (bf16[2,64,512]{2,1,0:T(8,128)(2,1)S(1)}, bf16[2,64,512]{2,1,0:T(8,128)(2,1)S(1)}, u32[]{:S(2)}, u32[]{:S(2)}) collective-permute-start(bf16[2,64,512]{2,1,0:T(8,128)(2,1)S(1)} %pad_maximum_fusion.12), channel_id=1, source_target_pairs={{0,128},{64,192},{128,0},{192,64},{256,384},{320,448},{384,256},{4... | collective-permute-start | bytes 393224 | tf_op jit(solution)/shard_map/ppermute | solution.py:113
  121.4 29.2 %copy-start.1 = (bf16[8,64,512]{2,1,0:T(8,128)(2,1)}, bf16[8,64,512]{2,1,0:T(8,128)(2,1)S(1)}, u32[]{:S(2)}) copy-start(bf16[8,64,512]{2,1,0:T(8,128)(2,1)S(1)} %pad_maximum_fusion.4.refs_0_) | copy-start | bytes 1572868
  121.4 16.6 %collective-permute-start.12 = (bf16[8,64,512]{2,1,0:T(8,128)(2,1)S(1)}, bf16[8,64,512]{2,1,0:T(8,128)(2,1)S(1)}, u32[]{:S(2)}, u32[]{:S(2)}) collective-permute-start(bf16[8,64,512]{2,1,0:T(8,128)(2,1)S(1)} %pad_maximum_fusion.4.refs_0_), channel_id=1, source_target_pairs={{0,16},{16,32},{32,48},{48,0},{1,17},{17,33},{33,49},{49,1},{2,18}... | collective-permute-start | bytes 1572872 | tf_op jit(solution)/shard_map/ppermute | solution.py:149
  124.8 15.1 %collective-permute-start.13 = (bf16[8,64,512]{2,1,0:T(8,128)(2,1)S(1)}, bf16[8,64,512]{2,1,0:T(8,128)(2,1)S(1)}, u32[]{:S(2)}, u32[]{:S(2)}) collective-permute-start(bf16[8,64,512]{2,1,0:T(8,128)(2,1)S(1)} %pad_maximum_fusion.4.refs_0_), channel_id=1, source_target_pairs={{0,48},{16,0},{32,16},{48,32},{1,49},{17,1},{33,17},{49,33},{2,50}... | collective-permute-start | bytes 1572872 | tf_op jit(solution)/shard_map/ppermute | solution.py:149
  128.5 9.2 %collective-permute-start.10 = (bf16[4,64,512]{2,1,0:T(8,128)(2,1)S(1)}, bf16[4,64,512]{2,1,0:T(8,128)(2,1)S(1)}, u32[]{:S(2)}, u32[]{:S(2)}) collective-permute-start(bf16[4,64,512]{2,1,0:T(8,128)(2,1)S(1)} %pad_maximum_fusion.8), channel_id=1, source_target_pairs={{0,64},{64,0},{128,192},{192,128},{256,320},{320,256},{384,448},{4... | collective-permute-start | bytes 786440 | tf_op jit(solution)/shard_map/ppermute | solution.py:113
  137.8 32.3 %copy-start = (bf16[8,64,512]{2,1,0:T(8,128)(2,1)}, bf16[8,64,512]{2,1,0:T(8,128)(2,1)S(1)}, u32[]{:S(2)}) copy-start(bf16[8,64,512]{2,1,0:T(8,128)(2,1)S(1)} %pad_maximum_fusion.3.refs_0_) | copy-start | bytes 1572868
  138.0 25.0 %copy-start.2 = (bf16[8,64,512]{2,1,0:T(8,128)(2,1)}, bf16[8,64,512]{2,1,0:T(8,128)(2,1)S(1)}, u32[]{:S(2)}) copy-start(bf16[8,64,512]{2,1,0:T(8,128)(2,1)S(1)} %collective-permute-done.12.refs_4_) | copy-start | bytes 1572868
  139.9 23.1 %copy-start.4 = (bf16[8,64,512]{2,1,0:T(8,128)(2,1)}, bf16[8,64,512]{2,1,0:T(8,128)(2,1)S(1)}, u32[]{:S(2)}) copy-start(bf16[8,64,512]{2,1,0:T(8,128)(2,1)S(1)} %collective-permute-done.13.refs_1_) | copy-start | bytes 1572868
  139.9 30.2 %collective-permute-start.15 = (bf16[8,64,512]{2,1,0:T(8,128)(2,1)S(1)}, bf16[8,64,512]{2,1,0:T(8,128)(2,1)S(1)}, u32[]{:S(2)}, u32[]{:S(2)}) collective-permute-start(bf16[8,64,512]{2,1,0:T(8,128)(2,1)S(1)} %pad_maximum_fusion.3.refs_0_), channel_id=1, source_target_pairs={{0,16},{16,32},{32,48},{48,0},{1,17},{17,33},{33,49},{49,1},{2,18}... | collective-permute-start | bytes 1572872 | tf_op jit(solution)/shard_map/ppermute | solution.py:154
  143.3 30.0 %collective-permute-start.14 = (bf16[8,64,512]{2,1,0:T(8,128)(2,1)S(1)}, bf16[8,64,512]{2,1,0:T(8,128)(2,1)S(1)}, u32[]{:S(2)}, u32[]{:S(2)}) collective-permute-start(bf16[8,64,512]{2,1,0:T(8,128)(2,1)S(1)} %pad_maximum_fusion.3.refs_0_), channel_id=1, source_target_pairs={{0,48},{16,0},{32,16},{48,32},{1,49},{17,1},{33,17},{49,33},{2,50}... | collective-permute-start | bytes 1572872 | tf_op jit(solution)/shard_map/ppermute | solution.py:154
  147.7 13.3 %collective-permute-start.16 = (bf16[4,64,512]{2,1,0:T(8,128)(2,1)}, bf16[4,64,512]{2,1,0:T(8,128)(2,1)S(1)}, u32[]{:S(2)}, u32[]{:S(2)}) collective-permute-start(bf16[4,64,512]{2,1,0:T(8,128)(2,1)} %slice.45), channel_id=1, source_target_pairs={{0,16},{16,32},{32,48},{48,0},{1,17},{17,33},{33,49},{49,1},{2,18}... | collective-permute-start | bytes 786440 | tf_op jit(solution)/shard_map/ppermute | solution.py:152
  150.6 12.4 %collective-permute-start.17 = (bf16[4,64,512]{2,1,0:T(8,128)(2,1)}, bf16[4,64,512]{2,1,0:T(8,128)(2,1)}, u32[]{:S(2)}, u32[]{:S(2)}) collective-permute-start(bf16[4,64,512]{2,1,0:T(8,128)(2,1)} %slice.46), channel_id=1, source_target_pairs={{0,48},{16,0},{32,16},{48,32},{1,49},{17,1},{33,17},{49,33},{2,50}... | collective-permute-start | bytes 786440 | tf_op jit(solution)/shard_map/ppermute | solution.py:152
  161.0 2.0 %copy-start.8 = (bf16[4,64,512]{2,1,0:T(8,128)(2,1)}, bf16[4,64,512]{2,1,0:T(8,128)(2,1)S(1)}, u32[]{:S(2)}) copy-start(bf16[4,64,512]{2,1,0:T(8,128)(2,1)S(1)} %collective-permute-done.16.refs_2_) | copy-start | bytes 786436
  170.2 11.5 %copy-start.3 = (bf16[8,64,512]{2,1,0:T(8,128)(2,1)}, bf16[8,64,512]{2,1,0:T(8,128)(2,1)S(1)}, u32[]{:S(2)}) copy-start(bf16[8,64,512]{2,1,0:T(8,128)(2,1)S(1)} %collective-permute-done.15.refs_4_) | copy-start | bytes 1572868
  170.2 9.5 %collective-permute-start.18 = (bf16[4,64,512]{2,1,0:T(8,128)(2,1)S(1)}, bf16[4,64,512]{2,1,0:T(8,128)(2,1)S(1)}, u32[]{:S(2)}, u32[]{:S(2)}) collective-permute-start(bf16[4,64,512]{2,1,0:T(8,128)(2,1)S(1)} %slice.44), channel_id=1, source_target_pairs={{0,16},{16,32},{32,48},{48,0},{1,17},{17,33},{33,49},{49,1},{2,18}... | collective-permute-start | bytes 786440 | tf_op jit(solution)/shard_map/ppermute | solution.py:157
  173.3 8.3 %copy-start.5 = (bf16[8,64,512]{2,1,0:T(8,128)(2,1)}, bf16[8,64,512]{2,1,0:T(8,128)(2,1)S(1)}, u32[]{:S(2)}) copy-start(bf16[8,64,512]{2,1,0:T(8,128)(2,1)S(1)} %collective-permute-done.14.refs_1_) | copy-start | bytes 1572868
  173.4 8.3 %collective-permute-start.19 = (bf16[4,64,512]{2,1,0:T(8,128)(2,1)S(1)}, bf16[4,64,512]{2,1,0:T(8,128)(2,1)S(1)}, u32[]{:S(2)}, u32[]{:S(2)}) collective-permute-start(bf16[4,64,512]{2,1,0:T(8,128)(2,1)S(1)} %slice.47), channel_id=1, source_target_pairs={{0,48},{16,0},{32,16},{48,32},{1,49},{17,1},{33,17},{49,33},{2,50}... | collective-permute-start | bytes 786440 | tf_op jit(solution)/shard_map/ppermute | solution.py:157
  179.7 2.0 copy-start.9
  181.7 0.7 copy-start.10
Sparse Core Ops, SparseCore 0:
  25.5 40.2 all-gather.3
  68.0 39.7 all-gather.5

commit v4 on v0

v4 whole, which is shorter than its diff:
```python
import jax
import jax.numpy as jnp
from jax import lax
from jax.experimental import pallas as pl
from jax.experimental.pallas import tpu as pltpu
from jax.sharding import Mesh, PartitionSpec as P

NZ, NY, HALVES = 8, 4, 2
NN_DIMS = (((1,), (0,)), ((), ()))
NT_DIMS = (((1,), (1,)), ((), ()))
RELATIVE = (0, 4, 2, 6, 1, 5, 3, 7)
VMEM_LIMIT = 24 * 1024 * 1024


def product(slots, place, left, blocks, dims, half, start=None, weight=None, out=None, dtype=jnp.float32):
    n, rows, depth = left.shape
    width = depth // NY
    columns = blocks[0][1][0].shape[2 if dims == NN_DIMS else 1]
    row_block = 0
    if half is not None and weight is None:
        rows, row_block = rows // HALVES, half
    operands = [slots, place, left]
    in_specs = [pl.BlockSpec((1, rows, depth), lambda s, slots, place: (slots[s], row_block, 0))]
    for _, cuts in blocks:
        first = 0
        for cut in cuts:
            size, *block = cut.shape
            in_specs.append(
                pl.BlockSpec(
                    (1, *block),
                    lambda s, slots, place, first=first, size=size: (jnp.clip(s - first, 0, size - 1), 0, 0),
                )
            )
            operands.append(cut)
            first += size
    if start is not None:
        in_specs.append(pl.BlockSpec((rows, columns), lambda s, slots, place: (row_block, 0)))
        operands.append(start)
    if weight is not None:
        in_specs.append(pl.BlockSpec((1, columns), lambda s, slots, place: (0, 0)))
        operands.append(weight)
    aliases = {}
    if out is not None:
        in_specs.append(pl.BlockSpec(memory_space=pl.ANY))
        aliases = {len(operands): 0}
        operands.append(out)

    def kernel(slots, place, left_ref, *refs):
        refs = list(refs)
        out_ref, total = refs[-2:]
        step = pl.program_id(0)
        cut_refs = [(d, [refs.pop(0) for _ in cuts]) for d, cuts in blocks]
        start_ref = refs.pop(0) if start is not None else None
        weight_ref = refs.pop(0) if weight is not None else None

        @pl.when(step == 0)
        def _():
            total[...] = jnp.zeros_like(total) if start_ref is None else start_ref[...]

        for d, cut in cut_refs:
            offset = pl.multiple_of(lax.rem(place[0] + d, NY) * width, width)
            right = cut[0][0] if len(cut) == 1 else jnp.where(step < n // 2, cut[0][0], cut[1][0])
            total[...] += lax.dot_general(
                left_ref[0, :, pl.ds(offset, width)], right, dims, preferred_element_type=jnp.float32
            )

        @pl.when(step == n - 1)
        def _():
            whole = total[...] if weight_ref is None else total[...] * weight_ref[...]
            out_ref[...] = whole.astype(out_ref.dtype)

    whole_out = weight is not None
    return pl.pallas_call(
        kernel,
        out_shape=jax.ShapeDtypeStruct((rows * HALVES if whole_out else rows, columns), dtype),
        grid_spec=pltpu.PrefetchScalarGridSpec(
            num_scalar_prefetch=2,
            grid=(n,),
            in_specs=in_specs,
            out_specs=pl.BlockSpec((rows, columns), lambda s, slots, place: (half if whole_out else 0, 0)),
            scratch_shapes=[pltpu.VMEM((rows, columns), jnp.float32)],
        ),
        input_output_aliases=aliases,
        compiler_params=pltpu.CompilerParams(vmem_limit_bytes=VMEM_LIMIT),
        cost_estimate=pl.CostEstimate(
            flops=2 * n * rows * columns * width * len(blocks),
            bytes_accessed=2 * n * (rows * depth + columns * width * len(blocks)),
            transcendentals=0,
        ),
        name="scores" if whole_out else "preconditioned",
    )(*operands)


def after(array, *earlier):
    return lax.optimization_barrier((array, earlier))[0]


def exchange(held, distance):
    other = lax.ppermute(held, "z", [(i, i ^ distance) for i in range(NZ)])
    return jnp.concatenate([held, other], axis=0)


def neighbours_y(own):
    return (
        lax.ppermute(own, "y", [(i, (i + 1) % NY) for i in range(NY)]),
        lax.ppermute(own, "y", [(i, (i - 1) % NY) for i in range(NY)]),
    )


def opposite_y(below, above):
    half = below.shape[0] // 2
    return (
        lax.ppermute(below[:half], "y", [(i, (i + 1) % NY) for i in range(NY)]),
        lax.ppermute(above[half:], "y", [(i, (i - 1) % NY) for i in range(NY)]),
    )


def local(query_features, inverse_gram, training_features, residual_weight):
    slots = lax.axis_index("z") ^ jnp.array(RELATIVE, jnp.int32)
    place = lax.axis_index("y").astype(jnp.int32)[None]
    ta = ("x", "core")

    query = lax.all_gather(query_features, ta, axis=0)
    gram = exchange(exchange(exchange(inverse_gram[None], 4), 2), 1)
    gram_below, gram_above = neighbours_y(gram)
    training = exchange(after(training_features[None], gram), 4)
    gram_far = opposite_y(after(gram_below, training), after(gram_above, training))
    training = exchange(training, 2)
    query = after(query, training)
    training = exchange(training, 1)
    near = product(
        slots, place, query, ((0, (gram,)), (1, (gram_above,)), (3, (gram_below,))), NN_DIMS, None
    )
    gathered = []
    for half in range(HALVES):
        pre = product(slots, place, query, ((2, gram_far),), NN_DIMS, half, start=near, dtype=jnp.bfloat16)
        gathered.append(lax.all_gather(pre, ta, axis=0))

    training = after(training, *gram_far)
    below, above = neighbours_y(training)
    far = opposite_y(below, above)
    weight = residual_weight[None, :]
    out = None
    for half, pre in enumerate(gathered):
        blocks = ((0, (training,)), (1, (above,)), (2, far), (3, (below,)))
        out = product(slots, place, pre, blocks, NT_DIMS, half, weight=weight, out=out)
    return out


def solution(mesh):
    fine = Mesh(mesh.devices.reshape(NZ, NY, 4, 2, 2), ("z", "y", "x", "core", "row"))
    pb, ta = ("z", "y"), ("x", "core")
    placed = (P(pb, ta), P(pb, ta), P(("row", *ta), pb), P(("row", *ta)))
    return jax.shard_map(
        local, mesh=fine, in_specs=placed, out_specs=P(pb, ("row", *ta)), check_vma=False
    )
```

time: 526 us -> 212 us (0.40)
  waiting for transfers between devices: 496 us -> 96.9 us
  starting transfers between devices: 0.12 us -> 50.9 us
  Pallas kernels: 0 us -> 27.7 us
  local copies, waits for them, and re-layouts: 0.01 us -> 18.9 us
  matrix products: 13.4 us -> 0 us
    all_gather x4 -> x3, waiting for transfers between devices: 494 us -> 0.02 us  [the longest x1 0.02 us: local(): query = lax.all_gather(query_features, ta, axis=0)]
    ppermute x0 -> x14, waiting for transfers between devices: none -> 96.1 us  [the longest x6 66.4 us: exchange(): other = lax.ppermute(held, 'z', [(i, i ^ distance) for i in range(NZ)])]
    ppermute x0 -> x14, starting transfers between devices: none -> 50.8 us  [the longest x6 23.1 us: exchange(): other = lax.ppermute(held, 'z', [(i, i ^ distance) for i in range(NZ)])]
    pallas_call x0 -> x5, Pallas kernels: none -> 27.7 us  [product(): pl.pallas_call(kernel, out_shape=jax.ShapeDtypeStruct((rows * HALVES if w...]
    unnamed x2 -> x41, local copies, waits for them, and re-layouts: 0.01 us -> 17 us
    dot_general x2 -> x0, matrix products: 13.4 us -> none  [the longest x1 6.8 us: local(): lax.dot_general(columns, lax.all_gather(training_features, 'pb', axis=1,...]
  transfers between devices with their start and end apart: 4 -> 17, of which waited for: 4 -> 10; matrix products, arithmetic and copies ran while one was open for 1% -> 2% of each run, Pallas kernels for 0% -> 8%
where the time goes in v4:
time: 212 us; the launch traced here: 210 us
  waiting for transfers between devices  96.9 us (46%)
  starting transfers between devices  50.9 us (24%)
  Pallas kernels  27.7 us (13%)
  local copies, waits for them, and re-layouts  18.9 us (9%)
  between operations  13.4 us (6%)
    ppermute x6, waiting for transfers between devices, exchange(): other = lax.ppermute(held, 'z', [(i, i ^ distance) for i in range(NZ)])  66.4 us
    pallas_call x5, Pallas kernels, product(): pl.pallas_call(kernel, out_shape=jax.ShapeDtypeStruct((rows * HALVES if w...  27.7 us
    ppermute x6, starting transfers between devices, exchange(): other = lax.ppermute(held, 'z', [(i, i ^ distance) for i in range(NZ)])  23.1 us
    ppermute x2, waiting for transfers between devices, neighbours_y(): lax.ppermute(own, 'y', [(i, (i + 1) % NY) for i in range(NY)])  19.6 us
    unnamed x41, local copies, waits for them, and re-layouts  17 us
    ppermute x2, starting transfers between devices, neighbours_y(): lax.ppermute(own, 'y', [(i, (i - 1) % NY) for i in range(NY)])  10.1 us
    ppermute x2, starting transfers between devices, opposite_y(): lax.ppermute(above[half:], 'y', [(i, (i - 1) % NY) for i in range(NY)])  9.97 us
    ppermute x2, waiting for transfers between devices, opposite_y(): lax.ppermute(below[:half], 'y', [(i, (i + 1) % NY) for i in range(NY)])  9.68 us
  transfers between devices with their start and end apart: 17, of which 10 were waited for; matrix products, arithmetic and copies ran while one was open for 2% of the time, Pallas kernels for 8%

profile of v4, /device:TPU:6, one launch (start us, length us, event | category | flops | bytes accessed | tf_op | source)
XLA Modules:
  0.0 209.9 jit_solution(13126272216392114343)
XLA Ops:
  6.5 0.0 all-gather.7.cloned.1.call-start
  6.5 0.7 all-gather.7.cloned.1.call-update
  7.3 0.0 all-gather.11.cloned.1.call-start
  7.3 9.1 %collective-permute-start = (bf16[1,128,512]{2,1,0:T(8,128)(2,1)}, bf16[1,128,512]{2,1,0:T(8,128)(2,1)S(1)}, u32[]{:S(2)}, u32[]{:S(2)}) collective-permute-start(bf16[1,128,512]{2,1,0:T(8,128)(2,1)} %bitcast.14), channel_id=1, source_target_pairs={{0,256},{64,320},{128,384},{192,448},{256,0},{320,64},{384,128},{4... | collective-permute-start | bytes 393224 | tf_op jit(solution)/shard_map/ppermute | solution.py:99
  16.4 12.1 %collective-permute-done = bf16[1,128,512]{2,1,0:T(8,128)(2,1)S(1)} collective-permute-done((bf16[1,128,512]{2,1,0:T(8,128)(2,1)}, bf16[1,128,512]{2,1,0:T(8,128)(2,1)S(1)}, u32[]{:S(2)}, u32[]{:S(2)}) %collective-permute-start) | collective-permute-done | bytes 131104 | tf_op jit(solution)/shard_map/ppermute | solution.py:99
  28.5 0.9 pad_maximum_fusion.3
  29.5 1.9 collective-permute-start.1
  31.4 14.0 %collective-permute-done.1 = bf16[2,128,512]{2,1,0:T(8,128)(2,1)S(1)} collective-permute-done((bf16[2,128,512]{2,1,0:T(8,128)(2,1)S(1)}, bf16[2,128,512]{2,1,0:T(8,128)(2,1)S(1)}, u32[]{:S(2)}, u32[]{:S(2)}) %collective-permute-start.1) | collective-permute-done | bytes 262176 | tf_op jit(solution)/shard_map/ppermute | solution.py:99
  45.4 1.0 pad_maximum_fusion.2
  46.3 0.0 copy-start.19
  46.4 1.9 collective-permute-start.2
  48.3 13.1 %collective-permute-done.2 = bf16[4,128,512]{2,1,0:T(8,128)(2,1)S(1)} collective-permute-done((bf16[4,128,512]{2,1,0:T(8,128)(2,1)S(1)}, bf16[4,128,512]{2,1,0:T(8,128)(2,1)S(1)}, u32[]{:S(2)}, u32[]{:S(2)}) %collective-permute-start.2) | collective-permute-done | bytes 524320 | tf_op jit(solution)/shard_map/ppermute | solution.py:99
  61.4 0.1 pad_maximum_fusion.refs_0_
  61.5 4.9 %collective-permute-start.7 = (bf16[8,128,512]{2,1,0:T(8,128)(2,1)S(1)}, bf16[8,128,512]{2,1,0:T(8,128)(2,1)S(1)}, u32[]{:S(2)}, u32[]{:S(2)}) collective-permute-start(bf16[8,128,512]{2,1,0:T(8,128)(2,1)S(1)} %pad_maximum_fusion.refs_0_), channel_id=1, source_target_pairs={{0,48},{16,0},{32,16},{48,32},{1,49},{17,1},{33,17},{49,33},{2,50}... | collective-permute-start | bytes 3145736 | tf_op jit(solution)/shard_map/ppermute | solution.py:106
  66.4 1.9 collective-permute-start.5
  68.4 0.0 copy-done.14
  68.4 5.4 %collective-permute-start.3 = (bf16[1,512,128]{2,1,0:T(8,128)(2,1)S(1)}, bf16[1,512,128]{2,1,0:T(8,128)(2,1)S(1)}, u32[]{:S(2)}, u32[]{:S(2)}) collective-permute-start(bf16[1,512,128]{2,1,0:T(8,128)(2,1)S(1)} %bitcast.18), channel_id=1, source_target_pairs={{0,256},{64,320},{128,384},{192,448},{256,0},{320,64},{384,128},{4... | collective-permute-start | bytes 393224 | tf_op jit(solution)/shard_map/ppermute | solution.py:99
  73.9 12.3 %collective-permute-done.3 = bf16[1,512,128]{2,1,0:T(8,128)(2,1)S(1)} collective-permute-done((bf16[1,512,128]{2,1,0:T(8,128)(2,1)S(1)}, bf16[1,512,128]{2,1,0:T(8,128)(2,1)S(1)}, u32[]{:S(2)}, u32[]{:S(2)}) %collective-permute-start.3) | collective-permute-done | bytes 131104 | tf_op jit(solution)/shard_map/ppermute | solution.py:99
  86.2 0.6 copy-done.15
  86.8 1.9 collective-permute-start.4
  88.7 0.0 collective-permute-done.7.refs_1_
  88.7 0.8 slice.13
  89.6 4.8 %collective-permute-start.8 = (bf16[4,128,512]{2,1,0:T(8,128)(2,1)}, bf16[4,128,512]{2,1,0:T(8,128)(2,1)}, u32[]{:S(2)}, u32[]{:S(2)}) collective-permute-start(bf16[4,128,512]{2,1,0:T(8,128)(2,1)} %slice.13), channel_id=1, source_target_pairs={{0,48},{16,0},{32,16},{48,32},{1,49},{17,1},{33,17},{49,33},{2,50}... | collective-permute-start | bytes 1572872 | tf_op jit(solution)/shard_map/ppermute | solution.py:114
  94.4 0.0 collective-permute-done.5.refs_2_
  94.4 0.9 slice.12
  95.3 1.0 copy-done.2
  96.3 1.9 collective-permute-start.6
  98.2 3.2 %collective-permute-done.4 = bf16[2,512,128]{2,1,0:T(8,128)(2,1)S(1)} collective-permute-done((bf16[2,512,128]{2,1,0:T(8,128)(2,1)S(1)}, bf16[2,512,128]{2,1,0:T(8,128)(2,1)S(1)}, u32[]{:S(2)}, u32[]{:S(2)}) %collective-permute-start.4) | collective-permute-done | bytes 262176 | tf_op jit(solution)/shard_map/ppermute | solution.py:99
  101.4 0.0 all-gather.7.cloned.1.call-done
  101.5 0.8 copy-done.17
  102.3 2.2 %copy-done = bf16[4096,512]{1,0:T(8,128)(2,1)S(1)} copy-done((bf16[4096,512]{1,0:T(8,128)(2,1)S(1)}, bf16[4096,512]{1,0:T(8,128)(2,1)}, u32[]{:S(2)}) %copy-start) | copy-done | bytes 4194328
  104.5 1.2 copy-done.3
  105.7 5.2 %preconditioned.3.refs_2_ = f32[512,512]{1,0:T(8,128)S(1)} custom-call(s32[8]{0:T(128)S(1)} %broadcast_xor_fusion.slots, s32[1]{0:T(128)} %bitcast.place, bf16[8,512,512]{2,1,0:T(8,128)(2,1)S(1)} %bitcast.7, bf16[8,128,512]{2,1,0:T(8,128)(2,1)S(1)} %pad_maximum_fusion.refs_0_, bf16[8,128,512]{2,1,0:T(8,128)(2,1)S(1)} %collective-permute-done.7.refs_1_, ...), custom_call_target="tpu_custom_call" | custom-call | flops 1610612736 | bytes 7340032 | tf_op jit(solution)/shard_map/preconditioned/pallas_call | solution.py:73
  110.9 0.0 collective-permute-done.8.refs_1_
  110.9 2.3 %collective-permute-done.6.refs_0_ = bf16[4,128,512]{2,1,0:T(8,128)(2,1)} collective-permute-done((bf16[4,128,512]{2,1,0:T(8,128)(2,1)}, bf16[4,128,512]{2,1,0:T(8,128)(2,1)}, u32[]{:S(2)}, u32[]{:S(2)}) %collective-permute-start.6) | collective-permute-done | bytes 524320 | tf_op jit(solution)/shard_map/ppermute | solution.py:113
  113.2 6.2 %preconditioned.5 = bf16[256,512]{1,0:T(8,128)(2,1)} custom-call(s32[8]{0:T(128)S(1)} %broadcast_xor_fusion.slots, s32[1]{0:T(128)} %bitcast.place, bf16[8,512,512]{2,1,0:T(8,128)(2,1)S(1)} %bitcast.8, bf16[4,128,512]{2,1,0:T(8,128)(2,1)} %collective-permute-done.6.refs_0_, bf16[4,128,512]{2,1,0:T(8,128)(2,1)} %collective-permute-done.8.refs_1_, ...), custom_call_target="tpu_custom_call" | custom-call | flops 268435456 | bytes 3145728 | tf_op jit(solution)/shard_map/preconditioned/pallas_call | solution.py:73
  119.4 0.0 all-gather.11.cloned.1.call-update
  119.4 0.0 all-gather.9.cloned.1.call-start
  119.5 2.2 %copy-done.1 = bf16[4096,512]{1,0:T(8,128)(2,1)S(1)} copy-done((bf16[4096,512]{1,0:T(8,128)(2,1)S(1)}, bf16[4096,512]{1,0:T(8,128)(2,1)}, u32[]{:S(2)}) %copy-start.1) | copy-done | bytes 4194328
  121.7 6.2 %preconditioned.4 = bf16[256,512]{1,0:T(8,128)(2,1)} custom-call(s32[8]{0:T(128)S(1)} %broadcast_xor_fusion.slots, s32[1]{0:T(128)} %bitcast.place, bf16[8,512,512]{2,1,0:T(8,128)(2,1)S(1)} %bitcast.9, bf16[4,128,512]{2,1,0:T(8,128)(2,1)} %collective-permute-done.6.refs_0_, bf16[4,128,512]{2,1,0:T(8,128)(2,1)} %collective-permute-done.8.refs_1_, ...), custom_call_target="tpu_custom_call" | custom-call | flops 268435456 | bytes 3145728 | tf_op jit(solution)/shard_map/preconditioned/pallas_call | solution.py:73
  127.9 0.0 all-gather.9.cloned.1.call-update
  127.9 0.0 copy-start.12
  127.9 2.8 %collective-permute-start.9 = (bf16[4,512,128]{2,1,0:T(8,128)(2,1)S(1)}, bf16[4,512,128]{2,1,0:T(8,128)(2,1)S(1)}, u32[]{:S(2)}, u32[]{:S(2)}) collective-permute-start(bf16[4,512,128]{2,1,0:T(8,128)(2,1)S(1)} %copy-done.18), channel_id=1, source_target_pairs={{0,64},{64,0},{128,192},{192,128},{256,320},{320,256},{384,448},{4... | collective-permute-start | bytes 1572872 | tf_op jit(solution)/shard_map/ppermute | solution.py:99
  130.7 11.7 %collective-permute-done.9 = bf16[4,512,128]{2,1,0:T(8,128)(2,1)S(1)} collective-permute-done((bf16[4,512,128]{2,1,0:T(8,128)(2,1)S(1)}, bf16[4,512,128]{2,1,0:T(8,128)(2,1)S(1)}, u32[]{:S(2)}, u32[]{:S(2)}) %collective-permute-start.9) | collective-permute-done | bytes 524320 | tf_op jit(solution)/shard_map/ppermute | solution.py:99
  142.5 0.1 pad_maximum_fusion.1.refs_0_
  142.6 1.9 collective-permute-start.11
  144.5 5.1 %collective-permute-start.10 = (bf16[8,512,128]{2,1,0:T(8,128)(2,1)S(1)}, bf16[8,512,128]{2,1,0:T(8,128)(2,1)S(1)}, u32[]{:S(2)}, u32[]{:S(2)}) collective-permute-start(bf16[8,512,128]{2,1,0:T(8,128)(2,1)S(1)} %pad_maximum_fusion.1.refs_0_), channel_id=1, source_target_pairs={{0,48},{16,0},{32,16},{48,32},{1,49},{17,1},{33,17},{49,33},{2,50}... | collective-permute-start | bytes 3145736 | tf_op jit(solution)/shard_map/ppermute | solution.py:106
  149.7 19.6 %collective-permute-done.11.refs_4_ = bf16[8,512,128]{2,1,0:T(8,128)(2,1)S(1)} collective-permute-done((bf16[8,512,128]{2,1,0:T(8,128)(2,1)S(1)}, bf16[8,512,128]{2,1,0:T(8,128)(2,1)S(1)}, u32[]{:S(2)}, u32[]{:S(2)}) %collective-permute-start.11) | collective-permute-done | bytes 1048608 | tf_op jit(solution)/shard_map/ppermute | solution.py:105
  169.3 1.9 collective-permute-start.12
  171.2 0.0 collective-permute-done.10.refs_1_
  171.3 5.1 %collective-permute-start.13 = (bf16[4,512,128]{2,1,0:T(8,128)(2,1)S(1)}, bf16[4,512,128]{2,1,0:T(8,128)(2,1)S(1)}, u32[]{:S(2)}, u32[]{:S(2)}) collective-permute-start(bf16[4,512,128]{2,1,0:T(8,128)(2,1)S(1)} %slice.17), channel_id=1, source_target_pairs={{0,48},{16,0},{32,16},{48,32},{1,49},{17,1},{33,17},{49,33},{2,50}... | collective-permute-start | bytes 1572872 | tf_op jit(solution)/shard_map/ppermute | solution.py:114
  176.4 7.4 %collective-permute-done.12.refs_2_ = bf16[4,512,128]{2,1,0:T(8,128)(2,1)S(1)} collective-permute-done((bf16[4,512,128]{2,1,0:T(8,128)(2,1)S(1)}, bf16[4,512,128]{2,1,0:T(8,128)(2,1)S(1)}, u32[]{:S(2)}, u32[]{:S(2)}) %collective-permute-start.12) | collective-permute-done | bytes 524320 | tf_op jit(solution)/shard_map/ppermute | solution.py:113
  183.8 0.8 copy-done.6
  184.6 0.4 collective-permute-done.13.refs_3_
  185.0 0.8 copy-done.9
  185.8 0.0 copy-done.12
  185.9 1.6 copy-done.4
  187.4 1.0 copy-done.7
  188.5 1.0 copy-done.10
  189.5 5.1 %scores.2.refs_6_ = f32[512,512]{1,0:T(8,128)} custom-call(s32[8]{0:T(128)S(1)} %broadcast_xor_fusion.slots, s32[1]{0:T(128)} %bitcast.place, bf16[8,256,512]{2,1,0:T(8,128)(2,1)S(1)} %bitcast.10, bf16[8,512,128]{2,1,0:T(8,128)(2,1)S(1)} %pad_maximum_fusion.1.refs_0_, bf16[8,512,128]{2,1,0:T(8,128)(2,1)S(1)} %collective-permute-done.10.refs_1_, ...), custom_call_target="tpu_custom_call" | custom-call | flops 1073741824 | bytes 6291456 | tf_op jit(solution)/shard_map/scores/pallas_call | solution.py:73
  194.6 1.6 copy-done.5
  196.2 1.0 copy-done.8
  197.2 1.0 copy-done.11
  198.3 5.1 %scores.3 = f32[512,512]{1,0:T(8,128)} custom-call(s32[8]{0:T(128)S(1)} %broadcast_xor_fusion.slots, s32[1]{0:T(128)} %bitcast.place, bf16[8,256,512]{2,1,0:T(8,128)(2,1)S(1)} %bitcast.11, bf16[8,512,128]{2,1,0:T(8,128)(2,1)S(1)} %pad_maximum_fusion.1.refs_0_, ...), custom_call_target="tpu_custom_call", output_to_operand_aliasing={{}: (9, {})} | custom-call | flops 1073741824 | bytes 6291456 | tf_op jit(solution)/shard_map/scores/pallas_call | solution.py:73
  (30 shorter events, 0.2 us)
Async XLA Ops:
  6.5 54.9 %copy-start.13 = (bf16[128,512]{1,0:T(8,128)(2,1)S(1)}, bf16[128,512]{1,0:T(8,128)(2,1)}, u32[]{:S(2)}) copy-start(bf16[128,512]{1,0:T(8,128)(2,1)} %param.6) | copy-start | bytes 393220
  6.5 61.8 %copy-start.14 = (bf16[512,128]{1,0:T(8,128)(2,1)S(1)}, bf16[512,128]{1,0:T(8,128)(2,1)}, u32[]{:S(2)}) copy-start(bf16[512,128]{1,0:T(8,128)(2,1)} %param.7) | copy-start | bytes 393220
  6.5 94.9 %all-gather.7.cloned.1.call-start = ((), (), s32[]{:S(2)}) async-start(), calls=%async_computation | async-start | bytes 4718592 | tf_op jit(solution)/shard_map/all_gather | solution.py:123
  7.3 178.6 %all-gather.11.cloned.1.call-start = ((), (), s32[]{:S(2)}) async-start(), calls=%async_computation.2 | async-start | bytes 2359296 | tf_op jit(solution)/shard_map/all_gather | solution.py:137
  7.3 21.2 %collective-permute-start = (bf16[1,128,512]{2,1,0:T(8,128)(2,1)}, bf16[1,128,512]{2,1,0:T(8,128)(2,1)S(1)}, u32[]{:S(2)}, u32[]{:S(2)}) collective-permute-start(bf16[1,128,512]{2,1,0:T(8,128)(2,1)} %bitcast.14), channel_id=1, source_target_pairs={{0,256},{64,320},{128,384},{192,448},{256,0},{320,64},{384,128},{4... | collective-permute-start | bytes 393224 | tf_op jit(solution)/shard_map/ppermute | solution.py:99
  29.5 15.9 %collective-permute-start.1 = (bf16[2,128,512]{2,1,0:T(8,128)(2,1)S(1)}, bf16[2,128,512]{2,1,0:T(8,128)(2,1)S(1)}, u32[]{:S(2)}, u32[]{:S(2)}) collective-permute-start(bf16[2,128,512]{2,1,0:T(8,128)(2,1)S(1)} %pad_maximum_fusion.3), channel_id=1, source_target_pairs={{0,128},{64,192},{128,0},{192,64},{256,384},{320,448},{384,256},{4... | collective-permute-start | bytes 786440 | tf_op jit(solution)/shard_map/ppermute | solution.py:99
  46.3 51.8 %copy-start.19 = (s32[8]{0:T(128)S(1)}, s32[8]{0:T(128)}, u32[]{:S(2)}) copy-start(s32[8]{0:T(128)} %constant.14.clone) | copy-start | bytes 100
  46.4 15.0 %collective-permute-start.2 = (bf16[4,128,512]{2,1,0:T(8,128)(2,1)S(1)}, bf16[4,128,512]{2,1,0:T(8,128)(2,1)S(1)}, u32[]{:S(2)}, u32[]{:S(2)}) collective-permute-start(bf16[4,128,512]{2,1,0:T(8,128)(2,1)S(1)} %pad_maximum_fusion.2), channel_id=1, source_target_pairs={{0,64},{64,0},{128,192},{192,128},{256,320},{320,256},{384,448},{4... | collective-permute-start | bytes 1572872 | tf_op jit(solution)/shard_map/ppermute | solution.py:99
  61.5 27.2 %collective-permute-start.7 = (bf16[8,128,512]{2,1,0:T(8,128)(2,1)S(1)}, bf16[8,128,512]{2,1,0:T(8,128)(2,1)S(1)}, u32[]{:S(2)}, u32[]{:S(2)}) collective-permute-start(bf16[8,128,512]{2,1,0:T(8,128)(2,1)S(1)} %pad_maximum_fusion.refs_0_), channel_id=1, source_target_pairs={{0,48},{16,0},{32,16},{48,32},{1,49},{17,1},{33,17},{49,33},{2,50}... | collective-permute-start | bytes 3145736 | tf_op jit(solution)/shard_map/ppermute | solution.py:106
  66.4 28.0 %collective-permute-start.5 = (bf16[8,128,512]{2,1,0:T(8,128)(2,1)S(1)}, bf16[8,128,512]{2,1,0:T(8,128)(2,1)S(1)}, u32[]{:S(2)}, u32[]{:S(2)}) collective-permute-start(bf16[8,128,512]{2,1,0:T(8,128)(2,1)S(1)} %pad_maximum_fusion.refs_0_), channel_id=1, source_target_pairs={{0,16},{16,32},{32,48},{48,0},{1,17},{17,33},{33,49},{49,1},{2,18}... | collective-permute-start | bytes 3145736 | tf_op jit(solution)/shard_map/ppermute | solution.py:105
  68.4 17.8 %collective-permute-start.3 = (bf16[1,512,128]{2,1,0:T(8,128)(2,1)S(1)}, bf16[1,512,128]{2,1,0:T(8,128)(2,1)S(1)}, u32[]{:S(2)}, u32[]{:S(2)}) collective-permute-start(bf16[1,512,128]{2,1,0:T(8,128)(2,1)S(1)} %bitcast.18), channel_id=1, source_target_pairs={{0,256},{64,320},{128,384},{192,448},{256,0},{320,64},{384,128},{4... | collective-permute-start | bytes 393224 | tf_op jit(solution)/shard_map/ppermute | solution.py:99
  86.1 0.7 copy-start.15
  86.8 14.6 %collective-permute-start.4 = (bf16[2,512,128]{2,1,0:T(8,128)(2,1)S(1)}, bf16[2,512,128]{2,1,0:T(8,128)(2,1)S(1)}, u32[]{:S(2)}, u32[]{:S(2)}) collective-permute-start(bf16[2,512,128]{2,1,0:T(8,128)(2,1)S(1)} %get-tuple-element.15), channel_id=1, source_target_pairs={{0,128},{64,192},{128,0},{192,64},{256,384},{320,448},{384,256},{4... | collective-permute-start | bytes 786440 | tf_op jit(solution)/shard_map/ppermute | solution.py:99
  89.6 21.4 %collective-permute-start.8 = (bf16[4,128,512]{2,1,0:T(8,128)(2,1)}, bf16[4,128,512]{2,1,0:T(8,128)(2,1)}, u32[]{:S(2)}, u32[]{:S(2)}) collective-permute-start(bf16[4,128,512]{2,1,0:T(8,128)(2,1)} %slice.13), channel_id=1, source_target_pairs={{0,48},{16,0},{32,16},{48,32},{1,49},{17,1},{33,17},{49,33},{2,50}... | collective-permute-start | bytes 1572872 | tf_op jit(solution)/shard_map/ppermute | solution.py:114
  95.3 1.0 copy-start.2
  96.3 16.9 %collective-permute-start.6 = (bf16[4,128,512]{2,1,0:T(8,128)(2,1)}, bf16[4,128,512]{2,1,0:T(8,128)(2,1)}, u32[]{:S(2)}, u32[]{:S(2)}) collective-permute-start(bf16[4,128,512]{2,1,0:T(8,128)(2,1)} %slice.12), channel_id=1, source_target_pairs={{0,16},{16,32},{32,48},{48,0},{1,17},{17,33},{33,49},{49,1},{2,18}... | collective-permute-start | bytes 1572872 | tf_op jit(solution)/shard_map/ppermute | solution.py:113
  101.4 0.8 copy-start.17
  102.3 2.2 %copy-start = (bf16[4096,512]{1,0:T(8,128)(2,1)S(1)}, bf16[4096,512]{1,0:T(8,128)(2,1)}, u32[]{:S(2)}) copy-start(bf16[4096,512]{1,0:T(8,128)(2,1)} %all-gather.7.cloned.1.call-done) | copy-start | bytes 12582916
  104.5 1.2 copy-start.3
  119.4 75.2 %all-gather.9.cloned.1.call-start = ((), (), s32[]{:S(2)}) async-start(), calls=%async_computation.1 | async-start | bytes 2359296 | tf_op jit(solution)/shard_map/all_gather | solution.py:137
  119.5 2.2 %copy-start.1 = (bf16[4096,512]{1,0:T(8,128)(2,1)S(1)}, bf16[4096,512]{1,0:T(8,128)(2,1)}, u32[]{:S(2)}) copy-start(bf16[4096,512]{1,0:T(8,128)(2,1)} %all-gather.7.cloned.1.call-done) | copy-start | bytes 12582916
  121.7 6.2 %copy-start.18 = (bf16[4,512,128]{2,1,0:T(8,128)(2,1)S(1)}, bf16[4,512,128]{2,1,0:T(8,128)(2,1)}, u32[]{:S(2)}) copy-start(bf16[4,512,128]{2,1,0:T(8,128)(2,1)} %copy-done.17) | copy-start | bytes 1572868
  121.7 20.8 %copy-start.16 = (bf16[1,512,128]{2,1,0:T(8,128)(2,1)S(1)}, bf16[1,512,128]{2,1,0:T(8,128)(2,1)}, u32[]{:S(2)}) copy-start(bf16[1,512,128]{2,1,0:T(8,128)(2,1)} %copy-done.15) | copy-start | bytes 393220
  127.9 57.9 %copy-start.12 = (f32[512]{0:T(512)S(1)}, f32[512]{0:T(512)}, u32[]{:S(2)}) copy-start(f32[512]{0:T(512)} %param.8) | copy-start | bytes 6148
  127.9 14.5 %collective-permute-start.9 = (bf16[4,512,128]{2,1,0:T(8,128)(2,1)S(1)}, bf16[4,512,128]{2,1,0:T(8,128)(2,1)S(1)}, u32[]{:S(2)}, u32[]{:S(2)}) collective-permute-start(bf16[4,512,128]{2,1,0:T(8,128)(2,1)S(1)} %copy-done.18), channel_id=1, source_target_pairs={{0,64},{64,0},{128,192},{192,128},{256,320},{320,256},{384,448},{4... | collective-permute-start | bytes 1572872 | tf_op jit(solution)/shard_map/ppermute | solution.py:99
  142.6 26.7 %collective-permute-start.11 = (bf16[8,512,128]{2,1,0:T(8,128)(2,1)S(1)}, bf16[8,512,128]{2,1,0:T(8,128)(2,1)S(1)}, u32[]{:S(2)}, u32[]{:S(2)}) collective-permute-start(bf16[8,512,128]{2,1,0:T(8,128)(2,1)S(1)} %pad_maximum_fusion.1.refs_0_), channel_id=1, source_target_pairs={{0,16},{16,32},{32,48},{48,0},{1,17},{17,33},{33,49},{49,1},{2,18}... | collective-permute-start | bytes 3145736 | tf_op jit(solution)/shard_map/ppermute | solution.py:105
  144.5 26.7 %collective-permute-start.10 = (bf16[8,512,128]{2,1,0:T(8,128)(2,1)S(1)}, bf16[8,512,128]{2,1,0:T(8,128)(2,1)S(1)}, u32[]{:S(2)}, u32[]{:S(2)}) collective-permute-start(bf16[8,512,128]{2,1,0:T(8,128)(2,1)S(1)} %pad_maximum_fusion.1.refs_0_), channel_id=1, source_target_pairs={{0,48},{16,0},{32,16},{48,32},{1,49},{17,1},{33,17},{49,33},{2,50}... | collective-permute-start | bytes 3145736 | tf_op jit(solution)/shard_map/ppermute | solution.py:106
  169.3 14.5 %collective-permute-start.12 = (bf16[4,512,128]{2,1,0:T(8,128)(2,1)S(1)}, bf16[4,512,128]{2,1,0:T(8,128)(2,1)S(1)}, u32[]{:S(2)}, u32[]{:S(2)}) collective-permute-start(bf16[4,512,128]{2,1,0:T(8,128)(2,1)S(1)} %slice.16), channel_id=1, source_target_pairs={{0,16},{16,32},{32,48},{48,0},{1,17},{17,33},{33,49},{49,1},{2,18}... | collective-permute-start | bytes 1572872 | tf_op jit(solution)/shard_map/ppermute | solution.py:113
  171.3 13.8 %collective-permute-start.13 = (bf16[4,512,128]{2,1,0:T(8,128)(2,1)S(1)}, bf16[4,512,128]{2,1,0:T(8,128)(2,1)S(1)}, u32[]{:S(2)}, u32[]{:S(2)}) collective-permute-start(bf16[4,512,128]{2,1,0:T(8,128)(2,1)S(1)} %slice.17), channel_id=1, source_target_pairs={{0,48},{16,0},{32,16},{48,32},{1,49},{17,1},{33,17},{49,33},{2,50}... | collective-permute-start | bytes 1572872 | tf_op jit(solution)/shard_map/ppermute | solution.py:114
  183.8 0.8 copy-start.6
  185.0 0.8 copy-start.9
  185.9 1.6 copy-start.4
  187.4 1.0 copy-start.7
  188.5 1.0 copy-start.10
  194.6 1.6 copy-start.5
  196.2 1.0 copy-start.8
  197.2 1.0 copy-start.11
Sparse Core Ops, SparseCore 0:
  9.5 42.3 all-gather.6
  119.6 29.8 all-gather.10
  151.6 33.0 all-gather.8

commit v5 on v2

v5 whole, which is shorter than its diff:
```python
import jax
import jax.numpy as jnp
from jax import lax
from jax.experimental import pallas as pl
from jax.experimental.pallas import tpu as pltpu
from jax.sharding import Mesh, PartitionSpec as P

NZ, NY, CHUNKS = 8, 4, 2
NT_DIMS = (((1,), (1,)), ((), ()))
RELATIVE = (0, 4, 2, 6, 1, 5, 3, 7)
VMEM_LIMIT = 24 * 1024 * 1024
UP = [(i, (i + 1) % NY) for i in range(NY)]
DOWN = [(i, (i - 1) % NY) for i in range(NY)]


def kernel_matrix(slots, gram, training):
    n, t, depth = training.shape
    rows = gram.shape[1]
    each = t // CHUNKS

    def kernel(slots, gram_ref, training_ref, *refs):
        out_refs, total = refs[:-1], refs[-1]
        step = pl.program_id(0)

        @pl.when(step == 0)
        def _():
            total[...] = jnp.zeros_like(total)

        total[...] += lax.dot_general(training_ref[0], gram_ref[0], NT_DIMS, preferred_element_type=jnp.float32)

        @pl.when(step == n - 1)
        def _():
            for c, out_ref in enumerate(out_refs):
                out_ref[...] = total[c * each : (c + 1) * each].astype(out_ref.dtype)

    return pl.pallas_call(
        kernel,
        out_shape=[jax.ShapeDtypeStruct((each, rows), jnp.bfloat16)] * CHUNKS,
        grid_spec=pltpu.PrefetchScalarGridSpec(
            num_scalar_prefetch=1,
            grid=(n,),
            in_specs=[
                pl.BlockSpec((1, rows, depth), lambda s, slots: (slots[s], 0, 0)),
                pl.BlockSpec((1, t, depth), lambda s, slots: (s, 0, 0)),
            ],
            out_specs=[pl.BlockSpec((each, rows), lambda s, slots: (0, 0))] * CHUNKS,
            scratch_shapes=[pltpu.VMEM((t, rows), jnp.float32)],
        ),
        compiler_params=pltpu.CompilerParams(vmem_limit_bytes=VMEM_LIMIT),
        cost_estimate=pl.CostEstimate(
            flops=2 * n * rows * t * depth, bytes_accessed=2 * n * depth * (rows + t), transcendentals=0
        ),
        name="kernel_matrix",
    )(slots, gram, training)


def score_columns(slots, place, query, blocks, weight, out, chunk):
    n, rows, depth = query.shape
    t = blocks[0][0].shape[1]
    width = NY * t
    columns = weight.shape[1]

    def kernel(slots, place, query_ref, weight_ref, *refs):
        refs = list(refs)
        cut_refs = [[refs.pop(0) for _ in cuts] for cuts in blocks]
        out_ref, ordered, total = refs[-3:]
        step = pl.program_id(0)

        @pl.when(step == 0)
        def _():
            total[...] = jnp.zeros_like(total)

        for d, cuts in enumerate(cut_refs):
            block = cuts[0][0] if len(cuts) == 1 else jnp.where(step < n // 2, cuts[0][0], cuts[1][0])
            ordered[lax.rem(place[0] + d, NY)] = block
        total[...] += lax.dot_general(
            query_ref[0], ordered[...].reshape(width, depth), NT_DIMS, preferred_element_type=jnp.float32
        )

        @pl.when(step == n - 1)
        def _():
            out_ref[...] = total[...] * weight_ref[...]

    operands = [slots, place, query, weight]
    in_specs = [
        pl.BlockSpec((1, rows, depth), lambda s, slots, place: (slots[s], 0, 0)),
        pl.BlockSpec((1, width), lambda s, slots, place: (0, chunk)),
    ]
    for cuts in blocks:
        first = 0
        for cut in cuts:
            size = cut.shape[0]
            in_specs.append(
                pl.BlockSpec(
                    (1, t, depth),
                    lambda s, slots, place, first=first, size=size: (jnp.clip(s - first, 0, size - 1), 0, 0),
                )
            )
            operands.append(cut)
            first += size
    aliases = {}
    if out is not None:
        in_specs.append(pl.BlockSpec(memory_space=pl.ANY))
        aliases = {len(operands): 0}
        operands.append(out)
    return pl.pallas_call(
        kernel,
        out_shape=jax.ShapeDtypeStruct((rows, columns), jnp.float32),
        grid_spec=pltpu.PrefetchScalarGridSpec(
            num_scalar_prefetch=2,
            grid=(n,),
            in_specs=in_specs,
            out_specs=pl.BlockSpec((rows, width), lambda s, slots, place: (0, chunk)),
            scratch_shapes=[pltpu.VMEM((NY, t, depth), jnp.bfloat16), pltpu.VMEM((rows, width), jnp.float32)],
        ),
        input_output_aliases=aliases,
        compiler_params=pltpu.CompilerParams(vmem_limit_bytes=VMEM_LIMIT),
        cost_estimate=pl.CostEstimate(
            flops=2 * n * rows * width * depth, bytes_accessed=2 * n * depth * (rows + width), transcendentals=0
        ),
        name="score_columns",
    )(*operands)


def after(array, *earlier):
    return lax.optimization_barrier((array, earlier))[0]


def exchange(held, distance):
    other = lax.ppermute(held, "z", [(i, i ^ distance) for i in range(NZ)])
    return jnp.concatenate([held, other], axis=0)


def local(query_features, inverse_gram, training_features, residual_weight):
    slots = lax.axis_index("z") ^ jnp.array(RELATIVE, jnp.int32)
    place = lax.axis_index("y").astype(jnp.int32)[None]
    columns, lanes = training_features.shape
    rows, depth = inverse_gram.shape
    t = columns // NY
    each = t // CHUNKS

    folds = depth // lanes
    pieces = training_features.reshape(CHUNKS, NY, each, lanes).transpose(1, 0, 2, 3)
    pieces = pieces.reshape(NY, folds, t // folds, lanes).transpose(0, 2, 1, 3).reshape(NY, t // folds, depth)
    sent = jnp.concatenate([jnp.broadcast_to(inverse_gram, (NY, rows, depth)), pieces], axis=1)
    got = lax.all_to_all(sent, "y", split_axis=0, concat_axis=0, tiled=True)
    gram_rows = got[:, :rows].reshape(NY * rows, depth)
    training = got[:, rows:].reshape(NY, t // folds, folds, lanes).transpose(2, 1, 0, 3).reshape(t, NY * lanes)

    gram = lax.all_gather(gram_rows, ("x", "core"), axis=0)
    query = lax.all_gather(after(query_features, gram_rows), ("x", "core"), axis=0)
    weight = residual_weight[None, :]

    training = exchange(exchange(exchange(training[None], 4), 2), 1)
    a, b = (block[None] for block in kernel_matrix(slots, gram, training))

    half = NZ // 2
    a = exchange(a, 4)
    b = exchange(after(b, a), 4)
    a = exchange(a, 2)
    b = exchange(after(b, a), 2)
    a = exchange(a, 1)
    b = exchange(after(b, a), 1)
    below, above = lax.ppermute(a, "y", UP), lax.ppermute(a, "y", DOWN)
    far = lax.ppermute(below[:half], "y", UP), lax.ppermute(above[half:], "y", DOWN)
    b = after(b, below, above, query)
    below_b, above_b = lax.ppermute(b, "y", UP), lax.ppermute(b, "y", DOWN)
    out = score_columns(slots, place, query, ((a,), (above,), far, (below,)), weight, None, 0)
    first, second = after(below_b[:half], out), after(above_b[half:], out)
    far_b = lax.ppermute(first, "y", UP), lax.ppermute(second, "y", DOWN)
    return score_columns(slots, place, query, ((b,), (above_b,), far_b, (below_b,)), weight, out, 1)


def solution(mesh):
    fine = Mesh(mesh.devices.reshape(NZ, NY, 4, 2, 2), ("z", "y", "x", "core", "row"))
    pb, ta = ("z", "y"), ("x", "core")
    placed = (P(pb, ta), P(pb, ta), P(("row", *ta), pb), P(("row", *ta)))
    return jax.shard_map(
        local, mesh=fine, in_specs=placed, out_specs=P(pb, ("row", *ta)), check_vma=False
    )
```

time: 180 us -> 197 us (1.094)
  waiting for transfers between devices: 32.8 us -> 66.7 us
  starting transfers between devices: 84.9 us -> 76.5 us
  other arithmetic: 5.76 us -> 0.42 us
  local copies, waits for them, and re-layouts: 11.5 us -> 8.78 us
    ppermute x12 -> x9, waiting for transfers between devices: 18.2 us -> 50 us  [exchange(): other = lax.ppermute(held, 'z', [(i, i ^ distance) for i in range(NZ)])]
    ppermute x12 -> x9, starting transfers between devices: 55.9 us -> 49.1 us  [exchange(): other = lax.ppermute(held, 'z', [(i, i ^ distance) for i in range(NZ)])]
    another operation x6 -> x0, other arithmetic: 5.43 us -> none  [gather_y(): return jnp.stack([own, above, far, below])]
    unnamed x23 -> x8, local copies, waits for them, and re-layouts: 8.61 us -> 4.38 us
    ppermute x8, waiting for transfers between devices: 13.1 us -> 15.9 us  [the longest x1 10.4 us: local(): lax.ppermute(below[:half], 'y', UP)]
    pallas_call x2 -> x1, Pallas kernels: 5.76 us -> 3.14 us  [kernel_matrix(): pl.pallas_call(kernel, out_shape=[jax.ShapeDtypeStruct((each, rows), jnp....]
    slice x9 -> x6, local copies, waits for them, and re-layouts: 0.23 us -> 2.32 us  [the longest x1 0.83 us: local(): gram_rows = got[:, :rows].reshape(NY * rows, depth)]
  transfers between devices with their start and end apart: 22 -> 19, of which waited for: 13 -> 10; matrix products, arithmetic and copies ran while one was open for 3% -> 1% of each run, Pallas kernels for 3% -> 5%
where the time goes in v5:
time: 197 us; the launch traced here: 195 us
  starting transfers between devices  76.5 us (39%)
  waiting for transfers between devices  66.7 us (34%)
  blocking collectives  15.1 us (8%)
  between operations  13.8 us (7%)
  Pallas kernels  13.7 us (7%)
  local copies, waits for them, and re-layouts  8.78 us (4%)
    ppermute x9, waiting for transfers between devices, exchange(): other = lax.ppermute(held, 'z', [(i, i ^ distance) for i in range(NZ)])  50 us
    ppermute x9, starting transfers between devices, exchange(): other = lax.ppermute(held, 'z', [(i, i ^ distance) for i in range(NZ)])  49.1 us
    all_to_all x1, blocking collectives, local(): got = lax.all_to_all(sent, 'y', split_axis=0, concat_axis=0, tiled=True)  15.1 us
    pallas_call x2, Pallas kernels, score_columns(): pl.pallas_call(kernel, out_shape=jax.ShapeDtypeStruct((rows, columns), jn...  10.6 us
    ppermute x1, waiting for transfers between devices, local(): lax.ppermute(below[:half], 'y', UP)  10.4 us
    ppermute x2, starting transfers between devices, local(): below_b, above_b = (lax.ppermute(b, 'y', UP), lax.ppermute(b, 'y', DOWN))  7.49 us
    ppermute x2, starting transfers between devices, local(): below, above = (lax.ppermute(a, 'y', UP), lax.ppermute(a, 'y', DOWN))  7.05 us
    ppermute x2, starting transfers between devices, local(): far_b = (lax.ppermute(first, 'y', UP), lax.ppermute(second, 'y', DOWN))  5.84 us
  transfers between devices with their start and end apart: 19, of which 10 were waited for; matrix products, arithmetic and copies ran while one was open for 1% of the time, Pallas kernels for 5%

profile of v5, /device:TPU:6, one launch (start us, length us, event | category | flops | bytes accessed | tf_op | source)
XLA Modules:
  0.0 195.1 jit_solution(18439742394408268345)
XLA Ops:
  6.5 0.0 all-gather.4.cloned.1.call-start
  6.5 0.9 copy.11
  7.5 0.9 broadcast_in_dim.17
  8.5 15.1 %all_to_all.5 = bf16[4,160,512]{2,1,0:T(8,128)(2,1)S(1)} all-to-all(bf16[4,160,512]{2,1,0:T(8,128)(2,1)S(1)} %pad_maximum_fusion.1), channel_id=1, replica_groups=mesh['z'=8,'y'=4,'x'=4,'core'=2,'row'=2] {'y'}, dimensions={0} | all-to-all | bytes 1310720 | tf_op jit(solution)/shard_map/all_to_all | solution.py:146
  23.6 0.8 slice.24
  24.5 0.0 all-gather.4.cloned.1.call-update
  24.5 0.0 all-gather.6.cloned.1.call-start
  24.5 0.7 all-gather.6.cloned.1.call-update
  25.2 0.0 copy-start.3
  25.3 0.1 copy.13
  25.4 0.1 broadcast_in_dim_reshape.3
  25.5 9.1 %collective-permute-start = (bf16[1,128,512]{2,1,0:T(8,128)(2,1)S(1)}, bf16[1,128,512]{2,1,0:T(8,128)(2,1)S(1)}, u32[]{:S(2)}, u32[]{:S(2)}) collective-permute-start(bf16[1,128,512]{2,1,0:T(8,128)(2,1)S(1)} %broadcast_in_dim_reshape.3), channel_id=1, source_target_pairs={{0,256},{64,320},{128,384},{192,448},{256,0},{320,64},{384,128},{4... | collective-permute-start | bytes 393224 | tf_op jit(solution)/shard_map/ppermute | solution.py:130
  34.6 10.7 %collective-permute-done = bf16[1,128,512]{2,1,0:T(8,128)(2,1)S(1)} collective-permute-done((bf16[1,128,512]{2,1,0:T(8,128)(2,1)S(1)}, bf16[1,128,512]{2,1,0:T(8,128)(2,1)S(1)}, u32[]{:S(2)}, u32[]{:S(2)}) %collective-permute-start) | collective-permute-done | bytes 131104 | tf_op jit(solution)/shard_map/ppermute | solution.py:130
  45.3 1.9 collective-permute-start.1
  47.3 11.8 %collective-permute-done.1 = bf16[2,128,512]{2,1,0:T(8,128)(2,1)S(1)} collective-permute-done((bf16[2,128,512]{2,1,0:T(8,128)(2,1)S(1)}, bf16[2,128,512]{2,1,0:T(8,128)(2,1)S(1)}, u32[]{:S(2)}, u32[]{:S(2)}) %collective-permute-start.1) | collective-permute-done | bytes 262176 | tf_op jit(solution)/shard_map/ppermute | solution.py:130
  59.0 0.1 pad_maximum_fusion.2
  59.1 1.9 collective-permute-start.2
  61.0 0.0 copy-done.3
  61.1 11.9 %collective-permute-done.2 = bf16[4,128,512]{2,1,0:T(8,128)(2,1)S(1)} collective-permute-done((bf16[4,128,512]{2,1,0:T(8,128)(2,1)S(1)}, bf16[4,128,512]{2,1,0:T(8,128)(2,1)S(1)}, u32[]{:S(2)}, u32[]{:S(2)}) %collective-permute-start.2) | collective-permute-done | bytes 524320 | tf_op jit(solution)/shard_map/ppermute | solution.py:130
  73.0 0.1 pad_maximum_fusion.training_ref
  73.1 0.0 all-gather.4.cloned.1.call-done.gram_ref
  73.1 0.0 copy-start.1
  73.1 2.2 %copy-done.1 = bf16[8,512,512]{2,1,0:T(8,128)(2,1)S(1)} copy-done((bf16[8,512,512]{2,1,0:T(8,128)(2,1)S(1)}, bf16[8,512,512]{2,1,0:T(8,128)(2,1)}, u32[]{:S(2)}) %copy-start.1) | copy-done | bytes 4194328
  75.3 3.1 %kernel_matrix.1 = (bf16[64,512]{1,0:T(8,128)(2,1)S(1)}, bf16[64,512]{1,0:T(8,128)(2,1)S(1)}) custom-call(s32[8]{0:T(128)S(1)} %broadcast_xor_fusion.slots, bf16[8,512,512]{2,1,0:T(8,128)(2,1)S(1)} %copy-done.1, bf16[8,128,512]{2,1,0:T(8,128)(2,1)S(1)} %pad_maximum_fusion.training_ref), custom_call_target="tpu_custom_call" | custom-call | flops 536870912 | bytes 5242880 | tf_op jit(solution)/shard_map/kernel_matrix/pallas_call | solution.py:36
  78.4 8.8 %collective-permute-start.3 = (bf16[1,64,512]{2,1,0:T(8,128)(2,1)S(1)}, bf16[1,64,512]{2,1,0:T(8,128)(2,1)S(1)}, u32[]{:S(2)}, u32[]{:S(2)}) collective-permute-start(bf16[1,64,512]{2,1,0:T(8,128)(2,1)S(1)} %bitcast.19), channel_id=1, source_target_pairs={{0,256},{64,320},{128,384},{192,448},{256,0},{320,64},{384,128},{4... | collective-permute-start | bytes 196616 | tf_op jit(solution)/shard_map/ppermute | solution.py:130
  87.3 2.2 %collective-permute-done.3 = bf16[1,64,512]{2,1,0:T(8,128)(2,1)S(1)} collective-permute-done((bf16[1,64,512]{2,1,0:T(8,128)(2,1)S(1)}, bf16[1,64,512]{2,1,0:T(8,128)(2,1)S(1)}, u32[]{:S(2)}, u32[]{:S(2)}) %collective-permute-start.3) | collective-permute-done | bytes 65568 | tf_op jit(solution)/shard_map/ppermute | solution.py:130
  89.5 5.3 %collective-permute-start.5 = (bf16[2,64,512]{2,1,0:T(8,128)(2,1)S(1)}, bf16[2,64,512]{2,1,0:T(8,128)(2,1)S(1)}, u32[]{:S(2)}, u32[]{:S(2)}) collective-permute-start(bf16[2,64,512]{2,1,0:T(8,128)(2,1)S(1)} %pad_maximum_fusion.8), channel_id=1, source_target_pairs={{0,128},{64,192},{128,0},{192,64},{256,384},{320,448},{384,256},{4... | collective-permute-start | bytes 393224 | tf_op jit(solution)/shard_map/ppermute | solution.py:130
  94.9 5.7 %collective-permute-done.5 = bf16[2,64,512]{2,1,0:T(8,128)(2,1)S(1)} collective-permute-done((bf16[2,64,512]{2,1,0:T(8,128)(2,1)S(1)}, bf16[2,64,512]{2,1,0:T(8,128)(2,1)S(1)}, u32[]{:S(2)}, u32[]{:S(2)}) %collective-permute-start.5) | collective-permute-done | bytes 131104 | tf_op jit(solution)/shard_map/ppermute | solution.py:130
  100.7 2.9 %collective-permute-start.7 = (bf16[4,64,512]{2,1,0:T(8,128)(2,1)S(1)}, bf16[4,64,512]{2,1,0:T(8,128)(2,1)S(1)}, u32[]{:S(2)}, u32[]{:S(2)}) collective-permute-start(bf16[4,64,512]{2,1,0:T(8,128)(2,1)S(1)} %pad_maximum_fusion.6), channel_id=1, source_target_pairs={{0,64},{64,0},{128,192},{192,128},{256,320},{320,256},{384,448},{4... | collective-permute-start | bytes 786440 | tf_op jit(solution)/shard_map/ppermute | solution.py:130
  103.6 8.2 %collective-permute-start.4 = (bf16[1,64,512]{2,1,0:T(8,128)(2,1)S(1)}, bf16[1,64,512]{2,1,0:T(8,128)(2,1)S(1)}, u32[]{:S(2)}, u32[]{:S(2)}) collective-permute-start(bf16[1,64,512]{2,1,0:T(8,128)(2,1)S(1)} %bitcast.23), channel_id=1, source_target_pairs={{0,256},{64,320},{128,384},{192,448},{256,0},{320,64},{384,128},{4... | collective-permute-start | bytes 196616 | tf_op jit(solution)/shard_map/ppermute | solution.py:130
  111.8 2.4 %collective-permute-done.4 = bf16[1,64,512]{2,1,0:T(8,128)(2,1)S(1)} collective-permute-done((bf16[1,64,512]{2,1,0:T(8,128)(2,1)S(1)}, bf16[1,64,512]{2,1,0:T(8,128)(2,1)S(1)}, u32[]{:S(2)}, u32[]{:S(2)}) %collective-permute-start.4) | collective-permute-done | bytes 65568 | tf_op jit(solution)/shard_map/ppermute | solution.py:130
  114.2 5.4 %collective-permute-start.6 = (bf16[2,64,512]{2,1,0:T(8,128)(2,1)S(1)}, bf16[2,64,512]{2,1,0:T(8,128)(2,1)S(1)}, u32[]{:S(2)}, u32[]{:S(2)}) collective-permute-start(bf16[2,64,512]{2,1,0:T(8,128)(2,1)S(1)} %pad_maximum_fusion.9), channel_id=1, source_target_pairs={{0,128},{64,192},{128,0},{192,64},{256,384},{320,448},{384,256},{4... | collective-permute-start | bytes 393224 | tf_op jit(solution)/shard_map/ppermute | solution.py:130
  119.6 0.0 collective-permute-done.7
  119.6 0.1 pad_maximum_fusion.3.refs_0_
  119.7 0.0 copy-start.2
  119.7 2.2 %collective-permute-start.9 = (bf16[8,64,512]{2,1,0:T(8,128)(2,1)S(1)}, bf16[8,64,512]{2,1,0:T(8,128)(2,1)S(1)}, u32[]{:S(2)}, u32[]{:S(2)}) collective-permute-start(bf16[8,64,512]{2,1,0:T(8,128)(2,1)S(1)} %pad_maximum_fusion.3.refs_0_), channel_id=1, source_target_pairs={{0,16},{16,32},{32,48},{48,0},{1,17},{17,33},{33,49},{49,1},{2,18}... | collective-permute-start | bytes 1572872 | tf_op jit(solution)/shard_map/ppermute | solution.py:164
  121.9 4.9 %collective-permute-start.10 = (bf16[8,64,512]{2,1,0:T(8,128)(2,1)S(1)}, bf16[8,64,512]{2,1,0:T(8,128)(2,1)S(1)}, u32[]{:S(2)}, u32[]{:S(2)}) collective-permute-start(bf16[8,64,512]{2,1,0:T(8,128)(2,1)S(1)} %pad_maximum_fusion.3.refs_0_), channel_id=1, source_target_pairs={{0,48},{16,0},{32,16},{48,32},{1,49},{17,1},{33,17},{49,33},{2,50}... | collective-permute-start | bytes 1572872 | tf_op jit(solution)/shard_map/ppermute | solution.py:164
  126.8 0.0 collective-permute-done.6
  126.8 5.4 %collective-permute-start.8 = (bf16[4,64,512]{2,1,0:T(8,128)(2,1)S(1)}, bf16[4,64,512]{2,1,0:T(8,128)(2,1)S(1)}, u32[]{:S(2)}, u32[]{:S(2)}) collective-permute-start(bf16[4,64,512]{2,1,0:T(8,128)(2,1)S(1)} %pad_maximum_fusion.7), channel_id=1, source_target_pairs={{0,64},{64,0},{128,192},{192,128},{256,320},{320,256},{384,448},{4... | collective-permute-start | bytes 786440 | tf_op jit(solution)/shard_map/ppermute | solution.py:130
  132.3 5.2 %collective-permute-done.8 = bf16[4,64,512]{2,1,0:T(8,128)(2,1)S(1)} collective-permute-done((bf16[4,64,512]{2,1,0:T(8,128)(2,1)S(1)}, bf16[4,64,512]{2,1,0:T(8,128)(2,1)S(1)}, u32[]{:S(2)}, u32[]{:S(2)}) %collective-permute-start.8) | collective-permute-done | bytes 262176 | tf_op jit(solution)/shard_map/ppermute | solution.py:130
  137.5 0.0 all-gather.6.cloned.1.call-done
  137.6 0.0 collective-permute-done.9.refs_4_
  137.6 0.0 collective-permute-done.10.refs_1_
  137.6 5.6 %collective-permute-start.11 = (bf16[8,64,512]{2,1,0:T(8,128)(2,1)S(1)}, bf16[8,64,512]{2,1,0:T(8,128)(2,1)S(1)}, u32[]{:S(2)}, u32[]{:S(2)}) collective-permute-start(bf16[8,64,512]{2,1,0:T(8,128)(2,1)S(1)} %pad_maximum_fusion.4.refs_0_), channel_id=1, source_target_pairs={{0,48},{16,0},{32,16},{48,32},{1,49},{17,1},{33,17},{49,33},{2,50}... | collective-permute-start | bytes 1572872 | tf_op jit(solution)/shard_map/ppermute | solution.py:167
  143.2 1.9 collective-permute-start.12
  145.1 0.7 slice.27
  145.8 1.9 collective-permute-start.13
  147.7 0.7 slice.28
  148.5 5.1 %collective-permute-start.14 = (bf16[4,64,512]{2,1,0:T(8,128)(2,1)}, bf16[4,64,512]{2,1,0:T(8,128)(2,1)}, u32[]{:S(2)}, u32[]{:S(2)}) collective-permute-start(bf16[4,64,512]{2,1,0:T(8,128)(2,1)} %slice.28), channel_id=1, source_target_pairs={{0,48},{16,0},{32,16},{48,32},{1,49},{17,1},{33,17},{49,33},{2,50}... | collective-permute-start | bytes 786440 | tf_op jit(solution)/shard_map/ppermute | solution.py:165
  153.6 10.4 %collective-permute-done.13.refs_2_ = bf16[4,64,512]{2,1,0:T(8,128)(2,1)S(1)} collective-permute-done((bf16[4,64,512]{2,1,0:T(8,128)(2,1)}, bf16[4,64,512]{2,1,0:T(8,128)(2,1)S(1)}, u32[]{:S(2)}, u32[]{:S(2)}) %collective-permute-start.13) | collective-permute-done | bytes 262176 | tf_op jit(solution)/shard_map/ppermute | solution.py:165
  164.0 0.0 collective-permute-done.14.refs_3_
  164.0 0.0 copy-done.2
  164.0 0.0 copy-start
  164.0 2.2 %copy-done = bf16[4096,512]{1,0:T(8,128)(2,1)S(1)} copy-done((bf16[4096,512]{1,0:T(8,128)(2,1)S(1)}, bf16[4096,512]{1,0:T(8,128)(2,1)}, u32[]{:S(2)}) %copy-start) | copy-done | bytes 4194328
  166.2 6.2 %score_columns.2.refs_5_ = f32[512,512]{1,0:T(8,128)} custom-call(s32[8]{0:T(128)S(1)} %broadcast_xor_fusion.slots, s32[1]{0:T(128)} %bitcast.place, bf16[8,512,512]{2,1,0:T(8,128)(2,1)S(1)} %bitcast.17, f32[1,512]{1,0:T(1,128)S(1)} %bitcast.25, bf16[8,64,512]{2,1,0:T(8,128)(2,1)S(1)} %pad_maximum_fusion.3.refs_0_, ...), custom_call_target="tpu_custom_call" | custom-call | flops 1073741824 | bytes 6291456 | tf_op jit(solution)/shard_map/score_columns/pallas_call | solution.py:106
  172.3 0.0 collective-permute-done.11.refs_1_
  172.4 1.9 collective-permute-start.16
  174.3 0.0 collective-permute-done.12.refs_4_
  174.3 3.9 %collective-permute-start.15 = (bf16[4,64,512]{2,1,0:T(8,128)(2,1)S(1)}, bf16[4,64,512]{2,1,0:T(8,128)(2,1)S(1)}, u32[]{:S(2)}, u32[]{:S(2)}) collective-permute-start(bf16[4,64,512]{2,1,0:T(8,128)(2,1)S(1)} %slice.26), channel_id=1, source_target_pairs={{0,16},{16,32},{32,48},{48,0},{1,17},{17,33},{33,49},{49,1},{2,18}... | collective-permute-start | bytes 786440 | tf_op jit(solution)/shard_map/ppermute | solution.py:170
  178.3 2.4 %collective-permute-done.16.refs_3_ = bf16[4,64,512]{2,1,0:T(8,128)(2,1)S(1)} collective-permute-done((bf16[4,64,512]{2,1,0:T(8,128)(2,1)S(1)}, bf16[4,64,512]{2,1,0:T(8,128)(2,1)S(1)}, u32[]{:S(2)}, u32[]{:S(2)}) %collective-permute-start.16) | collective-permute-done | bytes 262176 | tf_op jit(solution)/shard_map/ppermute | solution.py:170
  180.6 3.2 %collective-permute-done.15.refs_2_ = bf16[4,64,512]{2,1,0:T(8,128)(2,1)S(1)} collective-permute-done((bf16[4,64,512]{2,1,0:T(8,128)(2,1)S(1)}, bf16[4,64,512]{2,1,0:T(8,128)(2,1)S(1)}, u32[]{:S(2)}, u32[]{:S(2)}) %collective-permute-start.15) | collective-permute-done | bytes 262176 | tf_op jit(solution)/shard_map/ppermute | solution.py:170
  183.8 4.4 %score_columns.3 = f32[512,512]{1,0:T(8,128)} custom-call(s32[8]{0:T(128)S(1)} %broadcast_xor_fusion.slots, s32[1]{0:T(128)} %bitcast.place, bf16[8,512,512]{2,1,0:T(8,128)(2,1)S(1)} %bitcast.18, f32[1,512]{1,0:T(1,128)S(1)} %bitcast.26, bf16[8,64,512]{2,1,0:T(8,128)(2,1)S(1)} %pad_maximum_fusion.4.refs_0_, ...), custom_call_target="tpu_custom_call", output_to_operand_aliasing={{}: (9, {})} | custom-call | flops 1073741824 | bytes 6291456 | tf_op jit(solution)/shard_map/score_columns/pallas_call | solution.py:106
  (13 shorter events, 0.3 us)
Async XLA Ops:
  6.5 66.6 %all-gather.4.cloned.1.call-start = ((), (), s32[]{:S(2)}) async-start(), calls=%async_computation.1 | async-start | bytes 4718592 | tf_op jit(solution)/shard_map/all_gather | solution.py:150
  24.5 113.1 %all-gather.6.cloned.1.call-start = ((), (), s32[]{:S(2)}) async-start(), calls=%async_computation.2 | async-start | bytes 4718592 | tf_op jit(solution)/shard_map/all_gather | solution.py:151
  25.2 35.8 %copy-start.3 = (s32[8]{0:T(128)S(1)}, s32[8]{0:T(128)}, u32[]{:S(2)}) copy-start(s32[8]{0:T(128)} %constant.14.clone) | copy-start | bytes 100
  25.5 19.8 %collective-permute-start = (bf16[1,128,512]{2,1,0:T(8,128)(2,1)S(1)}, bf16[1,128,512]{2,1,0:T(8,128)(2,1)S(1)}, u32[]{:S(2)}, u32[]{:S(2)}) collective-permute-start(bf16[1,128,512]{2,1,0:T(8,128)(2,1)S(1)} %broadcast_in_dim_reshape.3), channel_id=1, source_target_pairs={{0,256},{64,320},{128,384},{192,448},{256,0},{320,64},{384,128},{4... | collective-permute-start | bytes 393224 | tf_op jit(solution)/shard_map/ppermute | solution.py:130
  45.3 13.7 %collective-permute-start.1 = (bf16[2,128,512]{2,1,0:T(8,128)(2,1)S(1)}, bf16[2,128,512]{2,1,0:T(8,128)(2,1)S(1)}, u32[]{:S(2)}, u32[]{:S(2)}) collective-permute-start(bf16[2,128,512]{2,1,0:T(8,128)(2,1)S(1)} %pad_maximum_fusion.5), channel_id=1, source_target_pairs={{0,128},{64,192},{128,0},{192,64},{256,384},{320,448},{384,256},{4... | collective-permute-start | bytes 786440 | tf_op jit(solution)/shard_map/ppermute | solution.py:130
  59.1 13.9 %collective-permute-start.2 = (bf16[4,128,512]{2,1,0:T(8,128)(2,1)S(1)}, bf16[4,128,512]{2,1,0:T(8,128)(2,1)S(1)}, u32[]{:S(2)}, u32[]{:S(2)}) collective-permute-start(bf16[4,128,512]{2,1,0:T(8,128)(2,1)S(1)} %pad_maximum_fusion.2), channel_id=1, source_target_pairs={{0,64},{64,0},{128,192},{192,128},{256,320},{320,256},{384,448},{4... | collective-permute-start | bytes 1572872 | tf_op jit(solution)/shard_map/ppermute | solution.py:130
  73.1 2.2 %copy-start.1 = (bf16[8,512,512]{2,1,0:T(8,128)(2,1)S(1)}, bf16[8,512,512]{2,1,0:T(8,128)(2,1)}, u32[]{:S(2)}) copy-start(bf16[8,512,512]{2,1,0:T(8,128)(2,1)} %all-gather.4.cloned.1.call-done.gram_ref) | copy-start | bytes 12582916
  78.4 11.1 %collective-permute-start.3 = (bf16[1,64,512]{2,1,0:T(8,128)(2,1)S(1)}, bf16[1,64,512]{2,1,0:T(8,128)(2,1)S(1)}, u32[]{:S(2)}, u32[]{:S(2)}) collective-permute-start(bf16[1,64,512]{2,1,0:T(8,128)(2,1)S(1)} %bitcast.19), channel_id=1, source_target_pairs={{0,256},{64,320},{128,384},{192,448},{256,0},{320,64},{384,128},{4... | collective-permute-start | bytes 196616 | tf_op jit(solution)/shard_map/ppermute | solution.py:130
  89.5 11.1 %collective-permute-start.5 = (bf16[2,64,512]{2,1,0:T(8,128)(2,1)S(1)}, bf16[2,64,512]{2,1,0:T(8,128)(2,1)S(1)}, u32[]{:S(2)}, u32[]{:S(2)}) collective-permute-start(bf16[2,64,512]{2,1,0:T(8,128)(2,1)S(1)} %pad_maximum_fusion.8), channel_id=1, source_target_pairs={{0,128},{64,192},{128,0},{192,64},{256,384},{320,448},{384,256},{4... | collective-permute-start | bytes 393224 | tf_op jit(solution)/shard_map/ppermute | solution.py:130
  100.7 19.0 %collective-permute-start.7 = (bf16[4,64,512]{2,1,0:T(8,128)(2,1)S(1)}, bf16[4,64,512]{2,1,0:T(8,128)(2,1)S(1)}, u32[]{:S(2)}, u32[]{:S(2)}) collective-permute-start(bf16[4,64,512]{2,1,0:T(8,128)(2,1)S(1)} %pad_maximum_fusion.6), channel_id=1, source_target_pairs={{0,64},{64,0},{128,192},{192,128},{256,320},{320,256},{384,448},{4... | collective-permute-start | bytes 786440 | tf_op jit(solution)/shard_map/ppermute | solution.py:130
  103.6 10.6 %collective-permute-start.4 = (bf16[1,64,512]{2,1,0:T(8,128)(2,1)S(1)}, bf16[1,64,512]{2,1,0:T(8,128)(2,1)S(1)}, u32[]{:S(2)}, u32[]{:S(2)}) collective-permute-start(bf16[1,64,512]{2,1,0:T(8,128)(2,1)S(1)} %bitcast.23), channel_id=1, source_target_pairs={{0,256},{64,320},{128,384},{192,448},{256,0},{320,64},{384,128},{4... | collective-permute-start | bytes 196616 | tf_op jit(solution)/shard_map/ppermute | solution.py:130
  114.2 12.6 %collective-permute-start.6 = (bf16[2,64,512]{2,1,0:T(8,128)(2,1)S(1)}, bf16[2,64,512]{2,1,0:T(8,128)(2,1)S(1)}, u32[]{:S(2)}, u32[]{:S(2)}) collective-permute-start(bf16[2,64,512]{2,1,0:T(8,128)(2,1)S(1)} %pad_maximum_fusion.9), channel_id=1, source_target_pairs={{0,128},{64,192},{128,0},{192,64},{256,384},{320,448},{384,256},{4... | collective-permute-start | bytes 393224 | tf_op jit(solution)/shard_map/ppermute | solution.py:130
  119.7 44.3 %copy-start.2 = (f32[512]{0:T(512)S(1)}, f32[512]{0:T(512)}, u32[]{:S(2)}) copy-start(f32[512]{0:T(512)} %param.8) | copy-start | bytes 6148
  119.7 17.9 %collective-permute-start.9 = (bf16[8,64,512]{2,1,0:T(8,128)(2,1)S(1)}, bf16[8,64,512]{2,1,0:T(8,128)(2,1)S(1)}, u32[]{:S(2)}, u32[]{:S(2)}) collective-permute-start(bf16[8,64,512]{2,1,0:T(8,128)(2,1)S(1)} %pad_maximum_fusion.3.refs_0_), channel_id=1, source_target_pairs={{0,16},{16,32},{32,48},{48,0},{1,17},{17,33},{33,49},{49,1},{2,18}... | collective-permute-start | bytes 1572872 | tf_op jit(solution)/shard_map/ppermute | solution.py:164
  121.9 15.7 %collective-permute-start.10 = (bf16[8,64,512]{2,1,0:T(8,128)(2,1)S(1)}, bf16[8,64,512]{2,1,0:T(8,128)(2,1)S(1)}, u32[]{:S(2)}, u32[]{:S(2)}) collective-permute-start(bf16[8,64,512]{2,1,0:T(8,128)(2,1)S(1)} %pad_maximum_fusion.3.refs_0_), channel_id=1, source_target_pairs={{0,48},{16,0},{32,16},{48,32},{1,49},{17,1},{33,17},{49,33},{2,50}... | collective-permute-start | bytes 1572872 | tf_op jit(solution)/shard_map/ppermute | solution.py:164
  126.8 10.7 %collective-permute-start.8 = (bf16[4,64,512]{2,1,0:T(8,128)(2,1)S(1)}, bf16[4,64,512]{2,1,0:T(8,128)(2,1)S(1)}, u32[]{:S(2)}, u32[]{:S(2)}) collective-permute-start(bf16[4,64,512]{2,1,0:T(8,128)(2,1)S(1)} %pad_maximum_fusion.7), channel_id=1, source_target_pairs={{0,64},{64,0},{128,192},{192,128},{256,320},{320,256},{384,448},{4... | collective-permute-start | bytes 786440 | tf_op jit(solution)/shard_map/ppermute | solution.py:130
  137.6 34.7 %collective-permute-start.11 = (bf16[8,64,512]{2,1,0:T(8,128)(2,1)S(1)}, bf16[8,64,512]{2,1,0:T(8,128)(2,1)S(1)}, u32[]{:S(2)}, u32[]{:S(2)}) collective-permute-start(bf16[8,64,512]{2,1,0:T(8,128)(2,1)S(1)} %pad_maximum_fusion.4.refs_0_), channel_id=1, source_target_pairs={{0,48},{16,0},{32,16},{48,32},{1,49},{17,1},{33,17},{49,33},{2,50}... | collective-permute-start | bytes 1572872 | tf_op jit(solution)/shard_map/ppermute | solution.py:167
  143.2 31.1 %collective-permute-start.12 = (bf16[8,64,512]{2,1,0:T(8,128)(2,1)S(1)}, bf16[8,64,512]{2,1,0:T(8,128)(2,1)S(1)}, u32[]{:S(2)}, u32[]{:S(2)}) collective-permute-start(bf16[8,64,512]{2,1,0:T(8,128)(2,1)S(1)} %pad_maximum_fusion.4.refs_0_), channel_id=1, source_target_pairs={{0,16},{16,32},{32,48},{48,0},{1,17},{17,33},{33,49},{49,1},{2,18}... | collective-permute-start | bytes 1572872 | tf_op jit(solution)/shard_map/ppermute | solution.py:167
  145.8 18.2 %collective-permute-start.13 = (bf16[4,64,512]{2,1,0:T(8,128)(2,1)}, bf16[4,64,512]{2,1,0:T(8,128)(2,1)S(1)}, u32[]{:S(2)}, u32[]{:S(2)}) collective-permute-start(bf16[4,64,512]{2,1,0:T(8,128)(2,1)} %slice.27), channel_id=1, source_target_pairs={{0,16},{16,32},{32,48},{48,0},{1,17},{17,33},{33,49},{49,1},{2,18}... | collective-permute-start | bytes 786440 | tf_op jit(solution)/shard_map/ppermute | solution.py:165
  148.5 15.5 %collective-permute-start.14 = (bf16[4,64,512]{2,1,0:T(8,128)(2,1)}, bf16[4,64,512]{2,1,0:T(8,128)(2,1)}, u32[]{:S(2)}, u32[]{:S(2)}) collective-permute-start(bf16[4,64,512]{2,1,0:T(8,128)(2,1)} %slice.28), channel_id=1, source_target_pairs={{0,48},{16,0},{32,16},{48,32},{1,49},{17,1},{33,17},{49,33},{2,50}... | collective-permute-start | bytes 786440 | tf_op jit(solution)/shard_map/ppermute | solution.py:165
  164.0 2.2 %copy-start = (bf16[4096,512]{1,0:T(8,128)(2,1)S(1)}, bf16[4096,512]{1,0:T(8,128)(2,1)}, u32[]{:S(2)}) copy-start(bf16[4096,512]{1,0:T(8,128)(2,1)} %all-gather.6.cloned.1.call-done) | copy-start | bytes 12582916
  172.4 8.3 %collective-permute-start.16 = (bf16[4,64,512]{2,1,0:T(8,128)(2,1)S(1)}, bf16[4,64,512]{2,1,0:T(8,128)(2,1)S(1)}, u32[]{:S(2)}, u32[]{:S(2)}) collective-permute-start(bf16[4,64,512]{2,1,0:T(8,128)(2,1)S(1)} %slice.29), channel_id=1, source_target_pairs={{0,48},{16,0},{32,16},{48,32},{1,49},{17,1},{33,17},{49,33},{2,50}... | collective-permute-start | bytes 786440 | tf_op jit(solution)/shard_map/ppermute | solution.py:170
  174.3 9.5 %collective-permute-start.15 = (bf16[4,64,512]{2,1,0:T(8,128)(2,1)S(1)}, bf16[4,64,512]{2,1,0:T(8,128)(2,1)S(1)}, u32[]{:S(2)}, u32[]{:S(2)}) collective-permute-start(bf16[4,64,512]{2,1,0:T(8,128)(2,1)S(1)} %slice.26), channel_id=1, source_target_pairs={{0,16},{16,32},{32,48},{48,0},{1,17},{17,33},{33,49},{49,1},{2,18}... | collective-permute-start | bytes 786440 | tf_op jit(solution)/shard_map/ppermute | solution.py:170
Sparse Core Ops, SparseCore 0:
  24.6 40.2 all-gather.3
  67.1 39.7 all-gather.5

commit v6 on v2

v6 whole, which is shorter than its diff:
```python
import jax
import jax.numpy as jnp
from jax import lax
from jax.experimental import pallas as pl
from jax.experimental.pallas import tpu as pltpu
from jax.sharding import Mesh, PartitionSpec as P

NZ, NY, CHUNKS = 8, 4, 2
NT_DIMS = (((1,), (1,)), ((), ()))
RELATIVE = (0, 4, 2, 6, 1, 5, 3, 7)
VMEM_LIMIT = 24 * 1024 * 1024
UP = [(i, (i + 1) % NY) for i in range(NY)]
DOWN = [(i, (i - 1) % NY) for i in range(NY)]


def kernel_matrix(slots, inverse_gram, training):
    n, t, depth = training.shape
    rows = inverse_gram.shape[1]

    def kernel(slots, gram_ref, training_ref, out_ref, total):
        step = pl.program_id(0)

        @pl.when(step == 0)
        def _():
            total[...] = jnp.zeros_like(total)

        total[...] += lax.dot_general(training_ref[0], gram_ref[0], NT_DIMS, preferred_element_type=jnp.float32)

        @pl.when(step == n - 1)
        def _():
            out_ref[...] = total[...].astype(out_ref.dtype)

    return pl.pallas_call(
        kernel,
        out_shape=jax.ShapeDtypeStruct((t, rows), jnp.bfloat16),
        grid_spec=pltpu.PrefetchScalarGridSpec(
            num_scalar_prefetch=1,
            grid=(n,),
            in_specs=[
                pl.BlockSpec((1, rows, depth), lambda s, slots: (slots[s], 0, 0)),
                pl.BlockSpec((1, t, depth), lambda s, slots: (s, 0, 0)),
            ],
            out_specs=pl.BlockSpec((t, rows), lambda s, slots: (0, 0)),
            scratch_shapes=[pltpu.VMEM((t, rows), jnp.float32)],
        ),
        compiler_params=pltpu.CompilerParams(vmem_limit_bytes=VMEM_LIMIT),
        cost_estimate=pl.CostEstimate(
            flops=2 * n * rows * t * depth, bytes_accessed=2 * n * depth * (rows + t), transcendentals=0
        ),
        name="kernel_matrix",
    )(slots, inverse_gram, training)


def score_columns(slots, place, query, chunks, weight, out):
    n, rows, depth = query.shape
    each = chunks[0].shape[1]
    t = each * len(chunks)
    columns = weight.shape[1]

    def kernel(slots, place, query_ref, weight_ref, *refs):
        out_ref, total = refs[-2:]
        step = pl.program_id(0)

        @pl.when(step == 0)
        def _():
            total[...] = jnp.zeros_like(total)

        block = jnp.concatenate([ref[0] for ref in refs[: len(chunks)]], axis=0)
        total[...] += lax.dot_general(query_ref[0], block, NT_DIMS, preferred_element_type=jnp.float32)

        @pl.when(step == n - 1)
        def _():
            out_ref[...] = total[...] * weight_ref[...]

    operands = [slots, place, query, weight, *chunks]
    in_specs = [
        pl.BlockSpec((1, rows, depth), lambda s, slots, place: (slots[s], 0, 0)),
        pl.BlockSpec((1, t), lambda s, slots, place: (0, place[0])),
    ] + [pl.BlockSpec((1, each, depth), lambda s, slots, place: (s, 0, 0))] * len(chunks)
    aliases = {}
    if out is not None:
        in_specs.append(pl.BlockSpec(memory_space=pl.ANY))
        aliases = {len(operands): 0}
        operands.append(out)
    return pl.pallas_call(
        kernel,
        out_shape=jax.ShapeDtypeStruct((rows, columns), jnp.float32),
        grid_spec=pltpu.PrefetchScalarGridSpec(
            num_scalar_prefetch=2,
            grid=(n,),
            in_specs=in_specs,
            out_specs=pl.BlockSpec((rows, t), lambda s, slots, place: (0, place[0])),
            scratch_shapes=[pltpu.VMEM((rows, t), jnp.float32)],
        ),
        input_output_aliases=aliases,
        compiler_params=pltpu.CompilerParams(vmem_limit_bytes=VMEM_LIMIT),
        cost_estimate=pl.CostEstimate(
            flops=2 * n * rows * t * depth, bytes_accessed=2 * n * depth * (rows + t), transcendentals=0
        ),
        name="score_columns",
    )(*operands)


def after(array, *earlier):
    return lax.optimization_barrier((array, earlier))[0]


def exchange(held, distance):
    other = lax.ppermute(held, "z", [(i, i ^ distance) for i in range(NZ)])
    return jnp.concatenate([held, other], axis=0)


def local(query_features, inverse_gram, training_features, residual_weight):
    slots = lax.axis_index("z") ^ jnp.array(RELATIVE, jnp.int32)
    y = lax.axis_index("y").astype(jnp.int32)
    columns, lanes = training_features.shape
    rows, depth = inverse_gram.shape
    t = columns // NY

    folds = depth // lanes
    pieces = training_features.reshape(NY, folds, t // folds, lanes)
    pieces = pieces.transpose(0, 2, 1, 3).reshape(NY, t // folds, depth)
    sent = jnp.concatenate([jnp.broadcast_to(inverse_gram, (NY, rows, depth)), pieces], axis=1)
    got = lax.all_to_all(sent, "y", split_axis=0, concat_axis=0, tiled=True)
    gram_rows = got[:, :rows].reshape(NY * rows, depth)
    training = got[:, rows:].reshape(NY, t // folds, folds, lanes).transpose(2, 1, 0, 3)
    training = training.reshape(CHUNKS, 1, t // CHUNKS, NY * lanes)

    gram = lax.all_gather(gram_rows, ("x", "core"), axis=0)
    query = lax.all_gather(after(query_features, gram_rows), ("x", "core"), axis=0)
    weight = residual_weight[None, :]

    a, b = training[0], training[1]
    for distance in (4, 2, 1):
        a, b = exchange(a, distance), exchange(b, distance)
    a, b = kernel_matrix(slots, gram, a)[None], kernel_matrix(slots, gram, b)[None]
    for distance in (4, 2, 1):
        a, b = exchange(a, distance), exchange(b, distance)

    below_a, above_a = lax.ppermute(a, "y", UP), lax.ppermute(a, "y", DOWN)
    below_b, above_b = lax.ppermute(b, "y", UP), lax.ppermute(b, "y", DOWN)

    def scores(distance, chunks, out):
        return score_columns(slots, lax.rem(y + distance, NY)[None], query, chunks, weight, out)

    out = scores(0, (a, b), None)
    far = lax.ppermute(after(below_a, out), "y", UP), lax.ppermute(after(above_b, out), "y", DOWN)
    out = scores(1, (above_a, above_b), out)
    out = scores(NY - 1, (below_a, below_b), out)
    return scores(2, far, out)


def solution(mesh):
    fine = Mesh(mesh.devices.reshape(NZ, NY, 4, 2, 2), ("z", "y", "x", "core", "row"))
    pb, ta = ("z", "y"), ("x", "core")
    placed = (P(pb, ta), P(pb, ta), P(("row", *ta), pb), P(("row", *ta)))
    return jax.shard_map(
        local, mesh=fine, in_specs=placed, out_specs=P(pb, ("row", *ta)), check_vma=False
    )
```

time: 180 us -> 167 us (0.928)
  Pallas kernels: 14.6 us -> 23.5 us
  waiting for transfers between devices: 32.8 us -> 24.1 us
  starting transfers between devices: 84.9 us -> 77.9 us
  other arithmetic: 5.76 us -> 0.44 us
  local copies, waits for them, and re-layouts: 11.5 us -> 9.57 us
    ppermute x8 -> x6, starting transfers between devices: 28.9 us -> 19.5 us  [the longest x2 7.05 us: local(): below_a, above_a = (lax.ppermute(a, 'y', UP), lax.ppermute(a, 'y', DOWN))]
    pallas_call x2 -> x4, Pallas kernels: 8.8 us -> 17.7 us  [score_columns(): pl.pallas_call(kernel, out_shape=jax.ShapeDtypeStruct((rows, columns), jn...]
    ppermute x8 -> x6, waiting for transfers between devices: 13.1 us -> 6.68 us  [the longest x1 3.71 us: local(): lax.ppermute(after(below_a, out), 'y', UP)]
    another operation x6 -> x0, other arithmetic: 5.43 us -> none  [gather_y(): return jnp.stack([own, above, far, below])]
    ppermute x12, waiting for transfers between devices: 18.2 us -> 14.9 us  [exchange(): other = lax.ppermute(held, 'z', [(i, i ^ distance) for i in range(NZ)])]
    ppermute x12, starting transfers between devices: 55.9 us -> 58.3 us  [exchange(): other = lax.ppermute(held, 'z', [(i, i ^ distance) for i in range(NZ)])]
    unnamed x23 -> x10, local copies, waits for them, and re-layouts: 8.61 us -> 6.56 us
  transfers between devices with their start and end apart: 22 -> 20, of which waited for: 13 -> 10; matrix products, arithmetic and copies ran while one was open for 3% -> 0% of each run, Pallas kernels for 3% -> 10%
where the time goes in v6:
time: 167 us; the launch traced here: 164 us
  starting transfers between devices  77.9 us (47%)
  waiting for transfers between devices  24.1 us (14%)
  Pallas kernels  23.5 us (14%)
  blocking collectives  15.1 us (9%)
  between operations  13.8 us (8%)
  local copies, waits for them, and re-layouts  9.57 us (6%)
    ppermute x12, starting transfers between devices, exchange(): other = lax.ppermute(held, 'z', [(i, i ^ distance) for i in range(NZ)])  58.3 us
    pallas_call x4, Pallas kernels, score_columns(): pl.pallas_call(kernel, out_shape=jax.ShapeDtypeStruct((rows, columns), jn...  17.7 us
    all_to_all x1, blocking collectives, local(): got = lax.all_to_all(sent, 'y', split_axis=0, concat_axis=0, tiled=True)  15.1 us
    ppermute x12, waiting for transfers between devices, exchange(): other = lax.ppermute(held, 'z', [(i, i ^ distance) for i in range(NZ)])  14.9 us
    ppermute x2, starting transfers between devices, local(): below_a, above_a = (lax.ppermute(a, 'y', UP), lax.ppermute(a, 'y', DOWN))  7.05 us
    ppermute x2, starting transfers between devices, local(): below_b, above_b = (lax.ppermute(b, 'y', UP), lax.ppermute(b, 'y', DOWN))  6.63 us
    unnamed x10, local copies, waits for them, and re-layouts  6.56 us
    pallas_call x2, Pallas kernels, kernel_matrix(): pl.pallas_call(kernel, out_shape=jax.ShapeDtypeStruct((t, rows), jnp.bflo...  5.76 us
  transfers between devices with their start and end apart: 20, of which 10 were waited for; matrix products, arithmetic and copies ran while one was open for 0% of the time, Pallas kernels for 10%

profile of v6, /device:TPU:6, one launch (start us, length us, event | category | flops | bytes accessed | tf_op | source)
XLA Modules:
  0.0 164.5 jit_solution(6258061089687954418)
XLA Ops:
  6.5 0.0 all-gather.4.cloned.1.call-start
  6.5 0.9 copy.18
  7.5 0.9 broadcast_in_dim.26
  8.5 15.1 %all_to_all.5 = bf16[4,160,512]{2,1,0:T(8,128)(2,1)S(1)} all-to-all(bf16[4,160,512]{2,1,0:T(8,128)(2,1)S(1)} %pad_maximum_fusion), channel_id=1, replica_groups=mesh['z'=8,'y'=4,'x'=4,'core'=2,'row'=2] {'y'}, dimensions={0} | all-to-all | bytes 1310720 | tf_op jit(solution)/shard_map/all_to_all | solution.py:124
  23.6 0.8 slice.18
  24.4 0.0 all-gather.4.cloned.1.call-update
  24.5 0.0 all-gather.6.cloned.1.call-start
  24.5 0.7 all-gather.6.cloned.1.call-update
  25.2 0.0 copy-start.4
  25.3 0.1 fusion
  25.4 0.1 copy.15
  25.5 9.1 %collective-permute-start.7 = (bf16[1,64,512]{2,1,0:T(8,128)(2,1)S(1)}, bf16[1,64,512]{2,1,0:T(8,128)(2,1)S(1)}, u32[]{:S(2)}, u32[]{:S(2)}) collective-permute-start(bf16[1,64,512]{2,1,0:T(8,128)(2,1)S(1)} %squeeze.7), channel_id=1, source_target_pairs={{0,256},{64,320},{128,384},{192,448},{256,0},{320,64},{384,128},{4... | collective-permute-start | bytes 196616 | tf_op jit(solution)/shard_map/ppermute | solution.py:109
  34.6 0.1 copy.14
  34.7 1.9 %collective-permute-start = (bf16[1,64,512]{2,1,0:T(8,128)(2,1)S(1)}, bf16[1,64,512]{2,1,0:T(8,128)(2,1)S(1)}, u32[]{:S(2)}, u32[]{:S(2)}) collective-permute-start(bf16[1,64,512]{2,1,0:T(8,128)(2,1)S(1)} %squeeze.6), channel_id=1, source_target_pairs={{0,256},{64,320},{128,384},{192,448},{256,0},{320,64},{384,128},{4... | collective-permute-start | bytes 196616 | tf_op jit(solution)/shard_map/ppermute | solution.py:109
  36.6 0.2 collective-permute-done.7
  36.9 8.5 %collective-permute-start.8 = (bf16[2,64,512]{2,1,0:T(8,128)(2,1)S(1)}, bf16[2,64,512]{2,1,0:T(8,128)(2,1)S(1)}, u32[]{:S(2)}, u32[]{:S(2)}) collective-permute-start(bf16[2,64,512]{2,1,0:T(8,128)(2,1)S(1)} %pad_maximum_fusion.11), channel_id=1, source_target_pairs={{0,128},{64,192},{128,0},{192,64},{256,384},{320,448},{384,256},{4... | collective-permute-start | bytes 393224 | tf_op jit(solution)/shard_map/ppermute | solution.py:109
  45.4 1.0 collective-permute-done
  46.4 4.2 %collective-permute-start.1 = (bf16[2,64,512]{2,1,0:T(8,128)(2,1)S(1)}, bf16[2,64,512]{2,1,0:T(8,128)(2,1)S(1)}, u32[]{:S(2)}, u32[]{:S(2)}) collective-permute-start(bf16[2,64,512]{2,1,0:T(8,128)(2,1)S(1)} %pad_maximum_fusion.9), channel_id=1, source_target_pairs={{0,128},{64,192},{128,0},{192,64},{256,384},{320,448},{384,256},{4... | collective-permute-start | bytes 393224 | tf_op jit(solution)/shard_map/ppermute | solution.py:109
  50.6 0.0 collective-permute-done.8
  50.7 6.3 %collective-permute-start.9 = (bf16[4,64,512]{2,1,0:T(8,128)(2,1)S(1)}, bf16[4,64,512]{2,1,0:T(8,128)(2,1)S(1)}, u32[]{:S(2)}, u32[]{:S(2)}) collective-permute-start(bf16[4,64,512]{2,1,0:T(8,128)(2,1)S(1)} %pad_maximum_fusion.7), channel_id=1, source_target_pairs={{0,64},{64,0},{128,192},{192,128},{256,320},{320,256},{384,448},{4... | collective-permute-start | bytes 786440 | tf_op jit(solution)/shard_map/ppermute | solution.py:109
  56.9 0.0 collective-permute-done.1
  57.0 3.1 %collective-permute-start.2 = (bf16[4,64,512]{2,1,0:T(8,128)(2,1)S(1)}, bf16[4,64,512]{2,1,0:T(8,128)(2,1)S(1)}, u32[]{:S(2)}, u32[]{:S(2)}) collective-permute-start(bf16[4,64,512]{2,1,0:T(8,128)(2,1)S(1)} %pad_maximum_fusion.5), channel_id=1, source_target_pairs={{0,64},{64,0},{128,192},{192,128},{256,320},{320,256},{384,448},{4... | collective-permute-start | bytes 786440 | tf_op jit(solution)/shard_map/ppermute | solution.py:109
  60.1 2.9 %collective-permute-done.9 = bf16[4,64,512]{2,1,0:T(8,128)(2,1)S(1)} collective-permute-done((bf16[4,64,512]{2,1,0:T(8,128)(2,1)S(1)}, bf16[4,64,512]{2,1,0:T(8,128)(2,1)S(1)}, u32[]{:S(2)}, u32[]{:S(2)}) %collective-permute-start.9) | collective-permute-done | bytes 262176 | tf_op jit(solution)/shard_map/ppermute | solution.py:109
  63.1 0.1 pad_maximum_fusion.3.training_ref
  63.1 1.8 %all-gather.4.cloned.1.call-done.gram_ref = bf16[8,512,512]{2,1,0:T(8,128)(2,1)} async-done(((bf16[1,512,512]{2,1,0:T(8,128)(2,1)}), bf16[8,512,512]{2,1,0:T(8,128)(2,1)}) %all-gather.4.cloned.1.call-update) | async-done | bytes 4194320 | tf_op jit(solution)/shard_map/all_gather | solution.py:129
  64.9 2.2 %copy-done.2 = bf16[8,512,512]{2,1,0:T(8,128)(2,1)S(1)} copy-done((bf16[8,512,512]{2,1,0:T(8,128)(2,1)S(1)}, bf16[8,512,512]{2,1,0:T(8,128)(2,1)}, u32[]{:S(2)}) %copy-start.2) | copy-done | bytes 4194328
  67.1 2.9 %kernel_matrix.3 = bf16[64,512]{1,0:T(8,128)(2,1)S(1)} custom-call(s32[8]{0:T(128)S(1)} %broadcast_xor_fusion.slots, bf16[8,512,512]{2,1,0:T(8,128)(2,1)S(1)} %copy-done.2, bf16[8,64,512]{2,1,0:T(8,128)(2,1)S(1)} %pad_maximum_fusion.3.training_ref), custom_call_target="tpu_custom_call" | custom-call | flops 268435456 | bytes 4718592 | tf_op jit(solution)/shard_map/kernel_matrix/pallas_call | solution.py:33
  70.0 7.6 %collective-permute-start.10 = (bf16[1,64,512]{2,1,0:T(8,128)(2,1)S(1)}, bf16[1,64,512]{2,1,0:T(8,128)(2,1)S(1)}, u32[]{:S(2)}, u32[]{:S(2)}) collective-permute-start(bf16[1,64,512]{2,1,0:T(8,128)(2,1)S(1)} %bitcast.21), channel_id=1, source_target_pairs={{0,256},{64,320},{128,384},{192,448},{256,0},{320,64},{384,128},{4... | collective-permute-start | bytes 196616 | tf_op jit(solution)/shard_map/ppermute | solution.py:109
  77.7 0.0 collective-permute-done.2
  77.7 0.1 pad_maximum_fusion.1.training_ref
  77.7 2.9 %kernel_matrix.2 = bf16[64,512]{1,0:T(8,128)(2,1)S(1)} custom-call(s32[8]{0:T(128)S(1)} %broadcast_xor_fusion.slots, bf16[8,512,512]{2,1,0:T(8,128)(2,1)S(1)} %copy-done.2, bf16[8,64,512]{2,1,0:T(8,128)(2,1)S(1)} %pad_maximum_fusion.1.training_ref), custom_call_target="tpu_custom_call" | custom-call | flops 268435456 | bytes 4718592 | tf_op jit(solution)/shard_map/kernel_matrix/pallas_call | solution.py:33
  80.6 2.1 %collective-permute-start.3 = (bf16[1,64,512]{2,1,0:T(8,128)(2,1)S(1)}, bf16[1,64,512]{2,1,0:T(8,128)(2,1)S(1)}, u32[]{:S(2)}, u32[]{:S(2)}) collective-permute-start(bf16[1,64,512]{2,1,0:T(8,128)(2,1)S(1)} %bitcast.25), channel_id=1, source_target_pairs={{0,256},{64,320},{128,384},{192,448},{256,0},{320,64},{384,128},{4... | collective-permute-start | bytes 196616 | tf_op jit(solution)/shard_map/ppermute | solution.py:109
  82.7 1.6 collective-permute-done.10
  84.4 2.9 %collective-permute-start.11 = (bf16[2,64,512]{2,1,0:T(8,128)(2,1)S(1)}, bf16[2,64,512]{2,1,0:T(8,128)(2,1)S(1)}, u32[]{:S(2)}, u32[]{:S(2)}) collective-permute-start(bf16[2,64,512]{2,1,0:T(8,128)(2,1)S(1)} %pad_maximum_fusion.12), channel_id=1, source_target_pairs={{0,128},{64,192},{128,0},{192,64},{256,384},{320,448},{384,256},{4... | collective-permute-start | bytes 393224 | tf_op jit(solution)/shard_map/ppermute | solution.py:109
  87.3 7.3 %collective-permute-done.3 = bf16[1,64,512]{2,1,0:T(8,128)(2,1)S(1)} collective-permute-done((bf16[1,64,512]{2,1,0:T(8,128)(2,1)S(1)}, bf16[1,64,512]{2,1,0:T(8,128)(2,1)S(1)}, u32[]{:S(2)}, u32[]{:S(2)}) %collective-permute-start.3) | collective-permute-done | bytes 65568 | tf_op jit(solution)/shard_map/ppermute | solution.py:109
  94.6 1.9 %collective-permute-start.4 = (bf16[2,64,512]{2,1,0:T(8,128)(2,1)S(1)}, bf16[2,64,512]{2,1,0:T(8,128)(2,1)S(1)}, u32[]{:S(2)}, u32[]{:S(2)}) collective-permute-start(bf16[2,64,512]{2,1,0:T(8,128)(2,1)S(1)} %pad_maximum_fusion.10), channel_id=1, source_target_pairs={{0,128},{64,192},{128,0},{192,64},{256,384},{320,448},{384,256},{4... | collective-permute-start | bytes 393224 | tf_op jit(solution)/shard_map/ppermute | solution.py:109
  96.5 0.0 collective-permute-done.11
  96.6 0.0 copy-start.3
  96.6 5.3 %collective-permute-start.12 = (bf16[4,64,512]{2,1,0:T(8,128)(2,1)S(1)}, bf16[4,64,512]{2,1,0:T(8,128)(2,1)S(1)}, u32[]{:S(2)}, u32[]{:S(2)}) collective-permute-start(bf16[4,64,512]{2,1,0:T(8,128)(2,1)S(1)} %pad_maximum_fusion.8), channel_id=1, source_target_pairs={{0,64},{64,0},{128,192},{192,128},{256,320},{320,256},{384,448},{4... | collective-permute-start | bytes 786440 | tf_op jit(solution)/shard_map/ppermute | solution.py:109
  101.9 0.6 collective-permute-done.4
  102.5 5.3 %collective-permute-start.5 = (bf16[4,64,512]{2,1,0:T(8,128)(2,1)S(1)}, bf16[4,64,512]{2,1,0:T(8,128)(2,1)S(1)}, u32[]{:S(2)}, u32[]{:S(2)}) collective-permute-start(bf16[4,64,512]{2,1,0:T(8,128)(2,1)S(1)} %pad_maximum_fusion.6), channel_id=1, source_target_pairs={{0,64},{64,0},{128,192},{192,128},{256,320},{320,256},{384,448},{4... | collective-permute-start | bytes 786440 | tf_op jit(solution)/shard_map/ppermute | solution.py:109
  107.8 1.3 collective-permute-done.12
  109.1 0.1 pad_maximum_fusion.4.refs_1_
  109.1 4.7 %collective-permute-start.14 = (bf16[8,64,512]{2,1,0:T(8,128)(2,1)S(1)}, bf16[8,64,512]{2,1,0:T(8,128)(2,1)S(1)}, u32[]{:S(2)}, u32[]{:S(2)}) collective-permute-start(bf16[8,64,512]{2,1,0:T(8,128)(2,1)S(1)} %pad_maximum_fusion.4.refs_1_), channel_id=1, source_target_pairs={{0,48},{16,0},{32,16},{48,32},{1,49},{17,1},{33,17},{49,33},{2,50}... | collective-permute-start | bytes 1572872 | tf_op jit(solution)/shard_map/ppermute | solution.py:141
  113.9 0.0 collective-permute-done.5
  113.9 0.1 pad_maximum_fusion.2.refs_0_
  113.9 3.1 %collective-permute-start.6 = (bf16[8,64,512]{2,1,0:T(8,128)(2,1)S(1)}, bf16[8,64,512]{2,1,0:T(8,128)(2,1)S(1)}, u32[]{:S(2)}, u32[]{:S(2)}) collective-permute-start(bf16[8,64,512]{2,1,0:T(8,128)(2,1)S(1)} %pad_maximum_fusion.2.refs_0_), channel_id=1, source_target_pairs={{0,16},{16,32},{32,48},{48,0},{1,17},{17,33},{33,49},{49,1},{2,18}... | collective-permute-start | bytes 1572872 | tf_op jit(solution)/shard_map/ppermute | solution.py:140
  117.0 4.0 %collective-permute-start.17 = (bf16[8,64,512]{2,1,0:T(8,128)(2,1)S(1)}, bf16[8,64,512]{2,1,0:T(8,128)(2,1)S(1)}, u32[]{:S(2)}, u32[]{:S(2)}) collective-permute-start(bf16[8,64,512]{2,1,0:T(8,128)(2,1)S(1)} %pad_maximum_fusion.2.refs_0_), channel_id=1, source_target_pairs={{0,48},{16,0},{32,16},{48,32},{1,49},{17,1},{33,17},{49,33},{2,50}... | collective-permute-start | bytes 1572872 | tf_op jit(solution)/shard_map/ppermute | solution.py:140
  121.0 1.9 %collective-permute-start.16 = (bf16[8,64,512]{2,1,0:T(8,128)(2,1)S(1)}, bf16[8,64,512]{2,1,0:T(8,128)(2,1)S(1)}, u32[]{:S(2)}, u32[]{:S(2)}) collective-permute-start(bf16[8,64,512]{2,1,0:T(8,128)(2,1)S(1)} %pad_maximum_fusion.4.refs_1_), channel_id=1, source_target_pairs={{0,16},{16,32},{32,48},{48,0},{1,17},{17,33},{33,49},{49,1},{2,18}... | collective-permute-start | bytes 1572872 | tf_op jit(solution)/shard_map/ppermute | solution.py:141
  122.9 0.0 all-gather.6.cloned.1.call-done
  123.0 2.2 %copy-done = bf16[4096,512]{1,0:T(8,128)(2,1)S(1)} copy-done((bf16[4096,512]{1,0:T(8,128)(2,1)S(1)}, bf16[4096,512]{1,0:T(8,128)(2,1)}, u32[]{:S(2)}) %copy-start) | copy-done | bytes 4194328
  125.2 3.8 %score_columns.4.refs_2_ = f32[512,512]{1,0:T(8,128)} custom-call(s32[8]{0:T(128)S(1)} %broadcast_xor_fusion.slots, s32[1]{0:T(128)} %bitcast.8.place, bf16[8,512,512]{2,1,0:T(8,128)(2,1)S(1)} %bitcast.17, f32[1,512]{1,0:T(1,128)S(1)} %bitcast.29, bf16[8,64,512]{2,1,0:T(8,128)(2,1)S(1)} %pad_maximum_fusion.2.refs_0_, ...), custom_call_target="tpu_custom_call" | custom-call | flops 536870912 | bytes 5242880 | tf_op jit(solution)/shard_map/score_columns/pallas_call | solution.py:85
  128.9 0.0 collective-permute-done.14.refs_1_
  128.9 3.0 %collective-permute-done.6.refs_0_ = bf16[8,64,512]{2,1,0:T(8,128)(2,1)S(1)} collective-permute-done((bf16[8,64,512]{2,1,0:T(8,128)(2,1)S(1)}, bf16[8,64,512]{2,1,0:T(8,128)(2,1)S(1)}, u32[]{:S(2)}, u32[]{:S(2)}) %collective-permute-start.6) | collective-permute-done | bytes 524320 | tf_op jit(solution)/shard_map/ppermute | solution.py:140
  131.9 3.1 %collective-permute-start.15 = (bf16[8,64,512]{2,1,0:T(8,128)(2,1)S(1)}, bf16[8,64,512]{2,1,0:T(8,128)(2,1)}, u32[]{:S(2)}, u32[]{:S(2)}) collective-permute-start(bf16[8,64,512]{2,1,0:T(8,128)(2,1)S(1)} %collective-permute-done.14.refs_1_), channel_id=1, source_target_pairs={{0,48},{16,0},{32,16},{48,32},{1,49},{17,1},{33,17},{49,33},{2,50}... | collective-permute-start | bytes 1572872 | tf_op jit(solution)/shard_map/ppermute | solution.py:147
  135.0 2.7 %collective-permute-start.13 = (bf16[8,64,512]{2,1,0:T(8,128)(2,1)S(1)}, bf16[8,64,512]{2,1,0:T(8,128)(2,1)}, u32[]{:S(2)}, u32[]{:S(2)}) collective-permute-start(bf16[8,64,512]{2,1,0:T(8,128)(2,1)S(1)} %collective-permute-done.6.refs_0_), channel_id=1, source_target_pairs={{0,16},{16,32},{32,48},{48,0},{1,17},{17,33},{33,49},{49,1},{2,18}... | collective-permute-start | bytes 1572872 | tf_op jit(solution)/shard_map/ppermute | solution.py:147
  137.8 0.0 collective-permute-done.17.refs_0_
  137.8 2.2 %copy-done.1 = bf16[4096,512]{1,0:T(8,128)(2,1)S(1)} copy-done((bf16[4096,512]{1,0:T(8,128)(2,1)S(1)}, bf16[4096,512]{1,0:T(8,128)(2,1)}, u32[]{:S(2)}) %copy-start.1) | copy-done | bytes 4194328
  140.0 3.8 %score_columns.5.refs_2_ = f32[512,512]{1,0:T(8,128)} custom-call(s32[8]{0:T(128)S(1)} %broadcast_xor_fusion.slots, s32[1]{0:T(128)} %bitcast.11.place, bf16[8,512,512]{2,1,0:T(8,128)(2,1)S(1)} %bitcast.18, f32[1,512]{1,0:T(1,128)S(1)} %bitcast.30, bf16[8,64,512]{2,1,0:T(8,128)(2,1)S(1)} %collective-permute-done.17.refs_0_, ...), custom_call_target="tpu_custom_call", output_to_operand_aliasing={{}: (6, {})} | custom-call | flops 536870912 | bytes 5242880 | tf_op jit(solution)/shard_map/score_columns/pallas_call | solution.py:85
  143.8 0.0 collective-permute-done.16.refs_1_
  143.8 3.8 %score_columns.6.refs_2_ = f32[512,512]{1,0:T(8,128)} custom-call(s32[8]{0:T(128)S(1)} %broadcast_xor_fusion.slots, s32[1]{0:T(128)} %bitcast.10.place, bf16[8,512,512]{2,1,0:T(8,128)(2,1)S(1)} %bitcast.19, f32[1,512]{1,0:T(1,128)S(1)} %bitcast.31, bf16[8,64,512]{2,1,0:T(8,128)(2,1)S(1)} %collective-permute-done.6.refs_0_, ...), custom_call_target="tpu_custom_call", output_to_operand_aliasing={{}: (6, {})} | custom-call | flops 536870912 | bytes 5242880 | tf_op jit(solution)/shard_map/score_columns/pallas_call | solution.py:85
  147.6 0.0 collective-permute-done.15.refs_1_
  147.6 3.7 %collective-permute-done.13.refs_0_ = bf16[8,64,512]{2,1,0:T(8,128)(2,1)} collective-permute-done((bf16[8,64,512]{2,1,0:T(8,128)(2,1)S(1)}, bf16[8,64,512]{2,1,0:T(8,128)(2,1)}, u32[]{:S(2)}, u32[]{:S(2)}) %collective-permute-start.13) | collective-permute-done | bytes 524320 | tf_op jit(solution)/shard_map/ppermute | solution.py:147
  151.3 6.3 %score_columns.7 = f32[512,512]{1,0:T(8,128)} custom-call(s32[8]{0:T(128)S(1)} %broadcast_xor_fusion.slots, s32[1]{0:T(128)} %bitcast.place, bf16[8,512,512]{2,1,0:T(8,128)(2,1)S(1)} %bitcast.20, f32[1,512]{1,0:T(1,128)S(1)} %bitcast.32, bf16[8,64,512]{2,1,0:T(8,128)(2,1)} %collective-permute-done.13.refs_0_, ...), custom_call_target="tpu_custom_call", output_to_operand_aliasing={{}: (6, {})} | custom-call | flops 536870912 | bytes 5242880 | tf_op jit(solution)/shard_map/score_columns/pallas_call | solution.py:85
  (19 shorter events, 0.3 us)
Async XLA Ops:
  6.5 58.4 %all-gather.4.cloned.1.call-start = ((), (), s32[]{:S(2)}) async-start(), calls=%async_computation.1 | async-start | bytes 4718592 | tf_op jit(solution)/shard_map/all_gather | solution.py:129
  24.5 98.5 %all-gather.6.cloned.1.call-start = ((), (), s32[]{:S(2)}) async-start(), calls=%async_computation.2 | async-start | bytes 4718592 | tf_op jit(solution)/shard_map/all_gather | solution.py:130
  25.2 34.9 %copy-start.4 = (s32[8]{0:T(128)S(1)}, s32[8]{0:T(128)}, u32[]{:S(2)}) copy-start(s32[8]{0:T(128)} %constant.30.clone) | copy-start | bytes 100
  25.5 11.4 %collective-permute-start.7 = (bf16[1,64,512]{2,1,0:T(8,128)(2,1)S(1)}, bf16[1,64,512]{2,1,0:T(8,128)(2,1)S(1)}, u32[]{:S(2)}, u32[]{:S(2)}) collective-permute-start(bf16[1,64,512]{2,1,0:T(8,128)(2,1)S(1)} %squeeze.7), channel_id=1, source_target_pairs={{0,256},{64,320},{128,384},{192,448},{256,0},{320,64},{384,128},{4... | collective-permute-start | bytes 196616 | tf_op jit(solution)/shard_map/ppermute | solution.py:109
  34.7 11.7 %collective-permute-start = (bf16[1,64,512]{2,1,0:T(8,128)(2,1)S(1)}, bf16[1,64,512]{2,1,0:T(8,128)(2,1)S(1)}, u32[]{:S(2)}, u32[]{:S(2)}) collective-permute-start(bf16[1,64,512]{2,1,0:T(8,128)(2,1)S(1)} %squeeze.6), channel_id=1, source_target_pairs={{0,256},{64,320},{128,384},{192,448},{256,0},{320,64},{384,128},{4... | collective-permute-start | bytes 196616 | tf_op jit(solution)/shard_map/ppermute | solution.py:109
  36.9 13.7 %collective-permute-start.8 = (bf16[2,64,512]{2,1,0:T(8,128)(2,1)S(1)}, bf16[2,64,512]{2,1,0:T(8,128)(2,1)S(1)}, u32[]{:S(2)}, u32[]{:S(2)}) collective-permute-start(bf16[2,64,512]{2,1,0:T(8,128)(2,1)S(1)} %pad_maximum_fusion.11), channel_id=1, source_target_pairs={{0,128},{64,192},{128,0},{192,64},{256,384},{320,448},{384,256},{4... | collective-permute-start | bytes 393224 | tf_op jit(solution)/shard_map/ppermute | solution.py:109
  46.4 10.6 %collective-permute-start.1 = (bf16[2,64,512]{2,1,0:T(8,128)(2,1)S(1)}, bf16[2,64,512]{2,1,0:T(8,128)(2,1)S(1)}, u32[]{:S(2)}, u32[]{:S(2)}) collective-permute-start(bf16[2,64,512]{2,1,0:T(8,128)(2,1)S(1)} %pad_maximum_fusion.9), channel_id=1, source_target_pairs={{0,128},{64,192},{128,0},{192,64},{256,384},{320,448},{384,256},{4... | collective-permute-start | bytes 393224 | tf_op jit(solution)/shard_map/ppermute | solution.py:109
  50.7 12.4 %collective-permute-start.9 = (bf16[4,64,512]{2,1,0:T(8,128)(2,1)S(1)}, bf16[4,64,512]{2,1,0:T(8,128)(2,1)S(1)}, u32[]{:S(2)}, u32[]{:S(2)}) collective-permute-start(bf16[4,64,512]{2,1,0:T(8,128)(2,1)S(1)} %pad_maximum_fusion.7), channel_id=1, source_target_pairs={{0,64},{64,0},{128,192},{192,128},{256,320},{320,256},{384,448},{4... | collective-permute-start | bytes 786440 | tf_op jit(solution)/shard_map/ppermute | solution.py:109
  57.0 20.7 %collective-permute-start.2 = (bf16[4,64,512]{2,1,0:T(8,128)(2,1)S(1)}, bf16[4,64,512]{2,1,0:T(8,128)(2,1)S(1)}, u32[]{:S(2)}, u32[]{:S(2)}) collective-permute-start(bf16[4,64,512]{2,1,0:T(8,128)(2,1)S(1)} %pad_maximum_fusion.5), channel_id=1, source_target_pairs={{0,64},{64,0},{128,192},{192,128},{256,320},{320,256},{384,448},{4... | collective-permute-start | bytes 786440 | tf_op jit(solution)/shard_map/ppermute | solution.py:109
  64.9 2.2 %copy-start.2 = (bf16[8,512,512]{2,1,0:T(8,128)(2,1)S(1)}, bf16[8,512,512]{2,1,0:T(8,128)(2,1)}, u32[]{:S(2)}) copy-start(bf16[8,512,512]{2,1,0:T(8,128)(2,1)} %all-gather.4.cloned.1.call-done.gram_ref) | copy-start | bytes 12582916
  70.0 14.4 %collective-permute-start.10 = (bf16[1,64,512]{2,1,0:T(8,128)(2,1)S(1)}, bf16[1,64,512]{2,1,0:T(8,128)(2,1)S(1)}, u32[]{:S(2)}, u32[]{:S(2)}) collective-permute-start(bf16[1,64,512]{2,1,0:T(8,128)(2,1)S(1)} %bitcast.21), channel_id=1, source_target_pairs={{0,256},{64,320},{128,384},{192,448},{256,0},{320,64},{384,128},{4... | collective-permute-start | bytes 196616 | tf_op jit(solution)/shard_map/ppermute | solution.py:109
  80.6 14.0 %collective-permute-start.3 = (bf16[1,64,512]{2,1,0:T(8,128)(2,1)S(1)}, bf16[1,64,512]{2,1,0:T(8,128)(2,1)S(1)}, u32[]{:S(2)}, u32[]{:S(2)}) collective-permute-start(bf16[1,64,512]{2,1,0:T(8,128)(2,1)S(1)} %bitcast.25), channel_id=1, source_target_pairs={{0,256},{64,320},{128,384},{192,448},{256,0},{320,64},{384,128},{4... | collective-permute-start | bytes 196616 | tf_op jit(solution)/shard_map/ppermute | solution.py:109
  84.4 12.1 %collective-permute-start.11 = (bf16[2,64,512]{2,1,0:T(8,128)(2,1)S(1)}, bf16[2,64,512]{2,1,0:T(8,128)(2,1)S(1)}, u32[]{:S(2)}, u32[]{:S(2)}) collective-permute-start(bf16[2,64,512]{2,1,0:T(8,128)(2,1)S(1)} %pad_maximum_fusion.12), channel_id=1, source_target_pairs={{0,128},{64,192},{128,0},{192,64},{256,384},{320,448},{384,256},{4... | collective-permute-start | bytes 393224 | tf_op jit(solution)/shard_map/ppermute | solution.py:109
  94.6 7.9 %collective-permute-start.4 = (bf16[2,64,512]{2,1,0:T(8,128)(2,1)S(1)}, bf16[2,64,512]{2,1,0:T(8,128)(2,1)S(1)}, u32[]{:S(2)}, u32[]{:S(2)}) collective-permute-start(bf16[2,64,512]{2,1,0:T(8,128)(2,1)S(1)} %pad_maximum_fusion.10), channel_id=1, source_target_pairs={{0,128},{64,192},{128,0},{192,64},{256,384},{320,448},{384,256},{4... | collective-permute-start | bytes 393224 | tf_op jit(solution)/shard_map/ppermute | solution.py:109
  96.6 26.4 %copy-start.3 = (f32[512]{0:T(512)S(1)}, f32[512]{0:T(512)}, u32[]{:S(2)}) copy-start(f32[512]{0:T(512)} %param.8) | copy-start | bytes 6148
  96.6 12.5 %collective-permute-start.12 = (bf16[4,64,512]{2,1,0:T(8,128)(2,1)S(1)}, bf16[4,64,512]{2,1,0:T(8,128)(2,1)S(1)}, u32[]{:S(2)}, u32[]{:S(2)}) collective-permute-start(bf16[4,64,512]{2,1,0:T(8,128)(2,1)S(1)} %pad_maximum_fusion.8), channel_id=1, source_target_pairs={{0,64},{64,0},{128,192},{192,128},{256,320},{320,256},{384,448},{4... | collective-permute-start | bytes 786440 | tf_op jit(solution)/shard_map/ppermute | solution.py:109
  102.5 11.4 %collective-permute-start.5 = (bf16[4,64,512]{2,1,0:T(8,128)(2,1)S(1)}, bf16[4,64,512]{2,1,0:T(8,128)(2,1)S(1)}, u32[]{:S(2)}, u32[]{:S(2)}) collective-permute-start(bf16[4,64,512]{2,1,0:T(8,128)(2,1)S(1)} %pad_maximum_fusion.6), channel_id=1, source_target_pairs={{0,64},{64,0},{128,192},{192,128},{256,320},{320,256},{384,448},{4... | collective-permute-start | bytes 786440 | tf_op jit(solution)/shard_map/ppermute | solution.py:109
  109.1 19.8 %collective-permute-start.14 = (bf16[8,64,512]{2,1,0:T(8,128)(2,1)S(1)}, bf16[8,64,512]{2,1,0:T(8,128)(2,1)S(1)}, u32[]{:S(2)}, u32[]{:S(2)}) collective-permute-start(bf16[8,64,512]{2,1,0:T(8,128)(2,1)S(1)} %pad_maximum_fusion.4.refs_1_), channel_id=1, source_target_pairs={{0,48},{16,0},{32,16},{48,32},{1,49},{17,1},{33,17},{49,33},{2,50}... | collective-permute-start | bytes 1572872 | tf_op jit(solution)/shard_map/ppermute | solution.py:141
  113.9 18.0 %collective-permute-start.6 = (bf16[8,64,512]{2,1,0:T(8,128)(2,1)S(1)}, bf16[8,64,512]{2,1,0:T(8,128)(2,1)S(1)}, u32[]{:S(2)}, u32[]{:S(2)}) collective-permute-start(bf16[8,64,512]{2,1,0:T(8,128)(2,1)S(1)} %pad_maximum_fusion.2.refs_0_), channel_id=1, source_target_pairs={{0,16},{16,32},{32,48},{48,0},{1,17},{17,33},{33,49},{49,1},{2,18}... | collective-permute-start | bytes 1572872 | tf_op jit(solution)/shard_map/ppermute | solution.py:140
  117.0 20.7 %collective-permute-start.17 = (bf16[8,64,512]{2,1,0:T(8,128)(2,1)S(1)}, bf16[8,64,512]{2,1,0:T(8,128)(2,1)S(1)}, u32[]{:S(2)}, u32[]{:S(2)}) collective-permute-start(bf16[8,64,512]{2,1,0:T(8,128)(2,1)S(1)} %pad_maximum_fusion.2.refs_0_), channel_id=1, source_target_pairs={{0,48},{16,0},{32,16},{48,32},{1,49},{17,1},{33,17},{49,33},{2,50}... | collective-permute-start | bytes 1572872 | tf_op jit(solution)/shard_map/ppermute | solution.py:140
  121.0 22.8 %collective-permute-start.16 = (bf16[8,64,512]{2,1,0:T(8,128)(2,1)S(1)}, bf16[8,64,512]{2,1,0:T(8,128)(2,1)S(1)}, u32[]{:S(2)}, u32[]{:S(2)}) collective-permute-start(bf16[8,64,512]{2,1,0:T(8,128)(2,1)S(1)} %pad_maximum_fusion.4.refs_1_), channel_id=1, source_target_pairs={{0,16},{16,32},{32,48},{48,0},{1,17},{17,33},{33,49},{49,1},{2,18}... | collective-permute-start | bytes 1572872 | tf_op jit(solution)/shard_map/ppermute | solution.py:141
  123.0 2.2 %copy-start = (bf16[4096,512]{1,0:T(8,128)(2,1)S(1)}, bf16[4096,512]{1,0:T(8,128)(2,1)}, u32[]{:S(2)}) copy-start(bf16[4096,512]{1,0:T(8,128)(2,1)} %all-gather.6.cloned.1.call-done) | copy-start | bytes 12582916
  131.9 15.7 %collective-permute-start.15 = (bf16[8,64,512]{2,1,0:T(8,128)(2,1)S(1)}, bf16[8,64,512]{2,1,0:T(8,128)(2,1)}, u32[]{:S(2)}, u32[]{:S(2)}) collective-permute-start(bf16[8,64,512]{2,1,0:T(8,128)(2,1)S(1)} %collective-permute-done.14.refs_1_), channel_id=1, source_target_pairs={{0,48},{16,0},{32,16},{48,32},{1,49},{17,1},{33,17},{49,33},{2,50}... | collective-permute-start | bytes 1572872 | tf_op jit(solution)/shard_map/ppermute | solution.py:147
  135.0 16.3 %collective-permute-start.13 = (bf16[8,64,512]{2,1,0:T(8,128)(2,1)S(1)}, bf16[8,64,512]{2,1,0:T(8,128)(2,1)}, u32[]{:S(2)}, u32[]{:S(2)}) collective-permute-start(bf16[8,64,512]{2,1,0:T(8,128)(2,1)S(1)} %collective-permute-done.6.refs_0_), channel_id=1, source_target_pairs={{0,16},{16,32},{32,48},{48,0},{1,17},{17,33},{33,49},{49,1},{2,18}... | collective-permute-start | bytes 1572872 | tf_op jit(solution)/shard_map/ppermute | solution.py:147
  137.8 2.2 %copy-start.1 = (bf16[4096,512]{1,0:T(8,128)(2,1)S(1)}, bf16[4096,512]{1,0:T(8,128)(2,1)}, u32[]{:S(2)}) copy-start(bf16[4096,512]{1,0:T(8,128)(2,1)} %all-gather.6.cloned.1.call-done) | copy-start | bytes 12582916
Sparse Core Ops, SparseCore 0:
  24.6 40.2 all-gather.3
  67.1 39.7 all-gather.5

commit v7 on v6

--- a/solution.py
+++ b/solution.py
@@ -8,7 +8,6 @@
 NZ, NY, CHUNKS = 8, 4, 2
 NT_DIMS = (((1,), (1,)), ((), ()))
 RELATIVE = (0, 4, 2, 6, 1, 5, 3, 7)
-VMEM_LIMIT = 24 * 1024 * 1024
 UP = [(i, (i + 1) % NY) for i in range(NY)]
 DOWN = [(i, (i - 1) % NY) for i in range(NY)]
 
@@ -43,7 +42,7 @@
             out_specs=pl.BlockSpec((t, rows), lambda s, slots: (0, 0)),
             scratch_shapes=[pltpu.VMEM((t, rows), jnp.float32)],
         ),
-        compiler_params=pltpu.CompilerParams(vmem_limit_bytes=VMEM_LIMIT),
+        compiler_params=pltpu.CompilerParams(vmem_limit_bytes=51 * 1024 * 1024),
         cost_estimate=pl.CostEstimate(
             flops=2 * n * rows * t * depth, bytes_accessed=2 * n * depth * (rows + t), transcendentals=0
         ),
@@ -93,7 +92,7 @@
             scratch_shapes=[pltpu.VMEM((rows, t), jnp.float32)],
         ),
         input_output_aliases=aliases,
-        compiler_params=pltpu.CompilerParams(vmem_limit_bytes=VMEM_LIMIT),
+        compiler_params=pltpu.CompilerParams(vmem_limit_bytes=8 * 1024 * 1024),
         cost_estimate=pl.CostEstimate(
             flops=2 * n * rows * t * depth, bytes_accessed=2 * n * depth * (rows + t), transcendentals=0
         ),

time: 167 us -> 171 us (1.024)
  the two profiles are of different devices: /device:TPU:6 before, /device:TPU:192 now
where the time goes in v7:
time: 171 us; the launch traced here: 170 us
  starting transfers between devices  72.1 us (42%)
  waiting for transfers between devices  30.5 us (18%)
  Pallas kernels  30.4 us (18%)
  blocking collectives  15.1 us (9%)
  between operations  13.8 us (8%)
  local copies, waits for them, and re-layouts  7.39 us (4%)
    ppermute x12, starting transfers between devices, exchange(): other = lax.ppermute(held, 'z', [(i, i ^ distance) for i in range(NZ)])  52.4 us
    ppermute x12, waiting for transfers between devices, exchange(): other = lax.ppermute(held, 'z', [(i, i ^ distance) for i in range(NZ)])  19.6 us
    pallas_call x4, Pallas kernels, score_columns(): pl.pallas_call(kernel, out_shape=jax.ShapeDtypeStruct((rows, columns), jn...  17.8 us
    all_to_all x1, blocking collectives, local(): got = lax.all_to_all(sent, 'y', split_axis=0, concat_axis=0, tiled=True)  15.1 us
    pallas_call x2, Pallas kernels, kernel_matrix(): pl.pallas_call(kernel, out_shape=jax.ShapeDtypeStruct((t, rows), jnp.bflo...  12.6 us
    ppermute x2, starting transfers between devices, local(): below_a, above_a = (lax.ppermute(a, 'y', UP), lax.ppermute(a, 'y', DOWN))  7.05 us
    ppermute x2, starting transfers between devices, local(): below_b, above_b = (lax.ppermute(b, 'y', UP), lax.ppermute(b, 'y', DOWN))  6.76 us
    ppermute x1, waiting for transfers between devices, local(): lax.ppermute(after(below_a, out), 'y', UP)  5.36 us
  transfers between devices with their start and end apart: 20, of which 10 were waited for; matrix products, arithmetic and copies ran while one was open for 0% of the time, Pallas kernels for 14%

profile of v7, /device:TPU:192, one launch (start us, length us, event | category | flops | bytes accessed | tf_op | source)
XLA Modules:
  0.0 169.7 jit_solution(13720282681757996945)
XLA Ops:
  6.5 0.0 all-gather.4.cloned.1.call-start
  6.5 0.9 copy.18
  7.5 0.9 broadcast_in_dim.26
  8.5 15.1 %all_to_all.5 = bf16[4,160,512]{2,1,0:T(8,128)(2,1)S(1)} all-to-all(bf16[4,160,512]{2,1,0:T(8,128)(2,1)S(1)} %pad_maximum_fusion), channel_id=1, replica_groups=mesh['z'=8,'y'=4,'x'=4,'core'=2,'row'=2] {'y'}, dimensions={0} | all-to-all | bytes 1310720 | tf_op jit(solution)/shard_map/all_to_all | solution.py:123
  23.6 0.8 slice.18
  24.4 0.0 all-gather.4.cloned.1.call-update
  24.5 0.0 all-gather.6.cloned.1.call-start
  24.5 0.7 all-gather.6.cloned.1.call-update
  25.2 0.0 copy-start.3
  25.3 0.1 fusion
  25.4 0.1 copy.15
  25.5 1.9 %collective-permute-start.7 = (bf16[1,64,512]{2,1,0:T(8,128)(2,1)S(1)}, bf16[1,64,512]{2,1,0:T(8,128)(2,1)S(1)}, u32[]{:S(2)}, u32[]{:S(2)}) collective-permute-start(bf16[1,64,512]{2,1,0:T(8,128)(2,1)S(1)} %squeeze.7), channel_id=1, source_target_pairs={{0,256},{64,320},{128,384},{192,448},{256,0},{320,64},{384,128},{4... | collective-permute-start | bytes 196616 | tf_op jit(solution)/shard_map/ppermute | solution.py:108
  27.4 0.1 copy.14
  27.5 7.8 %collective-permute-start = (bf16[1,64,512]{2,1,0:T(8,128)(2,1)S(1)}, bf16[1,64,512]{2,1,0:T(8,128)(2,1)S(1)}, u32[]{:S(2)}, u32[]{:S(2)}) collective-permute-start(bf16[1,64,512]{2,1,0:T(8,128)(2,1)S(1)} %squeeze.6), channel_id=1, source_target_pairs={{0,256},{64,320},{128,384},{192,448},{256,0},{320,64},{384,128},{4... | collective-permute-start | bytes 196616 | tf_op jit(solution)/shard_map/ppermute | solution.py:108
  35.4 4.1 %collective-permute-done.7 = bf16[1,64,512]{2,1,0:T(8,128)(2,1)S(1)} collective-permute-done((bf16[1,64,512]{2,1,0:T(8,128)(2,1)S(1)}, bf16[1,64,512]{2,1,0:T(8,128)(2,1)S(1)}, u32[]{:S(2)}, u32[]{:S(2)}) %collective-permute-start.7) | collective-permute-done | bytes 65568 | tf_op jit(solution)/shard_map/ppermute | solution.py:108
  39.5 1.9 %collective-permute-start.8 = (bf16[2,64,512]{2,1,0:T(8,128)(2,1)S(1)}, bf16[2,64,512]{2,1,0:T(8,128)(2,1)S(1)}, u32[]{:S(2)}, u32[]{:S(2)}) collective-permute-start(bf16[2,64,512]{2,1,0:T(8,128)(2,1)S(1)} %pad_maximum_fusion.11), channel_id=1, source_target_pairs={{0,128},{64,192},{128,0},{192,64},{256,384},{320,448},{384,256},{4... | collective-permute-start | bytes 393224 | tf_op jit(solution)/shard_map/ppermute | solution.py:108
  41.4 0.0 collective-permute-done
  41.5 4.8 %collective-permute-start.1 = (bf16[2,64,512]{2,1,0:T(8,128)(2,1)S(1)}, bf16[2,64,512]{2,1,0:T(8,128)(2,1)S(1)}, u32[]{:S(2)}, u32[]{:S(2)}) collective-permute-start(bf16[2,64,512]{2,1,0:T(8,128)(2,1)S(1)} %pad_maximum_fusion.9), channel_id=1, source_target_pairs={{0,128},{64,192},{128,0},{192,64},{256,384},{320,448},{384,256},{4... | collective-permute-start | bytes 393224 | tf_op jit(solution)/shard_map/ppermute | solution.py:108
  46.3 1.5 collective-permute-done.8
  47.8 7.6 %collective-permute-start.9 = (bf16[4,64,512]{2,1,0:T(8,128)(2,1)S(1)}, bf16[4,64,512]{2,1,0:T(8,128)(2,1)S(1)}, u32[]{:S(2)}, u32[]{:S(2)}) collective-permute-start(bf16[4,64,512]{2,1,0:T(8,128)(2,1)S(1)} %pad_maximum_fusion.7), channel_id=1, source_target_pairs={{0,64},{64,0},{128,192},{192,128},{256,320},{320,256},{384,448},{4... | collective-permute-start | bytes 786440 | tf_op jit(solution)/shard_map/ppermute | solution.py:108
  55.4 0.0 collective-permute-done.1
  55.5 2.6 %collective-permute-start.2 = (bf16[4,64,512]{2,1,0:T(8,128)(2,1)S(1)}, bf16[4,64,512]{2,1,0:T(8,128)(2,1)S(1)}, u32[]{:S(2)}, u32[]{:S(2)}) collective-permute-start(bf16[4,64,512]{2,1,0:T(8,128)(2,1)S(1)} %pad_maximum_fusion.5), channel_id=1, source_target_pairs={{0,64},{64,0},{128,192},{192,128},{256,320},{320,256},{384,448},{4... | collective-permute-start | bytes 786440 | tf_op jit(solution)/shard_map/ppermute | solution.py:108
  58.1 0.0 copy-done.3
  58.1 4.4 %collective-permute-done.9 = bf16[4,64,512]{2,1,0:T(8,128)(2,1)S(1)} collective-permute-done((bf16[4,64,512]{2,1,0:T(8,128)(2,1)S(1)}, bf16[4,64,512]{2,1,0:T(8,128)(2,1)S(1)}, u32[]{:S(2)}, u32[]{:S(2)}) %collective-permute-start.9) | collective-permute-done | bytes 262176 | tf_op jit(solution)/shard_map/ppermute | solution.py:108
  62.5 0.1 pad_maximum_fusion.3.training_ref
  62.6 2.1 %all-gather.4.cloned.1.call-done.gram_ref = bf16[8,512,512]{2,1,0:T(8,128)(2,1)} async-done(((bf16[1,512,512]{2,1,0:T(8,128)(2,1)}), bf16[8,512,512]{2,1,0:T(8,128)(2,1)}) %all-gather.4.cloned.1.call-update) | async-done | bytes 4194320 | tf_op jit(solution)/shard_map/all_gather | solution.py:128
  64.7 6.3 %kernel_matrix.3 = bf16[64,512]{1,0:T(8,128)(2,1)S(1)} custom-call(s32[8]{0:T(128)S(1)} %broadcast_xor_fusion.slots, bf16[8,512,512]{2,1,0:T(8,128)(2,1)} %all-gather.4.cloned.1.call-done.gram_ref, bf16[8,64,512]{2,1,0:T(8,128)(2,1)S(1)} %pad_maximum_fusion.3.training_ref), custom_call_target="tpu_custom_call" | custom-call | flops 268435456 | bytes 4718592 | tf_op jit(solution)/shard_map/kernel_matrix/pallas_call | solution.py:32
  71.0 2.1 %collective-permute-start.10 = (bf16[1,64,512]{2,1,0:T(8,128)(2,1)S(1)}, bf16[1,64,512]{2,1,0:T(8,128)(2,1)S(1)}, u32[]{:S(2)}, u32[]{:S(2)}) collective-permute-start(bf16[1,64,512]{2,1,0:T(8,128)(2,1)S(1)} %bitcast.21), channel_id=1, source_target_pairs={{0,256},{64,320},{128,384},{192,448},{256,0},{320,64},{384,128},{4... | collective-permute-start | bytes 196616 | tf_op jit(solution)/shard_map/ppermute | solution.py:108
  73.1 0.0 collective-permute-done.2
  73.1 0.1 pad_maximum_fusion.1.training_ref
  73.1 6.3 %kernel_matrix.2 = bf16[64,512]{1,0:T(8,128)(2,1)S(1)} custom-call(s32[8]{0:T(128)S(1)} %broadcast_xor_fusion.slots, bf16[8,512,512]{2,1,0:T(8,128)(2,1)} %all-gather.4.cloned.1.call-done.gram_ref, bf16[8,64,512]{2,1,0:T(8,128)(2,1)S(1)} %pad_maximum_fusion.1.training_ref), custom_call_target="tpu_custom_call" | custom-call | flops 268435456 | bytes 4718592 | tf_op jit(solution)/shard_map/kernel_matrix/pallas_call | solution.py:32
  79.5 7.7 %collective-permute-start.3 = (bf16[1,64,512]{2,1,0:T(8,128)(2,1)S(1)}, bf16[1,64,512]{2,1,0:T(8,128)(2,1)S(1)}, u32[]{:S(2)}, u32[]{:S(2)}) collective-permute-start(bf16[1,64,512]{2,1,0:T(8,128)(2,1)S(1)} %bitcast.25), channel_id=1, source_target_pairs={{0,256},{64,320},{128,384},{192,448},{256,0},{320,64},{384,128},{4... | collective-permute-start | bytes 196616 | tf_op jit(solution)/shard_map/ppermute | solution.py:108
  87.2 0.0 collective-permute-done.10
  87.2 2.2 %collective-permute-start.11 = (bf16[2,64,512]{2,1,0:T(8,128)(2,1)S(1)}, bf16[2,64,512]{2,1,0:T(8,128)(2,1)S(1)}, u32[]{:S(2)}, u32[]{:S(2)}) collective-permute-start(bf16[2,64,512]{2,1,0:T(8,128)(2,1)S(1)} %pad_maximum_fusion.12), channel_id=1, source_target_pairs={{0,128},{64,192},{128,0},{192,64},{256,384},{320,448},{384,256},{4... | collective-permute-start | bytes 393224 | tf_op jit(solution)/shard_map/ppermute | solution.py:108
  89.5 3.9 %collective-permute-done.3 = bf16[1,64,512]{2,1,0:T(8,128)(2,1)S(1)} collective-permute-done((bf16[1,64,512]{2,1,0:T(8,128)(2,1)S(1)}, bf16[1,64,512]{2,1,0:T(8,128)(2,1)S(1)}, u32[]{:S(2)}, u32[]{:S(2)}) %collective-permute-start.3) | collective-permute-done | bytes 65568 | tf_op jit(solution)/shard_map/ppermute | solution.py:108
  93.4 1.9 %collective-permute-start.4 = (bf16[2,64,512]{2,1,0:T(8,128)(2,1)S(1)}, bf16[2,64,512]{2,1,0:T(8,128)(2,1)S(1)}, u32[]{:S(2)}, u32[]{:S(2)}) collective-permute-start(bf16[2,64,512]{2,1,0:T(8,128)(2,1)S(1)} %pad_maximum_fusion.10), channel_id=1, source_target_pairs={{0,128},{64,192},{128,0},{192,64},{256,384},{320,448},{384,256},{4... | collective-permute-start | bytes 393224 | tf_op jit(solution)/shard_map/ppermute | solution.py:108
  95.3 1.0 collective-permute-done.11
  96.4 0.0 copy-start.2
  96.4 9.0 %collective-permute-start.12 = (bf16[4,64,512]{2,1,0:T(8,128)(2,1)S(1)}, bf16[4,64,512]{2,1,0:T(8,128)(2,1)S(1)}, u32[]{:S(2)}, u32[]{:S(2)}) collective-permute-start(bf16[4,64,512]{2,1,0:T(8,128)(2,1)S(1)} %pad_maximum_fusion.8), channel_id=1, source_target_pairs={{0,64},{64,0},{128,192},{192,128},{256,320},{320,256},{384,448},{4... | collective-permute-start | bytes 786440 | tf_op jit(solution)/shard_map/ppermute | solution.py:108
  105.4 0.0 collective-permute-done.4
  105.4 2.6 %collective-permute-start.5 = (bf16[4,64,512]{2,1,0:T(8,128)(2,1)S(1)}, bf16[4,64,512]{2,1,0:T(8,128)(2,1)S(1)}, u32[]{:S(2)}, u32[]{:S(2)}) collective-permute-start(bf16[4,64,512]{2,1,0:T(8,128)(2,1)S(1)} %pad_maximum_fusion.6), channel_id=1, source_target_pairs={{0,64},{64,0},{128,192},{192,128},{256,320},{320,256},{384,448},{4... | collective-permute-start | bytes 786440 | tf_op jit(solution)/shard_map/ppermute | solution.py:108
  108.1 4.4 %collective-permute-done.12 = bf16[4,64,512]{2,1,0:T(8,128)(2,1)S(1)} collective-permute-done((bf16[4,64,512]{2,1,0:T(8,128)(2,1)S(1)}, bf16[4,64,512]{2,1,0:T(8,128)(2,1)S(1)}, u32[]{:S(2)}, u32[]{:S(2)}) %collective-permute-start.12) | collective-permute-done | bytes 262176 | tf_op jit(solution)/shard_map/ppermute | solution.py:108
  112.5 0.1 pad_maximum_fusion.4.refs_1_
  112.5 4.6 %collective-permute-start.14 = (bf16[8,64,512]{2,1,0:T(8,128)(2,1)S(1)}, bf16[8,64,512]{2,1,0:T(8,128)(2,1)S(1)}, u32[]{:S(2)}, u32[]{:S(2)}) collective-permute-start(bf16[8,64,512]{2,1,0:T(8,128)(2,1)S(1)} %pad_maximum_fusion.4.refs_1_), channel_id=1, source_target_pairs={{0,48},{16,0},{32,16},{48,32},{1,49},{17,1},{33,17},{49,33},{2,50}... | collective-permute-start | bytes 1572872 | tf_op jit(solution)/shard_map/ppermute | solution.py:140
  117.1 0.3 collective-permute-done.5
  117.5 0.1 pad_maximum_fusion.2.refs_0_
  117.5 3.4 %collective-permute-start.6 = (bf16[8,64,512]{2,1,0:T(8,128)(2,1)S(1)}, bf16[8,64,512]{2,1,0:T(8,128)(2,1)S(1)}, u32[]{:S(2)}, u32[]{:S(2)}) collective-permute-start(bf16[8,64,512]{2,1,0:T(8,128)(2,1)S(1)} %pad_maximum_fusion.2.refs_0_), channel_id=1, source_target_pairs={{0,16},{16,32},{32,48},{48,0},{1,17},{17,33},{33,49},{49,1},{2,18}... | collective-permute-start | bytes 1572872 | tf_op jit(solution)/shard_map/ppermute | solution.py:139
  120.9 3.7 %collective-permute-start.17 = (bf16[8,64,512]{2,1,0:T(8,128)(2,1)S(1)}, bf16[8,64,512]{2,1,0:T(8,128)(2,1)S(1)}, u32[]{:S(2)}, u32[]{:S(2)}) collective-permute-start(bf16[8,64,512]{2,1,0:T(8,128)(2,1)S(1)} %pad_maximum_fusion.2.refs_0_), channel_id=1, source_target_pairs={{0,48},{16,0},{32,16},{48,32},{1,49},{17,1},{33,17},{49,33},{2,50}... | collective-permute-start | bytes 1572872 | tf_op jit(solution)/shard_map/ppermute | solution.py:139
  124.6 2.1 %collective-permute-start.16 = (bf16[8,64,512]{2,1,0:T(8,128)(2,1)S(1)}, bf16[8,64,512]{2,1,0:T(8,128)(2,1)S(1)}, u32[]{:S(2)}, u32[]{:S(2)}) collective-permute-start(bf16[8,64,512]{2,1,0:T(8,128)(2,1)S(1)} %pad_maximum_fusion.4.refs_1_), channel_id=1, source_target_pairs={{0,16},{16,32},{32,48},{48,0},{1,17},{17,33},{33,49},{49,1},{2,18}... | collective-permute-start | bytes 1572872 | tf_op jit(solution)/shard_map/ppermute | solution.py:140
  126.8 0.0 all-gather.6.cloned.1.call-done
  126.8 2.2 %copy-done = bf16[4096,512]{1,0:T(8,128)(2,1)S(1)} copy-done((bf16[4096,512]{1,0:T(8,128)(2,1)S(1)}, bf16[4096,512]{1,0:T(8,128)(2,1)}, u32[]{:S(2)}) %copy-start) | copy-done | bytes 4194328
  129.0 3.8 %score_columns.4.refs_2_ = f32[512,512]{1,0:T(8,128)} custom-call(s32[8]{0:T(128)S(1)} %broadcast_xor_fusion.slots, s32[1]{0:T(128)} %bitcast.8.place, bf16[8,512,512]{2,1,0:T(8,128)(2,1)S(1)} %bitcast.17, f32[1,512]{1,0:T(1,128)S(1)} %bitcast.29, bf16[8,64,512]{2,1,0:T(8,128)(2,1)S(1)} %pad_maximum_fusion.2.refs_0_, ...), custom_call_target="tpu_custom_call" | custom-call | flops 536870912 | bytes 5242880 | tf_op jit(solution)/shard_map/score_columns/pallas_call | solution.py:84
  132.8 0.0 collective-permute-done.14.refs_1_
  132.8 2.7 %collective-permute-done.6.refs_0_ = bf16[8,64,512]{2,1,0:T(8,128)(2,1)S(1)} collective-permute-done((bf16[8,64,512]{2,1,0:T(8,128)(2,1)S(1)}, bf16[8,64,512]{2,1,0:T(8,128)(2,1)S(1)}, u32[]{:S(2)}, u32[]{:S(2)}) %collective-permute-start.6) | collective-permute-done | bytes 524320 | tf_op jit(solution)/shard_map/ppermute | solution.py:139
  135.5 3.4 %collective-permute-start.15 = (bf16[8,64,512]{2,1,0:T(8,128)(2,1)S(1)}, bf16[8,64,512]{2,1,0:T(8,128)(2,1)}, u32[]{:S(2)}, u32[]{:S(2)}) collective-permute-start(bf16[8,64,512]{2,1,0:T(8,128)(2,1)S(1)} %collective-permute-done.14.refs_1_), channel_id=1, source_target_pairs={{0,48},{16,0},{32,16},{48,32},{1,49},{17,1},{33,17},{49,33},{2,50}... | collective-permute-start | bytes 1572872 | tf_op jit(solution)/shard_map/ppermute | solution.py:146
  138.9 2.4 %collective-permute-start.13 = (bf16[8,64,512]{2,1,0:T(8,128)(2,1)S(1)}, bf16[8,64,512]{2,1,0:T(8,128)(2,1)}, u32[]{:S(2)}, u32[]{:S(2)}) collective-permute-start(bf16[8,64,512]{2,1,0:T(8,128)(2,1)S(1)} %collective-permute-done.6.refs_0_), channel_id=1, source_target_pairs={{0,16},{16,32},{32,48},{48,0},{1,17},{17,33},{33,49},{49,1},{2,18}... | collective-permute-start | bytes 1572872 | tf_op jit(solution)/shard_map/ppermute | solution.py:146
  141.4 0.0 collective-permute-done.17.refs_0_
  141.4 2.2 %copy-done.1 = bf16[4096,512]{1,0:T(8,128)(2,1)S(1)} copy-done((bf16[4096,512]{1,0:T(8,128)(2,1)S(1)}, bf16[4096,512]{1,0:T(8,128)(2,1)}, u32[]{:S(2)}) %copy-start.1) | copy-done | bytes 4194328
  143.6 3.8 %score_columns.5.refs_2_ = f32[512,512]{1,0:T(8,128)} custom-call(s32[8]{0:T(128)S(1)} %broadcast_xor_fusion.slots, s32[1]{0:T(128)} %bitcast.11.place, bf16[8,512,512]{2,1,0:T(8,128)(2,1)S(1)} %bitcast.18, f32[1,512]{1,0:T(1,128)S(1)} %bitcast.30, bf16[8,64,512]{2,1,0:T(8,128)(2,1)S(1)} %collective-permute-done.17.refs_0_, ...), custom_call_target="tpu_custom_call", output_to_operand_aliasing={{}: (6, {})} | custom-call | flops 536870912 | bytes 5242880 | tf_op jit(solution)/shard_map/score_columns/pallas_call | solution.py:84
  147.4 0.0 collective-permute-done.16.refs_1_
  147.4 3.8 %score_columns.6.refs_2_ = f32[512,512]{1,0:T(8,128)} custom-call(s32[8]{0:T(128)S(1)} %broadcast_xor_fusion.slots, s32[1]{0:T(128)} %bitcast.10.place, bf16[8,512,512]{2,1,0:T(8,128)(2,1)S(1)} %bitcast.19, f32[1,512]{1,0:T(1,128)S(1)} %bitcast.31, bf16[8,64,512]{2,1,0:T(8,128)(2,1)S(1)} %collective-permute-done.6.refs_0_, ...), custom_call_target="tpu_custom_call", output_to_operand_aliasing={{}: (6, {})} | custom-call | flops 536870912 | bytes 5242880 | tf_op jit(solution)/shard_map/score_columns/pallas_call | solution.py:84
  151.2 0.0 collective-permute-done.15.refs_1_
  151.2 5.4 %collective-permute-done.13.refs_0_ = bf16[8,64,512]{2,1,0:T(8,128)(2,1)} collective-permute-done((bf16[8,64,512]{2,1,0:T(8,128)(2,1)S(1)}, bf16[8,64,512]{2,1,0:T(8,128)(2,1)}, u32[]{:S(2)}, u32[]{:S(2)}) %collective-permute-start.13) | collective-permute-done | bytes 524320 | tf_op jit(solution)/shard_map/ppermute | solution.py:146
  156.5 6.3 %score_columns.7 = f32[512,512]{1,0:T(8,128)} custom-call(s32[8]{0:T(128)S(1)} %broadcast_xor_fusion.slots, s32[1]{0:T(128)} %bitcast.place, bf16[8,512,512]{2,1,0:T(8,128)(2,1)S(1)} %bitcast.20, f32[1,512]{1,0:T(1,128)S(1)} %bitcast.32, bf16[8,64,512]{2,1,0:T(8,128)(2,1)} %collective-permute-done.13.refs_0_, ...), custom_call_target="tpu_custom_call", output_to_operand_aliasing={{}: (6, {})} | custom-call | flops 536870912 | bytes 5242880 | tf_op jit(solution)/shard_map/score_columns/pallas_call | solution.py:84
  (17 shorter events, 0.3 us)
Async XLA Ops:
  6.5 58.1 %all-gather.4.cloned.1.call-start = ((), (), s32[]{:S(2)}) async-start(), calls=%async_computation.1 | async-start | bytes 4718592 | tf_op jit(solution)/shard_map/all_gather | solution.py:128
  24.5 102.3 %all-gather.6.cloned.1.call-start = ((), (), s32[]{:S(2)}) async-start(), calls=%async_computation.2 | async-start | bytes 4718592 | tf_op jit(solution)/shard_map/all_gather | solution.py:129
  25.2 32.9 %copy-start.3 = (s32[8]{0:T(128)S(1)}, s32[8]{0:T(128)}, u32[]{:S(2)}) copy-start(s32[8]{0:T(128)} %constant.30.clone) | copy-start | bytes 100
  25.5 14.0 %collective-permute-start.7 = (bf16[1,64,512]{2,1,0:T(8,128)(2,1)S(1)}, bf16[1,64,512]{2,1,0:T(8,128)(2,1)S(1)}, u32[]{:S(2)}, u32[]{:S(2)}) collective-permute-start(bf16[1,64,512]{2,1,0:T(8,128)(2,1)S(1)} %squeeze.7), channel_id=1, source_target_pairs={{0,256},{64,320},{128,384},{192,448},{256,0},{320,64},{384,128},{4... | collective-permute-start | bytes 196616 | tf_op jit(solution)/shard_map/ppermute | solution.py:108
  27.5 13.9 %collective-permute-start = (bf16[1,64,512]{2,1,0:T(8,128)(2,1)S(1)}, bf16[1,64,512]{2,1,0:T(8,128)(2,1)S(1)}, u32[]{:S(2)}, u32[]{:S(2)}) collective-permute-start(bf16[1,64,512]{2,1,0:T(8,128)(2,1)S(1)} %squeeze.6), channel_id=1, source_target_pairs={{0,256},{64,320},{128,384},{192,448},{256,0},{320,64},{384,128},{4... | collective-permute-start | bytes 196616 | tf_op jit(solution)/shard_map/ppermute | solution.py:108
  39.5 8.3 %collective-permute-start.8 = (bf16[2,64,512]{2,1,0:T(8,128)(2,1)S(1)}, bf16[2,64,512]{2,1,0:T(8,128)(2,1)S(1)}, u32[]{:S(2)}, u32[]{:S(2)}) collective-permute-start(bf16[2,64,512]{2,1,0:T(8,128)(2,1)S(1)} %pad_maximum_fusion.11), channel_id=1, source_target_pairs={{0,128},{64,192},{128,0},{192,64},{256,384},{320,448},{384,256},{4... | collective-permute-start | bytes 393224 | tf_op jit(solution)/shard_map/ppermute | solution.py:108
  41.5 14.0 %collective-permute-start.1 = (bf16[2,64,512]{2,1,0:T(8,128)(2,1)S(1)}, bf16[2,64,512]{2,1,0:T(8,128)(2,1)S(1)}, u32[]{:S(2)}, u32[]{:S(2)}) collective-permute-start(bf16[2,64,512]{2,1,0:T(8,128)(2,1)S(1)} %pad_maximum_fusion.9), channel_id=1, source_target_pairs={{0,128},{64,192},{128,0},{192,64},{256,384},{320,448},{384,256},{4... | collective-permute-start | bytes 393224 | tf_op jit(solution)/shard_map/ppermute | solution.py:108
  47.8 14.7 %collective-permute-start.9 = (bf16[4,64,512]{2,1,0:T(8,128)(2,1)S(1)}, bf16[4,64,512]{2,1,0:T(8,128)(2,1)S(1)}, u32[]{:S(2)}, u32[]{:S(2)}) collective-permute-start(bf16[4,64,512]{2,1,0:T(8,128)(2,1)S(1)} %pad_maximum_fusion.7), channel_id=1, source_target_pairs={{0,64},{64,0},{128,192},{192,128},{256,320},{320,256},{384,448},{4... | collective-permute-start | bytes 786440 | tf_op jit(solution)/shard_map/ppermute | solution.py:108
  55.5 17.6 %collective-permute-start.2 = (bf16[4,64,512]{2,1,0:T(8,128)(2,1)S(1)}, bf16[4,64,512]{2,1,0:T(8,128)(2,1)S(1)}, u32[]{:S(2)}, u32[]{:S(2)}) collective-permute-start(bf16[4,64,512]{2,1,0:T(8,128)(2,1)S(1)} %pad_maximum_fusion.5), channel_id=1, source_target_pairs={{0,64},{64,0},{128,192},{192,128},{256,320},{320,256},{384,448},{4... | collective-permute-start | bytes 786440 | tf_op jit(solution)/shard_map/ppermute | solution.py:108
  71.0 16.2 %collective-permute-start.10 = (bf16[1,64,512]{2,1,0:T(8,128)(2,1)S(1)}, bf16[1,64,512]{2,1,0:T(8,128)(2,1)S(1)}, u32[]{:S(2)}, u32[]{:S(2)}) collective-permute-start(bf16[1,64,512]{2,1,0:T(8,128)(2,1)S(1)} %bitcast.21), channel_id=1, source_target_pairs={{0,256},{64,320},{128,384},{192,448},{256,0},{320,64},{384,128},{4... | collective-permute-start | bytes 196616 | tf_op jit(solution)/shard_map/ppermute | solution.py:108
  79.5 13.9 %collective-permute-start.3 = (bf16[1,64,512]{2,1,0:T(8,128)(2,1)S(1)}, bf16[1,64,512]{2,1,0:T(8,128)(2,1)S(1)}, u32[]{:S(2)}, u32[]{:S(2)}) collective-permute-start(bf16[1,64,512]{2,1,0:T(8,128)(2,1)S(1)} %bitcast.25), channel_id=1, source_target_pairs={{0,256},{64,320},{128,384},{192,448},{256,0},{320,64},{384,128},{4... | collective-permute-start | bytes 196616 | tf_op jit(solution)/shard_map/ppermute | solution.py:108
  87.2 9.1 %collective-permute-start.11 = (bf16[2,64,512]{2,1,0:T(8,128)(2,1)S(1)}, bf16[2,64,512]{2,1,0:T(8,128)(2,1)S(1)}, u32[]{:S(2)}, u32[]{:S(2)}) collective-permute-start(bf16[2,64,512]{2,1,0:T(8,128)(2,1)S(1)} %pad_maximum_fusion.12), channel_id=1, source_target_pairs={{0,128},{64,192},{128,0},{192,64},{256,384},{320,448},{384,256},{4... | collective-permute-start | bytes 393224 | tf_op jit(solution)/shard_map/ppermute | solution.py:108
  93.4 12.0 %collective-permute-start.4 = (bf16[2,64,512]{2,1,0:T(8,128)(2,1)S(1)}, bf16[2,64,512]{2,1,0:T(8,128)(2,1)S(1)}, u32[]{:S(2)}, u32[]{:S(2)}) collective-permute-start(bf16[2,64,512]{2,1,0:T(8,128)(2,1)S(1)} %pad_maximum_fusion.10), channel_id=1, source_target_pairs={{0,128},{64,192},{128,0},{192,64},{256,384},{320,448},{384,256},{4... | collective-permute-start | bytes 393224 | tf_op jit(solution)/shard_map/ppermute | solution.py:108
  96.4 30.4 %copy-start.2 = (f32[512]{0:T(512)S(1)}, f32[512]{0:T(512)}, u32[]{:S(2)}) copy-start(f32[512]{0:T(512)} %param.8) | copy-start | bytes 6148
  96.4 16.1 %collective-permute-start.12 = (bf16[4,64,512]{2,1,0:T(8,128)(2,1)S(1)}, bf16[4,64,512]{2,1,0:T(8,128)(2,1)S(1)}, u32[]{:S(2)}, u32[]{:S(2)}) collective-permute-start(bf16[4,64,512]{2,1,0:T(8,128)(2,1)S(1)} %pad_maximum_fusion.8), channel_id=1, source_target_pairs={{0,64},{64,0},{128,192},{192,128},{256,320},{320,256},{384,448},{4... | collective-permute-start | bytes 786440 | tf_op jit(solution)/shard_map/ppermute | solution.py:108
  105.4 12.1 %collective-permute-start.5 = (bf16[4,64,512]{2,1,0:T(8,128)(2,1)S(1)}, bf16[4,64,512]{2,1,0:T(8,128)(2,1)S(1)}, u32[]{:S(2)}, u32[]{:S(2)}) collective-permute-start(bf16[4,64,512]{2,1,0:T(8,128)(2,1)S(1)} %pad_maximum_fusion.6), channel_id=1, source_target_pairs={{0,64},{64,0},{128,192},{192,128},{256,320},{320,256},{384,448},{4... | collective-permute-start | bytes 786440 | tf_op jit(solution)/shard_map/ppermute | solution.py:108
  112.5 20.3 %collective-permute-start.14 = (bf16[8,64,512]{2,1,0:T(8,128)(2,1)S(1)}, bf16[8,64,512]{2,1,0:T(8,128)(2,1)S(1)}, u32[]{:S(2)}, u32[]{:S(2)}) collective-permute-start(bf16[8,64,512]{2,1,0:T(8,128)(2,1)S(1)} %pad_maximum_fusion.4.refs_1_), channel_id=1, source_target_pairs={{0,48},{16,0},{32,16},{48,32},{1,49},{17,1},{33,17},{49,33},{2,50}... | collective-permute-start | bytes 1572872 | tf_op jit(solution)/shard_map/ppermute | solution.py:140
  117.5 18.0 %collective-permute-start.6 = (bf16[8,64,512]{2,1,0:T(8,128)(2,1)S(1)}, bf16[8,64,512]{2,1,0:T(8,128)(2,1)S(1)}, u32[]{:S(2)}, u32[]{:S(2)}) collective-permute-start(bf16[8,64,512]{2,1,0:T(8,128)(2,1)S(1)} %pad_maximum_fusion.2.refs_0_), channel_id=1, source_target_pairs={{0,16},{16,32},{32,48},{48,0},{1,17},{17,33},{33,49},{49,1},{2,18}... | collective-permute-start | bytes 1572872 | tf_op jit(solution)/shard_map/ppermute | solution.py:139
  120.9 20.5 %collective-permute-start.17 = (bf16[8,64,512]{2,1,0:T(8,128)(2,1)S(1)}, bf16[8,64,512]{2,1,0:T(8,128)(2,1)S(1)}, u32[]{:S(2)}, u32[]{:S(2)}) collective-permute-start(bf16[8,64,512]{2,1,0:T(8,128)(2,1)S(1)} %pad_maximum_fusion.2.refs_0_), channel_id=1, source_target_pairs={{0,48},{16,0},{32,16},{48,32},{1,49},{17,1},{33,17},{49,33},{2,50}... | collective-permute-start | bytes 1572872 | tf_op jit(solution)/shard_map/ppermute | solution.py:139
  124.6 22.8 %collective-permute-start.16 = (bf16[8,64,512]{2,1,0:T(8,128)(2,1)S(1)}, bf16[8,64,512]{2,1,0:T(8,128)(2,1)S(1)}, u32[]{:S(2)}, u32[]{:S(2)}) collective-permute-start(bf16[8,64,512]{2,1,0:T(8,128)(2,1)S(1)} %pad_maximum_fusion.4.refs_1_), channel_id=1, source_target_pairs={{0,16},{16,32},{32,48},{48,0},{1,17},{17,33},{33,49},{49,1},{2,18}... | collective-permute-start | bytes 1572872 | tf_op jit(solution)/shard_map/ppermute | solution.py:140
  126.8 2.2 %copy-start = (bf16[4096,512]{1,0:T(8,128)(2,1)S(1)}, bf16[4096,512]{1,0:T(8,128)(2,1)}, u32[]{:S(2)}) copy-start(bf16[4096,512]{1,0:T(8,128)(2,1)} %all-gather.6.cloned.1.call-done) | copy-start | bytes 12582916
  135.5 15.7 %collective-permute-start.15 = (bf16[8,64,512]{2,1,0:T(8,128)(2,1)S(1)}, bf16[8,64,512]{2,1,0:T(8,128)(2,1)}, u32[]{:S(2)}, u32[]{:S(2)}) collective-permute-start(bf16[8,64,512]{2,1,0:T(8,128)(2,1)S(1)} %collective-permute-done.14.refs_1_), channel_id=1, source_target_pairs={{0,48},{16,0},{32,16},{48,32},{1,49},{17,1},{33,17},{49,33},{2,50}... | collective-permute-start | bytes 1572872 | tf_op jit(solution)/shard_map/ppermute | solution.py:146
  138.9 17.6 %collective-permute-start.13 = (bf16[8,64,512]{2,1,0:T(8,128)(2,1)S(1)}, bf16[8,64,512]{2,1,0:T(8,128)(2,1)}, u32[]{:S(2)}, u32[]{:S(2)}) collective-permute-start(bf16[8,64,512]{2,1,0:T(8,128)(2,1)S(1)} %collective-permute-done.6.refs_0_), channel_id=1, source_target_pairs={{0,16},{16,32},{32,48},{48,0},{1,17},{17,33},{33,49},{49,1},{2,18}... | collective-permute-start | bytes 1572872 | tf_op jit(solution)/shard_map/ppermute | solution.py:146
  141.4 2.2 %copy-start.1 = (bf16[4096,512]{1,0:T(8,128)(2,1)S(1)}, bf16[4096,512]{1,0:T(8,128)(2,1)}, u32[]{:S(2)}) copy-start(bf16[4096,512]{1,0:T(8,128)(2,1)} %all-gather.6.cloned.1.call-done) | copy-start | bytes 12582916
Sparse Core Ops, SparseCore 0:
  24.6 40.0 all-gather.3
  66.8 39.7 all-gather.5

commit v8 on v6

--- a/solution.py
+++ b/solution.py
@@ -65,7 +65,7 @@
         def _():
             total[...] = jnp.zeros_like(total)
 
-        block = jnp.concatenate([ref[0] for ref in refs[: len(chunks)]], axis=0)
+        block = jnp.concatenate([ref[step] for ref in refs[: len(chunks)]], axis=0)
         total[...] += lax.dot_general(query_ref[0], block, NT_DIMS, preferred_element_type=jnp.float32)
 
         @pl.when(step == n - 1)
@@ -76,7 +76,7 @@
     in_specs = [
         pl.BlockSpec((1, rows, depth), lambda s, slots, place: (slots[s], 0, 0)),
         pl.BlockSpec((1, t), lambda s, slots, place: (0, place[0])),
-    ] + [pl.BlockSpec((1, each, depth), lambda s, slots, place: (s, 0, 0))] * len(chunks)
+    ] + [pl.BlockSpec((n, each, depth), lambda s, slots, place: (0, 0, 0))] * len(chunks)
     aliases = {}
     if out is not None:
         in_specs.append(pl.BlockSpec(memory_space=pl.ANY))
@@ -144,7 +144,7 @@
         return score_columns(slots, lax.rem(y + distance, NY)[None], query, chunks, weight, out)
 
     out = scores(0, (a, b), None)
-    far = lax.ppermute(after(below_a, out), "y", UP), lax.ppermute(after(above_b, out), "y", DOWN)
+    far = lax.ppermute(below_a, "y", UP), lax.ppermute(above_b, "y", DOWN)
     out = scores(1, (above_a, above_b), out)
     out = scores(NY - 1, (below_a, below_b), out)
     return scores(2, far, out)

time: 167 us -> 164 us (0.982)
  local copies, waits for them, and re-layouts: 9.57 us -> 7.4 us
    ppermute x2, waiting for transfers between devices: 0.01 us -> 3.29 us  [local(): below_b, above_b = (lax.ppermute(b, 'y', UP), lax.ppermute(b, 'y', DOWN))]
    ppermute x2, waiting for transfers between devices: 2.96 us -> 0.09 us  [local(): below_a, above_a = (lax.ppermute(a, 'y', UP), lax.ppermute(a, 'y', DOWN))]
    unnamed x10, local copies, waits for them, and re-layouts: 6.56 us -> 4.39 us
    ppermute x2, waiting for transfers between devices: 3.71 us -> 1.73 us  [local(): far = (lax.ppermute(below_a, 'y', UP), lax.ppermute(above_b, 'y', DOWN))]
  transfers between devices with their start and end apart: 20 -> 20, of which waited for: 10 -> 11; matrix products, arithmetic and copies ran while one was open for 0% -> 0% of each run, Pallas kernels for 10% -> 12%
where the time goes in v8:
time: 164 us; the launch traced here: 162 us
  starting transfers between devices  79.5 us (48%)
  Pallas kernels  22.9 us (14%)
  waiting for transfers between devices  22.6 us (14%)
  blocking collectives  15.1 us (9%)
  between operations  13.8 us (8%)
  local copies, waits for them, and re-layouts  7.4 us (5%)
    ppermute x12, starting transfers between devices, exchange(): other = lax.ppermute(held, 'z', [(i, i ^ distance) for i in range(NZ)])  58.3 us
    pallas_call x4, Pallas kernels, score_columns(): pl.pallas_call(kernel, out_shape=jax.ShapeDtypeStruct((rows, columns), jn...  17.2 us
    all_to_all x1, blocking collectives, local(): got = lax.all_to_all(sent, 'y', split_axis=0, concat_axis=0, tiled=True)  15.1 us
    ppermute x12, waiting for transfers between devices, exchange(): other = lax.ppermute(held, 'z', [(i, i ^ distance) for i in range(NZ)])  14.9 us
    ppermute x2, starting transfers between devices, local(): far = (lax.ppermute(below_a, 'y', UP), lax.ppermute(above_b, 'y', DOWN))  7.5 us
    ppermute x2, starting transfers between devices, local(): below_a, above_a = (lax.ppermute(a, 'y', UP), lax.ppermute(a, 'y', DOWN))  7.05 us
    ppermute x2, starting transfers between devices, local(): below_b, above_b = (lax.ppermute(b, 'y', UP), lax.ppermute(b, 'y', DOWN))  6.63 us
    pallas_call x2, Pallas kernels, kernel_matrix(): pl.pallas_call(kernel, out_shape=jax.ShapeDtypeStruct((t, rows), jnp.bflo...  5.76 us
  transfers between devices with their start and end apart: 20, of which 11 were waited for; matrix products, arithmetic and copies ran while one was open for 0% of the time, Pallas kernels for 12%

profile of v8, /device:TPU:6, one launch (start us, length us, event | category | flops | bytes accessed | tf_op | source)
XLA Modules:
  0.0 161.8 jit_solution(6833770077662538771)
XLA Ops:
  6.5 0.0 all-gather.4.cloned.1.call-start
  6.5 0.9 copy.18
  7.5 0.9 broadcast_in_dim.26
  8.5 15.1 %all_to_all.5 = bf16[4,160,512]{2,1,0:T(8,128)(2,1)S(1)} all-to-all(bf16[4,160,512]{2,1,0:T(8,128)(2,1)S(1)} %pad_maximum_fusion), channel_id=1, replica_groups=mesh['z'=8,'y'=4,'x'=4,'core'=2,'row'=2] {'y'}, dimensions={0} | all-to-all | bytes 1310720 | tf_op jit(solution)/shard_map/all_to_all | solution.py:124
  23.6 0.8 slice.18
  24.4 0.0 all-gather.4.cloned.1.call-update
  24.5 0.0 all-gather.6.cloned.1.call-start
  24.5 0.7 all-gather.6.cloned.1.call-update
  25.2 0.0 copy-start.4
  25.3 0.1 fusion
  25.4 0.1 copy.15
  25.5 9.1 %collective-permute-start.8 = (bf16[1,64,512]{2,1,0:T(8,128)(2,1)S(1)}, bf16[1,64,512]{2,1,0:T(8,128)(2,1)S(1)}, u32[]{:S(2)}, u32[]{:S(2)}) collective-permute-start(bf16[1,64,512]{2,1,0:T(8,128)(2,1)S(1)} %squeeze.7), channel_id=1, source_target_pairs={{0,256},{64,320},{128,384},{192,448},{256,0},{320,64},{384,128},{4... | collective-permute-start | bytes 196616 | tf_op jit(solution)/shard_map/ppermute | solution.py:109
  34.6 0.1 copy.14
  34.7 1.9 %collective-permute-start = (bf16[1,64,512]{2,1,0:T(8,128)(2,1)S(1)}, bf16[1,64,512]{2,1,0:T(8,128)(2,1)S(1)}, u32[]{:S(2)}, u32[]{:S(2)}) collective-permute-start(bf16[1,64,512]{2,1,0:T(8,128)(2,1)S(1)} %squeeze.6), channel_id=1, source_target_pairs={{0,256},{64,320},{128,384},{192,448},{256,0},{320,64},{384,128},{4... | collective-permute-start | bytes 196616 | tf_op jit(solution)/shard_map/ppermute | solution.py:109
  36.6 0.2 collective-permute-done.8
  36.9 8.5 %collective-permute-start.9 = (bf16[2,64,512]{2,1,0:T(8,128)(2,1)S(1)}, bf16[2,64,512]{2,1,0:T(8,128)(2,1)S(1)}, u32[]{:S(2)}, u32[]{:S(2)}) collective-permute-start(bf16[2,64,512]{2,1,0:T(8,128)(2,1)S(1)} %pad_maximum_fusion.11), channel_id=1, source_target_pairs={{0,128},{64,192},{128,0},{192,64},{256,384},{320,448},{384,256},{4... | collective-permute-start | bytes 393224 | tf_op jit(solution)/shard_map/ppermute | solution.py:109
  45.4 1.0 collective-permute-done
  46.4 4.2 %collective-permute-start.1 = (bf16[2,64,512]{2,1,0:T(8,128)(2,1)S(1)}, bf16[2,64,512]{2,1,0:T(8,128)(2,1)S(1)}, u32[]{:S(2)}, u32[]{:S(2)}) collective-permute-start(bf16[2,64,512]{2,1,0:T(8,128)(2,1)S(1)} %pad_maximum_fusion.9), channel_id=1, source_target_pairs={{0,128},{64,192},{128,0},{192,64},{256,384},{320,448},{384,256},{4... | collective-permute-start | bytes 393224 | tf_op jit(solution)/shard_map/ppermute | solution.py:109
  50.6 0.0 collective-permute-done.9
  50.7 6.3 %collective-permute-start.10 = (bf16[4,64,512]{2,1,0:T(8,128)(2,1)S(1)}, bf16[4,64,512]{2,1,0:T(8,128)(2,1)S(1)}, u32[]{:S(2)}, u32[]{:S(2)}) collective-permute-start(bf16[4,64,512]{2,1,0:T(8,128)(2,1)S(1)} %pad_maximum_fusion.7), channel_id=1, source_target_pairs={{0,64},{64,0},{128,192},{192,128},{256,320},{320,256},{384,448},{4... | collective-permute-start | bytes 786440 | tf_op jit(solution)/shard_map/ppermute | solution.py:109
  56.9 0.0 collective-permute-done.1
  57.0 3.1 %collective-permute-start.2 = (bf16[4,64,512]{2,1,0:T(8,128)(2,1)S(1)}, bf16[4,64,512]{2,1,0:T(8,128)(2,1)S(1)}, u32[]{:S(2)}, u32[]{:S(2)}) collective-permute-start(bf16[4,64,512]{2,1,0:T(8,128)(2,1)S(1)} %pad_maximum_fusion.5), channel_id=1, source_target_pairs={{0,64},{64,0},{128,192},{192,128},{256,320},{320,256},{384,448},{4... | collective-permute-start | bytes 786440 | tf_op jit(solution)/shard_map/ppermute | solution.py:109
  60.1 0.0 copy-done.4
  60.1 2.9 %collective-permute-done.10 = bf16[4,64,512]{2,1,0:T(8,128)(2,1)S(1)} collective-permute-done((bf16[4,64,512]{2,1,0:T(8,128)(2,1)S(1)}, bf16[4,64,512]{2,1,0:T(8,128)(2,1)S(1)}, u32[]{:S(2)}, u32[]{:S(2)}) %collective-permute-start.10) | collective-permute-done | bytes 262176 | tf_op jit(solution)/shard_map/ppermute | solution.py:109
  63.1 0.1 pad_maximum_fusion.3.training_ref
  63.1 1.8 %all-gather.4.cloned.1.call-done.gram_ref = bf16[8,512,512]{2,1,0:T(8,128)(2,1)} async-done(((bf16[1,512,512]{2,1,0:T(8,128)(2,1)}), bf16[8,512,512]{2,1,0:T(8,128)(2,1)}) %all-gather.4.cloned.1.call-update) | async-done | bytes 4194320 | tf_op jit(solution)/shard_map/all_gather | solution.py:129
  64.9 2.2 %copy-done.2 = bf16[8,512,512]{2,1,0:T(8,128)(2,1)S(1)} copy-done((bf16[8,512,512]{2,1,0:T(8,128)(2,1)S(1)}, bf16[8,512,512]{2,1,0:T(8,128)(2,1)}, u32[]{:S(2)}) %copy-start.2) | copy-done | bytes 4194328
  67.1 2.9 %kernel_matrix.3 = bf16[64,512]{1,0:T(8,128)(2,1)S(1)} custom-call(s32[8]{0:T(128)S(1)} %broadcast_xor_fusion.slots, bf16[8,512,512]{2,1,0:T(8,128)(2,1)S(1)} %copy-done.2, bf16[8,64,512]{2,1,0:T(8,128)(2,1)S(1)} %pad_maximum_fusion.3.training_ref), custom_call_target="tpu_custom_call" | custom-call | flops 268435456 | bytes 4718592 | tf_op jit(solution)/shard_map/kernel_matrix/pallas_call | solution.py:33
  70.0 7.6 %collective-permute-start.11 = (bf16[1,64,512]{2,1,0:T(8,128)(2,1)S(1)}, bf16[1,64,512]{2,1,0:T(8,128)(2,1)S(1)}, u32[]{:S(2)}, u32[]{:S(2)}) collective-permute-start(bf16[1,64,512]{2,1,0:T(8,128)(2,1)S(1)} %bitcast.21), channel_id=1, source_target_pairs={{0,256},{64,320},{128,384},{192,448},{256,0},{320,64},{384,128},{4... | collective-permute-start | bytes 196616 | tf_op jit(solution)/shard_map/ppermute | solution.py:109
  77.7 0.0 collective-permute-done.2
  77.7 0.1 pad_maximum_fusion.1.training_ref
  77.7 2.9 %kernel_matrix.2 = bf16[64,512]{1,0:T(8,128)(2,1)S(1)} custom-call(s32[8]{0:T(128)S(1)} %broadcast_xor_fusion.slots, bf16[8,512,512]{2,1,0:T(8,128)(2,1)S(1)} %copy-done.2, bf16[8,64,512]{2,1,0:T(8,128)(2,1)S(1)} %pad_maximum_fusion.1.training_ref), custom_call_target="tpu_custom_call" | custom-call | flops 268435456 | bytes 4718592 | tf_op jit(solution)/shard_map/kernel_matrix/pallas_call | solution.py:33
  80.6 2.1 %collective-permute-start.3 = (bf16[1,64,512]{2,1,0:T(8,128)(2,1)S(1)}, bf16[1,64,512]{2,1,0:T(8,128)(2,1)S(1)}, u32[]{:S(2)}, u32[]{:S(2)}) collective-permute-start(bf16[1,64,512]{2,1,0:T(8,128)(2,1)S(1)} %bitcast.25), channel_id=1, source_target_pairs={{0,256},{64,320},{128,384},{192,448},{256,0},{320,64},{384,128},{4... | collective-permute-start | bytes 196616 | tf_op jit(solution)/shard_map/ppermute | solution.py:109
  82.7 1.6 %collective-permute-done.11 = bf16[1,64,512]{2,1,0:T(8,128)(2,1)S(1)} collective-permute-done((bf16[1,64,512]{2,1,0:T(8,128)(2,1)S(1)}, bf16[1,64,512]{2,1,0:T(8,128)(2,1)S(1)}, u32[]{:S(2)}, u32[]{:S(2)}) %collective-permute-start.11) | collective-permute-done | bytes 65568 | tf_op jit(solution)/shard_map/ppermute | solution.py:109
  84.4 2.9 %collective-permute-start.12 = (bf16[2,64,512]{2,1,0:T(8,128)(2,1)S(1)}, bf16[2,64,512]{2,1,0:T(8,128)(2,1)S(1)}, u32[]{:S(2)}, u32[]{:S(2)}) collective-permute-start(bf16[2,64,512]{2,1,0:T(8,128)(2,1)S(1)} %pad_maximum_fusion.12), channel_id=1, source_target_pairs={{0,128},{64,192},{128,0},{192,64},{256,384},{320,448},{384,256},{4... | collective-permute-start | bytes 393224 | tf_op jit(solution)/shard_map/ppermute | solution.py:109
  87.3 7.3 %collective-permute-done.3 = bf16[1,64,512]{2,1,0:T(8,128)(2,1)S(1)} collective-permute-done((bf16[1,64,512]{2,1,0:T(8,128)(2,1)S(1)}, bf16[1,64,512]{2,1,0:T(8,128)(2,1)S(1)}, u32[]{:S(2)}, u32[]{:S(2)}) %collective-permute-start.3) | collective-permute-done | bytes 65568 | tf_op jit(solution)/shard_map/ppermute | solution.py:109
  94.6 1.9 %collective-permute-start.4 = (bf16[2,64,512]{2,1,0:T(8,128)(2,1)S(1)}, bf16[2,64,512]{2,1,0:T(8,128)(2,1)S(1)}, u32[]{:S(2)}, u32[]{:S(2)}) collective-permute-start(bf16[2,64,512]{2,1,0:T(8,128)(2,1)S(1)} %pad_maximum_fusion.10), channel_id=1, source_target_pairs={{0,128},{64,192},{128,0},{192,64},{256,384},{320,448},{384,256},{4... | collective-permute-start | bytes 393224 | tf_op jit(solution)/shard_map/ppermute | solution.py:109
  96.5 0.0 collective-permute-done.12
  96.6 0.0 copy-start.3
  96.6 5.3 %collective-permute-start.13 = (bf16[4,64,512]{2,1,0:T(8,128)(2,1)S(1)}, bf16[4,64,512]{2,1,0:T(8,128)(2,1)S(1)}, u32[]{:S(2)}, u32[]{:S(2)}) collective-permute-start(bf16[4,64,512]{2,1,0:T(8,128)(2,1)S(1)} %pad_maximum_fusion.8), channel_id=1, source_target_pairs={{0,64},{64,0},{128,192},{192,128},{256,320},{320,256},{384,448},{4... | collective-permute-start | bytes 786440 | tf_op jit(solution)/shard_map/ppermute | solution.py:109
  101.9 0.6 collective-permute-done.4
  102.5 5.3 %collective-permute-start.5 = (bf16[4,64,512]{2,1,0:T(8,128)(2,1)S(1)}, bf16[4,64,512]{2,1,0:T(8,128)(2,1)S(1)}, u32[]{:S(2)}, u32[]{:S(2)}) collective-permute-start(bf16[4,64,512]{2,1,0:T(8,128)(2,1)S(1)} %pad_maximum_fusion.6), channel_id=1, source_target_pairs={{0,64},{64,0},{128,192},{192,128},{256,320},{320,256},{384,448},{4... | collective-permute-start | bytes 786440 | tf_op jit(solution)/shard_map/ppermute | solution.py:109
  107.8 1.3 collective-permute-done.13
  109.1 0.1 pad_maximum_fusion.4.refs_1_
  109.1 4.7 %collective-permute-start.14 = (bf16[8,64,512]{2,1,0:T(8,128)(2,1)S(1)}, bf16[8,64,512]{2,1,0:T(8,128)(2,1)S(1)}, u32[]{:S(2)}, u32[]{:S(2)}) collective-permute-start(bf16[8,64,512]{2,1,0:T(8,128)(2,1)S(1)} %pad_maximum_fusion.4.refs_1_), channel_id=1, source_target_pairs={{0,48},{16,0},{32,16},{48,32},{1,49},{17,1},{33,17},{49,33},{2,50}... | collective-permute-start | bytes 1572872 | tf_op jit(solution)/shard_map/ppermute | solution.py:141
  113.9 0.0 collective-permute-done.5
  113.9 0.1 pad_maximum_fusion.2.refs_0_
  113.9 3.1 %collective-permute-start.6 = (bf16[8,64,512]{2,1,0:T(8,128)(2,1)S(1)}, bf16[8,64,512]{2,1,0:T(8,128)(2,1)S(1)}, u32[]{:S(2)}, u32[]{:S(2)}) collective-permute-start(bf16[8,64,512]{2,1,0:T(8,128)(2,1)S(1)} %pad_maximum_fusion.2.refs_0_), channel_id=1, source_target_pairs={{0,16},{16,32},{32,48},{48,0},{1,17},{17,33},{33,49},{49,1},{2,18}... | collective-permute-start | bytes 1572872 | tf_op jit(solution)/shard_map/ppermute | solution.py:140
  117.0 4.0 %collective-permute-start.17 = (bf16[8,64,512]{2,1,0:T(8,128)(2,1)S(1)}, bf16[8,64,512]{2,1,0:T(8,128)(2,1)}, u32[]{:S(2)}, u32[]{:S(2)}) collective-permute-start(bf16[8,64,512]{2,1,0:T(8,128)(2,1)S(1)} %pad_maximum_fusion.2.refs_0_), channel_id=1, source_target_pairs={{0,48},{16,0},{32,16},{48,32},{1,49},{17,1},{33,17},{49,33},{2,50}... | collective-permute-start | bytes 1572872 | tf_op jit(solution)/shard_map/ppermute | solution.py:140
  121.0 1.9 %collective-permute-start.16 = (bf16[8,64,512]{2,1,0:T(8,128)(2,1)S(1)}, bf16[8,64,512]{2,1,0:T(8,128)(2,1)}, u32[]{:S(2)}, u32[]{:S(2)}) collective-permute-start(bf16[8,64,512]{2,1,0:T(8,128)(2,1)S(1)} %pad_maximum_fusion.4.refs_1_), channel_id=1, source_target_pairs={{0,16},{16,32},{32,48},{48,0},{1,17},{17,33},{33,49},{49,1},{2,18}... | collective-permute-start | bytes 1572872 | tf_op jit(solution)/shard_map/ppermute | solution.py:141
  122.9 3.3 %collective-permute-done.14.refs_1_ = bf16[8,64,512]{2,1,0:T(8,128)(2,1)S(1)} collective-permute-done((bf16[8,64,512]{2,1,0:T(8,128)(2,1)S(1)}, bf16[8,64,512]{2,1,0:T(8,128)(2,1)S(1)}, u32[]{:S(2)}, u32[]{:S(2)}) %collective-permute-start.14) | collective-permute-done | bytes 524320 | tf_op jit(solution)/shard_map/ppermute | solution.py:141
  126.2 5.6 %collective-permute-start.15 = (bf16[8,64,512]{2,1,0:T(8,128)(2,1)S(1)}, bf16[8,64,512]{2,1,0:T(8,128)(2,1)S(1)}, u32[]{:S(2)}, u32[]{:S(2)}) collective-permute-start(bf16[8,64,512]{2,1,0:T(8,128)(2,1)S(1)} %collective-permute-done.14.refs_1_), channel_id=1, source_target_pairs={{0,48},{16,0},{32,16},{48,32},{1,49},{17,1},{33,17},{49,33},{2,50}... | collective-permute-start | bytes 1572872 | tf_op jit(solution)/shard_map/ppermute | solution.py:147
  131.8 0.1 collective-permute-done.6.refs_0_
  131.9 1.9 %collective-permute-start.7 = (bf16[8,64,512]{2,1,0:T(8,128)(2,1)S(1)}, bf16[8,64,512]{2,1,0:T(8,128)(2,1)S(1)}, u32[]{:S(2)}, u32[]{:S(2)}) collective-permute-start(bf16[8,64,512]{2,1,0:T(8,128)(2,1)S(1)} %collective-permute-done.6.refs_0_), channel_id=1, source_target_pairs={{0,16},{16,32},{32,48},{48,0},{1,17},{17,33},{33,49},{49,1},{2,18}... | collective-permute-start | bytes 1572872 | tf_op jit(solution)/shard_map/ppermute | solution.py:147
  133.8 0.0 all-gather.6.cloned.1.call-done
  133.9 2.2 %copy-done = bf16[4096,512]{1,0:T(8,128)(2,1)S(1)} copy-done((bf16[4096,512]{1,0:T(8,128)(2,1)S(1)}, bf16[4096,512]{1,0:T(8,128)(2,1)}, u32[]{:S(2)}) %copy-start) | copy-done | bytes 4194328
  136.1 3.8 %score_columns.4.refs_2_ = f32[512,512]{1,0:T(8,128)} custom-call(s32[8]{0:T(128)S(1)} %broadcast_xor_fusion.slots, s32[1]{0:T(128)} %bitcast.11.place, bf16[8,512,512]{2,1,0:T(8,128)(2,1)S(1)} %bitcast.17, f32[1,512]{1,0:T(1,128)S(1)} %bitcast.29, bf16[8,64,512]{2,1,0:T(8,128)(2,1)S(1)} %pad_maximum_fusion.2.refs_0_, ...), custom_call_target="tpu_custom_call" | custom-call | flops 536870912 | bytes 5242880 | tf_op jit(solution)/shard_map/score_columns/pallas_call | solution.py:85
  139.8 0.0 collective-permute-done.17.refs_0_
  139.8 4.8 %score_columns.5.refs_2_ = f32[512,512]{1,0:T(8,128)} custom-call(s32[8]{0:T(128)S(1)} %broadcast_xor_fusion.slots, s32[1]{0:T(128)} %bitcast.10.place, bf16[8,512,512]{2,1,0:T(8,128)(2,1)S(1)} %bitcast.18, f32[1,512]{1,0:T(1,128)S(1)} %bitcast.30, bf16[8,64,512]{2,1,0:T(8,128)(2,1)} %collective-permute-done.17.refs_0_, ...), custom_call_target="tpu_custom_call", output_to_operand_aliasing={{}: (6, {})} | custom-call | flops 536870912 | bytes 5242880 | tf_op jit(solution)/shard_map/score_columns/pallas_call | solution.py:85
  144.6 0.0 collective-permute-done.16.refs_1_
  144.7 4.8 %score_columns.6.refs_2_ = f32[512,512]{1,0:T(8,128)} custom-call(s32[8]{0:T(128)S(1)} %broadcast_xor_fusion.slots, s32[1]{0:T(128)} %bitcast.9.place, bf16[8,512,512]{2,1,0:T(8,128)(2,1)S(1)} %bitcast.19, f32[1,512]{1,0:T(1,128)S(1)} %bitcast.31, bf16[8,64,512]{2,1,0:T(8,128)(2,1)S(1)} %collective-permute-done.6.refs_0_, ...), custom_call_target="tpu_custom_call", output_to_operand_aliasing={{}: (6, {})} | custom-call | flops 536870912 | bytes 5242880 | tf_op jit(solution)/shard_map/score_columns/pallas_call | solution.py:85
  149.5 0.0 collective-permute-done.15.refs_1_
  149.5 1.7 %collective-permute-done.7.refs_0_ = bf16[8,64,512]{2,1,0:T(8,128)(2,1)S(1)} collective-permute-done((bf16[8,64,512]{2,1,0:T(8,128)(2,1)S(1)}, bf16[8,64,512]{2,1,0:T(8,128)(2,1)S(1)}, u32[]{:S(2)}, u32[]{:S(2)}) %collective-permute-start.7) | collective-permute-done | bytes 524320 | tf_op jit(solution)/shard_map/ppermute | solution.py:147
  151.2 3.8 %score_columns.7 = f32[512,512]{1,0:T(8,128)} custom-call(s32[8]{0:T(128)S(1)} %broadcast_xor_fusion.slots, s32[1]{0:T(128)} %bitcast.place, bf16[8,512,512]{2,1,0:T(8,128)(2,1)S(1)} %bitcast.20, f32[1,512]{1,0:T(1,128)S(1)} %bitcast.32, bf16[8,64,512]{2,1,0:T(8,128)(2,1)S(1)} %collective-permute-done.7.refs_0_, ...), custom_call_target="tpu_custom_call", output_to_operand_aliasing={{}: (6, {})} | custom-call | flops 536870912 | bytes 5242880 | tf_op jit(solution)/shard_map/score_columns/pallas_call | solution.py:85
  (19 shorter events, 0.3 us)
Async XLA Ops:
  6.5 58.4 %all-gather.4.cloned.1.call-start = ((), (), s32[]{:S(2)}) async-start(), calls=%async_computation.1 | async-start | bytes 4718592 | tf_op jit(solution)/shard_map/all_gather | solution.py:129
  24.5 109.4 %all-gather.6.cloned.1.call-start = ((), (), s32[]{:S(2)}) async-start(), calls=%async_computation.2 | async-start | bytes 4718592 | tf_op jit(solution)/shard_map/all_gather | solution.py:130
  25.2 34.9 %copy-start.4 = (s32[8]{0:T(128)S(1)}, s32[8]{0:T(128)}, u32[]{:S(2)}) copy-start(s32[8]{0:T(128)} %constant.30.clone) | copy-start | bytes 100
  25.5 11.4 %collective-permute-start.8 = (bf16[1,64,512]{2,1,0:T(8,128)(2,1)S(1)}, bf16[1,64,512]{2,1,0:T(8,128)(2,1)S(1)}, u32[]{:S(2)}, u32[]{:S(2)}) collective-permute-start(bf16[1,64,512]{2,1,0:T(8,128)(2,1)S(1)} %squeeze.7), channel_id=1, source_target_pairs={{0,256},{64,320},{128,384},{192,448},{256,0},{320,64},{384,128},{4... | collective-permute-start | bytes 196616 | tf_op jit(solution)/shard_map/ppermute | solution.py:109
  34.7 11.7 %collective-permute-start = (bf16[1,64,512]{2,1,0:T(8,128)(2,1)S(1)}, bf16[1,64,512]{2,1,0:T(8,128)(2,1)S(1)}, u32[]{:S(2)}, u32[]{:S(2)}) collective-permute-start(bf16[1,64,512]{2,1,0:T(8,128)(2,1)S(1)} %squeeze.6), channel_id=1, source_target_pairs={{0,256},{64,320},{128,384},{192,448},{256,0},{320,64},{384,128},{4... | collective-permute-start | bytes 196616 | tf_op jit(solution)/shard_map/ppermute | solution.py:109
  36.9 13.7 %collective-permute-start.9 = (bf16[2,64,512]{2,1,0:T(8,128)(2,1)S(1)}, bf16[2,64,512]{2,1,0:T(8,128)(2,1)S(1)}, u32[]{:S(2)}, u32[]{:S(2)}) collective-permute-start(bf16[2,64,512]{2,1,0:T(8,128)(2,1)S(1)} %pad_maximum_fusion.11), channel_id=1, source_target_pairs={{0,128},{64,192},{128,0},{192,64},{256,384},{320,448},{384,256},{4... | collective-permute-start | bytes 393224 | tf_op jit(solution)/shard_map/ppermute | solution.py:109
  46.4 10.6 %collective-permute-start.1 = (bf16[2,64,512]{2,1,0:T(8,128)(2,1)S(1)}, bf16[2,64,512]{2,1,0:T(8,128)(2,1)S(1)}, u32[]{:S(2)}, u32[]{:S(2)}) collective-permute-start(bf16[2,64,512]{2,1,0:T(8,128)(2,1)S(1)} %pad_maximum_fusion.9), channel_id=1, source_target_pairs={{0,128},{64,192},{128,0},{192,64},{256,384},{320,448},{384,256},{4... | collective-permute-start | bytes 393224 | tf_op jit(solution)/shard_map/ppermute | solution.py:109
  50.7 12.4 %collective-permute-start.10 = (bf16[4,64,512]{2,1,0:T(8,128)(2,1)S(1)}, bf16[4,64,512]{2,1,0:T(8,128)(2,1)S(1)}, u32[]{:S(2)}, u32[]{:S(2)}) collective-permute-start(bf16[4,64,512]{2,1,0:T(8,128)(2,1)S(1)} %pad_maximum_fusion.7), channel_id=1, source_target_pairs={{0,64},{64,0},{128,192},{192,128},{256,320},{320,256},{384,448},{4... | collective-permute-start | bytes 786440 | tf_op jit(solution)/shard_map/ppermute | solution.py:109
  57.0 20.7 %collective-permute-start.2 = (bf16[4,64,512]{2,1,0:T(8,128)(2,1)S(1)}, bf16[4,64,512]{2,1,0:T(8,128)(2,1)S(1)}, u32[]{:S(2)}, u32[]{:S(2)}) collective-permute-start(bf16[4,64,512]{2,1,0:T(8,128)(2,1)S(1)} %pad_maximum_fusion.5), channel_id=1, source_target_pairs={{0,64},{64,0},{128,192},{192,128},{256,320},{320,256},{384,448},{4... | collective-permute-start | bytes 786440 | tf_op jit(solution)/shard_map/ppermute | solution.py:109
  64.9 2.2 %copy-start.2 = (bf16[8,512,512]{2,1,0:T(8,128)(2,1)S(1)}, bf16[8,512,512]{2,1,0:T(8,128)(2,1)}, u32[]{:S(2)}) copy-start(bf16[8,512,512]{2,1,0:T(8,128)(2,1)} %all-gather.4.cloned.1.call-done.gram_ref) | copy-start | bytes 12582916
  70.0 14.4 %collective-permute-start.11 = (bf16[1,64,512]{2,1,0:T(8,128)(2,1)S(1)}, bf16[1,64,512]{2,1,0:T(8,128)(2,1)S(1)}, u32[]{:S(2)}, u32[]{:S(2)}) collective-permute-start(bf16[1,64,512]{2,1,0:T(8,128)(2,1)S(1)} %bitcast.21), channel_id=1, source_target_pairs={{0,256},{64,320},{128,384},{192,448},{256,0},{320,64},{384,128},{4... | collective-permute-start | bytes 196616 | tf_op jit(solution)/shard_map/ppermute | solution.py:109
  80.6 14.0 %collective-permute-start.3 = (bf16[1,64,512]{2,1,0:T(8,128)(2,1)S(1)}, bf16[1,64,512]{2,1,0:T(8,128)(2,1)S(1)}, u32[]{:S(2)}, u32[]{:S(2)}) collective-permute-start(bf16[1,64,512]{2,1,0:T(8,128)(2,1)S(1)} %bitcast.25), channel_id=1, source_target_pairs={{0,256},{64,320},{128,384},{192,448},{256,0},{320,64},{384,128},{4... | collective-permute-start | bytes 196616 | tf_op jit(solution)/shard_map/ppermute | solution.py:109
  84.4 12.1 %collective-permute-start.12 = (bf16[2,64,512]{2,1,0:T(8,128)(2,1)S(1)}, bf16[2,64,512]{2,1,0:T(8,128)(2,1)S(1)}, u32[]{:S(2)}, u32[]{:S(2)}) collective-permute-start(bf16[2,64,512]{2,1,0:T(8,128)(2,1)S(1)} %pad_maximum_fusion.12), channel_id=1, source_target_pairs={{0,128},{64,192},{128,0},{192,64},{256,384},{320,448},{384,256},{4... | collective-permute-start | bytes 393224 | tf_op jit(solution)/shard_map/ppermute | solution.py:109
  94.6 7.9 %collective-permute-start.4 = (bf16[2,64,512]{2,1,0:T(8,128)(2,1)S(1)}, bf16[2,64,512]{2,1,0:T(8,128)(2,1)S(1)}, u32[]{:S(2)}, u32[]{:S(2)}) collective-permute-start(bf16[2,64,512]{2,1,0:T(8,128)(2,1)S(1)} %pad_maximum_fusion.10), channel_id=1, source_target_pairs={{0,128},{64,192},{128,0},{192,64},{256,384},{320,448},{384,256},{4... | collective-permute-start | bytes 393224 | tf_op jit(solution)/shard_map/ppermute | solution.py:109
  96.6 37.3 %copy-start.3 = (f32[512]{0:T(512)S(1)}, f32[512]{0:T(512)}, u32[]{:S(2)}) copy-start(f32[512]{0:T(512)} %param.8) | copy-start | bytes 6148
  96.6 12.5 %collective-permute-start.13 = (bf16[4,64,512]{2,1,0:T(8,128)(2,1)S(1)}, bf16[4,64,512]{2,1,0:T(8,128)(2,1)S(1)}, u32[]{:S(2)}, u32[]{:S(2)}) collective-permute-start(bf16[4,64,512]{2,1,0:T(8,128)(2,1)S(1)} %pad_maximum_fusion.8), channel_id=1, source_target_pairs={{0,64},{64,0},{128,192},{192,128},{256,320},{320,256},{384,448},{4... | collective-permute-start | bytes 786440 | tf_op jit(solution)/shard_map/ppermute | solution.py:109
  102.5 11.4 %collective-permute-start.5 = (bf16[4,64,512]{2,1,0:T(8,128)(2,1)S(1)}, bf16[4,64,512]{2,1,0:T(8,128)(2,1)S(1)}, u32[]{:S(2)}, u32[]{:S(2)}) collective-permute-start(bf16[4,64,512]{2,1,0:T(8,128)(2,1)S(1)} %pad_maximum_fusion.6), channel_id=1, source_target_pairs={{0,64},{64,0},{128,192},{192,128},{256,320},{320,256},{384,448},{4... | collective-permute-start | bytes 786440 | tf_op jit(solution)/shard_map/ppermute | solution.py:109
  109.1 17.1 %collective-permute-start.14 = (bf16[8,64,512]{2,1,0:T(8,128)(2,1)S(1)}, bf16[8,64,512]{2,1,0:T(8,128)(2,1)S(1)}, u32[]{:S(2)}, u32[]{:S(2)}) collective-permute-start(bf16[8,64,512]{2,1,0:T(8,128)(2,1)S(1)} %pad_maximum_fusion.4.refs_1_), channel_id=1, source_target_pairs={{0,48},{16,0},{32,16},{48,32},{1,49},{17,1},{33,17},{49,33},{2,50}... | collective-permute-start | bytes 1572872 | tf_op jit(solution)/shard_map/ppermute | solution.py:141
  113.9 18.0 %collective-permute-start.6 = (bf16[8,64,512]{2,1,0:T(8,128)(2,1)S(1)}, bf16[8,64,512]{2,1,0:T(8,128)(2,1)S(1)}, u32[]{:S(2)}, u32[]{:S(2)}) collective-permute-start(bf16[8,64,512]{2,1,0:T(8,128)(2,1)S(1)} %pad_maximum_fusion.2.refs_0_), channel_id=1, source_target_pairs={{0,16},{16,32},{32,48},{48,0},{1,17},{17,33},{33,49},{49,1},{2,18}... | collective-permute-start | bytes 1572872 | tf_op jit(solution)/shard_map/ppermute | solution.py:140
  117.0 22.8 %collective-permute-start.17 = (bf16[8,64,512]{2,1,0:T(8,128)(2,1)S(1)}, bf16[8,64,512]{2,1,0:T(8,128)(2,1)}, u32[]{:S(2)}, u32[]{:S(2)}) collective-permute-start(bf16[8,64,512]{2,1,0:T(8,128)(2,1)S(1)} %pad_maximum_fusion.2.refs_0_), channel_id=1, source_target_pairs={{0,48},{16,0},{32,16},{48,32},{1,49},{17,1},{33,17},{49,33},{2,50}... | collective-permute-start | bytes 1572872 | tf_op jit(solution)/shard_map/ppermute | solution.py:140
  121.0 23.7 %collective-permute-start.16 = (bf16[8,64,512]{2,1,0:T(8,128)(2,1)S(1)}, bf16[8,64,512]{2,1,0:T(8,128)(2,1)}, u32[]{:S(2)}, u32[]{:S(2)}) collective-permute-start(bf16[8,64,512]{2,1,0:T(8,128)(2,1)S(1)} %pad_maximum_fusion.4.refs_1_), channel_id=1, source_target_pairs={{0,16},{16,32},{32,48},{48,0},{1,17},{17,33},{33,49},{49,1},{2,18}... | collective-permute-start | bytes 1572872 | tf_op jit(solution)/shard_map/ppermute | solution.py:141
  126.2 23.3 %collective-permute-start.15 = (bf16[8,64,512]{2,1,0:T(8,128)(2,1)S(1)}, bf16[8,64,512]{2,1,0:T(8,128)(2,1)S(1)}, u32[]{:S(2)}, u32[]{:S(2)}) collective-permute-start(bf16[8,64,512]{2,1,0:T(8,128)(2,1)S(1)} %collective-permute-done.14.refs_1_), channel_id=1, source_target_pairs={{0,48},{16,0},{32,16},{48,32},{1,49},{17,1},{33,17},{49,33},{2,50}... | collective-permute-start | bytes 1572872 | tf_op jit(solution)/shard_map/ppermute | solution.py:147
  131.9 19.3 %collective-permute-start.7 = (bf16[8,64,512]{2,1,0:T(8,128)(2,1)S(1)}, bf16[8,64,512]{2,1,0:T(8,128)(2,1)S(1)}, u32[]{:S(2)}, u32[]{:S(2)}) collective-permute-start(bf16[8,64,512]{2,1,0:T(8,128)(2,1)S(1)} %collective-permute-done.6.refs_0_), channel_id=1, source_target_pairs={{0,16},{16,32},{32,48},{48,0},{1,17},{17,33},{33,49},{49,1},{2,18}... | collective-permute-start | bytes 1572872 | tf_op jit(solution)/shard_map/ppermute | solution.py:147
  133.9 2.2 %copy-start = (bf16[4096,512]{1,0:T(8,128)(2,1)S(1)}, bf16[4096,512]{1,0:T(8,128)(2,1)}, u32[]{:S(2)}) copy-start(bf16[4096,512]{1,0:T(8,128)(2,1)} %all-gather.6.cloned.1.call-done) | copy-start | bytes 12582916
  136.1 3.8 %copy-start.1 = (bf16[4096,512]{1,0:T(8,128)(2,1)S(1)}, bf16[4096,512]{1,0:T(8,128)(2,1)}, u32[]{:S(2)}) copy-start(bf16[4096,512]{1,0:T(8,128)(2,1)} %all-gather.6.cloned.1.call-done) | copy-start | bytes 12582916
Sparse Core Ops, SparseCore 0:
  24.6 40.2 all-gather.3
  67.1 39.7 all-gather.5

commit v9 on v8

--- a/solution.py
+++ b/solution.py
@@ -51,13 +51,14 @@
     )(slots, inverse_gram, training)
 
 
-def score_columns(slots, place, query, chunks, weight, out):
+def score_columns(slots, place, query, first, second, weight, out):
     n, rows, depth = query.shape
-    each = chunks[0].shape[1]
-    t = each * len(chunks)
+    each = first.shape[1]
+    t = each * CHUNKS
     columns = weight.shape[1]
+    half = n // 2
 
-    def kernel(slots, place, query_ref, weight_ref, *refs):
+    def kernel(slots, place, query_ref, weight_ref, first_ref, near_ref, other_ref, *refs):
         out_ref, total = refs[-2:]
         step = pl.program_id(0)
 
@@ -65,18 +66,22 @@
         def _():
             total[...] = jnp.zeros_like(total)
 
-        block = jnp.concatenate([ref[step] for ref in refs[: len(chunks)]], axis=0)
+        near, other = near_ref[0, jnp.minimum(step, half - 1)], other_ref[0, jnp.maximum(step - half, 0)]
+        block = jnp.concatenate([first_ref[step], jnp.where(step < half, near, other)], axis=0)
         total[...] += lax.dot_general(query_ref[0], block, NT_DIMS, preferred_element_type=jnp.float32)
 
         @pl.when(step == n - 1)
         def _():
             out_ref[...] = total[...] * weight_ref[...]
 
-    operands = [slots, place, query, weight, *chunks]
+    operands = [slots, place, query, weight, first] + [array for array, _ in second]
     in_specs = [
         pl.BlockSpec((1, rows, depth), lambda s, slots, place: (slots[s], 0, 0)),
         pl.BlockSpec((1, t), lambda s, slots, place: (0, place[0])),
-    ] + [pl.BlockSpec((n, each, depth), lambda s, slots, place: (0, 0, 0))] * len(chunks)
+        pl.BlockSpec((n, each, depth), lambda s, slots, place: (0, 0, 0)),
+    ] + [
+        pl.BlockSpec((1, half, each, depth), lambda s, slots, place, index=index: (index, 0, 0, 0)) for _, index in second
+    ]
     aliases = {}
     if out is not None:
         in_specs.append(pl.BlockSpec(memory_space=pl.ANY))
@@ -105,9 +110,12 @@
     return lax.optimization_barrier((array, earlier))[0]
 
 
+def swapped(held, distance):
+    return lax.ppermute(held, "z", [(i, i ^ distance) for i in range(NZ)])
+
+
 def exchange(held, distance):
-    other = lax.ppermute(held, "z", [(i, i ^ distance) for i in range(NZ)])
-    return jnp.concatenate([held, other], axis=0)
+    return jnp.concatenate([held, swapped(held, distance)], axis=0)
 
 
 def local(query_features, inverse_gram, training_features, residual_weight):
@@ -132,22 +140,29 @@
 
     a, b = training[0], training[1]
     for distance in (4, 2, 1):
-        a, b = exchange(a, distance), exchange(b, distance)
-    a, b = kernel_matrix(slots, gram, a)[None], kernel_matrix(slots, gram, b)[None]
-    for distance in (4, 2, 1):
-        a, b = exchange(a, distance), exchange(b, distance)
+        a, b = exchange(after(a, b), distance), exchange(b, distance)
+    b = kernel_matrix(slots, gram, b)[None]
+    a = kernel_matrix(slots, gram, after(a, b))[None]
+    for distance in (4, 2):
+        a, b = exchange(after(a, b), distance), exchange(b, distance)
 
+    b = b[None]
+    a = exchange(after(a, b), 1)
+    below_b, above_b = lax.ppermute(b, "y", UP), lax.ppermute(b, "y", DOWN)
+    far_b = lax.ppermute(above_b, "y", DOWN)
+    a = after(a, below_b, above_b)
     below_a, above_a = lax.ppermute(a, "y", UP), lax.ppermute(a, "y", DOWN)
-    below_b, above_b = lax.ppermute(b, "y", UP), lax.ppermute(b, "y", DOWN)
+    far_a = lax.ppermute(below_a, "y", UP)
+    own = swapped(b, 1)
+    near = swapped(after(jnp.concatenate([below_b, above_b], axis=0), own), 1)
 
-    def scores(distance, chunks, out):
-        return score_columns(slots, lax.rem(y + distance, NY)[None], query, chunks, weight, out)
+    def scores(distance, first, second, out):
+        return score_columns(slots, lax.rem(y + distance, NY)[None], query, first, second, weight, out)
 
-    out = scores(0, (a, b), None)
-    far = lax.ppermute(below_a, "y", UP), lax.ppermute(above_b, "y", DOWN)
-    out = scores(1, (above_a, above_b), out)
-    out = scores(NY - 1, (below_a, below_b), out)
-    return scores(2, far, out)
+    out = scores(0, a, ((b, 0), (own, 0)), None)
+    out = scores(1, above_a, ((above_b, 0), (near, 1)), out)
+    out = scores(NY - 1, below_a, ((below_b, 0), (near, 0)), out)
+    return scores(2, far_a, ((far_b, 0), (swapped(far_b, 1), 0)), out)
 
 
 def solution(mesh):

time: 164 us -> 183 us (1.12)
  waiting for transfers between devices: 22.6 us -> 38.2 us
    ppermute x14 -> x16, waiting for transfers between devices: 16.6 us -> 31.1 us  [the longest x14 26.7 us: swapped(): return lax.ppermute(held, 'z', [(i, i ^ distance) for i in range(NZ)])]
    unnamed x10 -> x16, local copies, waits for them, and re-layouts: 4.39 us -> 6.06 us
    ppermute x14 -> x16, starting transfers between devices: 65.8 us -> 66.9 us  [the longest x14 61.1 us: swapped(): return lax.ppermute(held, 'z', [(i, i ^ distance) for i in range(NZ)])]
  transfers between devices with their start and end apart: 20 -> 22, of which waited for: 11 -> 11; matrix products, arithmetic and copies ran while one was open for 0% -> 1% of each run, Pallas kernels for 12% -> 10%
where the time goes in v9:
time: 183 us; the launch traced here: 181 us
  starting transfers between devices  81.1 us (44%)
  waiting for transfers between devices  38.2 us (21%)
  Pallas kernels  22 us (12%)
  blocking collectives  15.1 us (8%)
  between operations  13.8 us (8%)
  local copies, waits for them, and re-layouts  9.08 us (5%)
    ppermute x14, starting transfers between devices, swapped(): return lax.ppermute(held, 'z', [(i, i ^ distance) for i in range(NZ)])  61.1 us
    ppermute x14, waiting for transfers between devices, swapped(): return lax.ppermute(held, 'z', [(i, i ^ distance) for i in range(NZ)])  26.7 us
    pallas_call x4, Pallas kernels, score_columns(): pl.pallas_call(kernel, out_shape=jax.ShapeDtypeStruct((rows, columns), jn...  16.2 us
    all_to_all x1, blocking collectives, local(): got = lax.all_to_all(sent, 'y', split_axis=0, concat_axis=0, tiled=True)  15.1 us
    ppermute x2, starting transfers between devices, local(): below_a, above_a = (lax.ppermute(a, 'y', UP), lax.ppermute(a, 'y', DOWN))  7.06 us
    ppermute x2, starting transfers between devices, local(): below_b, above_b = (lax.ppermute(b, 'y', UP), lax.ppermute(b, 'y', DOWN))  7.05 us
    unnamed x16, local copies, waits for them, and re-layouts  6.06 us
    pallas_call x2, Pallas kernels, kernel_matrix(): pl.pallas_call(kernel, out_shape=jax.ShapeDtypeStruct((t, rows), jnp.bflo...  5.76 us
  transfers between devices with their start and end apart: 22, of which 11 were waited for; matrix products, arithmetic and copies ran while one was open for 1% of the time, Pallas kernels for 10%

profile of v9, /device:TPU:6, one launch (start us, length us, event | category | flops | bytes accessed | tf_op | source)
XLA Modules:
  0.0 180.5 jit_solution(12812755278317412819)
XLA Ops:
  6.5 0.9 copy.18
  7.5 0.9 broadcast_in_dim.29
  8.5 15.1 %all_to_all.5 = bf16[4,160,512]{2,1,0:T(8,128)(2,1)S(1)} all-to-all(bf16[4,160,512]{2,1,0:T(8,128)(2,1)S(1)} %pad_maximum_fusion), channel_id=1, replica_groups=mesh['z'=8,'y'=4,'x'=4,'core'=2,'row'=2] {'y'}, dimensions={0} | all-to-all | bytes 1310720 | tf_op jit(solution)/shard_map/all_to_all | solution.py:132
  23.6 0.8 slice.18
  24.4 0.0 all-gather.4.cloned.1.call-update
  24.5 0.0 all-gather.6.cloned.1.call-start
  24.5 0.7 all-gather.6.cloned.1.call-update
  25.2 0.0 copy-start.6
  25.3 0.1 fusion
  25.4 0.1 copy.15
  25.5 9.1 %collective-permute-start.1 = (bf16[1,64,512]{2,1,0:T(8,128)(2,1)S(1)}, bf16[1,64,512]{2,1,0:T(8,128)(2,1)S(1)}, u32[]{:S(2)}, u32[]{:S(2)}) collective-permute-start(bf16[1,64,512]{2,1,0:T(8,128)(2,1)S(1)} %squeeze.7), channel_id=1, source_target_pairs={{0,256},{64,320},{128,384},{192,448},{256,0},{320,64},{384,128},{4... | collective-permute-start | bytes 196616 | tf_op jit(solution)/shard_map/ppermute | solution.py:114
  34.6 0.1 copy.14
  34.7 1.9 %collective-permute-start = (bf16[1,64,512]{2,1,0:T(8,128)(2,1)S(1)}, bf16[1,64,512]{2,1,0:T(8,128)(2,1)S(1)}, u32[]{:S(2)}, u32[]{:S(2)}) collective-permute-start(bf16[1,64,512]{2,1,0:T(8,128)(2,1)S(1)} %squeeze.6), channel_id=1, source_target_pairs={{0,256},{64,320},{128,384},{192,448},{256,0},{320,64},{384,128},{4... | collective-permute-start | bytes 196616 | tf_op jit(solution)/shard_map/ppermute | solution.py:114
  36.6 0.2 collective-permute-done.1
  36.9 8.5 %collective-permute-start.3 = (bf16[2,64,512]{2,1,0:T(8,128)(2,1)S(1)}, bf16[2,64,512]{2,1,0:T(8,128)(2,1)S(1)}, u32[]{:S(2)}, u32[]{:S(2)}) collective-permute-start(bf16[2,64,512]{2,1,0:T(8,128)(2,1)S(1)} %get-tuple-element.26), channel_id=1, source_target_pairs={{0,128},{64,192},{128,0},{192,64},{256,384},{320,448},{384,256},{4... | collective-permute-start | bytes 393224 | tf_op jit(solution)/shard_map/ppermute | solution.py:114
  45.4 1.0 collective-permute-done
  46.4 4.2 %collective-permute-start.2 = (bf16[2,64,512]{2,1,0:T(8,128)(2,1)S(1)}, bf16[2,64,512]{2,1,0:T(8,128)(2,1)S(1)}, u32[]{:S(2)}, u32[]{:S(2)}) collective-permute-start(bf16[2,64,512]{2,1,0:T(8,128)(2,1)S(1)} %pad_maximum_fusion.7), channel_id=1, source_target_pairs={{0,128},{64,192},{128,0},{192,64},{256,384},{320,448},{384,256},{4... | collective-permute-start | bytes 393224 | tf_op jit(solution)/shard_map/ppermute | solution.py:114
  50.6 0.0 collective-permute-done.3
  50.6 6.3 %collective-permute-start.5 = (bf16[4,64,512]{2,1,0:T(8,128)(2,1)S(1)}, bf16[4,64,512]{2,1,0:T(8,128)(2,1)S(1)}, u32[]{:S(2)}, u32[]{:S(2)}) collective-permute-start(bf16[4,64,512]{2,1,0:T(8,128)(2,1)S(1)} %constant_dynamic-update-slice_fusion.2), channel_id=1, source_target_pairs={{0,64},{64,0},{128,192},{192,128},{256,320},{320,256},{384,448},{4... | collective-permute-start | bytes 786440 | tf_op jit(solution)/shard_map/ppermute | solution.py:114
  56.9 0.0 collective-permute-done.2
  57.0 3.2 %collective-permute-start.4 = (bf16[4,64,512]{2,1,0:T(8,128)(2,1)S(1)}, bf16[4,64,512]{2,1,0:T(8,128)(2,1)S(1)}, u32[]{:S(2)}, u32[]{:S(2)}) collective-permute-start(bf16[4,64,512]{2,1,0:T(8,128)(2,1)S(1)} %pad_maximum_fusion.5), channel_id=1, source_target_pairs={{0,64},{64,0},{128,192},{192,128},{256,320},{320,256},{384,448},{4... | collective-permute-start | bytes 786440 | tf_op jit(solution)/shard_map/ppermute | solution.py:114
  60.1 2.9 %collective-permute-done.5 = bf16[4,64,512]{2,1,0:T(8,128)(2,1)S(1)} collective-permute-done((bf16[4,64,512]{2,1,0:T(8,128)(2,1)S(1)}, bf16[4,64,512]{2,1,0:T(8,128)(2,1)S(1)}, u32[]{:S(2)}, u32[]{:S(2)}) %collective-permute-start.5) | collective-permute-done | bytes 262176 | tf_op jit(solution)/shard_map/ppermute | solution.py:114
  63.0 0.1 pad_maximum_fusion.2.training_ref
  63.1 1.8 %all-gather.4.cloned.1.call-done.gram_ref = bf16[8,512,512]{2,1,0:T(8,128)(2,1)} async-done(((bf16[1,512,512]{2,1,0:T(8,128)(2,1)}), bf16[8,512,512]{2,1,0:T(8,128)(2,1)}) %all-gather.4.cloned.1.call-update) | async-done | bytes 4194320 | tf_op jit(solution)/shard_map/all_gather | solution.py:137
  64.9 2.2 %copy-done.2 = bf16[8,512,512]{2,1,0:T(8,128)(2,1)S(1)} copy-done((bf16[8,512,512]{2,1,0:T(8,128)(2,1)S(1)}, bf16[8,512,512]{2,1,0:T(8,128)(2,1)}, u32[]{:S(2)}) %copy-start.2) | copy-done | bytes 4194328
  67.1 2.9 %kernel_matrix.2 = bf16[64,512]{1,0:T(8,128)(2,1)S(1)} custom-call(s32[8]{0:T(128)S(1)} %broadcast_xor_fusion.slots, bf16[8,512,512]{2,1,0:T(8,128)(2,1)S(1)} %copy-done.2, bf16[8,64,512]{2,1,0:T(8,128)(2,1)S(1)} %pad_maximum_fusion.2.training_ref), custom_call_target="tpu_custom_call" | custom-call | flops 268435456 | bytes 4718592 | tf_op jit(solution)/shard_map/kernel_matrix/pallas_call | solution.py:33
  70.0 7.6 %collective-permute-start.7 = (bf16[1,64,512]{2,1,0:T(8,128)(2,1)S(1)}, bf16[1,64,512]{2,1,0:T(8,128)(2,1)S(1)}, u32[]{:S(2)}, u32[]{:S(2)}) collective-permute-start(bf16[1,64,512]{2,1,0:T(8,128)(2,1)S(1)} %bitcast.23), channel_id=1, source_target_pairs={{0,256},{64,320},{128,384},{192,448},{256,0},{320,64},{384,128},{4... | collective-permute-start | bytes 196616 | tf_op jit(solution)/shard_map/ppermute | solution.py:114
  77.7 0.0 collective-permute-done.4
  77.7 2.9 %kernel_matrix.3 = bf16[64,512]{1,0:T(8,128)(2,1)S(1)} custom-call(s32[8]{0:T(128)S(1)} %broadcast_xor_fusion.slots, bf16[8,512,512]{2,1,0:T(8,128)(2,1)S(1)} %copy-done.2, bf16[8,64,512]{2,1,0:T(8,128)(2,1)S(1)} %pad_maximum_fusion.1.training_ref), custom_call_target="tpu_custom_call" | custom-call | flops 268435456 | bytes 4718592 | tf_op jit(solution)/shard_map/kernel_matrix/pallas_call | solution.py:33
  80.6 2.1 %collective-permute-start.6 = (bf16[1,64,512]{2,1,0:T(8,128)(2,1)S(1)}, bf16[1,64,512]{2,1,0:T(8,128)(2,1)S(1)}, u32[]{:S(2)}, u32[]{:S(2)}) collective-permute-start(bf16[1,64,512]{2,1,0:T(8,128)(2,1)S(1)} %bitcast.26), channel_id=1, source_target_pairs={{0,256},{64,320},{128,384},{192,448},{256,0},{320,64},{384,128},{4... | collective-permute-start | bytes 196616 | tf_op jit(solution)/shard_map/ppermute | solution.py:114
  82.7 1.6 collective-permute-done.7
  84.4 2.9 %collective-permute-start.9 = (bf16[2,64,512]{2,1,0:T(8,128)(2,1)S(1)}, bf16[2,64,512]{2,1,0:T(8,128)(2,1)S(1)}, u32[]{:S(2)}, u32[]{:S(2)}) collective-permute-start(bf16[2,64,512]{2,1,0:T(8,128)(2,1)S(1)} %pad_maximum_fusion.9), channel_id=1, source_target_pairs={{0,128},{64,192},{128,0},{192,64},{256,384},{320,448},{384,256},{4... | collective-permute-start | bytes 393224 | tf_op jit(solution)/shard_map/ppermute | solution.py:114
  87.3 7.3 %collective-permute-done.6 = bf16[1,64,512]{2,1,0:T(8,128)(2,1)S(1)} collective-permute-done((bf16[1,64,512]{2,1,0:T(8,128)(2,1)S(1)}, bf16[1,64,512]{2,1,0:T(8,128)(2,1)S(1)}, u32[]{:S(2)}, u32[]{:S(2)}) %collective-permute-start.6) | collective-permute-done | bytes 65568 | tf_op jit(solution)/shard_map/ppermute | solution.py:114
  94.6 2.0 %collective-permute-start.8 = (bf16[2,64,512]{2,1,0:T(8,128)(2,1)S(1)}, bf16[2,64,512]{2,1,0:T(8,128)(2,1)S(1)}, u32[]{:S(2)}, u32[]{:S(2)}) collective-permute-start(bf16[2,64,512]{2,1,0:T(8,128)(2,1)S(1)} %pad_maximum_fusion.8), channel_id=1, source_target_pairs={{0,128},{64,192},{128,0},{192,64},{256,384},{320,448},{384,256},{4... | collective-permute-start | bytes 393224 | tf_op jit(solution)/shard_map/ppermute | solution.py:114
  96.6 0.0 collective-permute-done.9
  96.7 0.0 copy-start.5
  96.7 5.7 %collective-permute-done.8 = bf16[2,64,512]{2,1,0:T(8,128)(2,1)S(1)} collective-permute-done((bf16[2,64,512]{2,1,0:T(8,128)(2,1)S(1)}, bf16[2,64,512]{2,1,0:T(8,128)(2,1)S(1)}, u32[]{:S(2)}, u32[]{:S(2)}) %collective-permute-start.8) | collective-permute-done | bytes 131104 | tf_op jit(solution)/shard_map/ppermute | solution.py:114
  102.4 5.5 %collective-permute-start.10 = (bf16[4,64,512]{2,1,0:T(8,128)(2,1)S(1)}, bf16[4,64,512]{2,1,0:T(8,128)(2,1)S(1)}, u32[]{:S(2)}, u32[]{:S(2)}) collective-permute-start(bf16[4,64,512]{2,1,0:T(8,128)(2,1)S(1)} %pad_maximum_fusion.6), channel_id=1, source_target_pairs={{0,64},{64,0},{128,192},{192,128},{256,320},{320,256},{384,448},{4... | collective-permute-start | bytes 786440 | tf_op jit(solution)/shard_map/ppermute | solution.py:114
  107.9 3.4 %collective-permute-start.11 = (bf16[1,4,64,512]{3,2,1,0:T(8,128)(2,1)S(1)}, bf16[1,4,64,512]{3,2,1,0:T(8,128)(2,1)S(1)}, u32[]{:S(2)}, u32[]{:S(2)}) collective-permute-start(bf16[1,4,64,512]{3,2,1,0:T(8,128)(2,1)S(1)} %maximum_bitcast_fusion.near_ref), channel_id=1, source_target_pairs={{0,16},{16,32},{32,48},{48,0},{1,17},{17,33},{33,49},{49,1},{2,18}... | collective-permute-start | bytes 786440 | tf_op jit(solution)/shard_map/ppermute | solution.py:151
  111.3 3.6 %collective-permute-start.12 = (bf16[1,4,64,512]{3,2,1,0:T(8,128)(2,1)S(1)}, bf16[1,4,64,512]{3,2,1,0:T(8,128)(2,1)S(1)}, u32[]{:S(2)}, u32[]{:S(2)}) collective-permute-start(bf16[1,4,64,512]{3,2,1,0:T(8,128)(2,1)S(1)} %maximum_bitcast_fusion.near_ref), channel_id=1, source_target_pairs={{0,48},{16,0},{32,16},{48,32},{1,49},{17,1},{33,17},{49,33},{2,50}... | collective-permute-start | bytes 786440 | tf_op jit(solution)/shard_map/ppermute | solution.py:151
  114.9 0.0 collective-permute-done.10
  115.0 2.3 %collective-permute-done.11.near_ref = bf16[1,4,64,512]{3,2,1,0:T(8,128)(2,1)S(1)} collective-permute-done((bf16[1,4,64,512]{3,2,1,0:T(8,128)(2,1)S(1)}, bf16[1,4,64,512]{3,2,1,0:T(8,128)(2,1)S(1)}, u32[]{:S(2)}, u32[]{:S(2)}) %collective-permute-start.11) | collective-permute-done | bytes 262176 | tf_op jit(solution)/shard_map/ppermute | solution.py:151
  117.3 2.2 %collective-permute-done.12.near_ref = bf16[1,4,64,512]{3,2,1,0:T(8,128)(2,1)S(1)} collective-permute-done((bf16[1,4,64,512]{3,2,1,0:T(8,128)(2,1)S(1)}, bf16[1,4,64,512]{3,2,1,0:T(8,128)(2,1)S(1)}, u32[]{:S(2)}, u32[]{:S(2)}) %collective-permute-start.12) | collective-permute-done | bytes 262176 | tf_op jit(solution)/shard_map/ppermute | solution.py:151
  119.6 3.4 %collective-permute-start.13 = (bf16[8,64,512]{2,1,0:T(8,128)(2,1)S(1)}, bf16[8,64,512]{2,1,0:T(8,128)(2,1)S(1)}, u32[]{:S(2)}, u32[]{:S(2)}) collective-permute-start(bf16[8,64,512]{2,1,0:T(8,128)(2,1)S(1)} %pad_maximum_fusion.3.first_ref), channel_id=1, source_target_pairs={{0,16},{16,32},{32,48},{48,0},{1,17},{17,33},{33,49},{49,1},{2,18}... | collective-permute-start | bytes 1572872 | tf_op jit(solution)/shard_map/ppermute | solution.py:154
  123.0 1.9 %collective-permute-start.17 = (bf16[1,4,64,512]{3,2,1,0:T(8,128)(2,1)S(1)}, bf16[1,4,64,512]{3,2,1,0:T(8,128)(2,1)S(1)}, u32[]{:S(2)}, u32[]{:S(2)}) collective-permute-start(bf16[1,4,64,512]{3,2,1,0:T(8,128)(2,1)S(1)} %maximum_bitcast_fusion.near_ref), channel_id=1, source_target_pairs={{0,64},{64,0},{128,192},{192,128},{256,320},{320,256},{384,448},{4... | collective-permute-start | bytes 786440 | tf_op jit(solution)/shard_map/ppermute | solution.py:114
  124.9 0.9 pad_maximum_fusion.4
  125.7 7.9 %collective-permute-done.17.other_ref = bf16[1,4,64,512]{3,2,1,0:T(8,128)(2,1)S(1)} collective-permute-done((bf16[1,4,64,512]{3,2,1,0:T(8,128)(2,1)S(1)}, bf16[1,4,64,512]{3,2,1,0:T(8,128)(2,1)S(1)}, u32[]{:S(2)}, u32[]{:S(2)}) %collective-permute-start.17) | collective-permute-done | bytes 262176 | tf_op jit(solution)/shard_map/ppermute | solution.py:114
  133.7 0.7 copy-done.3
  134.4 1.9 %collective-permute-start.18 = (bf16[2,4,64,512]{3,2,1,0:T(8,128)(2,1)}, bf16[2,4,64,512]{3,2,1,0:T(8,128)(2,1)S(1)}, u32[]{:S(2)}, u32[]{:S(2)}) collective-permute-start(bf16[2,4,64,512]{3,2,1,0:T(8,128)(2,1)} %pad_maximum_fusion.4), channel_id=1, source_target_pairs={{0,64},{64,0},{128,192},{192,128},{256,320},{320,256},{384,448},{4... | collective-permute-start | bytes 1572872 | tf_op jit(solution)/shard_map/ppermute | solution.py:114
  136.3 3.7 %collective-permute-start.19 = (bf16[8,64,512]{2,1,0:T(8,128)(2,1)S(1)}, bf16[8,64,512]{2,1,0:T(8,128)(2,1)S(1)}, u32[]{:S(2)}, u32[]{:S(2)}) collective-permute-start(bf16[8,64,512]{2,1,0:T(8,128)(2,1)S(1)} %pad_maximum_fusion.3.first_ref), channel_id=1, source_target_pairs={{0,48},{16,0},{32,16},{48,32},{1,49},{17,1},{33,17},{49,33},{2,50}... | collective-permute-start | bytes 1572872 | tf_op jit(solution)/shard_map/ppermute | solution.py:154
  140.0 3.7 %collective-permute-start.15 = (bf16[1,4,64,512]{3,2,1,0:T(8,128)(2,1)S(1)}, bf16[1,4,64,512]{3,2,1,0:T(8,128)(2,1)}, u32[]{:S(2)}, u32[]{:S(2)}) collective-permute-start(bf16[1,4,64,512]{3,2,1,0:T(8,128)(2,1)S(1)} %collective-permute-done.12.near_ref), channel_id=1, source_target_pairs={{0,48},{16,0},{32,16},{48,32},{1,49},{17,1},{33,17},{49,33},{2,50}... | collective-permute-start | bytes 786440 | tf_op jit(solution)/shard_map/ppermute | solution.py:152
  143.7 0.0 collective-permute-done.13.first_ref
  143.7 2.1 %collective-permute-start.14 = (bf16[8,64,512]{2,1,0:T(8,128)(2,1)S(1)}, bf16[8,64,512]{2,1,0:T(8,128)(2,1)S(1)}, u32[]{:S(2)}, u32[]{:S(2)}) collective-permute-start(bf16[8,64,512]{2,1,0:T(8,128)(2,1)S(1)} %collective-permute-done.13.first_ref), channel_id=1, source_target_pairs={{0,16},{16,32},{32,48},{48,0},{1,17},{17,33},{33,49},{49,1},{2,18}... | collective-permute-start | bytes 1572872 | tf_op jit(solution)/shard_map/ppermute | solution.py:155
  145.9 4.4 %collective-permute-done.15.near_ref = bf16[1,4,64,512]{3,2,1,0:T(8,128)(2,1)} collective-permute-done((bf16[1,4,64,512]{3,2,1,0:T(8,128)(2,1)S(1)}, bf16[1,4,64,512]{3,2,1,0:T(8,128)(2,1)}, u32[]{:S(2)}, u32[]{:S(2)}) %collective-permute-start.15) | collective-permute-done | bytes 262176 | tf_op jit(solution)/shard_map/ppermute | solution.py:152
  150.3 3.9 %collective-permute-start.16 = (bf16[1,4,64,512]{3,2,1,0:T(8,128)(2,1)}, bf16[1,4,64,512]{3,2,1,0:T(8,128)(2,1)}, u32[]{:S(2)}, u32[]{:S(2)}) collective-permute-start(bf16[1,4,64,512]{3,2,1,0:T(8,128)(2,1)} %collective-permute-done.15.near_ref), channel_id=1, source_target_pairs={{0,64},{64,0},{128,192},{192,128},{256,320},{320,256},{384,448},{4... | collective-permute-start | bytes 786440 | tf_op jit(solution)/shard_map/ppermute | solution.py:114
  154.2 0.0 all-gather.6.cloned.1.call-done
  154.3 2.2 %copy-done = bf16[4096,512]{1,0:T(8,128)(2,1)S(1)} copy-done((bf16[4096,512]{1,0:T(8,128)(2,1)S(1)}, bf16[4096,512]{1,0:T(8,128)(2,1)}, u32[]{:S(2)}) %copy-start) | copy-done | bytes 4194328
  156.5 0.9 copy-done.4
  157.4 3.8 %score_columns.4.refs_0_ = f32[512,512]{1,0:T(8,128)} custom-call(s32[8]{0:T(128)S(1)} %broadcast_xor_fusion.slots, s32[1]{0:T(128)} %bitcast.12.place, bf16[8,512,512]{2,1,0:T(8,128)(2,1)S(1)} %bitcast.19, f32[1,512]{1,0:T(1,128)S(1)} %bitcast.28, bf16[8,64,512]{2,1,0:T(8,128)(2,1)S(1)} %pad_maximum_fusion.3.first_ref, ...), custom_call_target="tpu_custom_call" | custom-call | flops 536870912 | bytes 5242880 | tf_op jit(solution)/shard_map/score_columns/pallas_call | solution.py:90
  161.2 0.0 collective-permute-done.18.other_ref
  161.2 0.0 collective-permute-done.19.first_ref
  161.2 3.8 %score_columns.5.refs_0_ = f32[512,512]{1,0:T(8,128)} custom-call(s32[8]{0:T(128)S(1)} %broadcast_xor_fusion.slots, s32[1]{0:T(128)} %bitcast.11.place, bf16[8,512,512]{2,1,0:T(8,128)(2,1)S(1)} %bitcast.20, f32[1,512]{1,0:T(1,128)S(1)} %bitcast.29, bf16[8,64,512]{2,1,0:T(8,128)(2,1)S(1)} %collective-permute-done.19.first_ref, ...), custom_call_target="tpu_custom_call", output_to_operand_aliasing={{}: (7, {})} | custom-call | flops 536870912 | bytes 5242880 | tf_op jit(solution)/shard_map/score_columns/pallas_call | solution.py:90
  165.1 3.8 %score_columns.6.refs_0_ = f32[512,512]{1,0:T(8,128)} custom-call(s32[8]{0:T(128)S(1)} %broadcast_xor_fusion.slots, s32[1]{0:T(128)} %bitcast.10.place, bf16[8,512,512]{2,1,0:T(8,128)(2,1)S(1)} %bitcast.21, f32[1,512]{1,0:T(1,128)S(1)} %bitcast.30, bf16[8,64,512]{2,1,0:T(8,128)(2,1)S(1)} %collective-permute-done.13.first_ref, ...), custom_call_target="tpu_custom_call", output_to_operand_aliasing={{}: (7, {})} | custom-call | flops 536870912 | bytes 5242880 | tf_op jit(solution)/shard_map/score_columns/pallas_call | solution.py:90
  168.9 4.8 %score_columns.7 = f32[512,512]{1,0:T(8,128)} custom-call(s32[8]{0:T(128)S(1)} %broadcast_xor_fusion.slots, s32[1]{0:T(128)} %bitcast.place, bf16[8,512,512]{2,1,0:T(8,128)(2,1)S(1)} %bitcast.22, f32[1,512]{1,0:T(1,128)S(1)} %bitcast.31, bf16[8,64,512]{2,1,0:T(8,128)(2,1)S(1)} %collective-permute-done.14.first_ref, ...), custom_call_target="tpu_custom_call", output_to_operand_aliasing={{}: (7, {})} | custom-call | flops 536870912 | bytes 5242880 | tf_op jit(solution)/shard_map/score_columns/pallas_call | solution.py:90
  (28 shorter events, 0.4 us)
Async XLA Ops:
  6.5 58.4 %all-gather.4.cloned.1.call-start = ((), (), s32[]{:S(2)}) async-start(), calls=%async_computation.1 | async-start | bytes 4718592 | tf_op jit(solution)/shard_map/all_gather | solution.py:137
  24.5 129.8 %all-gather.6.cloned.1.call-start = ((), (), s32[]{:S(2)}) async-start(), calls=%async_computation.2 | async-start | bytes 4718592 | tf_op jit(solution)/shard_map/all_gather | solution.py:138
  25.2 34.9 %copy-start.6 = (s32[8]{0:T(128)S(1)}, s32[8]{0:T(128)}, u32[]{:S(2)}) copy-start(s32[8]{0:T(128)} %constant.30.clone) | copy-start | bytes 100
  25.5 11.4 %collective-permute-start.1 = (bf16[1,64,512]{2,1,0:T(8,128)(2,1)S(1)}, bf16[1,64,512]{2,1,0:T(8,128)(2,1)S(1)}, u32[]{:S(2)}, u32[]{:S(2)}) collective-permute-start(bf16[1,64,512]{2,1,0:T(8,128)(2,1)S(1)} %squeeze.7), channel_id=1, source_target_pairs={{0,256},{64,320},{128,384},{192,448},{256,0},{320,64},{384,128},{4... | collective-permute-start | bytes 196616 | tf_op jit(solution)/shard_map/ppermute | solution.py:114
  34.7 11.7 %collective-permute-start = (bf16[1,64,512]{2,1,0:T(8,128)(2,1)S(1)}, bf16[1,64,512]{2,1,0:T(8,128)(2,1)S(1)}, u32[]{:S(2)}, u32[]{:S(2)}) collective-permute-start(bf16[1,64,512]{2,1,0:T(8,128)(2,1)S(1)} %squeeze.6), channel_id=1, source_target_pairs={{0,256},{64,320},{128,384},{192,448},{256,0},{320,64},{384,128},{4... | collective-permute-start | bytes 196616 | tf_op jit(solution)/shard_map/ppermute | solution.py:114
  36.9 13.8 %collective-permute-start.3 = (bf16[2,64,512]{2,1,0:T(8,128)(2,1)S(1)}, bf16[2,64,512]{2,1,0:T(8,128)(2,1)S(1)}, u32[]{:S(2)}, u32[]{:S(2)}) collective-permute-start(bf16[2,64,512]{2,1,0:T(8,128)(2,1)S(1)} %get-tuple-element.26), channel_id=1, source_target_pairs={{0,128},{64,192},{128,0},{192,64},{256,384},{320,448},{384,256},{4... | collective-permute-start | bytes 393224 | tf_op jit(solution)/shard_map/ppermute | solution.py:114
  46.4 10.5 %collective-permute-start.2 = (bf16[2,64,512]{2,1,0:T(8,128)(2,1)S(1)}, bf16[2,64,512]{2,1,0:T(8,128)(2,1)S(1)}, u32[]{:S(2)}, u32[]{:S(2)}) collective-permute-start(bf16[2,64,512]{2,1,0:T(8,128)(2,1)S(1)} %pad_maximum_fusion.7), channel_id=1, source_target_pairs={{0,128},{64,192},{128,0},{192,64},{256,384},{320,448},{384,256},{4... | collective-permute-start | bytes 393224 | tf_op jit(solution)/shard_map/ppermute | solution.py:114
  50.6 12.4 %collective-permute-start.5 = (bf16[4,64,512]{2,1,0:T(8,128)(2,1)S(1)}, bf16[4,64,512]{2,1,0:T(8,128)(2,1)S(1)}, u32[]{:S(2)}, u32[]{:S(2)}) collective-permute-start(bf16[4,64,512]{2,1,0:T(8,128)(2,1)S(1)} %constant_dynamic-update-slice_fusion.2), channel_id=1, source_target_pairs={{0,64},{64,0},{128,192},{192,128},{256,320},{320,256},{384,448},{4... | collective-permute-start | bytes 786440 | tf_op jit(solution)/shard_map/ppermute | solution.py:114
  57.0 20.7 %collective-permute-start.4 = (bf16[4,64,512]{2,1,0:T(8,128)(2,1)S(1)}, bf16[4,64,512]{2,1,0:T(8,128)(2,1)S(1)}, u32[]{:S(2)}, u32[]{:S(2)}) collective-permute-start(bf16[4,64,512]{2,1,0:T(8,128)(2,1)S(1)} %pad_maximum_fusion.5), channel_id=1, source_target_pairs={{0,64},{64,0},{128,192},{192,128},{256,320},{320,256},{384,448},{4... | collective-permute-start | bytes 786440 | tf_op jit(solution)/shard_map/ppermute | solution.py:114
  64.9 2.2 %copy-start.2 = (bf16[8,512,512]{2,1,0:T(8,128)(2,1)S(1)}, bf16[8,512,512]{2,1,0:T(8,128)(2,1)}, u32[]{:S(2)}) copy-start(bf16[8,512,512]{2,1,0:T(8,128)(2,1)} %all-gather.4.cloned.1.call-done.gram_ref) | copy-start | bytes 12582916
  70.0 14.4 %collective-permute-start.7 = (bf16[1,64,512]{2,1,0:T(8,128)(2,1)S(1)}, bf16[1,64,512]{2,1,0:T(8,128)(2,1)S(1)}, u32[]{:S(2)}, u32[]{:S(2)}) collective-permute-start(bf16[1,64,512]{2,1,0:T(8,128)(2,1)S(1)} %bitcast.23), channel_id=1, source_target_pairs={{0,256},{64,320},{128,384},{192,448},{256,0},{320,64},{384,128},{4... | collective-permute-start | bytes 196616 | tf_op jit(solution)/shard_map/ppermute | solution.py:114
  80.6 14.0 %collective-permute-start.6 = (bf16[1,64,512]{2,1,0:T(8,128)(2,1)S(1)}, bf16[1,64,512]{2,1,0:T(8,128)(2,1)S(1)}, u32[]{:S(2)}, u32[]{:S(2)}) collective-permute-start(bf16[1,64,512]{2,1,0:T(8,128)(2,1)S(1)} %bitcast.26), channel_id=1, source_target_pairs={{0,256},{64,320},{128,384},{192,448},{256,0},{320,64},{384,128},{4... | collective-permute-start | bytes 196616 | tf_op jit(solution)/shard_map/ppermute | solution.py:114
  84.4 12.2 %collective-permute-start.9 = (bf16[2,64,512]{2,1,0:T(8,128)(2,1)S(1)}, bf16[2,64,512]{2,1,0:T(8,128)(2,1)S(1)}, u32[]{:S(2)}, u32[]{:S(2)}) collective-permute-start(bf16[2,64,512]{2,1,0:T(8,128)(2,1)S(1)} %pad_maximum_fusion.9), channel_id=1, source_target_pairs={{0,128},{64,192},{128,0},{192,64},{256,384},{320,448},{384,256},{4... | collective-permute-start | bytes 393224 | tf_op jit(solution)/shard_map/ppermute | solution.py:114
  94.6 7.8 %collective-permute-start.8 = (bf16[2,64,512]{2,1,0:T(8,128)(2,1)S(1)}, bf16[2,64,512]{2,1,0:T(8,128)(2,1)S(1)}, u32[]{:S(2)}, u32[]{:S(2)}) collective-permute-start(bf16[2,64,512]{2,1,0:T(8,128)(2,1)S(1)} %pad_maximum_fusion.8), channel_id=1, source_target_pairs={{0,128},{64,192},{128,0},{192,64},{256,384},{320,448},{384,256},{4... | collective-permute-start | bytes 393224 | tf_op jit(solution)/shard_map/ppermute | solution.py:114
  96.7 57.6 %copy-start.5 = (f32[512]{0:T(512)S(1)}, f32[512]{0:T(512)}, u32[]{:S(2)}) copy-start(f32[512]{0:T(512)} %param.8) | copy-start | bytes 6148
  102.4 12.6 %collective-permute-start.10 = (bf16[4,64,512]{2,1,0:T(8,128)(2,1)S(1)}, bf16[4,64,512]{2,1,0:T(8,128)(2,1)S(1)}, u32[]{:S(2)}, u32[]{:S(2)}) collective-permute-start(bf16[4,64,512]{2,1,0:T(8,128)(2,1)S(1)} %pad_maximum_fusion.6), channel_id=1, source_target_pairs={{0,64},{64,0},{128,192},{192,128},{256,320},{320,256},{384,448},{4... | collective-permute-start | bytes 786440 | tf_op jit(solution)/shard_map/ppermute | solution.py:114
  107.9 9.5 %collective-permute-start.11 = (bf16[1,4,64,512]{3,2,1,0:T(8,128)(2,1)S(1)}, bf16[1,4,64,512]{3,2,1,0:T(8,128)(2,1)S(1)}, u32[]{:S(2)}, u32[]{:S(2)}) collective-permute-start(bf16[1,4,64,512]{3,2,1,0:T(8,128)(2,1)S(1)} %maximum_bitcast_fusion.near_ref), channel_id=1, source_target_pairs={{0,16},{16,32},{32,48},{48,0},{1,17},{17,33},{33,49},{49,1},{2,18}... | collective-permute-start | bytes 786440 | tf_op jit(solution)/shard_map/ppermute | solution.py:151
  111.3 8.3 %collective-permute-start.12 = (bf16[1,4,64,512]{3,2,1,0:T(8,128)(2,1)S(1)}, bf16[1,4,64,512]{3,2,1,0:T(8,128)(2,1)S(1)}, u32[]{:S(2)}, u32[]{:S(2)}) collective-permute-start(bf16[1,4,64,512]{3,2,1,0:T(8,128)(2,1)S(1)} %maximum_bitcast_fusion.near_ref), channel_id=1, source_target_pairs={{0,48},{16,0},{32,16},{48,32},{1,49},{17,1},{33,17},{49,33},{2,50}... | collective-permute-start | bytes 786440 | tf_op jit(solution)/shard_map/ppermute | solution.py:151
  119.6 24.1 %collective-permute-start.13 = (bf16[8,64,512]{2,1,0:T(8,128)(2,1)S(1)}, bf16[8,64,512]{2,1,0:T(8,128)(2,1)S(1)}, u32[]{:S(2)}, u32[]{:S(2)}) collective-permute-start(bf16[8,64,512]{2,1,0:T(8,128)(2,1)S(1)} %pad_maximum_fusion.3.first_ref), channel_id=1, source_target_pairs={{0,16},{16,32},{32,48},{48,0},{1,17},{17,33},{33,49},{49,1},{2,18}... | collective-permute-start | bytes 1572872 | tf_op jit(solution)/shard_map/ppermute | solution.py:154
  123.0 10.7 %collective-permute-start.17 = (bf16[1,4,64,512]{3,2,1,0:T(8,128)(2,1)S(1)}, bf16[1,4,64,512]{3,2,1,0:T(8,128)(2,1)S(1)}, u32[]{:S(2)}, u32[]{:S(2)}) collective-permute-start(bf16[1,4,64,512]{3,2,1,0:T(8,128)(2,1)S(1)} %maximum_bitcast_fusion.near_ref), channel_id=1, source_target_pairs={{0,64},{64,0},{128,192},{192,128},{256,320},{320,256},{384,448},{4... | collective-permute-start | bytes 786440 | tf_op jit(solution)/shard_map/ppermute | solution.py:114
  133.7 0.7 copy-start.3
  134.4 26.8 %collective-permute-start.18 = (bf16[2,4,64,512]{3,2,1,0:T(8,128)(2,1)}, bf16[2,4,64,512]{3,2,1,0:T(8,128)(2,1)S(1)}, u32[]{:S(2)}, u32[]{:S(2)}) collective-permute-start(bf16[2,4,64,512]{3,2,1,0:T(8,128)(2,1)} %pad_maximum_fusion.4), channel_id=1, source_target_pairs={{0,64},{64,0},{128,192},{192,128},{256,320},{320,256},{384,448},{4... | collective-permute-start | bytes 1572872 | tf_op jit(solution)/shard_map/ppermute | solution.py:114
  136.3 24.9 %collective-permute-start.19 = (bf16[8,64,512]{2,1,0:T(8,128)(2,1)S(1)}, bf16[8,64,512]{2,1,0:T(8,128)(2,1)S(1)}, u32[]{:S(2)}, u32[]{:S(2)}) collective-permute-start(bf16[8,64,512]{2,1,0:T(8,128)(2,1)S(1)} %pad_maximum_fusion.3.first_ref), channel_id=1, source_target_pairs={{0,48},{16,0},{32,16},{48,32},{1,49},{17,1},{33,17},{49,33},{2,50}... | collective-permute-start | bytes 1572872 | tf_op jit(solution)/shard_map/ppermute | solution.py:154
  140.0 10.3 %collective-permute-start.15 = (bf16[1,4,64,512]{3,2,1,0:T(8,128)(2,1)S(1)}, bf16[1,4,64,512]{3,2,1,0:T(8,128)(2,1)}, u32[]{:S(2)}, u32[]{:S(2)}) collective-permute-start(bf16[1,4,64,512]{3,2,1,0:T(8,128)(2,1)S(1)} %collective-permute-done.12.near_ref), channel_id=1, source_target_pairs={{0,48},{16,0},{32,16},{48,32},{1,49},{17,1},{33,17},{49,33},{2,50}... | collective-permute-start | bytes 786440 | tf_op jit(solution)/shard_map/ppermute | solution.py:152
  143.7 25.1 %collective-permute-start.14 = (bf16[8,64,512]{2,1,0:T(8,128)(2,1)S(1)}, bf16[8,64,512]{2,1,0:T(8,128)(2,1)S(1)}, u32[]{:S(2)}, u32[]{:S(2)}) collective-permute-start(bf16[8,64,512]{2,1,0:T(8,128)(2,1)S(1)} %collective-permute-done.13.first_ref), channel_id=1, source_target_pairs={{0,16},{16,32},{32,48},{48,0},{1,17},{17,33},{33,49},{49,1},{2,18}... | collective-permute-start | bytes 1572872 | tf_op jit(solution)/shard_map/ppermute | solution.py:155
  150.3 18.6 %collective-permute-start.16 = (bf16[1,4,64,512]{3,2,1,0:T(8,128)(2,1)}, bf16[1,4,64,512]{3,2,1,0:T(8,128)(2,1)}, u32[]{:S(2)}, u32[]{:S(2)}) collective-permute-start(bf16[1,4,64,512]{3,2,1,0:T(8,128)(2,1)} %collective-permute-done.15.near_ref), channel_id=1, source_target_pairs={{0,64},{64,0},{128,192},{192,128},{256,320},{320,256},{384,448},{4... | collective-permute-start | bytes 786440 | tf_op jit(solution)/shard_map/ppermute | solution.py:114
  154.3 2.2 %copy-start = (bf16[4096,512]{1,0:T(8,128)(2,1)S(1)}, bf16[4096,512]{1,0:T(8,128)(2,1)}, u32[]{:S(2)}) copy-start(bf16[4096,512]{1,0:T(8,128)(2,1)} %all-gather.6.cloned.1.call-done) | copy-start | bytes 12582916
  156.5 0.9 copy-start.4
  157.4 3.8 %copy-start.1 = (bf16[4096,512]{1,0:T(8,128)(2,1)S(1)}, bf16[4096,512]{1,0:T(8,128)(2,1)}, u32[]{:S(2)}) copy-start(bf16[4096,512]{1,0:T(8,128)(2,1)} %all-gather.6.cloned.1.call-done) | copy-start | bytes 12582916
Sparse Core Ops, SparseCore 0:
  24.6 40.2 all-gather.3
  67.1 39.7 all-gather.5

commit v10 on v8

--- a/solution.py
+++ b/solution.py
@@ -13,42 +13,46 @@
 DOWN = [(i, (i - 1) % NY) for i in range(NY)]
 
 
-def kernel_matrix(slots, inverse_gram, training):
-    n, t, depth = training.shape
-    rows = inverse_gram.shape[1]
+def kernel_matrix(slots, gram, chunks):
+    n, t, depth = chunks[0].shape
+    rows = gram.shape[1]
+    count = len(chunks)
 
-    def kernel(slots, gram_ref, training_ref, out_ref, total):
+    def kernel(slots, gram_ref, *refs):
+        chunk_refs, out_refs, total = refs[:count], refs[count:-1], refs[-1]
         step = pl.program_id(0)
 
         @pl.when(step == 0)
         def _():
             total[...] = jnp.zeros_like(total)
 
-        total[...] += lax.dot_general(training_ref[0], gram_ref[0], NT_DIMS, preferred_element_type=jnp.float32)
+        both = jnp.concatenate([ref[0] for ref in chunk_refs], axis=0)
+        total[...] += lax.dot_general(both, gram_ref[0], NT_DIMS, preferred_element_type=jnp.float32)
 
         @pl.when(step == n - 1)
         def _():
-            out_ref[...] = total[...].astype(out_ref.dtype)
+            for c, out_ref in enumerate(out_refs):
+                out_ref[...] = total[c * t : (c + 1) * t].astype(out_ref.dtype)
 
     return pl.pallas_call(
         kernel,
-        out_shape=jax.ShapeDtypeStruct((t, rows), jnp.bfloat16),
+        out_shape=[jax.ShapeDtypeStruct((t, rows), jnp.bfloat16)] * count,
         grid_spec=pltpu.PrefetchScalarGridSpec(
             num_scalar_prefetch=1,
             grid=(n,),
-            in_specs=[
-                pl.BlockSpec((1, rows, depth), lambda s, slots: (slots[s], 0, 0)),
-                pl.BlockSpec((1, t, depth), lambda s, slots: (s, 0, 0)),
-            ],
-            out_specs=pl.BlockSpec((t, rows), lambda s, slots: (0, 0)),
-            scratch_shapes=[pltpu.VMEM((t, rows), jnp.float32)],
+            in_specs=[pl.BlockSpec((1, rows, depth), lambda s, slots: (slots[s], 0, 0))]
+            + [pl.BlockSpec((1, t, depth), lambda s, slots: (s, 0, 0))] * count,
+            out_specs=[pl.BlockSpec((t, rows), lambda s, slots: (0, 0))] * count,
+            scratch_shapes=[pltpu.VMEM((count * t, rows), jnp.float32)],
         ),
         compiler_params=pltpu.CompilerParams(vmem_limit_bytes=VMEM_LIMIT),
         cost_estimate=pl.CostEstimate(
-            flops=2 * n * rows * t * depth, bytes_accessed=2 * n * depth * (rows + t), transcendentals=0
+            flops=2 * n * rows * count * t * depth,
+            bytes_accessed=2 * n * depth * (rows + count * t),
+            transcendentals=0,
         ),
         name="kernel_matrix",
-    )(slots, inverse_gram, training)
+    )(slots, gram, *chunks)
 
 
 def score_columns(slots, place, query, chunks, weight, out):
@@ -133,7 +137,7 @@
     a, b = training[0], training[1]
     for distance in (4, 2, 1):
         a, b = exchange(a, distance), exchange(b, distance)
-    a, b = kernel_matrix(slots, gram, a)[None], kernel_matrix(slots, gram, b)[None]
+    a, b = (block[None] for block in kernel_matrix(slots, gram, (a, b)))
     for distance in (4, 2, 1):
         a, b = exchange(a, distance), exchange(b, distance)
 

time: 164 us -> 167 us (1.018)
  starting transfers between devices: 79.5 us -> 83.9 us
  Pallas kernels: 22.9 us -> 20.3 us
  waiting for transfers between devices: 22.6 us -> 25.1 us
    ppermute x12, starting transfers between devices: 58.3 us -> 66 us  [exchange(): other = lax.ppermute(held, 'z', [(i, i ^ distance) for i in range(NZ)])]
    pallas_call x2 -> x1, Pallas kernels: 5.76 us -> 3.15 us  [kernel_matrix(): pl.pallas_call(kernel, out_shape=[jax.ShapeDtypeStruct((t, rows), jnp.bfl...]
    ppermute x2, waiting for transfers between devices: 0.09 us -> 2.3 us  [local(): below_a, above_a = (lax.ppermute(a, 'y', UP), lax.ppermute(a, 'y', DOWN))]
    all_gather x1, waiting for transfers between devices: 1.8 us -> 0.02 us  [local(): gram = lax.all_gather(gram_rows, ('x', 'core'), axis=0)]
    ppermute x2, starting transfers between devices: 7.5 us -> 5.75 us  [local(): far = (lax.ppermute(below_a, 'y', UP), lax.ppermute(above_b, 'y', DOWN))]
  transfers between devices with their start and end apart: 20 -> 20, of which waited for: 11 -> 11; matrix products, arithmetic and copies ran while one was open for 0% -> 0% of each run, Pallas kernels for 12% -> 10%
where the time goes in v10:
time: 167 us; the launch traced here: 166 us
  starting transfers between devices  83.9 us (50%)
  waiting for transfers between devices  25.1 us (15%)
  Pallas kernels  20.3 us (12%)
  blocking collectives  15.1 us (9%)
  between operations  13.8 us (8%)
  local copies, waits for them, and re-layouts  7.39 us (4%)
    ppermute x12, starting transfers between devices, exchange(): other = lax.ppermute(held, 'z', [(i, i ^ distance) for i in range(NZ)])  66 us
    pallas_call x4, Pallas kernels, score_columns(): pl.pallas_call(kernel, out_shape=jax.ShapeDtypeStruct((rows, columns), jn...  17.2 us
    ppermute x12, waiting for transfers between devices, exchange(): other = lax.ppermute(held, 'z', [(i, i ^ distance) for i in range(NZ)])  15.9 us
    all_to_all x1, blocking collectives, local(): got = lax.all_to_all(sent, 'y', split_axis=0, concat_axis=0, tiled=True)  15.1 us
    ppermute x2, starting transfers between devices, local(): below_a, above_a = (lax.ppermute(a, 'y', UP), lax.ppermute(a, 'y', DOWN))  7.05 us
    ppermute x2, starting transfers between devices, local(): far = (lax.ppermute(below_a, 'y', UP), lax.ppermute(above_b, 'y', DOWN))  5.75 us
    ppermute x2, starting transfers between devices, local(): below_b, above_b = (lax.ppermute(b, 'y', UP), lax.ppermute(b, 'y', DOWN))  5 us
    unnamed x10, local copies, waits for them, and re-layouts  4.38 us
  transfers between devices with their start and end apart: 20, of which 11 were waited for; matrix products, arithmetic and copies ran while one was open for 0% of the time, Pallas kernels for 10%

profile of v10, /device:TPU:6, one launch (start us, length us, event | category | flops | bytes accessed | tf_op | source)
XLA Modules:
  0.0 166.1 jit_solution(11820793270431993661)
XLA Ops:
  6.5 0.9 copy.18
  7.5 0.9 broadcast_in_dim.26
  8.5 15.1 %all_to_all.5 = bf16[4,160,512]{2,1,0:T(8,128)(2,1)S(1)} all-to-all(bf16[4,160,512]{2,1,0:T(8,128)(2,1)S(1)} %pad_maximum_fusion), channel_id=1, replica_groups=mesh['z'=8,'y'=4,'x'=4,'core'=2,'row'=2] {'y'}, dimensions={0} | all-to-all | bytes 1310720 | tf_op jit(solution)/shard_map/all_to_all | solution.py:128
  23.6 0.8 slice.18
  24.4 0.0 all-gather.4.cloned.1.call-update
  24.5 0.0 all-gather.6.cloned.1.call-start
  24.5 0.7 all-gather.6.cloned.1.call-update
  25.2 0.0 copy-start.4
  25.3 0.1 fusion
  25.4 0.1 copy.15
  25.5 9.1 %collective-permute-start.3 = (bf16[1,64,512]{2,1,0:T(8,128)(2,1)S(1)}, bf16[1,64,512]{2,1,0:T(8,128)(2,1)S(1)}, u32[]{:S(2)}, u32[]{:S(2)}) collective-permute-start(bf16[1,64,512]{2,1,0:T(8,128)(2,1)S(1)} %squeeze.7), channel_id=1, source_target_pairs={{0,256},{64,320},{128,384},{192,448},{256,0},{320,64},{384,128},{4... | collective-permute-start | bytes 196616 | tf_op jit(solution)/shard_map/ppermute | solution.py:113
  34.6 0.1 copy.14
  34.7 1.9 %collective-permute-start = (bf16[1,64,512]{2,1,0:T(8,128)(2,1)S(1)}, bf16[1,64,512]{2,1,0:T(8,128)(2,1)S(1)}, u32[]{:S(2)}, u32[]{:S(2)}) collective-permute-start(bf16[1,64,512]{2,1,0:T(8,128)(2,1)S(1)} %squeeze.6), channel_id=1, source_target_pairs={{0,256},{64,320},{128,384},{192,448},{256,0},{320,64},{384,128},{4... | collective-permute-start | bytes 196616 | tf_op jit(solution)/shard_map/ppermute | solution.py:113
  36.6 0.2 collective-permute-done.3
  36.9 8.5 %collective-permute-start.4 = (bf16[2,64,512]{2,1,0:T(8,128)(2,1)S(1)}, bf16[2,64,512]{2,1,0:T(8,128)(2,1)S(1)}, u32[]{:S(2)}, u32[]{:S(2)}) collective-permute-start(bf16[2,64,512]{2,1,0:T(8,128)(2,1)S(1)} %pad_maximum_fusion.10), channel_id=1, source_target_pairs={{0,128},{64,192},{128,0},{192,64},{256,384},{320,448},{384,256},{4... | collective-permute-start | bytes 393224 | tf_op jit(solution)/shard_map/ppermute | solution.py:113
  45.4 1.0 collective-permute-done
  46.4 4.2 %collective-permute-start.1 = (bf16[2,64,512]{2,1,0:T(8,128)(2,1)S(1)}, bf16[2,64,512]{2,1,0:T(8,128)(2,1)S(1)}, u32[]{:S(2)}, u32[]{:S(2)}) collective-permute-start(bf16[2,64,512]{2,1,0:T(8,128)(2,1)S(1)} %pad_maximum_fusion.9), channel_id=1, source_target_pairs={{0,128},{64,192},{128,0},{192,64},{256,384},{320,448},{384,256},{4... | collective-permute-start | bytes 393224 | tf_op jit(solution)/shard_map/ppermute | solution.py:113
  50.6 0.0 collective-permute-done.4
  50.7 6.3 %collective-permute-start.5 = (bf16[4,64,512]{2,1,0:T(8,128)(2,1)S(1)}, bf16[4,64,512]{2,1,0:T(8,128)(2,1)S(1)}, u32[]{:S(2)}, u32[]{:S(2)}) collective-permute-start(bf16[4,64,512]{2,1,0:T(8,128)(2,1)S(1)} %pad_maximum_fusion.6), channel_id=1, source_target_pairs={{0,64},{64,0},{128,192},{192,128},{256,320},{320,256},{384,448},{4... | collective-permute-start | bytes 786440 | tf_op jit(solution)/shard_map/ppermute | solution.py:113
  56.9 0.0 collective-permute-done.1
  57.0 3.1 %collective-permute-start.2 = (bf16[4,64,512]{2,1,0:T(8,128)(2,1)S(1)}, bf16[4,64,512]{2,1,0:T(8,128)(2,1)S(1)}, u32[]{:S(2)}, u32[]{:S(2)}) collective-permute-start(bf16[4,64,512]{2,1,0:T(8,128)(2,1)S(1)} %pad_maximum_fusion.5), channel_id=1, source_target_pairs={{0,64},{64,0},{128,192},{192,128},{256,320},{320,256},{384,448},{4... | collective-permute-start | bytes 786440 | tf_op jit(solution)/shard_map/ppermute | solution.py:113
  60.1 2.9 %collective-permute-done.5 = bf16[4,64,512]{2,1,0:T(8,128)(2,1)S(1)} collective-permute-done((bf16[4,64,512]{2,1,0:T(8,128)(2,1)S(1)}, bf16[4,64,512]{2,1,0:T(8,128)(2,1)S(1)}, u32[]{:S(2)}, u32[]{:S(2)}) %collective-permute-start.5) | collective-permute-done | bytes 262176 | tf_op jit(solution)/shard_map/ppermute | solution.py:113
  63.1 0.1 pad_maximum_fusion.2.refs_1_
  63.1 4.3 %collective-permute-done.2 = bf16[4,64,512]{2,1,0:T(8,128)(2,1)S(1)} collective-permute-done((bf16[4,64,512]{2,1,0:T(8,128)(2,1)S(1)}, bf16[4,64,512]{2,1,0:T(8,128)(2,1)S(1)}, u32[]{:S(2)}, u32[]{:S(2)}) %collective-permute-start.2) | collective-permute-done | bytes 262176 | tf_op jit(solution)/shard_map/ppermute | solution.py:113
  67.5 0.1 pad_maximum_fusion.1.refs_0_
  67.5 0.0 all-gather.4.cloned.1.call-done.gram_ref
  67.6 0.0 copy-start.2
  67.6 2.2 %copy-done.2 = bf16[8,512,512]{2,1,0:T(8,128)(2,1)S(1)} copy-done((bf16[8,512,512]{2,1,0:T(8,128)(2,1)S(1)}, bf16[8,512,512]{2,1,0:T(8,128)(2,1)}, u32[]{:S(2)}) %copy-start.2) | copy-done | bytes 4194328
  69.7 3.1 %kernel_matrix.1 = (bf16[64,512]{1,0:T(8,128)(2,1)S(1)}, bf16[64,512]{1,0:T(8,128)(2,1)S(1)}) custom-call(s32[8]{0:T(128)S(1)} %broadcast_xor_fusion.slots, bf16[8,512,512]{2,1,0:T(8,128)(2,1)S(1)} %copy-done.2, bf16[8,64,512]{2,1,0:T(8,128)(2,1)S(1)} %pad_maximum_fusion.1.refs_0_, bf16[8,64,512]{2,1,0:T(8,128)(2,1)S(1)} %pad_maximum_fusion.2.refs_1_), custom_call_target="tpu_custom_call" | custom-call | flops 536870912 | bytes 5242880 | tf_op jit(solution)/shard_map/kernel_matrix/pallas_call | solution.py:37
  72.9 8.9 %collective-permute-start.11 = (bf16[1,64,512]{2,1,0:T(8,128)(2,1)S(1)}, bf16[1,64,512]{2,1,0:T(8,128)(2,1)S(1)}, u32[]{:S(2)}, u32[]{:S(2)}) collective-permute-start(bf16[1,64,512]{2,1,0:T(8,128)(2,1)S(1)} %bitcast.25), channel_id=1, source_target_pairs={{0,256},{64,320},{128,384},{192,448},{256,0},{320,64},{384,128},{4... | collective-permute-start | bytes 196616 | tf_op jit(solution)/shard_map/ppermute | solution.py:113
  81.8 1.9 %collective-permute-start.6 = (bf16[1,64,512]{2,1,0:T(8,128)(2,1)S(1)}, bf16[1,64,512]{2,1,0:T(8,128)(2,1)S(1)}, u32[]{:S(2)}, u32[]{:S(2)}) collective-permute-start(bf16[1,64,512]{2,1,0:T(8,128)(2,1)S(1)} %bitcast.21), channel_id=1, source_target_pairs={{0,256},{64,320},{128,384},{192,448},{256,0},{320,64},{384,128},{4... | collective-permute-start | bytes 196616 | tf_op jit(solution)/shard_map/ppermute | solution.py:113
  83.7 0.5 collective-permute-done.11
  84.2 8.6 %collective-permute-start.12 = (bf16[2,64,512]{2,1,0:T(8,128)(2,1)S(1)}, bf16[2,64,512]{2,1,0:T(8,128)(2,1)S(1)}, u32[]{:S(2)}, u32[]{:S(2)}) collective-permute-start(bf16[2,64,512]{2,1,0:T(8,128)(2,1)S(1)} %pad_maximum_fusion.12), channel_id=1, source_target_pairs={{0,128},{64,192},{128,0},{192,64},{256,384},{320,448},{384,256},{4... | collective-permute-start | bytes 393224 | tf_op jit(solution)/shard_map/ppermute | solution.py:113
  92.8 0.0 collective-permute-done.6
  92.9 4.4 %collective-permute-start.7 = (bf16[2,64,512]{2,1,0:T(8,128)(2,1)S(1)}, bf16[2,64,512]{2,1,0:T(8,128)(2,1)S(1)}, u32[]{:S(2)}, u32[]{:S(2)}) collective-permute-start(bf16[2,64,512]{2,1,0:T(8,128)(2,1)S(1)} %pad_maximum_fusion.11), channel_id=1, source_target_pairs={{0,128},{64,192},{128,0},{192,64},{256,384},{320,448},{384,256},{4... | collective-permute-start | bytes 393224 | tf_op jit(solution)/shard_map/ppermute | solution.py:113
  97.3 0.0 collective-permute-done.12
  97.3 0.0 copy-start.3
  97.3 7.1 %collective-permute-start.13 = (bf16[4,64,512]{2,1,0:T(8,128)(2,1)S(1)}, bf16[4,64,512]{2,1,0:T(8,128)(2,1)S(1)}, u32[]{:S(2)}, u32[]{:S(2)}) collective-permute-start(bf16[4,64,512]{2,1,0:T(8,128)(2,1)S(1)} %pad_maximum_fusion.8), channel_id=1, source_target_pairs={{0,64},{64,0},{128,192},{192,128},{256,320},{320,256},{384,448},{4... | collective-permute-start | bytes 786440 | tf_op jit(solution)/shard_map/ppermute | solution.py:113
  104.5 0.9 collective-permute-done.7
  105.4 1.9 %collective-permute-start.8 = (bf16[4,64,512]{2,1,0:T(8,128)(2,1)S(1)}, bf16[4,64,512]{2,1,0:T(8,128)(2,1)S(1)}, u32[]{:S(2)}, u32[]{:S(2)}) collective-permute-start(bf16[4,64,512]{2,1,0:T(8,128)(2,1)S(1)} %pad_maximum_fusion.7), channel_id=1, source_target_pairs={{0,64},{64,0},{128,192},{192,128},{256,320},{320,256},{384,448},{4... | collective-permute-start | bytes 786440 | tf_op jit(solution)/shard_map/ppermute | solution.py:113
  107.3 4.3 %collective-permute-done.13 = bf16[4,64,512]{2,1,0:T(8,128)(2,1)S(1)} collective-permute-done((bf16[4,64,512]{2,1,0:T(8,128)(2,1)S(1)}, bf16[4,64,512]{2,1,0:T(8,128)(2,1)S(1)}, u32[]{:S(2)}, u32[]{:S(2)}) %collective-permute-start.13) | collective-permute-done | bytes 262176 | tf_op jit(solution)/shard_map/ppermute | solution.py:113
  111.6 0.1 pad_maximum_fusion.4.refs_1_
  111.7 3.1 %collective-permute-start.14 = (bf16[8,64,512]{2,1,0:T(8,128)(2,1)S(1)}, bf16[8,64,512]{2,1,0:T(8,128)(2,1)S(1)}, u32[]{:S(2)}, u32[]{:S(2)}) collective-permute-start(bf16[8,64,512]{2,1,0:T(8,128)(2,1)S(1)} %pad_maximum_fusion.4.refs_1_), channel_id=1, source_target_pairs={{0,48},{16,0},{32,16},{48,32},{1,49},{17,1},{33,17},{49,33},{2,50}... | collective-permute-start | bytes 1572872 | tf_op jit(solution)/shard_map/ppermute | solution.py:145
  114.8 1.8 %collective-permute-done.8 = bf16[4,64,512]{2,1,0:T(8,128)(2,1)S(1)} collective-permute-done((bf16[4,64,512]{2,1,0:T(8,128)(2,1)S(1)}, bf16[4,64,512]{2,1,0:T(8,128)(2,1)S(1)}, u32[]{:S(2)}, u32[]{:S(2)}) %collective-permute-start.8) | collective-permute-done | bytes 262176 | tf_op jit(solution)/shard_map/ppermute | solution.py:113
  116.6 0.1 pad_maximum_fusion.3.refs_0_
  116.6 2.5 %collective-permute-start.9 = (bf16[8,64,512]{2,1,0:T(8,128)(2,1)S(1)}, bf16[8,64,512]{2,1,0:T(8,128)(2,1)S(1)}, u32[]{:S(2)}, u32[]{:S(2)}) collective-permute-start(bf16[8,64,512]{2,1,0:T(8,128)(2,1)S(1)} %pad_maximum_fusion.3.refs_0_), channel_id=1, source_target_pairs={{0,16},{16,32},{32,48},{48,0},{1,17},{17,33},{33,49},{49,1},{2,18}... | collective-permute-start | bytes 1572872 | tf_op jit(solution)/shard_map/ppermute | solution.py:144
  119.1 4.6 %collective-permute-start.17 = (bf16[8,64,512]{2,1,0:T(8,128)(2,1)S(1)}, bf16[8,64,512]{2,1,0:T(8,128)(2,1)}, u32[]{:S(2)}, u32[]{:S(2)}) collective-permute-start(bf16[8,64,512]{2,1,0:T(8,128)(2,1)S(1)} %pad_maximum_fusion.3.refs_0_), channel_id=1, source_target_pairs={{0,48},{16,0},{32,16},{48,32},{1,49},{17,1},{33,17},{49,33},{2,50}... | collective-permute-start | bytes 1572872 | tf_op jit(solution)/shard_map/ppermute | solution.py:144
  123.7 1.9 %collective-permute-start.16 = (bf16[8,64,512]{2,1,0:T(8,128)(2,1)S(1)}, bf16[8,64,512]{2,1,0:T(8,128)(2,1)}, u32[]{:S(2)}, u32[]{:S(2)}) collective-permute-start(bf16[8,64,512]{2,1,0:T(8,128)(2,1)S(1)} %pad_maximum_fusion.4.refs_1_), channel_id=1, source_target_pairs={{0,16},{16,32},{32,48},{48,0},{1,17},{17,33},{33,49},{49,1},{2,18}... | collective-permute-start | bytes 1572872 | tf_op jit(solution)/shard_map/ppermute | solution.py:145
  125.6 2.8 %collective-permute-done.14.refs_1_ = bf16[8,64,512]{2,1,0:T(8,128)(2,1)S(1)} collective-permute-done((bf16[8,64,512]{2,1,0:T(8,128)(2,1)S(1)}, bf16[8,64,512]{2,1,0:T(8,128)(2,1)S(1)}, u32[]{:S(2)}, u32[]{:S(2)}) %collective-permute-start.14) | collective-permute-done | bytes 524320 | tf_op jit(solution)/shard_map/ppermute | solution.py:145
  128.4 3.8 %collective-permute-start.15 = (bf16[8,64,512]{2,1,0:T(8,128)(2,1)S(1)}, bf16[8,64,512]{2,1,0:T(8,128)(2,1)S(1)}, u32[]{:S(2)}, u32[]{:S(2)}) collective-permute-start(bf16[8,64,512]{2,1,0:T(8,128)(2,1)S(1)} %collective-permute-done.14.refs_1_), channel_id=1, source_target_pairs={{0,48},{16,0},{32,16},{48,32},{1,49},{17,1},{33,17},{49,33},{2,50}... | collective-permute-start | bytes 1572872 | tf_op jit(solution)/shard_map/ppermute | solution.py:151
  132.3 2.3 %collective-permute-done.9.refs_0_ = bf16[8,64,512]{2,1,0:T(8,128)(2,1)S(1)} collective-permute-done((bf16[8,64,512]{2,1,0:T(8,128)(2,1)S(1)}, bf16[8,64,512]{2,1,0:T(8,128)(2,1)S(1)}, u32[]{:S(2)}, u32[]{:S(2)}) %collective-permute-start.9) | collective-permute-done | bytes 524320 | tf_op jit(solution)/shard_map/ppermute | solution.py:144
  134.6 1.9 %collective-permute-start.10 = (bf16[8,64,512]{2,1,0:T(8,128)(2,1)S(1)}, bf16[8,64,512]{2,1,0:T(8,128)(2,1)S(1)}, u32[]{:S(2)}, u32[]{:S(2)}) collective-permute-start(bf16[8,64,512]{2,1,0:T(8,128)(2,1)S(1)} %collective-permute-done.9.refs_0_), channel_id=1, source_target_pairs={{0,16},{16,32},{32,48},{48,0},{1,17},{17,33},{33,49},{49,1},{2,18}... | collective-permute-start | bytes 1572872 | tf_op jit(solution)/shard_map/ppermute | solution.py:151
  136.5 0.0 all-gather.6.cloned.1.call-done
  136.5 0.0 copy-done.3
  136.6 0.0 copy-start
  136.6 2.2 %copy-done = bf16[4096,512]{1,0:T(8,128)(2,1)S(1)} copy-done((bf16[4096,512]{1,0:T(8,128)(2,1)S(1)}, bf16[4096,512]{1,0:T(8,128)(2,1)}, u32[]{:S(2)}) %copy-start) | copy-done | bytes 4194328
  138.7 3.8 %score_columns.4.refs_2_ = f32[512,512]{1,0:T(8,128)} custom-call(s32[8]{0:T(128)S(1)} %broadcast_xor_fusion.slots, s32[1]{0:T(128)} %bitcast.11.place, bf16[8,512,512]{2,1,0:T(8,128)(2,1)S(1)} %bitcast.17, f32[1,512]{1,0:T(1,128)S(1)} %bitcast.29, bf16[8,64,512]{2,1,0:T(8,128)(2,1)S(1)} %pad_maximum_fusion.3.refs_0_, ...), custom_call_target="tpu_custom_call" | custom-call | flops 536870912 | bytes 5242880 | tf_op jit(solution)/shard_map/score_columns/pallas_call | solution.py:89
  142.5 0.0 collective-permute-done.17.refs_0_
  142.5 4.8 %score_columns.5.refs_2_ = f32[512,512]{1,0:T(8,128)} custom-call(s32[8]{0:T(128)S(1)} %broadcast_xor_fusion.slots, s32[1]{0:T(128)} %bitcast.10.place, bf16[8,512,512]{2,1,0:T(8,128)(2,1)S(1)} %bitcast.18, f32[1,512]{1,0:T(1,128)S(1)} %bitcast.30, bf16[8,64,512]{2,1,0:T(8,128)(2,1)} %collective-permute-done.17.refs_0_, ...), custom_call_target="tpu_custom_call", output_to_operand_aliasing={{}: (6, {})} | custom-call | flops 536870912 | bytes 5242880 | tf_op jit(solution)/shard_map/score_columns/pallas_call | solution.py:89
  147.3 0.0 collective-permute-done.16.refs_1_
  147.3 4.8 %score_columns.6.refs_2_ = f32[512,512]{1,0:T(8,128)} custom-call(s32[8]{0:T(128)S(1)} %broadcast_xor_fusion.slots, s32[1]{0:T(128)} %bitcast.9.place, bf16[8,512,512]{2,1,0:T(8,128)(2,1)S(1)} %bitcast.19, f32[1,512]{1,0:T(1,128)S(1)} %bitcast.31, bf16[8,64,512]{2,1,0:T(8,128)(2,1)S(1)} %collective-permute-done.9.refs_0_, ...), custom_call_target="tpu_custom_call", output_to_operand_aliasing={{}: (6, {})} | custom-call | flops 536870912 | bytes 5242880 | tf_op jit(solution)/shard_map/score_columns/pallas_call | solution.py:89
  152.1 0.0 collective-permute-done.15.refs_1_
  152.1 3.3 %collective-permute-done.10.refs_0_ = bf16[8,64,512]{2,1,0:T(8,128)(2,1)S(1)} collective-permute-done((bf16[8,64,512]{2,1,0:T(8,128)(2,1)S(1)}, bf16[8,64,512]{2,1,0:T(8,128)(2,1)S(1)}, u32[]{:S(2)}, u32[]{:S(2)}) %collective-permute-start.10) | collective-permute-done | bytes 524320 | tf_op jit(solution)/shard_map/ppermute | solution.py:151
  155.5 3.8 %score_columns.7 = f32[512,512]{1,0:T(8,128)} custom-call(s32[8]{0:T(128)S(1)} %broadcast_xor_fusion.slots, s32[1]{0:T(128)} %bitcast.place, bf16[8,512,512]{2,1,0:T(8,128)(2,1)S(1)} %bitcast.20, f32[1,512]{1,0:T(1,128)S(1)} %bitcast.32, bf16[8,64,512]{2,1,0:T(8,128)(2,1)S(1)} %collective-permute-done.10.refs_0_, ...), custom_call_target="tpu_custom_call", output_to_operand_aliasing={{}: (6, {})} | custom-call | flops 536870912 | bytes 5242880 | tf_op jit(solution)/shard_map/score_columns/pallas_call | solution.py:89
  (18 shorter events, 0.3 us)
Async XLA Ops:
  6.5 61.0 %all-gather.4.cloned.1.call-start = ((), (), s32[]{:S(2)}) async-start(), calls=%async_computation.1 | async-start | bytes 4718592 | tf_op jit(solution)/shard_map/all_gather | solution.py:133
  24.5 112.1 %all-gather.6.cloned.1.call-start = ((), (), s32[]{:S(2)}) async-start(), calls=%async_computation.2 | async-start | bytes 4718592 | tf_op jit(solution)/shard_map/all_gather | solution.py:134
  25.2 34.9 %copy-start.4 = (s32[8]{0:T(128)S(1)}, s32[8]{0:T(128)}, u32[]{:S(2)}) copy-start(s32[8]{0:T(128)} %constant.30.clone) | copy-start | bytes 100
  25.5 11.4 %collective-permute-start.3 = (bf16[1,64,512]{2,1,0:T(8,128)(2,1)S(1)}, bf16[1,64,512]{2,1,0:T(8,128)(2,1)S(1)}, u32[]{:S(2)}, u32[]{:S(2)}) collective-permute-start(bf16[1,64,512]{2,1,0:T(8,128)(2,1)S(1)} %squeeze.7), channel_id=1, source_target_pairs={{0,256},{64,320},{128,384},{192,448},{256,0},{320,64},{384,128},{4... | collective-permute-start | bytes 196616 | tf_op jit(solution)/shard_map/ppermute | solution.py:113
  34.7 11.7 %collective-permute-start = (bf16[1,64,512]{2,1,0:T(8,128)(2,1)S(1)}, bf16[1,64,512]{2,1,0:T(8,128)(2,1)S(1)}, u32[]{:S(2)}, u32[]{:S(2)}) collective-permute-start(bf16[1,64,512]{2,1,0:T(8,128)(2,1)S(1)} %squeeze.6), channel_id=1, source_target_pairs={{0,256},{64,320},{128,384},{192,448},{256,0},{320,64},{384,128},{4... | collective-permute-start | bytes 196616 | tf_op jit(solution)/shard_map/ppermute | solution.py:113
  36.9 13.7 %collective-permute-start.4 = (bf16[2,64,512]{2,1,0:T(8,128)(2,1)S(1)}, bf16[2,64,512]{2,1,0:T(8,128)(2,1)S(1)}, u32[]{:S(2)}, u32[]{:S(2)}) collective-permute-start(bf16[2,64,512]{2,1,0:T(8,128)(2,1)S(1)} %pad_maximum_fusion.10), channel_id=1, source_target_pairs={{0,128},{64,192},{128,0},{192,64},{256,384},{320,448},{384,256},{4... | collective-permute-start | bytes 393224 | tf_op jit(solution)/shard_map/ppermute | solution.py:113
  46.4 10.6 %collective-permute-start.1 = (bf16[2,64,512]{2,1,0:T(8,128)(2,1)S(1)}, bf16[2,64,512]{2,1,0:T(8,128)(2,1)S(1)}, u32[]{:S(2)}, u32[]{:S(2)}) collective-permute-start(bf16[2,64,512]{2,1,0:T(8,128)(2,1)S(1)} %pad_maximum_fusion.9), channel_id=1, source_target_pairs={{0,128},{64,192},{128,0},{192,64},{256,384},{320,448},{384,256},{4... | collective-permute-start | bytes 393224 | tf_op jit(solution)/shard_map/ppermute | solution.py:113
  50.7 12.4 %collective-permute-start.5 = (bf16[4,64,512]{2,1,0:T(8,128)(2,1)S(1)}, bf16[4,64,512]{2,1,0:T(8,128)(2,1)S(1)}, u32[]{:S(2)}, u32[]{:S(2)}) collective-permute-start(bf16[4,64,512]{2,1,0:T(8,128)(2,1)S(1)} %pad_maximum_fusion.6), channel_id=1, source_target_pairs={{0,64},{64,0},{128,192},{192,128},{256,320},{320,256},{384,448},{4... | collective-permute-start | bytes 786440 | tf_op jit(solution)/shard_map/ppermute | solution.py:113
  57.0 10.5 %collective-permute-start.2 = (bf16[4,64,512]{2,1,0:T(8,128)(2,1)S(1)}, bf16[4,64,512]{2,1,0:T(8,128)(2,1)S(1)}, u32[]{:S(2)}, u32[]{:S(2)}) collective-permute-start(bf16[4,64,512]{2,1,0:T(8,128)(2,1)S(1)} %pad_maximum_fusion.5), channel_id=1, source_target_pairs={{0,64},{64,0},{128,192},{192,128},{256,320},{320,256},{384,448},{4... | collective-permute-start | bytes 786440 | tf_op jit(solution)/shard_map/ppermute | solution.py:113
  67.6 2.2 %copy-start.2 = (bf16[8,512,512]{2,1,0:T(8,128)(2,1)S(1)}, bf16[8,512,512]{2,1,0:T(8,128)(2,1)}, u32[]{:S(2)}) copy-start(bf16[8,512,512]{2,1,0:T(8,128)(2,1)} %all-gather.4.cloned.1.call-done.gram_ref) | copy-start | bytes 12582916
  72.9 11.3 %collective-permute-start.11 = (bf16[1,64,512]{2,1,0:T(8,128)(2,1)S(1)}, bf16[1,64,512]{2,1,0:T(8,128)(2,1)S(1)}, u32[]{:S(2)}, u32[]{:S(2)}) collective-permute-start(bf16[1,64,512]{2,1,0:T(8,128)(2,1)S(1)} %bitcast.25), channel_id=1, source_target_pairs={{0,256},{64,320},{128,384},{192,448},{256,0},{320,64},{384,128},{4... | collective-permute-start | bytes 196616 | tf_op jit(solution)/shard_map/ppermute | solution.py:113
  81.8 11.0 %collective-permute-start.6 = (bf16[1,64,512]{2,1,0:T(8,128)(2,1)S(1)}, bf16[1,64,512]{2,1,0:T(8,128)(2,1)S(1)}, u32[]{:S(2)}, u32[]{:S(2)}) collective-permute-start(bf16[1,64,512]{2,1,0:T(8,128)(2,1)S(1)} %bitcast.21), channel_id=1, source_target_pairs={{0,256},{64,320},{128,384},{192,448},{256,0},{320,64},{384,128},{4... | collective-permute-start | bytes 196616 | tf_op jit(solution)/shard_map/ppermute | solution.py:113
  84.2 13.1 %collective-permute-start.12 = (bf16[2,64,512]{2,1,0:T(8,128)(2,1)S(1)}, bf16[2,64,512]{2,1,0:T(8,128)(2,1)S(1)}, u32[]{:S(2)}, u32[]{:S(2)}) collective-permute-start(bf16[2,64,512]{2,1,0:T(8,128)(2,1)S(1)} %pad_maximum_fusion.12), channel_id=1, source_target_pairs={{0,128},{64,192},{128,0},{192,64},{256,384},{320,448},{384,256},{4... | collective-permute-start | bytes 393224 | tf_op jit(solution)/shard_map/ppermute | solution.py:113
  92.9 12.5 %collective-permute-start.7 = (bf16[2,64,512]{2,1,0:T(8,128)(2,1)S(1)}, bf16[2,64,512]{2,1,0:T(8,128)(2,1)S(1)}, u32[]{:S(2)}, u32[]{:S(2)}) collective-permute-start(bf16[2,64,512]{2,1,0:T(8,128)(2,1)S(1)} %pad_maximum_fusion.11), channel_id=1, source_target_pairs={{0,128},{64,192},{128,0},{192,64},{256,384},{320,448},{384,256},{4... | collective-permute-start | bytes 393224 | tf_op jit(solution)/shard_map/ppermute | solution.py:113
  97.3 39.2 %copy-start.3 = (f32[512]{0:T(512)S(1)}, f32[512]{0:T(512)}, u32[]{:S(2)}) copy-start(f32[512]{0:T(512)} %param.8) | copy-start | bytes 6148
  97.3 14.3 %collective-permute-start.13 = (bf16[4,64,512]{2,1,0:T(8,128)(2,1)S(1)}, bf16[4,64,512]{2,1,0:T(8,128)(2,1)S(1)}, u32[]{:S(2)}, u32[]{:S(2)}) collective-permute-start(bf16[4,64,512]{2,1,0:T(8,128)(2,1)S(1)} %pad_maximum_fusion.8), channel_id=1, source_target_pairs={{0,64},{64,0},{128,192},{192,128},{256,320},{320,256},{384,448},{4... | collective-permute-start | bytes 786440 | tf_op jit(solution)/shard_map/ppermute | solution.py:113
  105.4 11.2 %collective-permute-start.8 = (bf16[4,64,512]{2,1,0:T(8,128)(2,1)S(1)}, bf16[4,64,512]{2,1,0:T(8,128)(2,1)S(1)}, u32[]{:S(2)}, u32[]{:S(2)}) collective-permute-start(bf16[4,64,512]{2,1,0:T(8,128)(2,1)S(1)} %pad_maximum_fusion.7), channel_id=1, source_target_pairs={{0,64},{64,0},{128,192},{192,128},{256,320},{320,256},{384,448},{4... | collective-permute-start | bytes 786440 | tf_op jit(solution)/shard_map/ppermute | solution.py:113
  111.7 16.8 %collective-permute-start.14 = (bf16[8,64,512]{2,1,0:T(8,128)(2,1)S(1)}, bf16[8,64,512]{2,1,0:T(8,128)(2,1)S(1)}, u32[]{:S(2)}, u32[]{:S(2)}) collective-permute-start(bf16[8,64,512]{2,1,0:T(8,128)(2,1)S(1)} %pad_maximum_fusion.4.refs_1_), channel_id=1, source_target_pairs={{0,48},{16,0},{32,16},{48,32},{1,49},{17,1},{33,17},{49,33},{2,50}... | collective-permute-start | bytes 1572872 | tf_op jit(solution)/shard_map/ppermute | solution.py:145
  116.6 18.0 %collective-permute-start.9 = (bf16[8,64,512]{2,1,0:T(8,128)(2,1)S(1)}, bf16[8,64,512]{2,1,0:T(8,128)(2,1)S(1)}, u32[]{:S(2)}, u32[]{:S(2)}) collective-permute-start(bf16[8,64,512]{2,1,0:T(8,128)(2,1)S(1)} %pad_maximum_fusion.3.refs_0_), channel_id=1, source_target_pairs={{0,16},{16,32},{32,48},{48,0},{1,17},{17,33},{33,49},{49,1},{2,18}... | collective-permute-start | bytes 1572872 | tf_op jit(solution)/shard_map/ppermute | solution.py:144
  119.1 23.4 %collective-permute-start.17 = (bf16[8,64,512]{2,1,0:T(8,128)(2,1)S(1)}, bf16[8,64,512]{2,1,0:T(8,128)(2,1)}, u32[]{:S(2)}, u32[]{:S(2)}) collective-permute-start(bf16[8,64,512]{2,1,0:T(8,128)(2,1)S(1)} %pad_maximum_fusion.3.refs_0_), channel_id=1, source_target_pairs={{0,48},{16,0},{32,16},{48,32},{1,49},{17,1},{33,17},{49,33},{2,50}... | collective-permute-start | bytes 1572872 | tf_op jit(solution)/shard_map/ppermute | solution.py:144
  123.7 23.6 %collective-permute-start.16 = (bf16[8,64,512]{2,1,0:T(8,128)(2,1)S(1)}, bf16[8,64,512]{2,1,0:T(8,128)(2,1)}, u32[]{:S(2)}, u32[]{:S(2)}) collective-permute-start(bf16[8,64,512]{2,1,0:T(8,128)(2,1)S(1)} %pad_maximum_fusion.4.refs_1_), channel_id=1, source_target_pairs={{0,16},{16,32},{32,48},{48,0},{1,17},{17,33},{33,49},{49,1},{2,18}... | collective-permute-start | bytes 1572872 | tf_op jit(solution)/shard_map/ppermute | solution.py:145
  128.4 23.7 %collective-permute-start.15 = (bf16[8,64,512]{2,1,0:T(8,128)(2,1)S(1)}, bf16[8,64,512]{2,1,0:T(8,128)(2,1)S(1)}, u32[]{:S(2)}, u32[]{:S(2)}) collective-permute-start(bf16[8,64,512]{2,1,0:T(8,128)(2,1)S(1)} %collective-permute-done.14.refs_1_), channel_id=1, source_target_pairs={{0,48},{16,0},{32,16},{48,32},{1,49},{17,1},{33,17},{49,33},{2,50}... | collective-permute-start | bytes 1572872 | tf_op jit(solution)/shard_map/ppermute | solution.py:151
  134.6 20.9 %collective-permute-start.10 = (bf16[8,64,512]{2,1,0:T(8,128)(2,1)S(1)}, bf16[8,64,512]{2,1,0:T(8,128)(2,1)S(1)}, u32[]{:S(2)}, u32[]{:S(2)}) collective-permute-start(bf16[8,64,512]{2,1,0:T(8,128)(2,1)S(1)} %collective-permute-done.9.refs_0_), channel_id=1, source_target_pairs={{0,16},{16,32},{32,48},{48,0},{1,17},{17,33},{33,49},{49,1},{2,18}... | collective-permute-start | bytes 1572872 | tf_op jit(solution)/shard_map/ppermute | solution.py:151
  136.6 2.2 %copy-start = (bf16[4096,512]{1,0:T(8,128)(2,1)S(1)}, bf16[4096,512]{1,0:T(8,128)(2,1)}, u32[]{:S(2)}) copy-start(bf16[4096,512]{1,0:T(8,128)(2,1)} %all-gather.6.cloned.1.call-done) | copy-start | bytes 12582916
  138.7 3.8 %copy-start.1 = (bf16[4096,512]{1,0:T(8,128)(2,1)S(1)}, bf16[4096,512]{1,0:T(8,128)(2,1)}, u32[]{:S(2)}) copy-start(bf16[4096,512]{1,0:T(8,128)(2,1)} %all-gather.6.cloned.1.call-done) | copy-start | bytes 12582916
Sparse Core Ops, SparseCore 0:
  24.6 40.2 all-gather.3
  67.1 39.7 all-gather.5

commit v11 on v8

--- a/solution.py
+++ b/solution.py
@@ -5,17 +5,17 @@
 from jax.experimental.pallas import tpu as pltpu
 from jax.sharding import Mesh, PartitionSpec as P
 
-NZ, NY, CHUNKS = 8, 4, 2
+NZ, NY = 8, 4
 NT_DIMS = (((1,), (1,)), ((), ()))
-RELATIVE = (0, 4, 2, 6, 1, 5, 3, 7)
+RELATIVE = (1, 5, 3, 7, 0, 4, 2, 6)
 VMEM_LIMIT = 24 * 1024 * 1024
 UP = [(i, (i + 1) % NY) for i in range(NY)]
 DOWN = [(i, (i - 1) % NY) for i in range(NY)]
 
 
-def kernel_matrix(slots, inverse_gram, training):
+def kernel_matrix(slots, gram, training):
     n, t, depth = training.shape
-    rows = inverse_gram.shape[1]
+    rows = gram.shape[1]
 
     def kernel(slots, gram_ref, training_ref, out_ref, total):
         step = pl.program_id(0)
@@ -48,16 +48,15 @@
             flops=2 * n * rows * t * depth, bytes_accessed=2 * n * depth * (rows + t), transcendentals=0
         ),
         name="kernel_matrix",
-    )(slots, inverse_gram, training)
+    )(slots, gram, training)
 
 
-def score_columns(slots, place, query, chunks, weight, out):
+def score_columns(slots, place, query, halves, weight, out):
     n, rows, depth = query.shape
-    each = chunks[0].shape[1]
-    t = each * len(chunks)
+    half, t, _ = halves[0].shape
     columns = weight.shape[1]
 
-    def kernel(slots, place, query_ref, weight_ref, *refs):
+    def kernel(slots, place, query_ref, weight_ref, first_ref, second_ref, *refs):
         out_ref, total = refs[-2:]
         step = pl.program_id(0)
 
@@ -65,18 +64,19 @@
         def _():
             total[...] = jnp.zeros_like(total)
 
-        block = jnp.concatenate([ref[step] for ref in refs[: len(chunks)]], axis=0)
+        first, second = first_ref[jnp.minimum(step, half - 1)], second_ref[jnp.maximum(step - half, 0)]
+        block = jnp.where(step < half, first, second)
         total[...] += lax.dot_general(query_ref[0], block, NT_DIMS, preferred_element_type=jnp.float32)
 
         @pl.when(step == n - 1)
         def _():
             out_ref[...] = total[...] * weight_ref[...]
 
-    operands = [slots, place, query, weight, *chunks]
+    operands = [slots, place, query, weight, *halves]
     in_specs = [
         pl.BlockSpec((1, rows, depth), lambda s, slots, place: (slots[s], 0, 0)),
         pl.BlockSpec((1, t), lambda s, slots, place: (0, place[0])),
-    ] + [pl.BlockSpec((n, each, depth), lambda s, slots, place: (0, 0, 0))] * len(chunks)
+    ] + [pl.BlockSpec((half, t, depth), lambda s, slots, place: (0, 0, 0))] * 2
     aliases = {}
     if out is not None:
         in_specs.append(pl.BlockSpec(memory_space=pl.ANY))
@@ -101,13 +101,15 @@
     )(*operands)
 
 
-def after(array, *earlier):
-    return lax.optimization_barrier((array, earlier))[0]
+def swapped(held, distance):
+    return lax.ppermute(held, "z", [(i, i ^ distance) for i in range(NZ)])
 
 
-def exchange(held, distance):
-    other = lax.ppermute(held, "z", [(i, i ^ distance) for i in range(NZ)])
-    return jnp.concatenate([held, other], axis=0)
+def gather_z(block):
+    pair = jnp.stack([block, swapped(block, 4)])
+    first = jnp.concatenate([swapped(pair, 1), swapped(pair, 3)], axis=0)
+    second = jnp.concatenate([pair, swapped(pair, 2)], axis=0)
+    return first, second
 
 
 def local(query_features, inverse_gram, training_features, residual_weight):
@@ -124,24 +126,20 @@
     got = lax.all_to_all(sent, "y", split_axis=0, concat_axis=0, tiled=True)
     gram_rows = got[:, :rows].reshape(NY * rows, depth)
     training = got[:, rows:].reshape(NY, t // folds, folds, lanes).transpose(2, 1, 0, 3)
-    training = training.reshape(CHUNKS, 1, t // CHUNKS, NY * lanes)
+    training = training.reshape(t, NY * lanes)
 
     gram = lax.all_gather(gram_rows, ("x", "core"), axis=0)
-    query = lax.all_gather(after(query_features, gram_rows), ("x", "core"), axis=0)
+    query = lax.all_gather(query_features, ("x", "core"), axis=0)
     weight = residual_weight[None, :]
 
-    a, b = training[0], training[1]
-    for distance in (4, 2, 1):
-        a, b = exchange(a, distance), exchange(b, distance)
-    a, b = kernel_matrix(slots, gram, a)[None], kernel_matrix(slots, gram, b)[None]
-    for distance in (4, 2, 1):
-        a, b = exchange(a, distance), exchange(b, distance)
+    training = jnp.concatenate(gather_z(training), axis=0)
+    a, b = gather_z(kernel_matrix(slots, gram, training))
 
     below_a, above_a = lax.ppermute(a, "y", UP), lax.ppermute(a, "y", DOWN)
     below_b, above_b = lax.ppermute(b, "y", UP), lax.ppermute(b, "y", DOWN)
 
-    def scores(distance, chunks, out):
-        return score_columns(slots, lax.rem(y + distance, NY)[None], query, chunks, weight, out)
+    def scores(distance, halves, out):
+        return score_columns(slots, lax.rem(y + distance, NY)[None], query, halves, weight, out)
 
     out = scores(0, (a, b), None)
     far = lax.ppermute(below_a, "y", UP), lax.ppermute(above_b, "y", DOWN)

time: 164 us -> 175 us (1.067)
  waiting for transfers between devices: 22.6 us -> 58.8 us
  starting transfers between devices: 79.5 us -> 55.8 us
  Pallas kernels: 22.9 us -> 20.5 us
    ppermute x12 -> x8, waiting for transfers between devices: 14.9 us -> 51.3 us  [swapped(): return lax.ppermute(held, 'z', [(i, i ^ distance) for i in range(NZ)])]
    ppermute x12 -> x8, starting transfers between devices: 58.3 us -> 36.7 us  [swapped(): return lax.ppermute(held, 'z', [(i, i ^ distance) for i in range(NZ)])]
    ppermute x2, waiting for transfers between devices: 0.09 us -> 3.82 us  [local(): below_a, above_a = (lax.ppermute(a, 'y', UP), lax.ppermute(a, 'y', DOWN))]
    ppermute x2, waiting for transfers between devices: 3.29 us -> 0.06 us  [local(): below_b, above_b = (lax.ppermute(b, 'y', UP), lax.ppermute(b, 'y', DOWN))]
    pallas_call x2 -> x1, Pallas kernels: 5.76 us -> 3.15 us  [kernel_matrix(): pl.pallas_call(kernel, out_shape=jax.ShapeDtypeStruct((t, rows), jnp.bflo...]
    all_gather x1, waiting for transfers between devices: 1.8 us -> 0.02 us  [local(): gram = lax.all_gather(gram_rows, ('x', 'core'), axis=0)]
    unnamed x10 -> x16, local copies, waits for them, and re-layouts: 4.39 us -> 4.47 us
  transfers between devices with their start and end apart: 20 -> 16, of which waited for: 11 -> 9; matrix products, arithmetic and copies ran while one was open for 0% -> 0% of each run, Pallas kernels for 12% -> 10%
where the time goes in v11:
time: 175 us; the launch traced here: 172 us
  waiting for transfers between devices  58.8 us (34%)
  starting transfers between devices  55.8 us (32%)
  Pallas kernels  20.5 us (12%)
  blocking collectives  15.1 us (9%)
  between operations  13.7 us (8%)
  local copies, waits for them, and re-layouts  7.42 us (4%)
    ppermute x8, waiting for transfers between devices, swapped(): return lax.ppermute(held, 'z', [(i, i ^ distance) for i in range(NZ)])  51.3 us
    ppermute x8, starting transfers between devices, swapped(): return lax.ppermute(held, 'z', [(i, i ^ distance) for i in range(NZ)])  36.7 us
    pallas_call x4, Pallas kernels, score_columns(): pl.pallas_call(kernel, out_shape=jax.ShapeDtypeStruct((rows, columns), jn...  17.4 us
    all_to_all x1, blocking collectives, local(): got = lax.all_to_all(sent, 'y', split_axis=0, concat_axis=0, tiled=True)  15.1 us
    ppermute x2, starting transfers between devices, local(): below_a, above_a = (lax.ppermute(a, 'y', UP), lax.ppermute(a, 'y', DOWN))  7.05 us
    ppermute x2, starting transfers between devices, local(): far = (lax.ppermute(below_a, 'y', UP), lax.ppermute(above_b, 'y', DOWN))  6.99 us
    ppermute x2, starting transfers between devices, local(): below_b, above_b = (lax.ppermute(b, 'y', UP), lax.ppermute(b, 'y', DOWN))  5 us
    unnamed x16, local copies, waits for them, and re-layouts  4.47 us
  transfers between devices with their start and end apart: 16, of which 9 were waited for; matrix products, arithmetic and copies ran while one was open for 0% of the time, Pallas kernels for 10%

profile of v11, /device:TPU:6, one launch (start us, length us, event | category | flops | bytes accessed | tf_op | source)
XLA Modules:
  0.0 171.5 jit_solution(16384496245802111499)
XLA Ops:
  6.5 0.0 all-gather.4.cloned.1.call-start
  6.5 0.9 copy.21
  7.5 0.9 broadcast_in_dim.20
  8.5 15.1 %all_to_all.5 = bf16[4,160,512]{2,1,0:T(8,128)(2,1)S(1)} all-to-all(bf16[4,160,512]{2,1,0:T(8,128)(2,1)S(1)} %pad_maximum_fusion), channel_id=1, replica_groups=mesh['z'=8,'y'=4,'x'=4,'core'=2,'row'=2] {'y'}, dimensions={0} | all-to-all | bytes 1310720 | tf_op jit(solution)/shard_map/all_to_all | solution.py:126
  23.6 0.8 slice.8
  24.4 0.0 all-gather.4.cloned.1.call-update
  24.5 0.0 copy-start.4
  24.5 0.0 all-gather.6.cloned.1.call-start
  24.5 0.7 all-gather.6.cloned.1.call-update
  25.3 0.1 copy.14
  25.4 9.1 %collective-permute-start = (bf16[128,512]{1,0:T(8,128)(2,1)S(1)}, bf16[128,512]{1,0:T(8,128)(2,1)S(1)}, u32[]{:S(2)}, u32[]{:S(2)}) collective-permute-start(bf16[128,512]{1,0:T(8,128)(2,1)S(1)} %bitcast.42), channel_id=1, source_target_pairs={{0,256},{64,320},{128,384},{192,448},{256,0},{320,64},{384,128},{4... | collective-permute-start | bytes 393224 | tf_op jit(solution)/shard_map/ppermute | solution.py:105
  34.5 0.1 stack_reshape.3
  34.6 10.8 %collective-permute-done = bf16[128,512]{1,0:T(8,128)(2,1)S(1)} collective-permute-done((bf16[128,512]{1,0:T(8,128)(2,1)S(1)}, bf16[128,512]{1,0:T(8,128)(2,1)S(1)}, u32[]{:S(2)}, u32[]{:S(2)}) %collective-permute-start) | collective-permute-done | bytes 131104 | tf_op jit(solution)/shard_map/ppermute | solution.py:105
  45.4 1.9 %collective-permute-start.1 = (bf16[2,128,512]{2,1,0:T(8,128)(2,1)S(1)}, bf16[2,128,512]{2,1,0:T(8,128)(2,1)S(1)}, u32[]{:S(2)}, u32[]{:S(2)}) collective-permute-start(bf16[2,128,512]{2,1,0:T(8,128)(2,1)S(1)} %pad_maximum_fusion.2), channel_id=1, source_target_pairs={{0,64},{64,0},{128,192},{192,128},{256,320},{320,256},{384,448},{4... | collective-permute-start | bytes 786440 | tf_op jit(solution)/shard_map/ppermute | solution.py:105
  47.3 4.3 %collective-permute-start.2 = (bf16[2,128,512]{2,1,0:T(8,128)(2,1)S(1)}, bf16[2,128,512]{2,1,0:T(8,128)(2,1)S(1)}, u32[]{:S(2)}, u32[]{:S(2)}) collective-permute-start(bf16[2,128,512]{2,1,0:T(8,128)(2,1)S(1)} %pad_maximum_fusion.2), channel_id=1, source_target_pairs={{0,192},{64,128},{128,64},{192,0},{256,448},{320,384},{384,320},{4... | collective-permute-start | bytes 786440 | tf_op jit(solution)/shard_map/ppermute | solution.py:105
  51.6 0.0 copy-done.4
  51.7 3.0 %collective-permute-start.3 = (bf16[2,128,512]{2,1,0:T(8,128)(2,1)S(1)}, bf16[2,128,512]{2,1,0:T(8,128)(2,1)S(1)}, u32[]{:S(2)}, u32[]{:S(2)}) collective-permute-start(bf16[2,128,512]{2,1,0:T(8,128)(2,1)S(1)} %pad_maximum_fusion.2), channel_id=1, source_target_pairs={{0,128},{64,192},{128,0},{192,64},{256,384},{320,448},{384,256},{4... | collective-permute-start | bytes 786440 | tf_op jit(solution)/shard_map/ppermute | solution.py:105
  54.7 0.0 collective-permute-done.1
  54.7 7.8 %collective-permute-done.2 = bf16[2,128,512]{2,1,0:T(8,128)(2,1)S(1)} collective-permute-done((bf16[2,128,512]{2,1,0:T(8,128)(2,1)S(1)}, bf16[2,128,512]{2,1,0:T(8,128)(2,1)S(1)}, u32[]{:S(2)}, u32[]{:S(2)}) %collective-permute-start.2) | collective-permute-done | bytes 262176 | tf_op jit(solution)/shard_map/ppermute | solution.py:105
  62.6 12.7 %collective-permute-done.3 = bf16[2,128,512]{2,1,0:T(8,128)(2,1)S(1)} collective-permute-done((bf16[2,128,512]{2,1,0:T(8,128)(2,1)S(1)}, bf16[2,128,512]{2,1,0:T(8,128)(2,1)S(1)}, u32[]{:S(2)}, u32[]{:S(2)}) %collective-permute-start.3) | collective-permute-done | bytes 262176 | tf_op jit(solution)/shard_map/ppermute | solution.py:105
  75.3 0.0 all-gather.4.cloned.1.call-done.gram_ref
  75.3 0.0 copy-start.2
  75.3 2.2 %copy-done.2 = bf16[8,512,512]{2,1,0:T(8,128)(2,1)S(1)} copy-done((bf16[8,512,512]{2,1,0:T(8,128)(2,1)S(1)}, bf16[8,512,512]{2,1,0:T(8,128)(2,1)}, u32[]{:S(2)}) %copy-start.2) | copy-done | bytes 4194328
  77.5 3.1 %kernel_matrix.1 = bf16[128,512]{1,0:T(8,128)(2,1)S(1)} custom-call(s32[8]{0:T(128)S(1)} %broadcast_xor_fusion.slots, bf16[8,512,512]{2,1,0:T(8,128)(2,1)S(1)} %copy-done.2, bf16[8,128,512]{2,1,0:T(8,128)(2,1)S(1)} %constant_dynamic-update-slice_fusion.training_ref), custom_call_target="tpu_custom_call" | custom-call | flops 536870912 | bytes 5242880 | tf_op jit(solution)/shard_map/kernel_matrix/pallas_call | solution.py:33
  80.6 8.3 %collective-permute-start.4 = (bf16[128,512]{1,0:T(8,128)(2,1)S(1)}, bf16[128,512]{1,0:T(8,128)(2,1)S(1)}, u32[]{:S(2)}, u32[]{:S(2)}) collective-permute-start(bf16[128,512]{1,0:T(8,128)(2,1)S(1)} %kernel_matrix.1), channel_id=1, source_target_pairs={{0,256},{64,320},{128,384},{192,448},{256,0},{320,64},{384,128},{4... | collective-permute-start | bytes 393224 | tf_op jit(solution)/shard_map/ppermute | solution.py:105
  88.9 10.1 %collective-permute-done.4 = bf16[128,512]{1,0:T(8,128)(2,1)S(1)} collective-permute-done((bf16[128,512]{1,0:T(8,128)(2,1)S(1)}, bf16[128,512]{1,0:T(8,128)(2,1)S(1)}, u32[]{:S(2)}, u32[]{:S(2)}) %collective-permute-start.4) | collective-permute-done | bytes 131104 | tf_op jit(solution)/shard_map/ppermute | solution.py:105
  99.0 0.0 copy-start.3
  99.1 1.9 %collective-permute-start.9 = (bf16[2,128,512]{2,1,0:T(8,128)(2,1)S(1)}, bf16[2,128,512]{2,1,0:T(8,128)(2,1)S(1)}, u32[]{:S(2)}, u32[]{:S(2)}) collective-permute-start(bf16[2,128,512]{2,1,0:T(8,128)(2,1)S(1)} %pad_maximum_fusion.3), channel_id=1, source_target_pairs={{0,128},{64,192},{128,0},{192,64},{256,384},{320,448},{384,256},{4... | collective-permute-start | bytes 786440 | tf_op jit(solution)/shard_map/ppermute | solution.py:105
  101.0 3.2 %collective-permute-start.5 = (bf16[2,128,512]{2,1,0:T(8,128)(2,1)S(1)}, bf16[2,128,512]{2,1,0:T(8,128)(2,1)S(1)}, u32[]{:S(2)}, u32[]{:S(2)}) collective-permute-start(bf16[2,128,512]{2,1,0:T(8,128)(2,1)S(1)} %pad_maximum_fusion.3), channel_id=1, source_target_pairs={{0,64},{64,0},{128,192},{192,128},{256,320},{320,256},{384,448},{4... | collective-permute-start | bytes 786440 | tf_op jit(solution)/shard_map/ppermute | solution.py:105
  104.2 5.0 %collective-permute-start.6 = (bf16[2,128,512]{2,1,0:T(8,128)(2,1)S(1)}, bf16[2,128,512]{2,1,0:T(8,128)(2,1)S(1)}, u32[]{:S(2)}, u32[]{:S(2)}) collective-permute-start(bf16[2,128,512]{2,1,0:T(8,128)(2,1)S(1)} %pad_maximum_fusion.3), channel_id=1, source_target_pairs={{0,192},{64,128},{128,64},{192,0},{256,448},{320,384},{384,320},{4... | collective-permute-start | bytes 786440 | tf_op jit(solution)/shard_map/ppermute | solution.py:105
  109.2 5.4 %collective-permute-done.9 = bf16[2,128,512]{2,1,0:T(8,128)(2,1)S(1)} collective-permute-done((bf16[2,128,512]{2,1,0:T(8,128)(2,1)S(1)}, bf16[2,128,512]{2,1,0:T(8,128)(2,1)S(1)}, u32[]{:S(2)}, u32[]{:S(2)}) %collective-permute-start.9) | collective-permute-done | bytes 262176 | tf_op jit(solution)/shard_map/ppermute | solution.py:105
  114.6 0.1 pad_maximum_fusion.1.second_ref
  114.7 3.1 %collective-permute-start.10 = (bf16[4,128,512]{2,1,0:T(8,128)(2,1)S(1)}, bf16[4,128,512]{2,1,0:T(8,128)(2,1)S(1)}, u32[]{:S(2)}, u32[]{:S(2)}) collective-permute-start(bf16[4,128,512]{2,1,0:T(8,128)(2,1)S(1)} %pad_maximum_fusion.1.second_ref), channel_id=1, source_target_pairs={{0,48},{16,0},{32,16},{48,32},{1,49},{17,1},{33,17},{49,33},{2,50}... | collective-permute-start | bytes 1572872 | tf_op jit(solution)/shard_map/ppermute | solution.py:139
  117.8 4.5 %collective-permute-done.5 = bf16[2,128,512]{2,1,0:T(8,128)(2,1)S(1)} collective-permute-done((bf16[2,128,512]{2,1,0:T(8,128)(2,1)S(1)}, bf16[2,128,512]{2,1,0:T(8,128)(2,1)S(1)}, u32[]{:S(2)}, u32[]{:S(2)}) %collective-permute-start.5) | collective-permute-done | bytes 262176 | tf_op jit(solution)/shard_map/ppermute | solution.py:105
  122.3 0.0 collective-permute-done.6
  122.3 2.5 %collective-permute-start.7 = (bf16[4,128,512]{2,1,0:T(8,128)(2,1)S(1)}, bf16[4,128,512]{2,1,0:T(8,128)(2,1)S(1)}, u32[]{:S(2)}, u32[]{:S(2)}) collective-permute-start(bf16[4,128,512]{2,1,0:T(8,128)(2,1)S(1)} %constant_dynamic-update-slice_fusion.5.first_ref), channel_id=1, source_target_pairs={{0,16},{16,32},{32,48},{48,0},{1,17},{17,33},{33,49},{49,1},{2,18}... | collective-permute-start | bytes 1572872 | tf_op jit(solution)/shard_map/ppermute | solution.py:138
  124.8 4.6 %collective-permute-start.13 = (bf16[4,128,512]{2,1,0:T(8,128)(2,1)S(1)}, bf16[4,128,512]{2,1,0:T(8,128)(2,1)}, u32[]{:S(2)}, u32[]{:S(2)}) collective-permute-start(bf16[4,128,512]{2,1,0:T(8,128)(2,1)S(1)} %constant_dynamic-update-slice_fusion.5.first_ref), channel_id=1, source_target_pairs={{0,48},{16,0},{32,16},{48,32},{1,49},{17,1},{33,17},{49,33},{2,50}... | collective-permute-start | bytes 1572872 | tf_op jit(solution)/shard_map/ppermute | solution.py:138
  129.4 1.9 %collective-permute-start.12 = (bf16[4,128,512]{2,1,0:T(8,128)(2,1)S(1)}, bf16[4,128,512]{2,1,0:T(8,128)(2,1)}, u32[]{:S(2)}, u32[]{:S(2)}) collective-permute-start(bf16[4,128,512]{2,1,0:T(8,128)(2,1)S(1)} %pad_maximum_fusion.1.second_ref), channel_id=1, source_target_pairs={{0,16},{16,32},{32,48},{48,0},{1,17},{17,33},{33,49},{49,1},{2,18}... | collective-permute-start | bytes 1572872 | tf_op jit(solution)/shard_map/ppermute | solution.py:139
  131.3 0.1 collective-permute-done.10.second_ref
  131.4 5.1 %collective-permute-start.11 = (bf16[4,128,512]{2,1,0:T(8,128)(2,1)S(1)}, bf16[4,128,512]{2,1,0:T(8,128)(2,1)S(1)}, u32[]{:S(2)}, u32[]{:S(2)}) collective-permute-start(bf16[4,128,512]{2,1,0:T(8,128)(2,1)S(1)} %collective-permute-done.10.second_ref), channel_id=1, source_target_pairs={{0,48},{16,0},{32,16},{48,32},{1,49},{17,1},{33,17},{49,33},{2,50}... | collective-permute-start | bytes 1572872 | tf_op jit(solution)/shard_map/ppermute | solution.py:145
  136.5 3.8 %collective-permute-done.7.first_ref = bf16[4,128,512]{2,1,0:T(8,128)(2,1)S(1)} collective-permute-done((bf16[4,128,512]{2,1,0:T(8,128)(2,1)S(1)}, bf16[4,128,512]{2,1,0:T(8,128)(2,1)S(1)}, u32[]{:S(2)}, u32[]{:S(2)}) %collective-permute-start.7) | collective-permute-done | bytes 524320 | tf_op jit(solution)/shard_map/ppermute | solution.py:138
  140.3 1.9 %collective-permute-start.8 = (bf16[4,128,512]{2,1,0:T(8,128)(2,1)S(1)}, bf16[4,128,512]{2,1,0:T(8,128)(2,1)S(1)}, u32[]{:S(2)}, u32[]{:S(2)}) collective-permute-start(bf16[4,128,512]{2,1,0:T(8,128)(2,1)S(1)} %collective-permute-done.7.first_ref), channel_id=1, source_target_pairs={{0,16},{16,32},{32,48},{48,0},{1,17},{17,33},{33,49},{49,1},{2,18}... | collective-permute-start | bytes 1572872 | tf_op jit(solution)/shard_map/ppermute | solution.py:145
  142.2 0.0 all-gather.6.cloned.1.call-done
  142.2 0.0 copy-done.3
  142.3 0.0 copy-start
  142.3 2.2 %copy-done = bf16[4096,512]{1,0:T(8,128)(2,1)S(1)} copy-done((bf16[4096,512]{1,0:T(8,128)(2,1)S(1)}, bf16[4096,512]{1,0:T(8,128)(2,1)}, u32[]{:S(2)}) %copy-start) | copy-done | bytes 4194328
  144.4 0.0 copy-start.1
  144.4 3.8 %score_columns.4.refs_0_ = f32[512,512]{1,0:T(8,128)} custom-call(s32[8]{0:T(128)S(1)} %broadcast_xor_fusion.slots, s32[1]{0:T(128)} %bitcast.12.place, bf16[8,512,512]{2,1,0:T(8,128)(2,1)S(1)} %bitcast.24, f32[1,512]{1,0:T(1,128)S(1)} %bitcast.30, bf16[4,128,512]{2,1,0:T(8,128)(2,1)S(1)} %constant_dynamic-update-slice_fusion.5.first_ref, ...), custom_call_target="tpu_custom_call" | custom-call | flops 536870912 | bytes 5242880 | tf_op jit(solution)/shard_map/score_columns/pallas_call | solution.py:85
  148.3 0.0 collective-permute-done.13.first_ref
  148.3 0.0 copy-done.1
  148.3 4.9 %score_columns.5.refs_0_ = f32[512,512]{1,0:T(8,128)} custom-call(s32[8]{0:T(128)S(1)} %broadcast_xor_fusion.slots, s32[1]{0:T(128)} %bitcast.11.place, bf16[8,512,512]{2,1,0:T(8,128)(2,1)S(1)} %bitcast.25, f32[1,512]{1,0:T(1,128)S(1)} %bitcast.31, bf16[4,128,512]{2,1,0:T(8,128)(2,1)} %collective-permute-done.13.first_ref, ...), custom_call_target="tpu_custom_call", output_to_operand_aliasing={{}: (6, {})} | custom-call | flops 536870912 | bytes 5242880 | tf_op jit(solution)/shard_map/score_columns/pallas_call | solution.py:85
  153.1 0.0 collective-permute-done.12.second_ref
  153.1 4.9 %score_columns.6.refs_0_ = f32[512,512]{1,0:T(8,128)} custom-call(s32[8]{0:T(128)S(1)} %broadcast_xor_fusion.slots, s32[1]{0:T(128)} %bitcast.10.place, bf16[8,512,512]{2,1,0:T(8,128)(2,1)S(1)} %bitcast.26, f32[1,512]{1,0:T(1,128)S(1)} %bitcast.32, bf16[4,128,512]{2,1,0:T(8,128)(2,1)S(1)} %collective-permute-done.7.first_ref, ...), custom_call_target="tpu_custom_call", output_to_operand_aliasing={{}: (6, {})} | custom-call | flops 536870912 | bytes 5242880 | tf_op jit(solution)/shard_map/score_columns/pallas_call | solution.py:85
  158.0 0.0 collective-permute-done.11.second_ref
  158.0 2.9 %collective-permute-done.8.first_ref = bf16[4,128,512]{2,1,0:T(8,128)(2,1)S(1)} collective-permute-done((bf16[4,128,512]{2,1,0:T(8,128)(2,1)S(1)}, bf16[4,128,512]{2,1,0:T(8,128)(2,1)S(1)}, u32[]{:S(2)}, u32[]{:S(2)}) %collective-permute-start.8) | collective-permute-done | bytes 524320 | tf_op jit(solution)/shard_map/ppermute | solution.py:145
  160.9 3.8 %score_columns.7 = f32[512,512]{1,0:T(8,128)} custom-call(s32[8]{0:T(128)S(1)} %broadcast_xor_fusion.slots, s32[1]{0:T(128)} %bitcast.place, bf16[8,512,512]{2,1,0:T(8,128)(2,1)S(1)} %bitcast.27, f32[1,512]{1,0:T(1,128)S(1)} %bitcast.33, bf16[4,128,512]{2,1,0:T(8,128)(2,1)S(1)} %collective-permute-done.8.first_ref, ...), custom_call_target="tpu_custom_call", output_to_operand_aliasing={{}: (6, {})} | custom-call | flops 536870912 | bytes 5242880 | tf_op jit(solution)/shard_map/score_columns/pallas_call | solution.py:85
  (14 shorter events, 0.3 us)
Async XLA Ops:
  6.5 68.7 %all-gather.4.cloned.1.call-start = ((), (), s32[]{:S(2)}) async-start(), calls=%async_computation.1 | async-start | bytes 4718592 | tf_op jit(solution)/shard_map/all_gather | solution.py:131
  24.5 27.2 %copy-start.4 = (s32[8]{0:T(128)S(1)}, s32[8]{0:T(128)}, u32[]{:S(2)}) copy-start(s32[8]{0:T(128)} %constant.30.clone) | copy-start | bytes 100
  24.5 117.8 %all-gather.6.cloned.1.call-start = ((), (), s32[]{:S(2)}) async-start(), calls=%async_computation.2 | async-start | bytes 4718592 | tf_op jit(solution)/shard_map/all_gather | solution.py:132
  25.4 19.9 %collective-permute-start = (bf16[128,512]{1,0:T(8,128)(2,1)S(1)}, bf16[128,512]{1,0:T(8,128)(2,1)S(1)}, u32[]{:S(2)}, u32[]{:S(2)}) collective-permute-start(bf16[128,512]{1,0:T(8,128)(2,1)S(1)} %bitcast.42), channel_id=1, source_target_pairs={{0,256},{64,320},{128,384},{192,448},{256,0},{320,64},{384,128},{4... | collective-permute-start | bytes 393224 | tf_op jit(solution)/shard_map/ppermute | solution.py:105
  45.4 9.3 %collective-permute-start.1 = (bf16[2,128,512]{2,1,0:T(8,128)(2,1)S(1)}, bf16[2,128,512]{2,1,0:T(8,128)(2,1)S(1)}, u32[]{:S(2)}, u32[]{:S(2)}) collective-permute-start(bf16[2,128,512]{2,1,0:T(8,128)(2,1)S(1)} %pad_maximum_fusion.2), channel_id=1, source_target_pairs={{0,64},{64,0},{128,192},{192,128},{256,320},{320,256},{384,448},{4... | collective-permute-start | bytes 786440 | tf_op jit(solution)/shard_map/ppermute | solution.py:105
  47.3 15.2 %collective-permute-start.2 = (bf16[2,128,512]{2,1,0:T(8,128)(2,1)S(1)}, bf16[2,128,512]{2,1,0:T(8,128)(2,1)S(1)}, u32[]{:S(2)}, u32[]{:S(2)}) collective-permute-start(bf16[2,128,512]{2,1,0:T(8,128)(2,1)S(1)} %pad_maximum_fusion.2), channel_id=1, source_target_pairs={{0,192},{64,128},{128,64},{192,0},{256,448},{320,384},{384,320},{4... | collective-permute-start | bytes 786440 | tf_op jit(solution)/shard_map/ppermute | solution.py:105
  51.7 23.6 %collective-permute-start.3 = (bf16[2,128,512]{2,1,0:T(8,128)(2,1)S(1)}, bf16[2,128,512]{2,1,0:T(8,128)(2,1)S(1)}, u32[]{:S(2)}, u32[]{:S(2)}) collective-permute-start(bf16[2,128,512]{2,1,0:T(8,128)(2,1)S(1)} %pad_maximum_fusion.2), channel_id=1, source_target_pairs={{0,128},{64,192},{128,0},{192,64},{256,384},{320,448},{384,256},{4... | collective-permute-start | bytes 786440 | tf_op jit(solution)/shard_map/ppermute | solution.py:105
  75.3 2.2 %copy-start.2 = (bf16[8,512,512]{2,1,0:T(8,128)(2,1)S(1)}, bf16[8,512,512]{2,1,0:T(8,128)(2,1)}, u32[]{:S(2)}) copy-start(bf16[8,512,512]{2,1,0:T(8,128)(2,1)} %all-gather.4.cloned.1.call-done.gram_ref) | copy-start | bytes 12582916
  80.6 18.4 %collective-permute-start.4 = (bf16[128,512]{1,0:T(8,128)(2,1)S(1)}, bf16[128,512]{1,0:T(8,128)(2,1)S(1)}, u32[]{:S(2)}, u32[]{:S(2)}) collective-permute-start(bf16[128,512]{1,0:T(8,128)(2,1)S(1)} %kernel_matrix.1), channel_id=1, source_target_pairs={{0,256},{64,320},{128,384},{192,448},{256,0},{320,64},{384,128},{4... | collective-permute-start | bytes 393224 | tf_op jit(solution)/shard_map/ppermute | solution.py:105
  99.0 43.2 %copy-start.3 = (f32[512]{0:T(512)S(1)}, f32[512]{0:T(512)}, u32[]{:S(2)}) copy-start(f32[512]{0:T(512)} %param.8) | copy-start | bytes 6148
  99.1 15.5 %collective-permute-start.9 = (bf16[2,128,512]{2,1,0:T(8,128)(2,1)S(1)}, bf16[2,128,512]{2,1,0:T(8,128)(2,1)S(1)}, u32[]{:S(2)}, u32[]{:S(2)}) collective-permute-start(bf16[2,128,512]{2,1,0:T(8,128)(2,1)S(1)} %pad_maximum_fusion.3), channel_id=1, source_target_pairs={{0,128},{64,192},{128,0},{192,64},{256,384},{320,448},{384,256},{4... | collective-permute-start | bytes 786440 | tf_op jit(solution)/shard_map/ppermute | solution.py:105
  101.0 21.3 %collective-permute-start.5 = (bf16[2,128,512]{2,1,0:T(8,128)(2,1)S(1)}, bf16[2,128,512]{2,1,0:T(8,128)(2,1)S(1)}, u32[]{:S(2)}, u32[]{:S(2)}) collective-permute-start(bf16[2,128,512]{2,1,0:T(8,128)(2,1)S(1)} %pad_maximum_fusion.3), channel_id=1, source_target_pairs={{0,64},{64,0},{128,192},{192,128},{256,320},{320,256},{384,448},{4... | collective-permute-start | bytes 786440 | tf_op jit(solution)/shard_map/ppermute | solution.py:105
  104.2 18.0 %collective-permute-start.6 = (bf16[2,128,512]{2,1,0:T(8,128)(2,1)S(1)}, bf16[2,128,512]{2,1,0:T(8,128)(2,1)S(1)}, u32[]{:S(2)}, u32[]{:S(2)}) collective-permute-start(bf16[2,128,512]{2,1,0:T(8,128)(2,1)S(1)} %pad_maximum_fusion.3), channel_id=1, source_target_pairs={{0,192},{64,128},{128,64},{192,0},{256,448},{320,384},{384,320},{4... | collective-permute-start | bytes 786440 | tf_op jit(solution)/shard_map/ppermute | solution.py:105
  114.7 16.7 %collective-permute-start.10 = (bf16[4,128,512]{2,1,0:T(8,128)(2,1)S(1)}, bf16[4,128,512]{2,1,0:T(8,128)(2,1)S(1)}, u32[]{:S(2)}, u32[]{:S(2)}) collective-permute-start(bf16[4,128,512]{2,1,0:T(8,128)(2,1)S(1)} %pad_maximum_fusion.1.second_ref), channel_id=1, source_target_pairs={{0,48},{16,0},{32,16},{48,32},{1,49},{17,1},{33,17},{49,33},{2,50}... | collective-permute-start | bytes 1572872 | tf_op jit(solution)/shard_map/ppermute | solution.py:139
  122.3 18.0 %collective-permute-start.7 = (bf16[4,128,512]{2,1,0:T(8,128)(2,1)S(1)}, bf16[4,128,512]{2,1,0:T(8,128)(2,1)S(1)}, u32[]{:S(2)}, u32[]{:S(2)}) collective-permute-start(bf16[4,128,512]{2,1,0:T(8,128)(2,1)S(1)} %constant_dynamic-update-slice_fusion.5.first_ref), channel_id=1, source_target_pairs={{0,16},{16,32},{32,48},{48,0},{1,17},{17,33},{33,49},{49,1},{2,18}... | collective-permute-start | bytes 1572872 | tf_op jit(solution)/shard_map/ppermute | solution.py:138
  124.8 23.4 %collective-permute-start.13 = (bf16[4,128,512]{2,1,0:T(8,128)(2,1)S(1)}, bf16[4,128,512]{2,1,0:T(8,128)(2,1)}, u32[]{:S(2)}, u32[]{:S(2)}) collective-permute-start(bf16[4,128,512]{2,1,0:T(8,128)(2,1)S(1)} %constant_dynamic-update-slice_fusion.5.first_ref), channel_id=1, source_target_pairs={{0,48},{16,0},{32,16},{48,32},{1,49},{17,1},{33,17},{49,33},{2,50}... | collective-permute-start | bytes 1572872 | tf_op jit(solution)/shard_map/ppermute | solution.py:138
  129.4 23.7 %collective-permute-start.12 = (bf16[4,128,512]{2,1,0:T(8,128)(2,1)S(1)}, bf16[4,128,512]{2,1,0:T(8,128)(2,1)}, u32[]{:S(2)}, u32[]{:S(2)}) collective-permute-start(bf16[4,128,512]{2,1,0:T(8,128)(2,1)S(1)} %pad_maximum_fusion.1.second_ref), channel_id=1, source_target_pairs={{0,16},{16,32},{32,48},{48,0},{1,17},{17,33},{33,49},{49,1},{2,18}... | collective-permute-start | bytes 1572872 | tf_op jit(solution)/shard_map/ppermute | solution.py:139
  131.4 26.6 %collective-permute-start.11 = (bf16[4,128,512]{2,1,0:T(8,128)(2,1)S(1)}, bf16[4,128,512]{2,1,0:T(8,128)(2,1)S(1)}, u32[]{:S(2)}, u32[]{:S(2)}) collective-permute-start(bf16[4,128,512]{2,1,0:T(8,128)(2,1)S(1)} %collective-permute-done.10.second_ref), channel_id=1, source_target_pairs={{0,48},{16,0},{32,16},{48,32},{1,49},{17,1},{33,17},{49,33},{2,50}... | collective-permute-start | bytes 1572872 | tf_op jit(solution)/shard_map/ppermute | solution.py:145
  140.3 20.6 %collective-permute-start.8 = (bf16[4,128,512]{2,1,0:T(8,128)(2,1)S(1)}, bf16[4,128,512]{2,1,0:T(8,128)(2,1)S(1)}, u32[]{:S(2)}, u32[]{:S(2)}) collective-permute-start(bf16[4,128,512]{2,1,0:T(8,128)(2,1)S(1)} %collective-permute-done.7.first_ref), channel_id=1, source_target_pairs={{0,16},{16,32},{32,48},{48,0},{1,17},{17,33},{33,49},{49,1},{2,18}... | collective-permute-start | bytes 1572872 | tf_op jit(solution)/shard_map/ppermute | solution.py:145
  142.3 2.2 %copy-start = (bf16[4096,512]{1,0:T(8,128)(2,1)S(1)}, bf16[4096,512]{1,0:T(8,128)(2,1)}, u32[]{:S(2)}) copy-start(bf16[4096,512]{1,0:T(8,128)(2,1)} %all-gather.6.cloned.1.call-done) | copy-start | bytes 12582916
  144.4 3.8 %copy-start.1 = (bf16[4096,512]{1,0:T(8,128)(2,1)S(1)}, bf16[4096,512]{1,0:T(8,128)(2,1)}, u32[]{:S(2)}) copy-start(bf16[4096,512]{1,0:T(8,128)(2,1)} %all-gather.6.cloned.1.call-done) | copy-start | bytes 12582916
Sparse Core Ops, SparseCore 0:
  24.6 40.2 all-gather.3
  67.1 39.7 all-gather.5

commit v12 on v8

v12 whole, which is shorter than its diff:
```python
import jax
import jax.numpy as jnp
from jax import lax
from jax.experimental import pallas as pl
from jax.experimental.pallas import tpu as pltpu
from jax.sharding import Mesh, PartitionSpec as P

NZ, NY, CHUNKS = 8, 4, 2
NT_DIMS = (((1,), (1,)), ((), ()))
RELATIVE = (0, 4, 2, 6, 1, 5, 3, 7)
VMEM_LIMIT = 16 * 1024 * 1024
UP = [(i, (i + 1) % NY) for i in range(NY)]
DOWN = [(i, (i - 1) % NY) for i in range(NY)]


def pack(inverse_gram, training_features):
    rows, depth = inverse_gram.shape
    columns, lanes = training_features.shape
    t, folds = columns // NY, depth // lanes
    each = t // folds

    def kernel(gram_ref, training_ref, out_ref):
        for k in range(NY):
            out_ref[k, :rows] = gram_ref[...]
            for f in range(folds):
                first = k * t + f * each
                out_ref[k, rows:, f * lanes : (f + 1) * lanes] = training_ref[first : first + each]

    return pl.pallas_call(
        kernel,
        out_shape=jax.ShapeDtypeStruct((NY, rows + each, depth), jnp.bfloat16),
        in_specs=[pl.BlockSpec(memory_space=pltpu.VMEM)] * 2,
        out_specs=pl.BlockSpec(memory_space=pltpu.VMEM),
        compiler_params=pltpu.CompilerParams(vmem_limit_bytes=VMEM_LIMIT),
        name="pack",
    )(inverse_gram, training_features)


def kernel_matrix(slots, gram, training):
    n, t, depth = training.shape
    rows = gram.shape[1]

    def kernel(slots, gram_ref, training_ref, out_ref):
        total = jnp.zeros((t, rows), jnp.float32)
        for s in range(n):
            total += lax.dot_general(training_ref[s], gram_ref[slots[s]], NT_DIMS, preferred_element_type=jnp.float32)
        out_ref[...] = total.astype(out_ref.dtype)

    return pl.pallas_call(
        kernel,
        out_shape=jax.ShapeDtypeStruct((t, rows), jnp.bfloat16),
        in_specs=[pl.BlockSpec(memory_space=pltpu.SMEM)] + [pl.BlockSpec(memory_space=pltpu.VMEM)] * 2,
        out_specs=pl.BlockSpec(memory_space=pltpu.VMEM),
        compiler_params=pltpu.CompilerParams(vmem_limit_bytes=VMEM_LIMIT),
        cost_estimate=pl.CostEstimate(
            flops=2 * n * rows * t * depth, bytes_accessed=2 * n * depth * (rows + t), transcendentals=0
        ),
        name="kernel_matrix",
    )(slots, gram, training)


def score_columns(slots, place, query, chunks, weight, out):
    n, rows, depth = query.shape
    t = sum(chunk.shape[1] for chunk in chunks)
    columns = weight.shape[1]

    def kernel(slots, place, query_ref, weight_ref, *refs):
        chunk_refs = refs[: len(chunks)]
        out_ref, total, sent = refs[-3:]
        span = pl.ds(pl.multiple_of(place[0] * t, t), t)
        for s in range(n):
            block = jnp.concatenate([ref[s] for ref in chunk_refs], axis=0)
            product = lax.dot_general(query_ref[slots[s]], block, NT_DIMS, preferred_element_type=jnp.float32)
            if s == 0:
                total[...] = product
            elif s < n - 1:
                total[...] += product
            else:
                total[...] = (total[...] + product) * weight_ref[:, span]
        copy = pltpu.make_async_copy(total, out_ref.at[:, span], sent)
        copy.start()
        copy.wait()

    operands = [slots, place, query, weight, *chunks]
    in_specs = [pl.BlockSpec(memory_space=pltpu.SMEM)] * 2 + [pl.BlockSpec(memory_space=pltpu.VMEM)] * (2 + len(chunks))
    aliases = {}
    if out is not None:
        in_specs.append(pl.BlockSpec(memory_space=pl.ANY))
        aliases = {len(operands): 0}
        operands.append(out)
    return pl.pallas_call(
        kernel,
        out_shape=jax.ShapeDtypeStruct((rows, columns), jnp.float32),
        in_specs=in_specs,
        out_specs=pl.BlockSpec(memory_space=pl.ANY),
        scratch_shapes=[pltpu.VMEM((rows, t), jnp.float32), pltpu.SemaphoreType.DMA],
        input_output_aliases=aliases,
        compiler_params=pltpu.CompilerParams(vmem_limit_bytes=VMEM_LIMIT),
        cost_estimate=pl.CostEstimate(
            flops=2 * n * rows * t * depth, bytes_accessed=2 * n * depth * (rows + t), transcendentals=0
        ),
        name="score_columns",
    )(*operands)


def after(array, *earlier):
    return lax.optimization_barrier((array, earlier))[0]


def exchange(held, distance):
    other = lax.ppermute(held, "z", [(i, i ^ distance) for i in range(NZ)])
    return jnp.concatenate([held, other], axis=0)


def local(query_features, inverse_gram, training_features, residual_weight):
    slots = lax.axis_index("z") ^ jnp.array(RELATIVE, jnp.int32)
    y = lax.axis_index("y").astype(jnp.int32)
    columns, lanes = training_features.shape
    rows, depth = inverse_gram.shape
    t = columns // NY

    folds = depth // lanes
    sent = pack(inverse_gram, training_features)
    got = lax.all_to_all(sent, "y", split_axis=0, concat_axis=0, tiled=True)
    gram_rows = got[:, :rows].reshape(NY * rows, depth)
    training = got[:, rows:].reshape(NY, t // folds, folds, lanes).transpose(2, 1, 0, 3)
    training = training.reshape(CHUNKS, 1, t // CHUNKS, NY * lanes)

    gram = lax.all_gather(gram_rows, ("x", "core"), axis=0)
    query = lax.all_gather(after(query_features, gram_rows), ("x", "core"), axis=0)
    weight = residual_weight[None, :]

    a, b = training[0], training[1]
    for distance in (4, 2, 1):
        a, b = exchange(a, distance), exchange(b, distance)
    a, b = kernel_matrix(slots, gram, a)[None], kernel_matrix(slots, gram, b)[None]
    for distance in (4, 2, 1):
        a, b = exchange(a, distance), exchange(b, distance)

    below_a, above_a = lax.ppermute(a, "y", UP), lax.ppermute(a, "y", DOWN)
    below_b, above_b = lax.ppermute(b, "y", UP), lax.ppermute(b, "y", DOWN)

    def scores(distance, chunks, out):
        return score_columns(slots, lax.rem(y + distance, NY)[None], query, chunks, weight, out)

    out = scores(0, (a, b), None)
    far = lax.ppermute(below_a, "y", UP), lax.ppermute(above_b, "y", DOWN)
    out = scores(1, (above_a, above_b), out)
    out = scores(NY - 1, (below_a, below_b), out)
    return scores(2, far, out)


def solution(mesh):
    fine = Mesh(mesh.devices.reshape(NZ, NY, 4, 2, 2), ("z", "y", "x", "core", "row"))
    pb, ta = ("z", "y"), ("x", "core")
    placed = (P(pb, ta), P(pb, ta), P(("row", *ta), pb), P(("row", *ta)))
    return jax.shard_map(
        local, mesh=fine, in_specs=placed, out_specs=P(pb, ("row", *ta)), check_vma=False
    )
```

time: 164 us -> 163 us (level)
  the two profiles are of different devices: /device:TPU:6 before, /device:TPU:192 now
where the time goes in v12:
time: 163 us; the launch traced here: 162 us
  starting transfers between devices  75.7 us (46%)
  waiting for transfers between devices  34.8 us (21%)
  blocking collectives  15.1 us (9%)
  Pallas kernels  14.9 us (9%)
  between operations  13.8 us (8%)
  local copies, waits for them, and re-layouts  7.29 us (4%)
    ppermute x12, starting transfers between devices, exchange(): other = lax.ppermute(held, 'z', [(i, i ^ distance) for i in range(NZ)])  54 us
    ppermute x12, waiting for transfers between devices, exchange(): other = lax.ppermute(held, 'z', [(i, i ^ distance) for i in range(NZ)])  21.2 us
    all_to_all x1, blocking collectives, local(): got = lax.all_to_all(sent, 'y', split_axis=0, concat_axis=0, tiled=True)  15.1 us
    pallas_call x4, Pallas kernels, score_columns(): pl.pallas_call(kernel, out_shape=jax.ShapeDtypeStruct((rows, columns), jn...  11 us
    ppermute x2, starting transfers between devices, local(): far = (lax.ppermute(below_a, 'y', UP), lax.ppermute(above_b, 'y', DOWN))  7.76 us
    ppermute x2, starting transfers between devices, local(): below_a, above_a = (lax.ppermute(a, 'y', UP), lax.ppermute(a, 'y', DOWN))  7.05 us
    ppermute x2, starting transfers between devices, local(): below_b, above_b = (lax.ppermute(b, 'y', UP), lax.ppermute(b, 'y', DOWN))  6.83 us
    ppermute x2, waiting for transfers between devices, local(): far = (lax.ppermute(below_a, 'y', UP), lax.ppermute(above_b, 'y', DOWN))  6.6 us
  transfers between devices with their start and end apart: 20, of which 12 were waited for; matrix products, arithmetic and copies ran while one was open for 0% of the time, Pallas kernels for 8%

profile of v12, /device:TPU:192, one launch (start us, length us, event | category | flops | bytes accessed | tf_op | source)
XLA Modules:
  0.0 162.1 jit_solution(17378070332244847869)
XLA Ops:
  6.5 0.0 all-gather.4.cloned.1.call-start
  6.5 0.9 copy-done.3
  7.5 0.9 copy-done.4
  8.4 0.1 pack.1
  8.4 15.1 %all_to_all.5 = bf16[4,160,512]{2,1,0:T(8,128)(2,1)S(1)} all-to-all(bf16[4,160,512]{2,1,0:T(8,128)(2,1)S(1)} %pack.1), channel_id=1, replica_groups=mesh['z'=8,'y'=4,'x'=4,'core'=2,'row'=2] {'y'}, dimensions={0} | all-to-all | bytes 1310720 | tf_op jit(solution)/shard_map/all_to_all | solution.py:124
  23.6 0.8 slice.18
  24.4 0.0 all-gather.4.cloned.1.call-update
  24.4 0.0 all-gather.6.cloned.1.call-start
  24.5 0.7 all-gather.6.cloned.1.call-update
  25.2 0.1 copy.12
  25.4 1.9 %collective-permute-start.8 = (bf16[1,64,512]{2,1,0:T(8,128)(2,1)S(1)}, bf16[1,64,512]{2,1,0:T(8,128)(2,1)S(1)}, u32[]{:S(2)}, u32[]{:S(2)}) collective-permute-start(bf16[1,64,512]{2,1,0:T(8,128)(2,1)S(1)} %squeeze.7), channel_id=1, source_target_pairs={{0,256},{64,320},{128,384},{192,448},{256,0},{320,64},{384,128},{4... | collective-permute-start | bytes 196616 | tf_op jit(solution)/shard_map/ppermute | solution.py:111
  27.4 7.8 %collective-permute-start = (bf16[1,64,512]{2,1,0:T(8,128)(2,1)S(1)}, bf16[1,64,512]{2,1,0:T(8,128)(2,1)S(1)}, u32[]{:S(2)}, u32[]{:S(2)}) collective-permute-start(bf16[1,64,512]{2,1,0:T(8,128)(2,1)S(1)} %squeeze.6), channel_id=1, source_target_pairs={{0,256},{64,320},{128,384},{192,448},{256,0},{320,64},{384,128},{4... | collective-permute-start | bytes 196616 | tf_op jit(solution)/shard_map/ppermute | solution.py:111
  35.2 4.1 %collective-permute-done.8 = bf16[1,64,512]{2,1,0:T(8,128)(2,1)S(1)} collective-permute-done((bf16[1,64,512]{2,1,0:T(8,128)(2,1)S(1)}, bf16[1,64,512]{2,1,0:T(8,128)(2,1)S(1)}, u32[]{:S(2)}, u32[]{:S(2)}) %collective-permute-start.8) | collective-permute-done | bytes 65568 | tf_op jit(solution)/shard_map/ppermute | solution.py:111
  39.4 1.9 %collective-permute-start.9 = (bf16[2,64,512]{2,1,0:T(8,128)(2,1)S(1)}, bf16[2,64,512]{2,1,0:T(8,128)(2,1)S(1)}, u32[]{:S(2)}, u32[]{:S(2)}) collective-permute-start(bf16[2,64,512]{2,1,0:T(8,128)(2,1)S(1)} %pad_maximum_fusion.10), channel_id=1, source_target_pairs={{0,128},{64,192},{128,0},{192,64},{256,384},{320,448},{384,256},{4... | collective-permute-start | bytes 393224 | tf_op jit(solution)/shard_map/ppermute | solution.py:111
  41.3 0.0 collective-permute-done
  41.4 4.8 %collective-permute-start.1 = (bf16[2,64,512]{2,1,0:T(8,128)(2,1)S(1)}, bf16[2,64,512]{2,1,0:T(8,128)(2,1)S(1)}, u32[]{:S(2)}, u32[]{:S(2)}) collective-permute-start(bf16[2,64,512]{2,1,0:T(8,128)(2,1)S(1)} %pad_maximum_fusion.8), channel_id=1, source_target_pairs={{0,128},{64,192},{128,0},{192,64},{256,384},{320,448},{384,256},{4... | collective-permute-start | bytes 393224 | tf_op jit(solution)/shard_map/ppermute | solution.py:111
  46.2 1.9 %collective-permute-done.9 = bf16[2,64,512]{2,1,0:T(8,128)(2,1)S(1)} collective-permute-done((bf16[2,64,512]{2,1,0:T(8,128)(2,1)S(1)}, bf16[2,64,512]{2,1,0:T(8,128)(2,1)S(1)}, u32[]{:S(2)}, u32[]{:S(2)}) %collective-permute-start.9) | collective-permute-done | bytes 131104 | tf_op jit(solution)/shard_map/ppermute | solution.py:111
  48.1 7.6 %collective-permute-start.10 = (bf16[4,64,512]{2,1,0:T(8,128)(2,1)S(1)}, bf16[4,64,512]{2,1,0:T(8,128)(2,1)S(1)}, u32[]{:S(2)}, u32[]{:S(2)}) collective-permute-start(bf16[4,64,512]{2,1,0:T(8,128)(2,1)S(1)} %pad_maximum_fusion.6), channel_id=1, source_target_pairs={{0,64},{64,0},{128,192},{192,128},{256,320},{320,256},{384,448},{4... | collective-permute-start | bytes 786440 | tf_op jit(solution)/shard_map/ppermute | solution.py:111
  55.7 0.0 collective-permute-done.1
  55.7 2.7 %collective-permute-start.2 = (bf16[4,64,512]{2,1,0:T(8,128)(2,1)S(1)}, bf16[4,64,512]{2,1,0:T(8,128)(2,1)S(1)}, u32[]{:S(2)}, u32[]{:S(2)}) collective-permute-start(bf16[4,64,512]{2,1,0:T(8,128)(2,1)S(1)} %pad_maximum_fusion.4), channel_id=1, source_target_pairs={{0,64},{64,0},{128,192},{192,128},{256,320},{320,256},{384,448},{4... | collective-permute-start | bytes 786440 | tf_op jit(solution)/shard_map/ppermute | solution.py:111
  58.4 0.0 copy-done.6
  58.4 4.4 %collective-permute-done.10 = bf16[4,64,512]{2,1,0:T(8,128)(2,1)S(1)} collective-permute-done((bf16[4,64,512]{2,1,0:T(8,128)(2,1)S(1)}, bf16[4,64,512]{2,1,0:T(8,128)(2,1)S(1)}, u32[]{:S(2)}, u32[]{:S(2)}) %collective-permute-start.10) | collective-permute-done | bytes 262176 | tf_op jit(solution)/shard_map/ppermute | solution.py:111
  62.8 0.1 pad_maximum_fusion.2.training_ref
  62.8 1.8 %all-gather.4.cloned.1.call-done.gram_ref = bf16[8,512,512]{2,1,0:T(8,128)(2,1)} async-done(((bf16[1,512,512]{2,1,0:T(8,128)(2,1)}), bf16[8,512,512]{2,1,0:T(8,128)(2,1)}) %all-gather.4.cloned.1.call-update) | async-done | bytes 4194320 | tf_op jit(solution)/shard_map/all_gather | solution.py:129
  64.6 2.2 %copy-done.2 = bf16[8,512,512]{2,1,0:T(8,128)(2,1)S(1)} copy-done((bf16[8,512,512]{2,1,0:T(8,128)(2,1)S(1)}, bf16[8,512,512]{2,1,0:T(8,128)(2,1)}, u32[]{:S(2)}) %copy-start.2) | copy-done | bytes 4194328
  66.8 1.9 %kernel_matrix.3 = bf16[64,512]{1,0:T(8,128)(2,1)S(1)} custom-call(s32[8]{0:T(128)S(1)} %broadcast_xor_fusion.slots, bf16[8,512,512]{2,1,0:T(8,128)(2,1)S(1)} %copy-done.2, bf16[8,64,512]{2,1,0:T(8,128)(2,1)S(1)} %pad_maximum_fusion.2.training_ref), custom_call_target="tpu_custom_call" | custom-call | flops 268435456 | bytes 4718592 | tf_op jit(solution)/shard_map/kernel_matrix/pallas_call | solution.py:49
  68.7 2.1 %collective-permute-start.11 = (bf16[1,64,512]{2,1,0:T(8,128)(2,1)S(1)}, bf16[1,64,512]{2,1,0:T(8,128)(2,1)S(1)}, u32[]{:S(2)}, u32[]{:S(2)}) collective-permute-start(bf16[1,64,512]{2,1,0:T(8,128)(2,1)S(1)} %bitcast.16), channel_id=1, source_target_pairs={{0,256},{64,320},{128,384},{192,448},{256,0},{320,64},{384,128},{4... | collective-permute-start | bytes 196616 | tf_op jit(solution)/shard_map/ppermute | solution.py:111
  70.8 0.0 collective-permute-done.2
  70.8 0.1 pad_maximum_fusion.training_ref
  70.9 0.0 copy-start.5
  70.9 1.9 %kernel_matrix.2 = bf16[64,512]{1,0:T(8,128)(2,1)S(1)} custom-call(s32[8]{0:T(128)S(1)} %broadcast_xor_fusion.slots, bf16[8,512,512]{2,1,0:T(8,128)(2,1)S(1)} %copy-done.2, bf16[8,64,512]{2,1,0:T(8,128)(2,1)S(1)} %pad_maximum_fusion.training_ref), custom_call_target="tpu_custom_call" | custom-call | flops 268435456 | bytes 4718592 | tf_op jit(solution)/shard_map/kernel_matrix/pallas_call | solution.py:49
  72.8 7.6 %collective-permute-start.3 = (bf16[1,64,512]{2,1,0:T(8,128)(2,1)S(1)}, bf16[1,64,512]{2,1,0:T(8,128)(2,1)S(1)}, u32[]{:S(2)}, u32[]{:S(2)}) collective-permute-start(bf16[1,64,512]{2,1,0:T(8,128)(2,1)S(1)} %bitcast.20), channel_id=1, source_target_pairs={{0,256},{64,320},{128,384},{192,448},{256,0},{320,64},{384,128},{4... | collective-permute-start | bytes 196616 | tf_op jit(solution)/shard_map/ppermute | solution.py:111
  80.5 3.9 %collective-permute-done.11 = bf16[1,64,512]{2,1,0:T(8,128)(2,1)S(1)} collective-permute-done((bf16[1,64,512]{2,1,0:T(8,128)(2,1)S(1)}, bf16[1,64,512]{2,1,0:T(8,128)(2,1)S(1)}, u32[]{:S(2)}, u32[]{:S(2)}) %collective-permute-start.11) | collective-permute-done | bytes 65568 | tf_op jit(solution)/shard_map/ppermute | solution.py:111
  84.4 1.9 %collective-permute-start.12 = (bf16[2,64,512]{2,1,0:T(8,128)(2,1)S(1)}, bf16[2,64,512]{2,1,0:T(8,128)(2,1)S(1)}, u32[]{:S(2)}, u32[]{:S(2)}) collective-permute-start(bf16[2,64,512]{2,1,0:T(8,128)(2,1)S(1)} %pad_maximum_fusion.11), channel_id=1, source_target_pairs={{0,128},{64,192},{128,0},{192,64},{256,384},{320,448},{384,256},{4... | collective-permute-start | bytes 393224 | tf_op jit(solution)/shard_map/ppermute | solution.py:111
  86.3 0.0 collective-permute-done.3
  86.3 4.8 %collective-permute-start.4 = (bf16[2,64,512]{2,1,0:T(8,128)(2,1)S(1)}, bf16[2,64,512]{2,1,0:T(8,128)(2,1)S(1)}, u32[]{:S(2)}, u32[]{:S(2)}) collective-permute-start(bf16[2,64,512]{2,1,0:T(8,128)(2,1)S(1)} %pad_maximum_fusion.9), channel_id=1, source_target_pairs={{0,128},{64,192},{128,0},{192,64},{256,384},{320,448},{384,256},{4... | collective-permute-start | bytes 393224 | tf_op jit(solution)/shard_map/ppermute | solution.py:111
  91.2 2.3 %collective-permute-done.12 = bf16[2,64,512]{2,1,0:T(8,128)(2,1)S(1)} collective-permute-done((bf16[2,64,512]{2,1,0:T(8,128)(2,1)S(1)}, bf16[2,64,512]{2,1,0:T(8,128)(2,1)S(1)}, u32[]{:S(2)}, u32[]{:S(2)}) %collective-permute-start.12) | collective-permute-done | bytes 131104 | tf_op jit(solution)/shard_map/ppermute | solution.py:111
  93.5 8.1 %collective-permute-start.13 = (bf16[4,64,512]{2,1,0:T(8,128)(2,1)S(1)}, bf16[4,64,512]{2,1,0:T(8,128)(2,1)S(1)}, u32[]{:S(2)}, u32[]{:S(2)}) collective-permute-start(bf16[4,64,512]{2,1,0:T(8,128)(2,1)S(1)} %pad_maximum_fusion.7), channel_id=1, source_target_pairs={{0,64},{64,0},{128,192},{192,128},{256,320},{320,256},{384,448},{4... | collective-permute-start | bytes 786440 | tf_op jit(solution)/shard_map/ppermute | solution.py:111
  101.6 0.0 collective-permute-done.4
  101.7 2.7 %collective-permute-start.5 = (bf16[4,64,512]{2,1,0:T(8,128)(2,1)S(1)}, bf16[4,64,512]{2,1,0:T(8,128)(2,1)S(1)}, u32[]{:S(2)}, u32[]{:S(2)}) collective-permute-start(bf16[4,64,512]{2,1,0:T(8,128)(2,1)S(1)} %pad_maximum_fusion.5), channel_id=1, source_target_pairs={{0,64},{64,0},{128,192},{192,128},{256,320},{320,256},{384,448},{4... | collective-permute-start | bytes 786440 | tf_op jit(solution)/shard_map/ppermute | solution.py:111
  104.3 4.4 %collective-permute-done.13 = bf16[4,64,512]{2,1,0:T(8,128)(2,1)S(1)} collective-permute-done((bf16[4,64,512]{2,1,0:T(8,128)(2,1)S(1)}, bf16[4,64,512]{2,1,0:T(8,128)(2,1)S(1)}, u32[]{:S(2)}, u32[]{:S(2)}) %collective-permute-start.13) | collective-permute-done | bytes 262176 | tf_op jit(solution)/shard_map/ppermute | solution.py:111
  108.7 0.1 pad_maximum_fusion.3.refs_1_
  108.8 4.6 %collective-permute-start.14 = (bf16[8,64,512]{2,1,0:T(8,128)(2,1)S(1)}, bf16[8,64,512]{2,1,0:T(8,128)(2,1)S(1)}, u32[]{:S(2)}, u32[]{:S(2)}) collective-permute-start(bf16[8,64,512]{2,1,0:T(8,128)(2,1)S(1)} %pad_maximum_fusion.3.refs_1_), channel_id=1, source_target_pairs={{0,48},{16,0},{32,16},{48,32},{1,49},{17,1},{33,17},{49,33},{2,50}... | collective-permute-start | bytes 1572872 | tf_op jit(solution)/shard_map/ppermute | solution.py:141
  113.4 0.3 collective-permute-done.5
  113.7 0.1 pad_maximum_fusion.1.refs_0_
  113.8 3.4 %collective-permute-start.6 = (bf16[8,64,512]{2,1,0:T(8,128)(2,1)S(1)}, bf16[8,64,512]{2,1,0:T(8,128)(2,1)S(1)}, u32[]{:S(2)}, u32[]{:S(2)}) collective-permute-start(bf16[8,64,512]{2,1,0:T(8,128)(2,1)S(1)} %pad_maximum_fusion.1.refs_0_), channel_id=1, source_target_pairs={{0,16},{16,32},{32,48},{48,0},{1,17},{17,33},{33,49},{49,1},{2,18}... | collective-permute-start | bytes 1572872 | tf_op jit(solution)/shard_map/ppermute | solution.py:140
  117.2 3.7 %collective-permute-start.17 = (bf16[8,64,512]{2,1,0:T(8,128)(2,1)S(1)}, bf16[8,64,512]{2,1,0:T(8,128)(2,1)}, u32[]{:S(2)}, u32[]{:S(2)}) collective-permute-start(bf16[8,64,512]{2,1,0:T(8,128)(2,1)S(1)} %pad_maximum_fusion.1.refs_0_), channel_id=1, source_target_pairs={{0,48},{16,0},{32,16},{48,32},{1,49},{17,1},{33,17},{49,33},{2,50}... | collective-permute-start | bytes 1572872 | tf_op jit(solution)/shard_map/ppermute | solution.py:140
  120.9 2.2 %collective-permute-start.16 = (bf16[8,64,512]{2,1,0:T(8,128)(2,1)S(1)}, bf16[8,64,512]{2,1,0:T(8,128)(2,1)}, u32[]{:S(2)}, u32[]{:S(2)}) collective-permute-start(bf16[8,64,512]{2,1,0:T(8,128)(2,1)S(1)} %pad_maximum_fusion.3.refs_1_), channel_id=1, source_target_pairs={{0,16},{16,32},{32,48},{48,0},{1,17},{17,33},{33,49},{49,1},{2,18}... | collective-permute-start | bytes 1572872 | tf_op jit(solution)/shard_map/ppermute | solution.py:141
  123.1 2.7 %collective-permute-done.14.refs_1_ = bf16[8,64,512]{2,1,0:T(8,128)(2,1)S(1)} collective-permute-done((bf16[8,64,512]{2,1,0:T(8,128)(2,1)S(1)}, bf16[8,64,512]{2,1,0:T(8,128)(2,1)S(1)}, u32[]{:S(2)}, u32[]{:S(2)}) %collective-permute-start.14) | collective-permute-done | bytes 524320 | tf_op jit(solution)/shard_map/ppermute | solution.py:141
  125.8 5.6 %collective-permute-start.15 = (bf16[8,64,512]{2,1,0:T(8,128)(2,1)S(1)}, bf16[8,64,512]{2,1,0:T(8,128)(2,1)S(1)}, u32[]{:S(2)}, u32[]{:S(2)}) collective-permute-start(bf16[8,64,512]{2,1,0:T(8,128)(2,1)S(1)} %collective-permute-done.14.refs_1_), channel_id=1, source_target_pairs={{0,48},{16,0},{32,16},{48,32},{1,49},{17,1},{33,17},{49,33},{2,50}... | collective-permute-start | bytes 1572872 | tf_op jit(solution)/shard_map/ppermute | solution.py:147
  131.4 0.4 collective-permute-done.6.refs_0_
  131.8 2.2 %collective-permute-start.7 = (bf16[8,64,512]{2,1,0:T(8,128)(2,1)S(1)}, bf16[8,64,512]{2,1,0:T(8,128)(2,1)S(1)}, u32[]{:S(2)}, u32[]{:S(2)}) collective-permute-start(bf16[8,64,512]{2,1,0:T(8,128)(2,1)S(1)} %collective-permute-done.6.refs_0_), channel_id=1, source_target_pairs={{0,16},{16,32},{32,48},{48,0},{1,17},{17,33},{33,49},{49,1},{2,18}... | collective-permute-start | bytes 1572872 | tf_op jit(solution)/shard_map/ppermute | solution.py:147
  133.9 0.0 all-gather.6.cloned.1.call-done
  134.0 0.0 copy-done.5
  134.0 0.0 copy-start
  134.0 2.2 %copy-done = bf16[4096,512]{1,0:T(8,128)(2,1)S(1)} copy-done((bf16[4096,512]{1,0:T(8,128)(2,1)S(1)}, bf16[4096,512]{1,0:T(8,128)(2,1)}, u32[]{:S(2)}) %copy-start) | copy-done | bytes 4194328
  136.2 2.5 %score_columns.4.refs_2_ = f32[512,512]{1,0:T(8,128)} custom-call(s32[8]{0:T(128)S(1)} %broadcast_xor_fusion.slots, s32[1]{0:T(128)} %bitcast.9.place, bf16[8,512,512]{2,1,0:T(8,128)(2,1)S(1)} %bitcast.12, f32[1,512]{1,0:T(1,128)S(1)} %bitcast.24, bf16[8,64,512]{2,1,0:T(8,128)(2,1)S(1)} %pad_maximum_fusion.1.refs_0_, ...), custom_call_target="tpu_custom_call" | custom-call | flops 536870912 | bytes 5242880 | tf_op jit(solution)/shard_map/score_columns/pallas_call | solution.py:91
  138.7 0.0 collective-permute-done.17.refs_0_
  138.7 3.0 %score_columns.5.refs_2_ = f32[512,512]{1,0:T(8,128)} custom-call(s32[8]{0:T(128)S(1)} %broadcast_xor_fusion.slots, s32[1]{0:T(128)} %bitcast.8.place, bf16[8,512,512]{2,1,0:T(8,128)(2,1)S(1)} %bitcast.13, f32[1,512]{1,0:T(1,128)S(1)} %bitcast.25, bf16[8,64,512]{2,1,0:T(8,128)(2,1)} %collective-permute-done.17.refs_0_, ...), custom_call_target="tpu_custom_call", output_to_operand_aliasing={{}: (6, {})} | custom-call | flops 536870912 | bytes 5242880 | tf_op jit(solution)/shard_map/score_columns/pallas_call | solution.py:91
  141.7 1.4 collective-permute-done.16.refs_1_
  143.1 3.0 %score_columns.6.refs_2_ = f32[512,512]{1,0:T(8,128)} custom-call(s32[8]{0:T(128)S(1)} %broadcast_xor_fusion.slots, s32[1]{0:T(128)} %bitcast.7.place, bf16[8,512,512]{2,1,0:T(8,128)(2,1)S(1)} %bitcast.14, f32[1,512]{1,0:T(1,128)S(1)} %bitcast.26, bf16[8,64,512]{2,1,0:T(8,128)(2,1)S(1)} %collective-permute-done.6.refs_0_, ...), custom_call_target="tpu_custom_call", output_to_operand_aliasing={{}: (6, {})} | custom-call | flops 536870912 | bytes 5242880 | tf_op jit(solution)/shard_map/score_columns/pallas_call | solution.py:91
  146.1 0.0 collective-permute-done.15.refs_1_
  146.1 6.6 %collective-permute-done.7.refs_0_ = bf16[8,64,512]{2,1,0:T(8,128)(2,1)S(1)} collective-permute-done((bf16[8,64,512]{2,1,0:T(8,128)(2,1)S(1)}, bf16[8,64,512]{2,1,0:T(8,128)(2,1)S(1)}, u32[]{:S(2)}, u32[]{:S(2)}) %collective-permute-start.7) | collective-permute-done | bytes 524320 | tf_op jit(solution)/shard_map/ppermute | solution.py:147
  152.7 2.5 %score_columns.7 = f32[512,512]{1,0:T(8,128)} custom-call(s32[8]{0:T(128)S(1)} %broadcast_xor_fusion.slots, s32[1]{0:T(128)} %bitcast.place, bf16[8,512,512]{2,1,0:T(8,128)(2,1)S(1)} %bitcast.15, f32[1,512]{1,0:T(1,128)S(1)} %bitcast.27, bf16[8,64,512]{2,1,0:T(8,128)(2,1)S(1)} %collective-permute-done.7.refs_0_, ...), custom_call_target="tpu_custom_call", output_to_operand_aliasing={{}: (6, {})} | custom-call | flops 536870912 | bytes 5242880 | tf_op jit(solution)/shard_map/score_columns/pallas_call | solution.py:91
  (20 shorter events, 0.3 us)
Async XLA Ops:
  6.5 51.9 %copy-start.6 = (s32[8]{0:T(128)S(1)}, s32[8]{0:T(128)}, u32[]{:S(2)}) copy-start(s32[8]{0:T(128)} %constant.30.clone) | copy-start | bytes 100
  6.5 58.1 %all-gather.4.cloned.1.call-start = ((), (), s32[]{:S(2)}) async-start(), calls=%async_computation.1 | async-start | bytes 4718592 | tf_op jit(solution)/shard_map/all_gather | solution.py:129
  6.5 0.9 copy-start.3
  7.5 0.9 copy-start.4
  24.4 109.5 %all-gather.6.cloned.1.call-start = ((), (), s32[]{:S(2)}) async-start(), calls=%async_computation.2 | async-start | bytes 4718592 | tf_op jit(solution)/shard_map/all_gather | solution.py:130
  25.4 14.0 %collective-permute-start.8 = (bf16[1,64,512]{2,1,0:T(8,128)(2,1)S(1)}, bf16[1,64,512]{2,1,0:T(8,128)(2,1)S(1)}, u32[]{:S(2)}, u32[]{:S(2)}) collective-permute-start(bf16[1,64,512]{2,1,0:T(8,128)(2,1)S(1)} %squeeze.7), channel_id=1, source_target_pairs={{0,256},{64,320},{128,384},{192,448},{256,0},{320,64},{384,128},{4... | collective-permute-start | bytes 196616 | tf_op jit(solution)/shard_map/ppermute | solution.py:111
  27.4 13.9 %collective-permute-start = (bf16[1,64,512]{2,1,0:T(8,128)(2,1)S(1)}, bf16[1,64,512]{2,1,0:T(8,128)(2,1)S(1)}, u32[]{:S(2)}, u32[]{:S(2)}) collective-permute-start(bf16[1,64,512]{2,1,0:T(8,128)(2,1)S(1)} %squeeze.6), channel_id=1, source_target_pairs={{0,256},{64,320},{128,384},{192,448},{256,0},{320,64},{384,128},{4... | collective-permute-start | bytes 196616 | tf_op jit(solution)/shard_map/ppermute | solution.py:111
  39.4 8.7 %collective-permute-start.9 = (bf16[2,64,512]{2,1,0:T(8,128)(2,1)S(1)}, bf16[2,64,512]{2,1,0:T(8,128)(2,1)S(1)}, u32[]{:S(2)}, u32[]{:S(2)}) collective-permute-start(bf16[2,64,512]{2,1,0:T(8,128)(2,1)S(1)} %pad_maximum_fusion.10), channel_id=1, source_target_pairs={{0,128},{64,192},{128,0},{192,64},{256,384},{320,448},{384,256},{4... | collective-permute-start | bytes 393224 | tf_op jit(solution)/shard_map/ppermute | solution.py:111
  41.4 14.3 %collective-permute-start.1 = (bf16[2,64,512]{2,1,0:T(8,128)(2,1)S(1)}, bf16[2,64,512]{2,1,0:T(8,128)(2,1)S(1)}, u32[]{:S(2)}, u32[]{:S(2)}) collective-permute-start(bf16[2,64,512]{2,1,0:T(8,128)(2,1)S(1)} %pad_maximum_fusion.8), channel_id=1, source_target_pairs={{0,128},{64,192},{128,0},{192,64},{256,384},{320,448},{384,256},{4... | collective-permute-start | bytes 393224 | tf_op jit(solution)/shard_map/ppermute | solution.py:111
  48.1 14.7 %collective-permute-start.10 = (bf16[4,64,512]{2,1,0:T(8,128)(2,1)S(1)}, bf16[4,64,512]{2,1,0:T(8,128)(2,1)S(1)}, u32[]{:S(2)}, u32[]{:S(2)}) collective-permute-start(bf16[4,64,512]{2,1,0:T(8,128)(2,1)S(1)} %pad_maximum_fusion.6), channel_id=1, source_target_pairs={{0,64},{64,0},{128,192},{192,128},{256,320},{320,256},{384,448},{4... | collective-permute-start | bytes 786440 | tf_op jit(solution)/shard_map/ppermute | solution.py:111
  55.7 15.1 %collective-permute-start.2 = (bf16[4,64,512]{2,1,0:T(8,128)(2,1)S(1)}, bf16[4,64,512]{2,1,0:T(8,128)(2,1)S(1)}, u32[]{:S(2)}, u32[]{:S(2)}) collective-permute-start(bf16[4,64,512]{2,1,0:T(8,128)(2,1)S(1)} %pad_maximum_fusion.4), channel_id=1, source_target_pairs={{0,64},{64,0},{128,192},{192,128},{256,320},{320,256},{384,448},{4... | collective-permute-start | bytes 786440 | tf_op jit(solution)/shard_map/ppermute | solution.py:111
  64.6 2.2 %copy-start.2 = (bf16[8,512,512]{2,1,0:T(8,128)(2,1)S(1)}, bf16[8,512,512]{2,1,0:T(8,128)(2,1)}, u32[]{:S(2)}) copy-start(bf16[8,512,512]{2,1,0:T(8,128)(2,1)} %all-gather.4.cloned.1.call-done.gram_ref) | copy-start | bytes 12582916
  68.7 15.6 %collective-permute-start.11 = (bf16[1,64,512]{2,1,0:T(8,128)(2,1)S(1)}, bf16[1,64,512]{2,1,0:T(8,128)(2,1)S(1)}, u32[]{:S(2)}, u32[]{:S(2)}) collective-permute-start(bf16[1,64,512]{2,1,0:T(8,128)(2,1)S(1)} %bitcast.16), channel_id=1, source_target_pairs={{0,256},{64,320},{128,384},{192,448},{256,0},{320,64},{384,128},{4... | collective-permute-start | bytes 196616 | tf_op jit(solution)/shard_map/ppermute | solution.py:111
  70.9 63.1 %copy-start.5 = (f32[512]{0:T(512)S(1)}, f32[512]{0:T(512)}, u32[]{:S(2)}) copy-start(f32[512]{0:T(512)} %param.8) | copy-start | bytes 6148
  72.8 13.5 %collective-permute-start.3 = (bf16[1,64,512]{2,1,0:T(8,128)(2,1)S(1)}, bf16[1,64,512]{2,1,0:T(8,128)(2,1)S(1)}, u32[]{:S(2)}, u32[]{:S(2)}) collective-permute-start(bf16[1,64,512]{2,1,0:T(8,128)(2,1)S(1)} %bitcast.20), channel_id=1, source_target_pairs={{0,256},{64,320},{128,384},{192,448},{256,0},{320,64},{384,128},{4... | collective-permute-start | bytes 196616 | tf_op jit(solution)/shard_map/ppermute | solution.py:111
  84.4 9.1 %collective-permute-start.12 = (bf16[2,64,512]{2,1,0:T(8,128)(2,1)S(1)}, bf16[2,64,512]{2,1,0:T(8,128)(2,1)S(1)}, u32[]{:S(2)}, u32[]{:S(2)}) collective-permute-start(bf16[2,64,512]{2,1,0:T(8,128)(2,1)S(1)} %pad_maximum_fusion.11), channel_id=1, source_target_pairs={{0,128},{64,192},{128,0},{192,64},{256,384},{320,448},{384,256},{4... | collective-permute-start | bytes 393224 | tf_op jit(solution)/shard_map/ppermute | solution.py:111
  86.3 15.3 %collective-permute-start.4 = (bf16[2,64,512]{2,1,0:T(8,128)(2,1)S(1)}, bf16[2,64,512]{2,1,0:T(8,128)(2,1)S(1)}, u32[]{:S(2)}, u32[]{:S(2)}) collective-permute-start(bf16[2,64,512]{2,1,0:T(8,128)(2,1)S(1)} %pad_maximum_fusion.9), channel_id=1, source_target_pairs={{0,128},{64,192},{128,0},{192,64},{256,384},{320,448},{384,256},{4... | collective-permute-start | bytes 393224 | tf_op jit(solution)/shard_map/ppermute | solution.py:111
  93.5 15.2 %collective-permute-start.13 = (bf16[4,64,512]{2,1,0:T(8,128)(2,1)S(1)}, bf16[4,64,512]{2,1,0:T(8,128)(2,1)S(1)}, u32[]{:S(2)}, u32[]{:S(2)}) collective-permute-start(bf16[4,64,512]{2,1,0:T(8,128)(2,1)S(1)} %pad_maximum_fusion.7), channel_id=1, source_target_pairs={{0,64},{64,0},{128,192},{192,128},{256,320},{320,256},{384,448},{4... | collective-permute-start | bytes 786440 | tf_op jit(solution)/shard_map/ppermute | solution.py:111
  101.7 12.1 %collective-permute-start.5 = (bf16[4,64,512]{2,1,0:T(8,128)(2,1)S(1)}, bf16[4,64,512]{2,1,0:T(8,128)(2,1)S(1)}, u32[]{:S(2)}, u32[]{:S(2)}) collective-permute-start(bf16[4,64,512]{2,1,0:T(8,128)(2,1)S(1)} %pad_maximum_fusion.5), channel_id=1, source_target_pairs={{0,64},{64,0},{128,192},{192,128},{256,320},{320,256},{384,448},{4... | collective-permute-start | bytes 786440 | tf_op jit(solution)/shard_map/ppermute | solution.py:111
  108.8 17.0 %collective-permute-start.14 = (bf16[8,64,512]{2,1,0:T(8,128)(2,1)S(1)}, bf16[8,64,512]{2,1,0:T(8,128)(2,1)S(1)}, u32[]{:S(2)}, u32[]{:S(2)}) collective-permute-start(bf16[8,64,512]{2,1,0:T(8,128)(2,1)S(1)} %pad_maximum_fusion.3.refs_1_), channel_id=1, source_target_pairs={{0,48},{16,0},{32,16},{48,32},{1,49},{17,1},{33,17},{49,33},{2,50}... | collective-permute-start | bytes 1572872 | tf_op jit(solution)/shard_map/ppermute | solution.py:141
  113.8 18.0 %collective-permute-start.6 = (bf16[8,64,512]{2,1,0:T(8,128)(2,1)S(1)}, bf16[8,64,512]{2,1,0:T(8,128)(2,1)S(1)}, u32[]{:S(2)}, u32[]{:S(2)}) collective-permute-start(bf16[8,64,512]{2,1,0:T(8,128)(2,1)S(1)} %pad_maximum_fusion.1.refs_0_), channel_id=1, source_target_pairs={{0,16},{16,32},{32,48},{48,0},{1,17},{17,33},{33,49},{49,1},{2,18}... | collective-permute-start | bytes 1572872 | tf_op jit(solution)/shard_map/ppermute | solution.py:140
  117.2 21.5 %collective-permute-start.17 = (bf16[8,64,512]{2,1,0:T(8,128)(2,1)S(1)}, bf16[8,64,512]{2,1,0:T(8,128)(2,1)}, u32[]{:S(2)}, u32[]{:S(2)}) collective-permute-start(bf16[8,64,512]{2,1,0:T(8,128)(2,1)S(1)} %pad_maximum_fusion.1.refs_0_), channel_id=1, source_target_pairs={{0,48},{16,0},{32,16},{48,32},{1,49},{17,1},{33,17},{49,33},{2,50}... | collective-permute-start | bytes 1572872 | tf_op jit(solution)/shard_map/ppermute | solution.py:140
  120.9 22.2 %collective-permute-start.16 = (bf16[8,64,512]{2,1,0:T(8,128)(2,1)S(1)}, bf16[8,64,512]{2,1,0:T(8,128)(2,1)}, u32[]{:S(2)}, u32[]{:S(2)}) collective-permute-start(bf16[8,64,512]{2,1,0:T(8,128)(2,1)S(1)} %pad_maximum_fusion.3.refs_1_), channel_id=1, source_target_pairs={{0,16},{16,32},{32,48},{48,0},{1,17},{17,33},{33,49},{49,1},{2,18}... | collective-permute-start | bytes 1572872 | tf_op jit(solution)/shard_map/ppermute | solution.py:141
  125.8 20.4 %collective-permute-start.15 = (bf16[8,64,512]{2,1,0:T(8,128)(2,1)S(1)}, bf16[8,64,512]{2,1,0:T(8,128)(2,1)S(1)}, u32[]{:S(2)}, u32[]{:S(2)}) collective-permute-start(bf16[8,64,512]{2,1,0:T(8,128)(2,1)S(1)} %collective-permute-done.14.refs_1_), channel_id=1, source_target_pairs={{0,48},{16,0},{32,16},{48,32},{1,49},{17,1},{33,17},{49,33},{2,50}... | collective-permute-start | bytes 1572872 | tf_op jit(solution)/shard_map/ppermute | solution.py:147
  131.8 21.0 %collective-permute-start.7 = (bf16[8,64,512]{2,1,0:T(8,128)(2,1)S(1)}, bf16[8,64,512]{2,1,0:T(8,128)(2,1)S(1)}, u32[]{:S(2)}, u32[]{:S(2)}) collective-permute-start(bf16[8,64,512]{2,1,0:T(8,128)(2,1)S(1)} %collective-permute-done.6.refs_0_), channel_id=1, source_target_pairs={{0,16},{16,32},{32,48},{48,0},{1,17},{17,33},{33,49},{49,1},{2,18}... | collective-permute-start | bytes 1572872 | tf_op jit(solution)/shard_map/ppermute | solution.py:147
  134.0 2.2 %copy-start = (bf16[4096,512]{1,0:T(8,128)(2,1)S(1)}, bf16[4096,512]{1,0:T(8,128)(2,1)}, u32[]{:S(2)}) copy-start(bf16[4096,512]{1,0:T(8,128)(2,1)} %all-gather.6.cloned.1.call-done) | copy-start | bytes 12582916
  136.2 2.5 %copy-start.1 = (bf16[4096,512]{1,0:T(8,128)(2,1)S(1)}, bf16[4096,512]{1,0:T(8,128)(2,1)}, u32[]{:S(2)}) copy-start(bf16[4096,512]{1,0:T(8,128)(2,1)} %all-gather.6.cloned.1.call-done) | copy-start | bytes 12582916
Sparse Core Ops, SparseCore 0:
  24.5 40.0 all-gather.3
  66.7 39.7 all-gather.5

commit v13 on v12

v13 whole, which is shorter than its diff:
```python
import jax
import jax.numpy as jnp
from jax import lax
from jax.experimental import pallas as pl
from jax.experimental.pallas import tpu as pltpu
from jax.sharding import Mesh, PartitionSpec as P

NZ, NY, CHUNKS = 8, 4, 2
NT_DIMS = (((1,), (1,)), ((), ()))
RELATIVE = (0, 4, 2, 6, 1, 5, 3, 7)
VMEM_LIMIT = 16 * 1024 * 1024
UP = [(i, (i + 1) % NY) for i in range(NY)]
DOWN = [(i, (i - 1) % NY) for i in range(NY)]


def pack(inverse_gram, training_features):
    rows, depth = inverse_gram.shape
    columns, lanes = training_features.shape
    t, folds = columns // NY, depth // lanes
    each = t // folds

    def kernel(gram_ref, training_ref, out_ref):
        for k in range(NY):
            out_ref[k, :rows] = gram_ref[...]
            for f in range(folds):
                first = k * t + f * each
                out_ref[k, rows:, f * lanes : (f + 1) * lanes] = training_ref[first : first + each]

    return pl.pallas_call(
        kernel,
        out_shape=jax.ShapeDtypeStruct((NY, rows + each, depth), jnp.bfloat16),
        in_specs=[pl.BlockSpec(memory_space=pltpu.VMEM)] * 2,
        out_specs=pl.BlockSpec(memory_space=pltpu.VMEM),
        compiler_params=pltpu.CompilerParams(vmem_limit_bytes=VMEM_LIMIT),
        name="pack",
    )(inverse_gram, training_features)


def kernel_matrix(slots, gram, chunks):
    n, each, depth = chunks[0].shape
    t, rows = each * len(chunks), gram.shape[1]

    def kernel(slots, gram_ref, *refs):
        chunk_refs, out_ref = refs[:-1], refs[-1]
        total = jnp.zeros((t, rows), jnp.float32)
        for s in range(n):
            block = jnp.concatenate([ref[s] for ref in chunk_refs], axis=0)
            total += lax.dot_general(block, gram_ref[slots[s]], NT_DIMS, preferred_element_type=jnp.float32)
        out_ref[...] = total.astype(out_ref.dtype)

    return pl.pallas_call(
        kernel,
        out_shape=jax.ShapeDtypeStruct((t, rows), jnp.bfloat16),
        in_specs=[pl.BlockSpec(memory_space=pltpu.SMEM)] + [pl.BlockSpec(memory_space=pltpu.VMEM)] * (1 + len(chunks)),
        out_specs=pl.BlockSpec(memory_space=pltpu.VMEM),
        compiler_params=pltpu.CompilerParams(vmem_limit_bytes=VMEM_LIMIT),
        cost_estimate=pl.CostEstimate(
            flops=2 * n * rows * t * depth, bytes_accessed=2 * n * depth * (rows + t), transcendentals=0
        ),
        name="kernel_matrix",
    )(slots, gram, *chunks)


def partial_scores(slots, query, blocks):
    _, rows, depth = query.shape
    t = blocks[0][0].shape[1]
    n = sum(array.shape[0] for array in blocks[0])
    width = t * len(blocks)
    arrays = [array for block in blocks for array in block]

    def kernel(slots, query_ref, *refs):
        array_refs, outs = list(refs[: len(arrays)]), refs[len(arrays) :]
        pieces = []
        for block in blocks:
            pieces.append([])
            for array in block:
                ref = array_refs.pop(0)
                pieces[-1].extend((ref, s) for s in range(array.shape[0]))
        for s in range(n):
            right = jnp.concatenate([piece[s][0][piece[s][1]] for piece in pieces], axis=0)
            for flip, out_ref in enumerate(outs):
                product = lax.dot_general(query_ref[slots[s] ^ flip], right, NT_DIMS, preferred_element_type=jnp.float32)
                out_ref[...] = product if s == 0 else out_ref[...] + product

    return pl.pallas_call(
        kernel,
        out_shape=[jax.ShapeDtypeStruct((rows, width), jnp.float32)] * 2,
        in_specs=[pl.BlockSpec(memory_space=pltpu.SMEM)] + [pl.BlockSpec(memory_space=pltpu.VMEM)] * (1 + len(arrays)),
        out_specs=[pl.BlockSpec(memory_space=pltpu.VMEM)] * 2,
        compiler_params=pltpu.CompilerParams(vmem_limit_bytes=VMEM_LIMIT),
        cost_estimate=pl.CostEstimate(
            flops=4 * n * rows * width * depth, bytes_accessed=2 * n * depth * (2 * rows + width), transcendentals=0
        ),
        name="partial_scores",
    )(slots, query, *arrays)


def finish(places, pairs, weight, out):
    columns = weight.shape[1]
    t = columns // NY
    rows = pairs[0][0].shape[0]
    count = places.shape[0]
    arrays = [array for pair in pairs for array in pair]

    def kernel(places, weight_ref, *refs):
        out_ref, total, sent = refs[-3:]
        sources = [(k, j) for k, pair in enumerate(pairs) for j in range(pair[0].shape[1] // t)]
        copies = []
        for p, (k, j) in enumerate(sources):
            span = pl.ds(pl.multiple_of(places[p] * t, t), t)
            mine, theirs = refs[2 * k][:, j * t : (j + 1) * t], refs[2 * k + 1][:, j * t : (j + 1) * t]
            total[p] = (mine + theirs) * weight_ref[:, span]
            copies.append(pltpu.make_async_copy(total.at[p], out_ref.at[:, span], sent.at[p]))
            copies[-1].start()
        for copy in copies:
            copy.wait()

    operands = [places, weight, *arrays]
    in_specs = [pl.BlockSpec(memory_space=pltpu.SMEM)] + [pl.BlockSpec(memory_space=pltpu.VMEM)] * (1 + len(arrays))
    aliases = {}
    if out is not None:
        in_specs.append(pl.BlockSpec(memory_space=pl.ANY))
        aliases = {len(operands): 0}
        operands.append(out)
    return pl.pallas_call(
        kernel,
        out_shape=jax.ShapeDtypeStruct((rows, columns), jnp.float32),
        in_specs=in_specs,
        out_specs=pl.BlockSpec(memory_space=pl.ANY),
        scratch_shapes=[pltpu.VMEM((count, rows, t), jnp.float32), pltpu.SemaphoreType.DMA((count,))],
        input_output_aliases=aliases,
        compiler_params=pltpu.CompilerParams(vmem_limit_bytes=VMEM_LIMIT),
        cost_estimate=pl.CostEstimate(
            flops=2 * count * rows * t, bytes_accessed=12 * count * rows * t, transcendentals=0
        ),
        name="finish",
    )(*operands)


def after(array, *earlier):
    return lax.optimization_barrier((array, earlier))[0]


def swapped(held, distance):
    return lax.ppermute(held, "z", [(i, i ^ distance) for i in range(NZ)])


def exchange(held, distance):
    return jnp.concatenate([held, swapped(held, distance)], axis=0)


def local(query_features, inverse_gram, training_features, residual_weight):
    slots = lax.axis_index("z") ^ jnp.array(RELATIVE, jnp.int32)
    ta = ("x", "core")
    columns, lanes = training_features.shape
    rows, depth = inverse_gram.shape
    t = columns // NY

    folds = depth // lanes
    sent = pack(inverse_gram, training_features)
    got = lax.all_to_all(sent, "y", split_axis=0, concat_axis=0, tiled=True)
    gram_rows = got[:, :rows].reshape(NY * rows, depth)
    training = got[:, rows:].reshape(NY, t // folds, folds, lanes).transpose(2, 1, 0, 3)
    training = training.reshape(CHUNKS, 1, t // CHUNKS, NY * lanes)

    gram = lax.all_gather(gram_rows, ta, axis=0)

    parity = [(2 * z + c, 2 * z + c if c == z % 2 else 2 * (z ^ 1) + (c ^ 1)) for z in range(NZ) for c in range(2)]
    mixed = lax.ppermute(query_features, ("z", "core"), parity)
    a, b = training[0], training[1]
    for distance in (4, 2):
        a, b = exchange(a, distance), exchange(b, distance)
    query = lax.all_gather(after(mixed, a, b), ta, axis=0)
    a, b = exchange(a, 1), exchange(b, 1)

    own = exchange(exchange(kernel_matrix(slots, gram, (a, b))[None], 4), 2)
    half = slots[: NZ // 2]
    below, above = lax.ppermute(own, "y", UP), lax.ppermute(own, "y", DOWN)
    quarter = NZ // 4
    far = lax.ppermute(below[:quarter], "y", UP), lax.ppermute(above[quarter:], "y", DOWN)

    def scores(*blocks):
        mine, other = partial_scores(half, query, blocks)
        return mine, swapped(other, 1)

    y = lax.axis_index("y").astype(jnp.int32)
    weight = residual_weight[None, :]
    places = lax.rem(y + jnp.array([0, 1, NY - 1, 2], jnp.int32), NY)
    out = finish(places[:3], (scores([own]), scores([above], [below])), weight, None)
    return finish(places[3:], (scores(far),), weight, out)


def solution(mesh):
    fine = Mesh(mesh.devices.reshape(NZ, NY, 4, 2, 2), ("z", "y", "x", "core", "row"))
    pb, ta = ("z", "y"), ("x", "core")
    placed = (P(pb, ta), P(pb, ta), P(("row", *ta), pb), P(("row", *ta)))
    return jax.shard_map(
        local, mesh=fine, in_specs=placed, out_specs=P(pb, ("row", *ta)), check_vma=False
    )
```

time: 163 us -> 176 us (1.080)
  the two profiles are of different devices: /device:TPU:192 before, /device:TPU:6 now
where the time goes in v13:
time: 176 us; the launch traced here: 175 us
  waiting for transfers between devices  62.6 us (36%)
  starting transfers between devices  61.8 us (35%)
  blocking collectives  15.1 us (9%)
  between operations  13.8 us (8%)
  Pallas kernels  11 us (6%)
  local copies, waits for them, and re-layouts  10.2 us (6%)
    ppermute x11, waiting for transfers between devices, swapped(): return lax.ppermute(held, 'z', [(i, i ^ distance) for i in range(NZ)])  52.6 us
    ppermute x11, starting transfers between devices, swapped(): return lax.ppermute(held, 'z', [(i, i ^ distance) for i in range(NZ)])  46 us
    all_to_all x1, blocking collectives, local(): got = lax.all_to_all(sent, 'y', split_axis=0, concat_axis=0, tiled=True)  15.1 us
    ppermute x2, waiting for transfers between devices, local(): below, above = (lax.ppermute(own, 'y', UP), lax.ppermute(own, 'y', DOWN))  9.89 us
    ppermute x2, starting transfers between devices, local(): below, above = (lax.ppermute(own, 'y', UP), lax.ppermute(own, 'y', DOWN))  7.05 us
    unnamed x20, local copies, waits for them, and re-layouts  7.01 us
    pallas_call x3, Pallas kernels, partial_scores(): pl.pallas_call(kernel, out_shape=[jax.ShapeDtypeStruct((rows, width), jnp...  6.06 us
    ppermute x1, starting transfers between devices, local(): lax.ppermute(above[quarter:], 'y', DOWN)  5.12 us
  transfers between devices with their start and end apart: 18, of which 11 were waited for; matrix products, arithmetic and copies ran while one was open for 1% of the time, Pallas kernels for 5%

profile of v13, /device:TPU:6, one launch (start us, length us, event | category | flops | bytes accessed | tf_op | source)
XLA Modules:
  0.0 174.8 jit_solution(2566644016929904062)
XLA Ops:
  6.5 0.9 copy-done.2
  7.5 0.9 copy-done.3
  8.4 0.1 pack.1
  8.4 15.1 %all_to_all.5 = bf16[4,160,512]{2,1,0:T(8,128)(2,1)S(1)} all-to-all(bf16[4,160,512]{2,1,0:T(8,128)(2,1)S(1)} %pack.1), channel_id=1, replica_groups=mesh['z'=8,'y'=4,'x'=4,'core'=2,'row'=2] {'y'}, dimensions={0} | all-to-all | bytes 1310720 | tf_op jit(solution)/shard_map/all_to_all | solution.py:161
  23.6 0.9 slice.41
  24.4 0.0 all-gather.4.cloned.1.call-update
  24.5 0.0 all-gather.6.cloned.1.call-start
  24.5 1.7 collective-permute-start
  26.3 0.1 copy.11
  26.5 9.1 %collective-permute-start.3 = (bf16[1,64,512]{2,1,0:T(8,128)(2,1)S(1)}, bf16[1,64,512]{2,1,0:T(8,128)(2,1)S(1)}, u32[]{:S(2)}, u32[]{:S(2)}) collective-permute-start(bf16[1,64,512]{2,1,0:T(8,128)(2,1)S(1)} %squeeze.7), channel_id=1, source_target_pairs={{0,256},{64,320},{128,384},{192,448},{256,0},{320,64},{384,128},{4... | collective-permute-start | bytes 196616 | tf_op jit(solution)/shard_map/ppermute | solution.py:145
  35.6 1.9 %collective-permute-start.1 = (bf16[1,64,512]{2,1,0:T(8,128)(2,1)S(1)}, bf16[1,64,512]{2,1,0:T(8,128)(2,1)S(1)}, u32[]{:S(2)}, u32[]{:S(2)}) collective-permute-start(bf16[1,64,512]{2,1,0:T(8,128)(2,1)S(1)} %squeeze.6), channel_id=1, source_target_pairs={{0,256},{64,320},{128,384},{192,448},{256,0},{320,64},{384,128},{4... | collective-permute-start | bytes 196616 | tf_op jit(solution)/shard_map/ppermute | solution.py:145
  37.6 0.5 collective-permute-done.3
  38.1 10.5 %collective-permute-start.4 = (bf16[2,64,512]{2,1,0:T(8,128)(2,1)S(1)}, bf16[2,64,512]{2,1,0:T(8,128)(2,1)S(1)}, u32[]{:S(2)}, u32[]{:S(2)}) collective-permute-start(bf16[2,64,512]{2,1,0:T(8,128)(2,1)S(1)} %pad_maximum_fusion.5), channel_id=1, source_target_pairs={{0,128},{64,192},{128,0},{192,64},{256,384},{320,448},{384,256},{4... | collective-permute-start | bytes 393224 | tf_op jit(solution)/shard_map/ppermute | solution.py:145
  48.6 1.3 collective-permute-done.1
  49.9 1.9 %collective-permute-start.2 = (bf16[2,64,512]{2,1,0:T(8,128)(2,1)S(1)}, bf16[2,64,512]{2,1,0:T(8,128)(2,1)S(1)}, u32[]{:S(2)}, u32[]{:S(2)}) collective-permute-start(bf16[2,64,512]{2,1,0:T(8,128)(2,1)S(1)} %pad_maximum_fusion.4), channel_id=1, source_target_pairs={{0,128},{64,192},{128,0},{192,64},{256,384},{320,448},{384,256},{4... | collective-permute-start | bytes 393224 | tf_op jit(solution)/shard_map/ppermute | solution.py:145
  51.9 4.0 %collective-permute-done.4 = bf16[2,64,512]{2,1,0:T(8,128)(2,1)S(1)} collective-permute-done((bf16[2,64,512]{2,1,0:T(8,128)(2,1)S(1)}, bf16[2,64,512]{2,1,0:T(8,128)(2,1)S(1)}, u32[]{:S(2)}, u32[]{:S(2)}) %collective-permute-start.4) | collective-permute-done | bytes 131104 | tf_op jit(solution)/shard_map/ppermute | solution.py:145
  55.9 4.2 %collective-permute-done.2 = bf16[2,64,512]{2,1,0:T(8,128)(2,1)S(1)} collective-permute-done((bf16[2,64,512]{2,1,0:T(8,128)(2,1)S(1)}, bf16[2,64,512]{2,1,0:T(8,128)(2,1)S(1)}, u32[]{:S(2)}, u32[]{:S(2)}) %collective-permute-start.2) | collective-permute-done | bytes 131104 | tf_op jit(solution)/shard_map/ppermute | solution.py:145
  60.2 0.0 collective-permute-done
  60.2 0.0 copy-start.5
  60.2 0.8 copy-done.5
  61.0 0.0 all-gather.6.cloned.1.call-update
  61.0 1.9 %collective-permute-start.6 = (bf16[4,64,512]{2,1,0:T(8,128)(2,1)S(1)}, bf16[4,64,512]{2,1,0:T(8,128)(2,1)S(1)}, u32[]{:S(2)}, u32[]{:S(2)}) collective-permute-start(bf16[4,64,512]{2,1,0:T(8,128)(2,1)S(1)} %constant_dynamic-update-slice_fusion.3), channel_id=1, source_target_pairs={{0,64},{64,0},{128,192},{192,128},{256,320},{320,256},{384,448},{4... | collective-permute-start | bytes 786440 | tf_op jit(solution)/shard_map/ppermute | solution.py:145
  62.9 3.9 %collective-permute-start.5 = (bf16[4,64,512]{2,1,0:T(8,128)(2,1)S(1)}, bf16[4,64,512]{2,1,0:T(8,128)(2,1)S(1)}, u32[]{:S(2)}, u32[]{:S(2)}) collective-permute-start(bf16[4,64,512]{2,1,0:T(8,128)(2,1)S(1)} %constant_dynamic-update-slice_fusion), channel_id=1, source_target_pairs={{0,64},{64,0},{128,192},{192,128},{256,320},{320,256},{384,448},{4... | collective-permute-start | bytes 786440 | tf_op jit(solution)/shard_map/ppermute | solution.py:145
  66.9 5.1 %collective-permute-done.6 = bf16[4,64,512]{2,1,0:T(8,128)(2,1)S(1)} collective-permute-done((bf16[4,64,512]{2,1,0:T(8,128)(2,1)S(1)}, bf16[4,64,512]{2,1,0:T(8,128)(2,1)S(1)}, u32[]{:S(2)}, u32[]{:S(2)}) %collective-permute-start.6) | collective-permute-done | bytes 262176 | tf_op jit(solution)/shard_map/ppermute | solution.py:145
  72.0 0.1 pad_maximum_fusion.1.refs_1_
  72.1 4.9 %collective-permute-done.5 = bf16[4,64,512]{2,1,0:T(8,128)(2,1)S(1)} collective-permute-done((bf16[4,64,512]{2,1,0:T(8,128)(2,1)S(1)}, bf16[4,64,512]{2,1,0:T(8,128)(2,1)S(1)}, u32[]{:S(2)}, u32[]{:S(2)}) %collective-permute-start.5) | collective-permute-done | bytes 262176 | tf_op jit(solution)/shard_map/ppermute | solution.py:145
  77.0 0.1 pad_maximum_fusion.refs_0_
  77.1 0.0 all-gather.4.cloned.1.call-done.gram_ref
  77.1 0.0 copy-start.1
  77.1 2.2 %copy-done.1 = bf16[8,512,512]{2,1,0:T(8,128)(2,1)S(1)} copy-done((bf16[8,512,512]{2,1,0:T(8,128)(2,1)S(1)}, bf16[8,512,512]{2,1,0:T(8,128)(2,1)}, u32[]{:S(2)}) %copy-start.1) | copy-done | bytes 4194328
  79.3 2.0 %kernel_matrix.1 = bf16[128,512]{1,0:T(8,128)(2,1)S(1)} custom-call(s32[8]{0:T(128)S(1)} %broadcast_xor_fusion.slots, bf16[8,512,512]{2,1,0:T(8,128)(2,1)S(1)} %copy-done.1, bf16[8,64,512]{2,1,0:T(8,128)(2,1)S(1)} %pad_maximum_fusion.refs_0_, bf16[8,64,512]{2,1,0:T(8,128)(2,1)S(1)} %pad_maximum_fusion.1.refs_1_), custom_call_target="tpu_custom_call" | custom-call | flops 536870912 | bytes 5242880 | tf_op jit(solution)/shard_map/kernel_matrix/pallas_call | solution.py:51
  81.3 7.0 %collective-permute-start.7 = (bf16[1,128,512]{2,1,0:T(8,128)(2,1)S(1)}, bf16[1,128,512]{2,1,0:T(8,128)(2,1)S(1)}, u32[]{:S(2)}, u32[]{:S(2)}) collective-permute-start(bf16[1,128,512]{2,1,0:T(8,128)(2,1)S(1)} %bitcast.12), channel_id=1, source_target_pairs={{0,256},{64,320},{128,384},{192,448},{256,0},{320,64},{384,128},{4... | collective-permute-start | bytes 393224 | tf_op jit(solution)/shard_map/ppermute | solution.py:145
  88.3 9.4 %collective-permute-done.7 = bf16[1,128,512]{2,1,0:T(8,128)(2,1)S(1)} collective-permute-done((bf16[1,128,512]{2,1,0:T(8,128)(2,1)S(1)}, bf16[1,128,512]{2,1,0:T(8,128)(2,1)S(1)}, u32[]{:S(2)}, u32[]{:S(2)}) %collective-permute-start.7) | collective-permute-done | bytes 131104 | tf_op jit(solution)/shard_map/ppermute | solution.py:145
  97.7 1.9 %collective-permute-start.8 = (bf16[2,128,512]{2,1,0:T(8,128)(2,1)S(1)}, bf16[2,128,512]{2,1,0:T(8,128)(2,1)S(1)}, u32[]{:S(2)}, u32[]{:S(2)}) collective-permute-start(bf16[2,128,512]{2,1,0:T(8,128)(2,1)S(1)} %pad_maximum_fusion.3), channel_id=1, source_target_pairs={{0,128},{64,192},{128,0},{192,64},{256,384},{320,448},{384,256},{4... | collective-permute-start | bytes 786440 | tf_op jit(solution)/shard_map/ppermute | solution.py:145
  99.7 11.8 %collective-permute-done.8 = bf16[2,128,512]{2,1,0:T(8,128)(2,1)S(1)} collective-permute-done((bf16[2,128,512]{2,1,0:T(8,128)(2,1)S(1)}, bf16[2,128,512]{2,1,0:T(8,128)(2,1)S(1)}, u32[]{:S(2)}, u32[]{:S(2)}) %collective-permute-start.8) | collective-permute-done | bytes 262176 | tf_op jit(solution)/shard_map/ppermute | solution.py:145
  111.4 0.1 pad_maximum_fusion.2.refs_0_
  111.5 2.4 %collective-permute-start.9 = (bf16[4,128,512]{2,1,0:T(8,128)(2,1)S(1)}, bf16[4,128,512]{2,1,0:T(8,128)(2,1)S(1)}, u32[]{:S(2)}, u32[]{:S(2)}) collective-permute-start(bf16[4,128,512]{2,1,0:T(8,128)(2,1)S(1)} %pad_maximum_fusion.2.refs_0_), channel_id=1, source_target_pairs={{0,16},{16,32},{32,48},{48,0},{1,17},{17,33},{33,49},{49,1},{2,18}... | collective-permute-start | bytes 1572872 | tf_op jit(solution)/shard_map/ppermute | solution.py:178
  113.9 4.6 %collective-permute-start.11 = (bf16[4,128,512]{2,1,0:T(8,128)(2,1)S(1)}, bf16[4,128,512]{2,1,0:T(8,128)(2,1)S(1)}, u32[]{:S(2)}, u32[]{:S(2)}) collective-permute-start(bf16[4,128,512]{2,1,0:T(8,128)(2,1)S(1)} %pad_maximum_fusion.2.refs_0_), channel_id=1, source_target_pairs={{0,48},{16,0},{32,16},{48,32},{1,49},{17,1},{33,17},{49,33},{2,50}... | collective-permute-start | bytes 1572872 | tf_op jit(solution)/shard_map/ppermute | solution.py:178
  118.5 9.9 %collective-permute-done.9.refs_1_ = bf16[4,128,512]{2,1,0:T(8,128)(2,1)S(1)} collective-permute-done((bf16[4,128,512]{2,1,0:T(8,128)(2,1)S(1)}, bf16[4,128,512]{2,1,0:T(8,128)(2,1)S(1)}, u32[]{:S(2)}, u32[]{:S(2)}) %collective-permute-start.9) | collective-permute-done | bytes 524320 | tf_op jit(solution)/shard_map/ppermute | solution.py:178
  128.4 0.7 slice.42
  129.2 1.9 %collective-permute-start.10 = (bf16[2,128,512]{2,1,0:T(8,128)(2,1)}, bf16[2,128,512]{2,1,0:T(8,128)(2,1)S(1)}, u32[]{:S(2)}, u32[]{:S(2)}) collective-permute-start(bf16[2,128,512]{2,1,0:T(8,128)(2,1)} %slice.42), channel_id=1, source_target_pairs={{0,16},{16,32},{32,48},{48,0},{1,17},{17,33},{33,49},{49,1},{2,18}... | collective-permute-start | bytes 786440 | tf_op jit(solution)/shard_map/ppermute | solution.py:180
  131.1 0.0 collective-permute-done.11.refs_0_
  131.1 0.7 slice.43
  131.8 5.1 %collective-permute-start.12 = (bf16[2,128,512]{2,1,0:T(8,128)(2,1)}, bf16[2,128,512]{2,1,0:T(8,128)(2,1)S(1)}, u32[]{:S(2)}, u32[]{:S(2)}) collective-permute-start(bf16[2,128,512]{2,1,0:T(8,128)(2,1)} %slice.43), channel_id=1, source_target_pairs={{0,48},{16,0},{32,16},{48,32},{1,49},{17,1},{33,17},{49,33},{2,50}... | collective-permute-start | bytes 786440 | tf_op jit(solution)/shard_map/ppermute | solution.py:180
  136.9 0.0 all-gather.6.cloned.1.call-done
  137.0 0.0 copy-start
  137.0 2.2 %copy-done = bf16[4096,512]{1,0:T(8,128)(2,1)S(1)} copy-done((bf16[4096,512]{1,0:T(8,128)(2,1)S(1)}, bf16[4096,512]{1,0:T(8,128)(2,1)}, u32[]{:S(2)}) %copy-start) | copy-done | bytes 4194328
  139.1 1.8 %partial_scores.5 = (f32[512,256]{1,0:T(8,128)S(1)}, f32[512,256]{1,0:T(8,128)S(1)}) custom-call(s32[4]{0:T(128)S(1)} %bitcast.17, bf16[8,512,512]{2,1,0:T(8,128)(2,1)S(1)} %bitcast.9, bf16[4,128,512]{2,1,0:T(8,128)(2,1)S(1)} %collective-permute-done.11.refs_0_, bf16[4,128,512]{2,1,0:T(8,128)(2,1)S(1)} %collective-permute-done.9.refs_1_), custom_call_target="tpu_custom_call" | custom-call | flops 1073741824 | bytes 5242880 | tf_op jit(solution)/shard_map/partial_scores/pallas_call | solution.py:85
  141.0 0.0 copy-start.6
  141.0 0.0 copy-start.4
  141.0 1.9 %collective-permute-start.15 = (f32[512,256]{1,0:T(8,128)S(1)}, f32[512,256]{1,0:T(8,128)S(1)}, u32[]{:S(2)}, u32[]{:S(2)}) collective-permute-start(f32[512,256]{1,0:T(8,128)S(1)} %get-tuple-element.18), channel_id=1, source_target_pairs={{0,64},{64,0},{128,192},{192,128},{256,320},{320,256},{384,448},{4... | collective-permute-start | bytes 1572872 | tf_op jit(solution)/shard_map/ppermute | solution.py:145
  142.9 1.8 %partial_scores.4 = (f32[512,128]{1,0:T(8,128)S(1)}, f32[512,128]{1,0:T(8,128)S(1)}) custom-call(s32[4]{0:T(128)S(1)} %bitcast.18, bf16[8,512,512]{2,1,0:T(8,128)(2,1)S(1)} %bitcast.10, bf16[4,128,512]{2,1,0:T(8,128)(2,1)S(1)} %pad_maximum_fusion.2.refs_0_), custom_call_target="tpu_custom_call" | custom-call | flops 536870912 | bytes 4718592 | tf_op jit(solution)/shard_map/partial_scores/pallas_call | solution.py:85
  144.7 3.9 %collective-permute-start.14 = (f32[512,128]{1,0:T(8,128)S(1)}, f32[512,128]{1,0:T(8,128)S(1)}, u32[]{:S(2)}, u32[]{:S(2)}) collective-permute-start(f32[512,128]{1,0:T(8,128)S(1)} %get-tuple-element.16), channel_id=1, source_target_pairs={{0,64},{64,0},{128,192},{192,128},{256,320},{320,256},{384,448},{4... | collective-permute-start | bytes 786440 | tf_op jit(solution)/shard_map/ppermute | solution.py:145
  148.6 0.0 collective-permute-done.10.refs_0_
  148.6 0.0 collective-permute-done.12.refs_1_
  148.7 2.5 %partial_scores.3 = (f32[512,128]{1,0:T(8,128)S(1)}, f32[512,128]{1,0:T(8,128)}) custom-call(s32[4]{0:T(128)S(1)} %bitcast.19, bf16[8,512,512]{2,1,0:T(8,128)(2,1)S(1)} %bitcast.11, bf16[2,128,512]{2,1,0:T(8,128)(2,1)S(1)} %collective-permute-done.10.refs_0_, bf16[2,128,512]{2,1,0:T(8,128)(2,1)S(1)} %collective-permute-done.12.refs_1_), custom_call_target="tpu_custom_call" | custom-call | flops 536870912 | bytes 4718592 | tf_op jit(solution)/shard_map/partial_scores/pallas_call | solution.py:85
  151.1 1.9 %collective-permute-start.13 = (f32[512,128]{1,0:T(8,128)}, f32[512,128]{1,0:T(8,128)S(1)}, u32[]{:S(2)}, u32[]{:S(2)}) collective-permute-start(f32[512,128]{1,0:T(8,128)} %get-tuple-element.14), channel_id=1, source_target_pairs={{0,64},{64,0},{128,192},{192,128},{256,320},{320,256},{384,448},{4... | collective-permute-start | bytes 786440 | tf_op jit(solution)/shard_map/ppermute | solution.py:145
  153.1 0.0 copy-done.6
  153.1 0.6 slice.29.places
  153.7 9.7 %collective-permute-done.14.refs_1_ = f32[512,128]{1,0:T(8,128)S(1)} collective-permute-done((f32[512,128]{1,0:T(8,128)S(1)}, f32[512,128]{1,0:T(8,128)S(1)}, u32[]{:S(2)}, u32[]{:S(2)}) %collective-permute-start.14) | collective-permute-done | bytes 262176 | tf_op jit(solution)/shard_map/ppermute | solution.py:145
  163.4 0.0 collective-permute-done.15.refs_3_
  163.4 1.5 finish.2.refs_2_
  164.8 1.7 collective-permute-done.13.refs_1_
  166.6 1.4 finish.3
  (22 shorter events, 0.3 us)
Async XLA Ops:
  6.5 60.3 %copy-start.7 = (s32[8]{0:T(128)S(1)}, s32[8]{0:T(128)}, u32[]{:S(2)}) copy-start(s32[8]{0:T(128)} %constant.21.clone) | copy-start | bytes 100
  6.5 70.5 %all-gather.4.cloned.1.call-start = ((), (), s32[]{:S(2)}) async-start(), calls=%async_computation.1 | async-start | bytes 4718592 | tf_op jit(solution)/shard_map/all_gather | solution.py:166
  6.5 0.9 copy-start.2
  7.5 0.9 copy-start.3
  24.5 112.5 %all-gather.6.cloned.1.call-start = ((), (), s32[]{:S(2)}) async-start(), calls=%async_computation.2 | async-start | bytes 4718592 | tf_op jit(solution)/shard_map/all_gather | solution.py:173
  24.5 35.7 %collective-permute-start = (bf16[512,512]{1,0:T(8,128)(2,1)}, bf16[512,512]{1,0:T(8,128)(2,1)S(1)}, u32[]{:S(2)}, u32[]{:S(2)}) collective-permute-start(bf16[512,512]{1,0:T(8,128)(2,1)} %param.6), channel_id=1, source_target_pairs={{0,0},{2,64},{64,2},{66,66},{128,128},{130,192},{192,130},{194,194... | collective-permute-start | bytes 1572872 | tf_op jit(solution)/shard_map/ppermute | solution.py:169
  26.5 11.6 %collective-permute-start.3 = (bf16[1,64,512]{2,1,0:T(8,128)(2,1)S(1)}, bf16[1,64,512]{2,1,0:T(8,128)(2,1)S(1)}, u32[]{:S(2)}, u32[]{:S(2)}) collective-permute-start(bf16[1,64,512]{2,1,0:T(8,128)(2,1)S(1)} %squeeze.7), channel_id=1, source_target_pairs={{0,256},{64,320},{128,384},{192,448},{256,0},{320,64},{384,128},{4... | collective-permute-start | bytes 196616 | tf_op jit(solution)/shard_map/ppermute | solution.py:145
  35.6 14.3 %collective-permute-start.1 = (bf16[1,64,512]{2,1,0:T(8,128)(2,1)S(1)}, bf16[1,64,512]{2,1,0:T(8,128)(2,1)S(1)}, u32[]{:S(2)}, u32[]{:S(2)}) collective-permute-start(bf16[1,64,512]{2,1,0:T(8,128)(2,1)S(1)} %squeeze.6), channel_id=1, source_target_pairs={{0,256},{64,320},{128,384},{192,448},{256,0},{320,64},{384,128},{4... | collective-permute-start | bytes 196616 | tf_op jit(solution)/shard_map/ppermute | solution.py:145
  38.1 17.8 %collective-permute-start.4 = (bf16[2,64,512]{2,1,0:T(8,128)(2,1)S(1)}, bf16[2,64,512]{2,1,0:T(8,128)(2,1)S(1)}, u32[]{:S(2)}, u32[]{:S(2)}) collective-permute-start(bf16[2,64,512]{2,1,0:T(8,128)(2,1)S(1)} %pad_maximum_fusion.5), channel_id=1, source_target_pairs={{0,128},{64,192},{128,0},{192,64},{256,384},{320,448},{384,256},{4... | collective-permute-start | bytes 393224 | tf_op jit(solution)/shard_map/ppermute | solution.py:145
  49.9 10.2 %collective-permute-start.2 = (bf16[2,64,512]{2,1,0:T(8,128)(2,1)S(1)}, bf16[2,64,512]{2,1,0:T(8,128)(2,1)S(1)}, u32[]{:S(2)}, u32[]{:S(2)}) collective-permute-start(bf16[2,64,512]{2,1,0:T(8,128)(2,1)S(1)} %pad_maximum_fusion.4), channel_id=1, source_target_pairs={{0,128},{64,192},{128,0},{192,64},{256,384},{320,448},{384,256},{4... | collective-permute-start | bytes 393224 | tf_op jit(solution)/shard_map/ppermute | solution.py:145
  60.2 0.8 copy-start.5
  61.0 11.0 %collective-permute-start.6 = (bf16[4,64,512]{2,1,0:T(8,128)(2,1)S(1)}, bf16[4,64,512]{2,1,0:T(8,128)(2,1)S(1)}, u32[]{:S(2)}, u32[]{:S(2)}) collective-permute-start(bf16[4,64,512]{2,1,0:T(8,128)(2,1)S(1)} %constant_dynamic-update-slice_fusion.3), channel_id=1, source_target_pairs={{0,64},{64,0},{128,192},{192,128},{256,320},{320,256},{384,448},{4... | collective-permute-start | bytes 786440 | tf_op jit(solution)/shard_map/ppermute | solution.py:145
  62.9 14.1 %collective-permute-start.5 = (bf16[4,64,512]{2,1,0:T(8,128)(2,1)S(1)}, bf16[4,64,512]{2,1,0:T(8,128)(2,1)S(1)}, u32[]{:S(2)}, u32[]{:S(2)}) collective-permute-start(bf16[4,64,512]{2,1,0:T(8,128)(2,1)S(1)} %constant_dynamic-update-slice_fusion), channel_id=1, source_target_pairs={{0,64},{64,0},{128,192},{192,128},{256,320},{320,256},{384,448},{4... | collective-permute-start | bytes 786440 | tf_op jit(solution)/shard_map/ppermute | solution.py:145
  77.1 2.2 %copy-start.1 = (bf16[8,512,512]{2,1,0:T(8,128)(2,1)S(1)}, bf16[8,512,512]{2,1,0:T(8,128)(2,1)}, u32[]{:S(2)}) copy-start(bf16[8,512,512]{2,1,0:T(8,128)(2,1)} %all-gather.4.cloned.1.call-done.gram_ref) | copy-start | bytes 12582916
  81.3 16.4 %collective-permute-start.7 = (bf16[1,128,512]{2,1,0:T(8,128)(2,1)S(1)}, bf16[1,128,512]{2,1,0:T(8,128)(2,1)S(1)}, u32[]{:S(2)}, u32[]{:S(2)}) collective-permute-start(bf16[1,128,512]{2,1,0:T(8,128)(2,1)S(1)} %bitcast.12), channel_id=1, source_target_pairs={{0,256},{64,320},{128,384},{192,448},{256,0},{320,64},{384,128},{4... | collective-permute-start | bytes 393224 | tf_op jit(solution)/shard_map/ppermute | solution.py:145
  97.7 13.7 %collective-permute-start.8 = (bf16[2,128,512]{2,1,0:T(8,128)(2,1)S(1)}, bf16[2,128,512]{2,1,0:T(8,128)(2,1)S(1)}, u32[]{:S(2)}, u32[]{:S(2)}) collective-permute-start(bf16[2,128,512]{2,1,0:T(8,128)(2,1)S(1)} %pad_maximum_fusion.3), channel_id=1, source_target_pairs={{0,128},{64,192},{128,0},{192,64},{256,384},{320,448},{384,256},{4... | collective-permute-start | bytes 786440 | tf_op jit(solution)/shard_map/ppermute | solution.py:145
  111.5 17.0 %collective-permute-start.9 = (bf16[4,128,512]{2,1,0:T(8,128)(2,1)S(1)}, bf16[4,128,512]{2,1,0:T(8,128)(2,1)S(1)}, u32[]{:S(2)}, u32[]{:S(2)}) collective-permute-start(bf16[4,128,512]{2,1,0:T(8,128)(2,1)S(1)} %pad_maximum_fusion.2.refs_0_), channel_id=1, source_target_pairs={{0,16},{16,32},{32,48},{48,0},{1,17},{17,33},{33,49},{49,1},{2,18}... | collective-permute-start | bytes 1572872 | tf_op jit(solution)/shard_map/ppermute | solution.py:178
  113.9 17.1 %collective-permute-start.11 = (bf16[4,128,512]{2,1,0:T(8,128)(2,1)S(1)}, bf16[4,128,512]{2,1,0:T(8,128)(2,1)S(1)}, u32[]{:S(2)}, u32[]{:S(2)}) collective-permute-start(bf16[4,128,512]{2,1,0:T(8,128)(2,1)S(1)} %pad_maximum_fusion.2.refs_0_), channel_id=1, source_target_pairs={{0,48},{16,0},{32,16},{48,32},{1,49},{17,1},{33,17},{49,33},{2,50}... | collective-permute-start | bytes 1572872 | tf_op jit(solution)/shard_map/ppermute | solution.py:178
  129.2 19.5 %collective-permute-start.10 = (bf16[2,128,512]{2,1,0:T(8,128)(2,1)}, bf16[2,128,512]{2,1,0:T(8,128)(2,1)S(1)}, u32[]{:S(2)}, u32[]{:S(2)}) collective-permute-start(bf16[2,128,512]{2,1,0:T(8,128)(2,1)} %slice.42), channel_id=1, source_target_pairs={{0,16},{16,32},{32,48},{48,0},{1,17},{17,33},{33,49},{49,1},{2,18}... | collective-permute-start | bytes 786440 | tf_op jit(solution)/shard_map/ppermute | solution.py:180
  131.8 16.8 %collective-permute-start.12 = (bf16[2,128,512]{2,1,0:T(8,128)(2,1)}, bf16[2,128,512]{2,1,0:T(8,128)(2,1)S(1)}, u32[]{:S(2)}, u32[]{:S(2)}) collective-permute-start(bf16[2,128,512]{2,1,0:T(8,128)(2,1)} %slice.43), channel_id=1, source_target_pairs={{0,48},{16,0},{32,16},{48,32},{1,49},{17,1},{33,17},{49,33},{2,50}... | collective-permute-start | bytes 786440 | tf_op jit(solution)/shard_map/ppermute | solution.py:180
  137.0 2.2 %copy-start = (bf16[4096,512]{1,0:T(8,128)(2,1)S(1)}, bf16[4096,512]{1,0:T(8,128)(2,1)}, u32[]{:S(2)}) copy-start(bf16[4096,512]{1,0:T(8,128)(2,1)} %all-gather.6.cloned.1.call-done) | copy-start | bytes 12582916
  141.0 12.1 %copy-start.6 = (s32[4]{0:T(128)S(1)}, s32[4]{0:T(128)}, u32[]{:S(2)}) copy-start(s32[4]{0:T(128)} %constant.22.clone) | copy-start | bytes 52
  141.0 22.4 %copy-start.4 = (f32[512]{0:T(512)S(1)}, f32[512]{0:T(512)}, u32[]{:S(2)}) copy-start(f32[512]{0:T(512)} %param.9) | copy-start | bytes 6148
  141.0 22.4 %collective-permute-start.15 = (f32[512,256]{1,0:T(8,128)S(1)}, f32[512,256]{1,0:T(8,128)S(1)}, u32[]{:S(2)}, u32[]{:S(2)}) collective-permute-start(f32[512,256]{1,0:T(8,128)S(1)} %get-tuple-element.18), channel_id=1, source_target_pairs={{0,64},{64,0},{128,192},{192,128},{256,320},{320,256},{384,448},{4... | collective-permute-start | bytes 1572872 | tf_op jit(solution)/shard_map/ppermute | solution.py:145
  144.7 18.7 %collective-permute-start.14 = (f32[512,128]{1,0:T(8,128)S(1)}, f32[512,128]{1,0:T(8,128)S(1)}, u32[]{:S(2)}, u32[]{:S(2)}) collective-permute-start(f32[512,128]{1,0:T(8,128)S(1)} %get-tuple-element.16), channel_id=1, source_target_pairs={{0,64},{64,0},{128,192},{192,128},{256,320},{320,256},{384,448},{4... | collective-permute-start | bytes 786440 | tf_op jit(solution)/shard_map/ppermute | solution.py:145
  151.1 15.4 %collective-permute-start.13 = (f32[512,128]{1,0:T(8,128)}, f32[512,128]{1,0:T(8,128)S(1)}, u32[]{:S(2)}, u32[]{:S(2)}) collective-permute-start(f32[512,128]{1,0:T(8,128)} %get-tuple-element.14), channel_id=1, source_target_pairs={{0,64},{64,0},{128,192},{192,128},{256,320},{320,256},{384,448},{4... | collective-permute-start | bytes 786440 | tf_op jit(solution)/shard_map/ppermute | solution.py:145
Sparse Core Ops, SparseCore 0:
  24.6 40.2 all-gather.3
  67.1 39.7 all-gather.5

commit v14 on v13

--- a/solution.py
+++ b/solution.py
@@ -165,19 +165,23 @@
 
     gram = lax.all_gather(gram_rows, ta, axis=0)
 
+    a, b = training[0], training[1]
+    for distance in (4, 2, 1):
+        a, b = exchange(a, distance), exchange(b, distance)
+
     parity = [(2 * z + c, 2 * z + c if c == z % 2 else 2 * (z ^ 1) + (c ^ 1)) for z in range(NZ) for c in range(2)]
-    mixed = lax.ppermute(query_features, ("z", "core"), parity)
-    a, b = training[0], training[1]
-    for distance in (4, 2):
-        a, b = exchange(a, distance), exchange(b, distance)
-    query = lax.all_gather(after(mixed, a, b), ta, axis=0)
-    a, b = exchange(a, 1), exchange(b, 1)
-
-    own = exchange(exchange(kernel_matrix(slots, gram, (a, b))[None], 4), 2)
+    mixed = lax.ppermute(after(query_features, a, b), ("z", "core"), parity)
+    tile = kernel_matrix(slots, gram, (a, b))[None]
+    query = lax.all_gather(after(mixed, tile), ta, axis=0)
+
+    own = exchange(exchange(tile, 4), 2)
     half = slots[: NZ // 2]
     below, above = lax.ppermute(own, "y", UP), lax.ppermute(own, "y", DOWN)
+    mine, other = partial_scores(half, query, ([own],))
     quarter = NZ // 4
-    far = lax.ppermute(below[:quarter], "y", UP), lax.ppermute(above[quarter:], "y", DOWN)
+    first, second = after(below[:quarter], other), after(above[quarter:], other)
+    far = lax.ppermute(first, "y", UP), lax.ppermute(second, "y", DOWN)
+    own_pair = mine, swapped(other, 1)
 
     def scores(*blocks):
         mine, other = partial_scores(half, query, blocks)
@@ -186,7 +190,7 @@
     y = lax.axis_index("y").astype(jnp.int32)
     weight = residual_weight[None, :]
     places = lax.rem(y + jnp.array([0, 1, NY - 1, 2], jnp.int32), NY)
-    out = finish(places[:3], (scores([own]), scores([above], [below])), weight, None)
+    out = finish(places[:3], (own_pair, scores([above], [below])), weight, None)
     return finish(places[3:], (scores(far),), weight, out)
 
 

time: 176 us -> 172 us (0.977)
  the two profiles are of different devices: /device:TPU:6 before, /device:TPU:1 now
where the time goes in v14:
time: 172 us; the launch traced here: 171 us
  starting transfers between devices  70.8 us (41%)
  waiting for transfers between devices  54.7 us (32%)
  between operations  13.9 us (8%)
  blocking collectives  12.6 us (7%)
  Pallas kernels  10.2 us (6%)
  local copies, waits for them, and re-layouts  8.82 us (5%)
    ppermute x11, starting transfers between devices, swapped(): return lax.ppermute(held, 'z', [(i, i ^ distance) for i in range(NZ)])  54.4 us
    ppermute x11, waiting for transfers between devices, swapped(): return lax.ppermute(held, 'z', [(i, i ^ distance) for i in range(NZ)])  41.5 us
    all_to_all x1, blocking collectives, local(): got = lax.all_to_all(sent, 'y', split_axis=0, concat_axis=0, tiled=True)  12.6 us
    ppermute x2, waiting for transfers between devices, local(): below, above = (lax.ppermute(own, 'y', UP), lax.ppermute(own, 'y', DOWN))  10.5 us
    unnamed x24, local copies, waits for them, and re-layouts  7.04 us
    ppermute x2, starting transfers between devices, local(): far = (lax.ppermute(first, 'y', UP), lax.ppermute(second, 'y', DOWN))  6.62 us
    pallas_call x3, Pallas kernels, partial_scores(): pl.pallas_call(kernel, out_shape=[jax.ShapeDtypeStruct((rows, width), jnp...  5.34 us
    ppermute x2, starting transfers between devices, local(): below, above = (lax.ppermute(own, 'y', UP), lax.ppermute(own, 'y', DOWN))  5.28 us
  transfers between devices with their start and end apart: 18, of which 10 were waited for; matrix products, arithmetic and copies ran while one was open for 1% of the time, Pallas kernels for 4%

profile of v14, /device:TPU:1, one launch (start us, length us, event | category | flops | bytes accessed | tf_op | source)
XLA Modules:
  0.0 171.0 jit_solution(7826474433503988660)
XLA Ops:
  6.5 0.0 all-gather.4.cloned.1.call-start
  6.5 0.0 copy-start.2
  6.5 0.9 copy-done.2
  7.5 0.9 copy-done.3
  8.4 0.1 pack.1
  8.4 12.6 %all_to_all.5 = bf16[4,160,512]{2,1,0:T(8,128)(2,1)S(1)} all-to-all(bf16[4,160,512]{2,1,0:T(8,128)(2,1)S(1)} %pack.1), channel_id=1, replica_groups=mesh['z'=8,'y'=4,'x'=4,'core'=2,'row'=2] {'y'}, dimensions={0} | all-to-all | bytes 1310720 | tf_op jit(solution)/shard_map/all_to_all | solution.py:161
  21.0 0.8 slice.41
  21.8 0.0 all-gather.4.cloned.1.call-update
  21.9 0.0 all-gather.6.cloned.1.call-start
  22.0 0.1 copy.11
  22.2 11.2 %collective-permute-start = (bf16[1,64,512]{2,1,0:T(8,128)(2,1)S(1)}, bf16[1,64,512]{2,1,0:T(8,128)(2,1)S(1)}, u32[]{:S(2)}, u32[]{:S(2)}) collective-permute-start(bf16[1,64,512]{2,1,0:T(8,128)(2,1)S(1)} %squeeze.6), channel_id=1, source_target_pairs={{0,256},{64,320},{128,384},{192,448},{256,0},{320,64},{384,128},{4... | collective-permute-start | bytes 196616 | tf_op jit(solution)/shard_map/ppermute | solution.py:145
  33.4 1.9 %collective-permute-start.3 = (bf16[1,64,512]{2,1,0:T(8,128)(2,1)S(1)}, bf16[1,64,512]{2,1,0:T(8,128)(2,1)S(1)}, u32[]{:S(2)}, u32[]{:S(2)}) collective-permute-start(bf16[1,64,512]{2,1,0:T(8,128)(2,1)S(1)} %squeeze.7), channel_id=1, source_target_pairs={{0,256},{64,320},{128,384},{192,448},{256,0},{320,64},{384,128},{4... | collective-permute-start | bytes 196616 | tf_op jit(solution)/shard_map/ppermute | solution.py:145
  35.3 0.0 collective-permute-done
  35.4 4.9 %collective-permute-start.1 = (bf16[2,64,512]{2,1,0:T(8,128)(2,1)S(1)}, bf16[2,64,512]{2,1,0:T(8,128)(2,1)S(1)}, u32[]{:S(2)}, u32[]{:S(2)}) collective-permute-start(bf16[2,64,512]{2,1,0:T(8,128)(2,1)S(1)} %pad_maximum_fusion.4), channel_id=1, source_target_pairs={{0,128},{64,192},{128,0},{192,64},{256,384},{320,448},{384,256},{4... | collective-permute-start | bytes 393224 | tf_op jit(solution)/shard_map/ppermute | solution.py:145
  40.3 2.1 %collective-permute-done.3 = bf16[1,64,512]{2,1,0:T(8,128)(2,1)S(1)} collective-permute-done((bf16[1,64,512]{2,1,0:T(8,128)(2,1)S(1)}, bf16[1,64,512]{2,1,0:T(8,128)(2,1)S(1)}, u32[]{:S(2)}, u32[]{:S(2)}) %collective-permute-start.3) | collective-permute-done | bytes 65568 | tf_op jit(solution)/shard_map/ppermute | solution.py:145
  42.4 4.9 %collective-permute-start.4 = (bf16[2,64,512]{2,1,0:T(8,128)(2,1)S(1)}, bf16[2,64,512]{2,1,0:T(8,128)(2,1)S(1)}, u32[]{:S(2)}, u32[]{:S(2)}) collective-permute-start(bf16[2,64,512]{2,1,0:T(8,128)(2,1)S(1)} %pad_maximum_fusion.5), channel_id=1, source_target_pairs={{0,128},{64,192},{128,0},{192,64},{256,384},{320,448},{384,256},{4... | collective-permute-start | bytes 393224 | tf_op jit(solution)/shard_map/ppermute | solution.py:145
  47.3 0.0 collective-permute-done.1
  47.4 9.6 %collective-permute-start.2 = (bf16[4,64,512]{2,1,0:T(8,128)(2,1)S(1)}, bf16[4,64,512]{2,1,0:T(8,128)(2,1)S(1)}, u32[]{:S(2)}, u32[]{:S(2)}) collective-permute-start(bf16[4,64,512]{2,1,0:T(8,128)(2,1)S(1)} %pad_maximum_fusion.1), channel_id=1, source_target_pairs={{0,64},{64,0},{128,192},{192,128},{256,320},{320,256},{384,448},{4... | collective-permute-start | bytes 786440 | tf_op jit(solution)/shard_map/ppermute | solution.py:145
  57.0 0.0 collective-permute-done.4
  57.1 2.8 %collective-permute-start.5 = (bf16[4,64,512]{2,1,0:T(8,128)(2,1)S(1)}, bf16[4,64,512]{2,1,0:T(8,128)(2,1)S(1)}, u32[]{:S(2)}, u32[]{:S(2)}) collective-permute-start(bf16[4,64,512]{2,1,0:T(8,128)(2,1)S(1)} %pad_maximum_fusion.2), channel_id=1, source_target_pairs={{0,64},{64,0},{128,192},{192,128},{256,320},{320,256},{384,448},{4... | collective-permute-start | bytes 786440 | tf_op jit(solution)/shard_map/ppermute | solution.py:145
  59.9 3.4 %collective-permute-done.2 = bf16[4,64,512]{2,1,0:T(8,128)(2,1)S(1)} collective-permute-done((bf16[4,64,512]{2,1,0:T(8,128)(2,1)S(1)}, bf16[4,64,512]{2,1,0:T(8,128)(2,1)S(1)}, u32[]{:S(2)}, u32[]{:S(2)}) %collective-permute-start.2) | collective-permute-done | bytes 262176 | tf_op jit(solution)/shard_map/ppermute | solution.py:145
  63.2 5.5 %collective-permute-done.5 = bf16[4,64,512]{2,1,0:T(8,128)(2,1)S(1)} collective-permute-done((bf16[4,64,512]{2,1,0:T(8,128)(2,1)S(1)}, bf16[4,64,512]{2,1,0:T(8,128)(2,1)S(1)}, u32[]{:S(2)}, u32[]{:S(2)}) %collective-permute-start.5) | collective-permute-done | bytes 262176 | tf_op jit(solution)/shard_map/ppermute | solution.py:145
  68.8 0.0 copy-done.6
  68.8 4.4 %collective-permute-start.6 = (bf16[512,512]{1,0:T(8,128)(2,1)S(1)}, bf16[512,512]{1,0:T(8,128)(2,1)S(1)}, u32[]{:S(2)}, u32[]{:S(2)}) collective-permute-start(bf16[512,512]{1,0:T(8,128)(2,1)S(1)} %copy-done.6), channel_id=1, source_target_pairs={{0,0},{2,64},{64,2},{66,66},{128,128},{130,192},{192,130},{194,194... | collective-permute-start | bytes 1572872 | tf_op jit(solution)/shard_map/ppermute | solution.py:173
  73.2 0.0 copy-done.8
  73.2 0.0 all-gather.4.cloned.1.call-done.gram_ref
  73.2 0.0 copy-start.1
  73.2 2.2 %copy-done.1 = bf16[8,512,512]{2,1,0:T(8,128)(2,1)S(1)} copy-done((bf16[8,512,512]{2,1,0:T(8,128)(2,1)S(1)}, bf16[8,512,512]{2,1,0:T(8,128)(2,1)}, u32[]{:S(2)}) %copy-start.1) | copy-done | bytes 4194328
  75.4 2.0 %kernel_matrix.1 = bf16[128,512]{1,0:T(8,128)(2,1)S(1)} custom-call(s32[8]{0:T(128)S(1)} %broadcast_xor_fusion.slots, bf16[8,512,512]{2,1,0:T(8,128)(2,1)S(1)} %copy-done.1, bf16[8,64,512]{2,1,0:T(8,128)(2,1)S(1)} %constant_dynamic-update-slice_fusion.refs_0_, bf16[8,64,512]{2,1,0:T(8,128)(2,1)S(1)} %constant_dynamic-update-slice_fusion.4.refs_1_), custom_call_target="tpu_custom_call" | custom-call | flops 536870912 | bytes 5242880 | tf_op jit(solution)/shard_map/kernel_matrix/pallas_call | solution.py:51
  77.4 2.6 %collective-permute-done.6 = bf16[512,512]{1,0:T(8,128)(2,1)S(1)} collective-permute-done((bf16[512,512]{1,0:T(8,128)(2,1)S(1)}, bf16[512,512]{1,0:T(8,128)(2,1)S(1)}, u32[]{:S(2)}, u32[]{:S(2)}) %collective-permute-start.6) | collective-permute-done | bytes 524320 | tf_op jit(solution)/shard_map/ppermute | solution.py:173
  80.0 0.8 copy-done.5
  80.8 0.0 all-gather.6.cloned.1.call-update
  80.8 9.1 %collective-permute-start.7 = (bf16[1,128,512]{2,1,0:T(8,128)(2,1)S(1)}, bf16[1,128,512]{2,1,0:T(8,128)(2,1)S(1)}, u32[]{:S(2)}, u32[]{:S(2)}) collective-permute-start(bf16[1,128,512]{2,1,0:T(8,128)(2,1)S(1)} %bitcast.12), channel_id=1, source_target_pairs={{0,256},{64,320},{128,384},{192,448},{256,0},{320,64},{384,128},{4... | collective-permute-start | bytes 393224 | tf_op jit(solution)/shard_map/ppermute | solution.py:145
  90.0 6.7 %collective-permute-done.7 = bf16[1,128,512]{2,1,0:T(8,128)(2,1)S(1)} collective-permute-done((bf16[1,128,512]{2,1,0:T(8,128)(2,1)S(1)}, bf16[1,128,512]{2,1,0:T(8,128)(2,1)S(1)}, u32[]{:S(2)}, u32[]{:S(2)}) %collective-permute-start.7) | collective-permute-done | bytes 131104 | tf_op jit(solution)/shard_map/ppermute | solution.py:145
  96.7 2.8 %collective-permute-start.8 = (bf16[2,128,512]{2,1,0:T(8,128)(2,1)S(1)}, bf16[2,128,512]{2,1,0:T(8,128)(2,1)S(1)}, u32[]{:S(2)}, u32[]{:S(2)}) collective-permute-start(bf16[2,128,512]{2,1,0:T(8,128)(2,1)S(1)} %pad_maximum_fusion.3), channel_id=1, source_target_pairs={{0,128},{64,192},{128,0},{192,64},{256,384},{320,448},{384,256},{4... | collective-permute-start | bytes 786440 | tf_op jit(solution)/shard_map/ppermute | solution.py:145
  99.5 8.4 %collective-permute-done.8 = bf16[2,128,512]{2,1,0:T(8,128)(2,1)S(1)} collective-permute-done((bf16[2,128,512]{2,1,0:T(8,128)(2,1)S(1)}, bf16[2,128,512]{2,1,0:T(8,128)(2,1)S(1)}, u32[]{:S(2)}, u32[]{:S(2)}) %collective-permute-start.8) | collective-permute-done | bytes 262176 | tf_op jit(solution)/shard_map/ppermute | solution.py:145
  107.9 0.1 pad_maximum_fusion.refs_0_
  107.9 1.9 %collective-permute-start.11 = (bf16[4,128,512]{2,1,0:T(8,128)(2,1)S(1)}, bf16[4,128,512]{2,1,0:T(8,128)(2,1)S(1)}, u32[]{:S(2)}, u32[]{:S(2)}) collective-permute-start(bf16[4,128,512]{2,1,0:T(8,128)(2,1)S(1)} %pad_maximum_fusion.refs_0_), channel_id=1, source_target_pairs={{0,48},{16,0},{32,16},{48,32},{1,49},{17,1},{33,17},{49,33},{2,50}... | collective-permute-start | bytes 1572872 | tf_op jit(solution)/shard_map/ppermute | solution.py:179
  109.9 3.4 %collective-permute-start.9 = (bf16[4,128,512]{2,1,0:T(8,128)(2,1)S(1)}, bf16[4,128,512]{2,1,0:T(8,128)(2,1)S(1)}, u32[]{:S(2)}, u32[]{:S(2)}) collective-permute-start(bf16[4,128,512]{2,1,0:T(8,128)(2,1)S(1)} %pad_maximum_fusion.refs_0_), channel_id=1, source_target_pairs={{0,16},{16,32},{32,48},{48,0},{1,17},{17,33},{33,49},{49,1},{2,18}... | collective-permute-start | bytes 1572872 | tf_op jit(solution)/shard_map/ppermute | solution.py:179
  113.2 4.9 %collective-permute-done.11.refs_0_ = bf16[4,128,512]{2,1,0:T(8,128)(2,1)S(1)} collective-permute-done((bf16[4,128,512]{2,1,0:T(8,128)(2,1)S(1)}, bf16[4,128,512]{2,1,0:T(8,128)(2,1)S(1)}, u32[]{:S(2)}, u32[]{:S(2)}) %collective-permute-start.11) | collective-permute-done | bytes 524320 | tf_op jit(solution)/shard_map/ppermute | solution.py:179
  118.2 5.6 %collective-permute-done.9.refs_1_ = bf16[4,128,512]{2,1,0:T(8,128)(2,1)S(1)} collective-permute-done((bf16[4,128,512]{2,1,0:T(8,128)(2,1)S(1)}, bf16[4,128,512]{2,1,0:T(8,128)(2,1)S(1)}, u32[]{:S(2)}, u32[]{:S(2)}) %collective-permute-start.9) | collective-permute-done | bytes 524320 | tf_op jit(solution)/shard_map/ppermute | solution.py:179
  123.8 0.0 all-gather.6.cloned.1.call-done
  123.8 0.0 copy-start
  123.8 2.2 %copy-done = bf16[4096,512]{1,0:T(8,128)(2,1)S(1)} copy-done((bf16[4096,512]{1,0:T(8,128)(2,1)S(1)}, bf16[4096,512]{1,0:T(8,128)(2,1)}, u32[]{:S(2)}) %copy-start) | copy-done | bytes 4194328
  126.0 1.8 %partial_scores.3 = (f32[512,128]{1,0:T(8,128)S(1)}, f32[512,128]{1,0:T(8,128)S(1)}) custom-call(s32[4]{0:T(128)S(1)} %bitcast.17, bf16[8,512,512]{2,1,0:T(8,128)(2,1)S(1)} %bitcast.9, bf16[4,128,512]{2,1,0:T(8,128)(2,1)S(1)} %pad_maximum_fusion.refs_0_), custom_call_target="tpu_custom_call" | custom-call | flops 536870912 | bytes 4718592 | tf_op jit(solution)/shard_map/partial_scores/pallas_call | solution.py:85
  127.8 0.0 copy-start.7
  127.8 0.0 copy-start.4
  127.8 2.1 %collective-permute-start.10 = (bf16[2,128,512]{2,1,0:T(8,128)(2,1)S(1)}, bf16[2,128,512]{2,1,0:T(8,128)(2,1)S(1)}, u32[]{:S(2)}, u32[]{:S(2)}) collective-permute-start(bf16[2,128,512]{2,1,0:T(8,128)(2,1)S(1)} %slice.42), channel_id=1, source_target_pairs={{0,16},{16,32},{32,48},{48,0},{1,17},{17,33},{33,49},{49,1},{2,18}... | collective-permute-start | bytes 786440 | tf_op jit(solution)/shard_map/ppermute | solution.py:183
  129.9 4.6 %collective-permute-start.12 = (bf16[2,128,512]{2,1,0:T(8,128)(2,1)S(1)}, bf16[2,128,512]{2,1,0:T(8,128)(2,1)S(1)}, u32[]{:S(2)}, u32[]{:S(2)}) collective-permute-start(bf16[2,128,512]{2,1,0:T(8,128)(2,1)S(1)} %slice.43), channel_id=1, source_target_pairs={{0,48},{16,0},{32,16},{48,32},{1,49},{17,1},{33,17},{49,33},{2,50}... | collective-permute-start | bytes 786440 | tf_op jit(solution)/shard_map/ppermute | solution.py:183
  134.5 1.8 %partial_scores.5 = (f32[512,256]{1,0:T(8,128)S(1)}, f32[512,256]{1,0:T(8,128)S(1)}) custom-call(s32[4]{0:T(128)S(1)} %bitcast.18, bf16[8,512,512]{2,1,0:T(8,128)(2,1)S(1)} %bitcast.10, bf16[4,128,512]{2,1,0:T(8,128)(2,1)S(1)} %collective-permute-done.11.refs_0_, bf16[4,128,512]{2,1,0:T(8,128)(2,1)S(1)} %collective-permute-done.9.refs_1_), custom_call_target="tpu_custom_call" | custom-call | flops 1073741824 | bytes 5242880 | tf_op jit(solution)/shard_map/partial_scores/pallas_call | solution.py:85
  136.3 1.9 %collective-permute-start.15 = (f32[512,256]{1,0:T(8,128)S(1)}, f32[512,256]{1,0:T(8,128)S(1)}, u32[]{:S(2)}, u32[]{:S(2)}) collective-permute-start(f32[512,256]{1,0:T(8,128)S(1)} %get-tuple-element.24), channel_id=1, source_target_pairs={{0,64},{64,0},{128,192},{192,128},{256,320},{320,256},{384,448},{4... | collective-permute-start | bytes 1572872 | tf_op jit(solution)/shard_map/ppermute | solution.py:145
  138.2 3.4 %collective-permute-start.14 = (f32[512,128]{1,0:T(8,128)S(1)}, f32[512,128]{1,0:T(8,128)S(1)}, u32[]{:S(2)}, u32[]{:S(2)}) collective-permute-start(f32[512,128]{1,0:T(8,128)S(1)} %get-tuple-element.17), channel_id=1, source_target_pairs={{0,64},{64,0},{128,192},{192,128},{256,320},{320,256},{384,448},{4... | collective-permute-start | bytes 786440 | tf_op jit(solution)/shard_map/ppermute | solution.py:145
  141.6 0.0 collective-permute-done.10.refs_0_
  141.6 0.0 collective-permute-done.12.refs_1_
  141.6 1.8 %partial_scores.4 = (f32[512,128]{1,0:T(8,128)S(1)}, f32[512,128]{1,0:T(8,128)S(1)}) custom-call(s32[4]{0:T(128)S(1)} %bitcast.19, bf16[8,512,512]{2,1,0:T(8,128)(2,1)S(1)} %bitcast.11, bf16[2,128,512]{2,1,0:T(8,128)(2,1)S(1)} %collective-permute-done.10.refs_0_, bf16[2,128,512]{2,1,0:T(8,128)(2,1)S(1)} %collective-permute-done.12.refs_1_), custom_call_target="tpu_custom_call" | custom-call | flops 536870912 | bytes 4718592 | tf_op jit(solution)/shard_map/partial_scores/pallas_call | solution.py:85
  143.4 1.9 %collective-permute-start.13 = (f32[512,128]{1,0:T(8,128)S(1)}, f32[512,128]{1,0:T(8,128)S(1)}, u32[]{:S(2)}, u32[]{:S(2)}) collective-permute-start(f32[512,128]{1,0:T(8,128)S(1)} %get-tuple-element.21), channel_id=1, source_target_pairs={{0,64},{64,0},{128,192},{192,128},{256,320},{320,256},{384,448},{4... | collective-permute-start | bytes 786440 | tf_op jit(solution)/shard_map/ppermute | solution.py:145
  145.3 0.0 copy-done.7
  145.3 0.6 slice.29.places
  145.9 11.8 %collective-permute-done.14.refs_1_ = f32[512,128]{1,0:T(8,128)S(1)} collective-permute-done((f32[512,128]{1,0:T(8,128)S(1)}, f32[512,128]{1,0:T(8,128)S(1)}, u32[]{:S(2)}, u32[]{:S(2)}) %collective-permute-start.14) | collective-permute-done | bytes 262176 | tf_op jit(solution)/shard_map/ppermute | solution.py:145
  157.7 0.0 collective-permute-done.15.refs_3_
  157.7 0.0 copy-done.4
  157.7 1.5 finish.2.refs_2_
  159.2 3.6 %collective-permute-done.13.refs_1_ = f32[512,128]{1,0:T(8,128)S(1)} collective-permute-done((f32[512,128]{1,0:T(8,128)S(1)}, f32[512,128]{1,0:T(8,128)S(1)}, u32[]{:S(2)}, u32[]{:S(2)}) %collective-permute-start.13) | collective-permute-done | bytes 262176 | tf_op jit(solution)/shard_map/ppermute | solution.py:145
  162.8 1.3 finish.3
  (26 shorter events, 0.4 us)
Async XLA Ops:
  6.5 66.6 %copy-start.8 = (s32[8]{0:T(128)S(1)}, s32[8]{0:T(128)}, u32[]{:S(2)}) copy-start(s32[8]{0:T(128)} %constant.21.clone) | copy-start | bytes 100
  6.5 66.7 %all-gather.4.cloned.1.call-start = ((), (), s32[]{:S(2)}) async-start(), calls=%async_computation.1 | async-start | bytes 4718592 | tf_op jit(solution)/shard_map/all_gather | solution.py:166
  6.5 0.9 copy-start.2
  7.5 0.9 copy-start.3
  8.4 60.4 %copy-start.6 = (bf16[512,512]{1,0:T(8,128)(2,1)S(1)}, bf16[512,512]{1,0:T(8,128)(2,1)}, u32[]{:S(2)}) copy-start(bf16[512,512]{1,0:T(8,128)(2,1)} %param.6) | copy-start | bytes 1572868
  21.9 102.0 %all-gather.6.cloned.1.call-start = ((), (), s32[]{:S(2)}) async-start(), calls=%async_computation.2 | async-start | bytes 4718592 | tf_op jit(solution)/shard_map/all_gather | solution.py:175
  22.2 13.1 %collective-permute-start = (bf16[1,64,512]{2,1,0:T(8,128)(2,1)S(1)}, bf16[1,64,512]{2,1,0:T(8,128)(2,1)S(1)}, u32[]{:S(2)}, u32[]{:S(2)}) collective-permute-start(bf16[1,64,512]{2,1,0:T(8,128)(2,1)S(1)} %squeeze.6), channel_id=1, source_target_pairs={{0,256},{64,320},{128,384},{192,448},{256,0},{320,64},{384,128},{4... | collective-permute-start | bytes 196616 | tf_op jit(solution)/shard_map/ppermute | solution.py:145
  33.4 9.0 %collective-permute-start.3 = (bf16[1,64,512]{2,1,0:T(8,128)(2,1)S(1)}, bf16[1,64,512]{2,1,0:T(8,128)(2,1)S(1)}, u32[]{:S(2)}, u32[]{:S(2)}) collective-permute-start(bf16[1,64,512]{2,1,0:T(8,128)(2,1)S(1)} %squeeze.7), channel_id=1, source_target_pairs={{0,256},{64,320},{128,384},{192,448},{256,0},{320,64},{384,128},{4... | collective-permute-start | bytes 196616 | tf_op jit(solution)/shard_map/ppermute | solution.py:145
  35.4 12.0 %collective-permute-start.1 = (bf16[2,64,512]{2,1,0:T(8,128)(2,1)S(1)}, bf16[2,64,512]{2,1,0:T(8,128)(2,1)S(1)}, u32[]{:S(2)}, u32[]{:S(2)}) collective-permute-start(bf16[2,64,512]{2,1,0:T(8,128)(2,1)S(1)} %pad_maximum_fusion.4), channel_id=1, source_target_pairs={{0,128},{64,192},{128,0},{192,64},{256,384},{320,448},{384,256},{4... | collective-permute-start | bytes 393224 | tf_op jit(solution)/shard_map/ppermute | solution.py:145
  42.4 14.6 %collective-permute-start.4 = (bf16[2,64,512]{2,1,0:T(8,128)(2,1)S(1)}, bf16[2,64,512]{2,1,0:T(8,128)(2,1)S(1)}, u32[]{:S(2)}, u32[]{:S(2)}) collective-permute-start(bf16[2,64,512]{2,1,0:T(8,128)(2,1)S(1)} %pad_maximum_fusion.5), channel_id=1, source_target_pairs={{0,128},{64,192},{128,0},{192,64},{256,384},{320,448},{384,256},{4... | collective-permute-start | bytes 393224 | tf_op jit(solution)/shard_map/ppermute | solution.py:145
  47.4 15.8 %collective-permute-start.2 = (bf16[4,64,512]{2,1,0:T(8,128)(2,1)S(1)}, bf16[4,64,512]{2,1,0:T(8,128)(2,1)S(1)}, u32[]{:S(2)}, u32[]{:S(2)}) collective-permute-start(bf16[4,64,512]{2,1,0:T(8,128)(2,1)S(1)} %pad_maximum_fusion.1), channel_id=1, source_target_pairs={{0,64},{64,0},{128,192},{192,128},{256,320},{320,256},{384,448},{4... | collective-permute-start | bytes 786440 | tf_op jit(solution)/shard_map/ppermute | solution.py:145
  57.1 11.7 %collective-permute-start.5 = (bf16[4,64,512]{2,1,0:T(8,128)(2,1)S(1)}, bf16[4,64,512]{2,1,0:T(8,128)(2,1)S(1)}, u32[]{:S(2)}, u32[]{:S(2)}) collective-permute-start(bf16[4,64,512]{2,1,0:T(8,128)(2,1)S(1)} %pad_maximum_fusion.2), channel_id=1, source_target_pairs={{0,64},{64,0},{128,192},{192,128},{256,320},{320,256},{384,448},{4... | collective-permute-start | bytes 786440 | tf_op jit(solution)/shard_map/ppermute | solution.py:145
  68.8 11.2 %collective-permute-start.6 = (bf16[512,512]{1,0:T(8,128)(2,1)S(1)}, bf16[512,512]{1,0:T(8,128)(2,1)S(1)}, u32[]{:S(2)}, u32[]{:S(2)}) collective-permute-start(bf16[512,512]{1,0:T(8,128)(2,1)S(1)} %copy-done.6), channel_id=1, source_target_pairs={{0,0},{2,64},{64,2},{66,66},{128,128},{130,192},{192,130},{194,194... | collective-permute-start | bytes 1572872 | tf_op jit(solution)/shard_map/ppermute | solution.py:173
  73.2 2.2 %copy-start.1 = (bf16[8,512,512]{2,1,0:T(8,128)(2,1)S(1)}, bf16[8,512,512]{2,1,0:T(8,128)(2,1)}, u32[]{:S(2)}) copy-start(bf16[8,512,512]{2,1,0:T(8,128)(2,1)} %all-gather.4.cloned.1.call-done.gram_ref) | copy-start | bytes 12582916
  80.0 0.8 copy-start.5
  80.8 15.8 %collective-permute-start.7 = (bf16[1,128,512]{2,1,0:T(8,128)(2,1)S(1)}, bf16[1,128,512]{2,1,0:T(8,128)(2,1)S(1)}, u32[]{:S(2)}, u32[]{:S(2)}) collective-permute-start(bf16[1,128,512]{2,1,0:T(8,128)(2,1)S(1)} %bitcast.12), channel_id=1, source_target_pairs={{0,256},{64,320},{128,384},{192,448},{256,0},{320,64},{384,128},{4... | collective-permute-start | bytes 393224 | tf_op jit(solution)/shard_map/ppermute | solution.py:145
  96.7 11.2 %collective-permute-start.8 = (bf16[2,128,512]{2,1,0:T(8,128)(2,1)S(1)}, bf16[2,128,512]{2,1,0:T(8,128)(2,1)S(1)}, u32[]{:S(2)}, u32[]{:S(2)}) collective-permute-start(bf16[2,128,512]{2,1,0:T(8,128)(2,1)S(1)} %pad_maximum_fusion.3), channel_id=1, source_target_pairs={{0,128},{64,192},{128,0},{192,64},{256,384},{320,448},{384,256},{4... | collective-permute-start | bytes 786440 | tf_op jit(solution)/shard_map/ppermute | solution.py:145
  107.9 10.2 %collective-permute-start.11 = (bf16[4,128,512]{2,1,0:T(8,128)(2,1)S(1)}, bf16[4,128,512]{2,1,0:T(8,128)(2,1)S(1)}, u32[]{:S(2)}, u32[]{:S(2)}) collective-permute-start(bf16[4,128,512]{2,1,0:T(8,128)(2,1)S(1)} %pad_maximum_fusion.refs_0_), channel_id=1, source_target_pairs={{0,48},{16,0},{32,16},{48,32},{1,49},{17,1},{33,17},{49,33},{2,50}... | collective-permute-start | bytes 1572872 | tf_op jit(solution)/shard_map/ppermute | solution.py:179
  109.9 13.9 %collective-permute-start.9 = (bf16[4,128,512]{2,1,0:T(8,128)(2,1)S(1)}, bf16[4,128,512]{2,1,0:T(8,128)(2,1)S(1)}, u32[]{:S(2)}, u32[]{:S(2)}) collective-permute-start(bf16[4,128,512]{2,1,0:T(8,128)(2,1)S(1)} %pad_maximum_fusion.refs_0_), channel_id=1, source_target_pairs={{0,16},{16,32},{32,48},{48,0},{1,17},{17,33},{33,49},{49,1},{2,18}... | collective-permute-start | bytes 1572872 | tf_op jit(solution)/shard_map/ppermute | solution.py:179
  123.8 2.2 %copy-start = (bf16[4096,512]{1,0:T(8,128)(2,1)S(1)}, bf16[4096,512]{1,0:T(8,128)(2,1)}, u32[]{:S(2)}) copy-start(bf16[4096,512]{1,0:T(8,128)(2,1)} %all-gather.6.cloned.1.call-done) | copy-start | bytes 12582916
  127.8 17.5 %copy-start.7 = (s32[4]{0:T(128)S(1)}, s32[4]{0:T(128)}, u32[]{:S(2)}) copy-start(s32[4]{0:T(128)} %constant.22.clone) | copy-start | bytes 52
  127.8 29.9 %copy-start.4 = (f32[512]{0:T(512)S(1)}, f32[512]{0:T(512)}, u32[]{:S(2)}) copy-start(f32[512]{0:T(512)} %param.9) | copy-start | bytes 6148
  127.8 13.8 %collective-permute-start.10 = (bf16[2,128,512]{2,1,0:T(8,128)(2,1)S(1)}, bf16[2,128,512]{2,1,0:T(8,128)(2,1)S(1)}, u32[]{:S(2)}, u32[]{:S(2)}) collective-permute-start(bf16[2,128,512]{2,1,0:T(8,128)(2,1)S(1)} %slice.42), channel_id=1, source_target_pairs={{0,16},{16,32},{32,48},{48,0},{1,17},{17,33},{33,49},{49,1},{2,18}... | collective-permute-start | bytes 786440 | tf_op jit(solution)/shard_map/ppermute | solution.py:183
  129.9 11.7 %collective-permute-start.12 = (bf16[2,128,512]{2,1,0:T(8,128)(2,1)S(1)}, bf16[2,128,512]{2,1,0:T(8,128)(2,1)S(1)}, u32[]{:S(2)}, u32[]{:S(2)}) collective-permute-start(bf16[2,128,512]{2,1,0:T(8,128)(2,1)S(1)} %slice.43), channel_id=1, source_target_pairs={{0,48},{16,0},{32,16},{48,32},{1,49},{17,1},{33,17},{49,33},{2,50}... | collective-permute-start | bytes 786440 | tf_op jit(solution)/shard_map/ppermute | solution.py:183
  136.3 21.5 %collective-permute-start.15 = (f32[512,256]{1,0:T(8,128)S(1)}, f32[512,256]{1,0:T(8,128)S(1)}, u32[]{:S(2)}, u32[]{:S(2)}) collective-permute-start(f32[512,256]{1,0:T(8,128)S(1)} %get-tuple-element.24), channel_id=1, source_target_pairs={{0,64},{64,0},{128,192},{192,128},{256,320},{320,256},{384,448},{4... | collective-permute-start | bytes 1572872 | tf_op jit(solution)/shard_map/ppermute | solution.py:145
  138.2 19.5 %collective-permute-start.14 = (f32[512,128]{1,0:T(8,128)S(1)}, f32[512,128]{1,0:T(8,128)S(1)}, u32[]{:S(2)}, u32[]{:S(2)}) collective-permute-start(f32[512,128]{1,0:T(8,128)S(1)} %get-tuple-element.17), channel_id=1, source_target_pairs={{0,64},{64,0},{128,192},{192,128},{256,320},{320,256},{384,448},{4... | collective-permute-start | bytes 786440 | tf_op jit(solution)/shard_map/ppermute | solution.py:145
  143.4 19.5 %collective-permute-start.13 = (f32[512,128]{1,0:T(8,128)S(1)}, f32[512,128]{1,0:T(8,128)S(1)}, u32[]{:S(2)}, u32[]{:S(2)}) collective-permute-start(f32[512,128]{1,0:T(8,128)S(1)} %get-tuple-element.21), channel_id=1, source_target_pairs={{0,64},{64,0},{128,192},{192,128},{256,320},{320,256},{384,448},{4... | collective-permute-start | bytes 786440 | tf_op jit(solution)/shard_map/ppermute | solution.py:145
Sparse Core Ops, SparseCore 0:
  22.0 46.1 all-gather.3
  80.9 38.6 all-gather.5

commit v15 on v13

--- a/solution.py
+++ b/solution.py
@@ -157,7 +157,9 @@
     t = columns // NY
 
     folds = depth // lanes
-    sent = pack(inverse_gram, training_features)
+    parity = [(2 * z + c, 2 * z + c if c == z % 2 else 2 * (z ^ 1) + (c ^ 1)) for z in range(NZ) for c in range(2)]
+    mixed = lax.ppermute(query_features, ("z", "core"), parity)
+    sent = after(pack(inverse_gram, training_features), mixed)
     got = lax.all_to_all(sent, "y", split_axis=0, concat_axis=0, tiled=True)
     gram_rows = got[:, :rows].reshape(NY * rows, depth)
     training = got[:, rows:].reshape(NY, t // folds, folds, lanes).transpose(2, 1, 0, 3)
@@ -165,8 +167,6 @@
 
     gram = lax.all_gather(gram_rows, ta, axis=0)
 
-    parity = [(2 * z + c, 2 * z + c if c == z % 2 else 2 * (z ^ 1) + (c ^ 1)) for z in range(NZ) for c in range(2)]
-    mixed = lax.ppermute(query_features, ("z", "core"), parity)
     a, b = training[0], training[1]
     for distance in (4, 2):
         a, b = exchange(a, distance), exchange(b, distance)
@@ -175,9 +175,13 @@
 
     own = exchange(exchange(kernel_matrix(slots, gram, (a, b))[None], 4), 2)
     half = slots[: NZ // 2]
+    own = after(own, query)
     below, above = lax.ppermute(own, "y", UP), lax.ppermute(own, "y", DOWN)
+    mine, other = partial_scores(half, query, ([own],))
+    own_pair = mine, swapped(other, 1)
     quarter = NZ // 4
-    far = lax.ppermute(below[:quarter], "y", UP), lax.ppermute(above[quarter:], "y", DOWN)
+    first, second = after(below[:quarter], other), after(above[quarter:], other)
+    far = lax.ppermute(first, "y", UP), lax.ppermute(second, "y", DOWN)
 
     def scores(*blocks):
         mine, other = partial_scores(half, query, blocks)
@@ -186,7 +190,7 @@
     y = lax.axis_index("y").astype(jnp.int32)
     weight = residual_weight[None, :]
     places = lax.rem(y + jnp.array([0, 1, NY - 1, 2], jnp.int32), NY)
-    out = finish(places[:3], (scores([own]), scores([above], [below])), weight, None)
+    out = finish(places[:3], (own_pair, scores([after(above, own_pair[1])], [below])), weight, None)
     return finish(places[3:], (scores(far),), weight, out)
 
 

time: 176 us -> 173 us (0.983)
  local copies, waits for them, and re-layouts: 10.2 us -> 8.07 us
  blocking collectives: 15.1 us -> 13.1 us
  starting transfers between devices: 61.8 us -> 63.6 us
    ppermute x2, waiting for transfers between devices: 9.89 us -> 0.01 us  [local(): below, above = (lax.ppermute(own, 'y', UP), lax.ppermute(own, 'y', DOWN))]
    ppermute x11, waiting for transfers between devices: 52.6 us -> 56.8 us  [swapped(): return lax.ppermute(held, 'z', [(i, i ^ distance) for i in range(NZ)])]
    ppermute x2, waiting for transfers between devices: 0.01 us -> 2.6 us  [local(): far = (lax.ppermute(first, 'y', UP), lax.ppermute(second, 'y', DOWN))]
    ppermute x11, starting transfers between devices: 46 us -> 48.4 us  [swapped(): return lax.ppermute(held, 'z', [(i, i ^ distance) for i in range(NZ)])]
    all_gather x1, waiting for transfers between devices: 0.02 us -> 2.15 us  [local(): query = lax.all_gather(after(mixed, a, b), ta, axis=0)]
    all_to_all x1, blocking collectives: 15.1 us -> 13.1 us  [local(): got = lax.all_to_all(sent, 'y', split_axis=0, concat_axis=0, tiled=True)]
  transfers between devices with their start and end apart: 18 -> 18, of which waited for: 11 -> 12; matrix products, arithmetic and copies ran while one was open for 1% -> 1% of each run, Pallas kernels for 5% -> 5%
where the time goes in v15:
time: 173 us; the launch traced here: 171 us
  starting transfers between devices  63.6 us (37%)
  waiting for transfers between devices  61.7 us (36%)
  between operations  13.8 us (8%)
  blocking collectives  13.1 us (8%)
  Pallas kernels  10.3 us (6%)
  local copies, waits for them, and re-layouts  8.07 us (5%)
    ppermute x11, waiting for transfers between devices, swapped(): return lax.ppermute(held, 'z', [(i, i ^ distance) for i in range(NZ)])  56.8 us
    ppermute x11, starting transfers between devices, swapped(): return lax.ppermute(held, 'z', [(i, i ^ distance) for i in range(NZ)])  48.4 us
    all_to_all x1, blocking collectives, local(): got = lax.all_to_all(sent, 'y', split_axis=0, concat_axis=0, tiled=True)  13.1 us
    ppermute x2, starting transfers between devices, local(): far = (lax.ppermute(first, 'y', UP), lax.ppermute(second, 'y', DOWN))  6.78 us
    ppermute x2, starting transfers between devices, local(): below, above = (lax.ppermute(own, 'y', UP), lax.ppermute(own, 'y', DOWN))  6.56 us
    unnamed x20, local copies, waits for them, and re-layouts  6.22 us
    pallas_call x3, Pallas kernels, partial_scores(): pl.pallas_call(kernel, out_shape=[jax.ShapeDtypeStruct((rows, width), jnp...  5.36 us
  transfers between devices with their start and end apart: 18, of which 12 were waited for; matrix products, arithmetic and copies ran while one was open for 1% of the time, Pallas kernels for 5%

profile of v15, /device:TPU:6, one launch (start us, length us, event | category | flops | bytes accessed | tf_op | source)
XLA Modules:
  0.0 170.7 jit_solution(16796796504417535063)
XLA Ops:
  6.5 0.0 all-gather.4.cloned.1.call-start
  6.5 1.8 %collective-permute-start = (bf16[512,512]{1,0:T(8,128)(2,1)}, bf16[512,512]{1,0:T(8,128)(2,1)S(1)}, u32[]{:S(2)}, u32[]{:S(2)}) collective-permute-start(bf16[512,512]{1,0:T(8,128)(2,1)} %param.6), channel_id=1, source_target_pairs={{0,0},{2,64},{64,2},{66,66},{128,128},{130,192},{192,130},{194,194... | collective-permute-start | bytes 1572872 | tf_op jit(solution)/shard_map/ppermute | solution.py:161
  8.4 0.9 copy-done.2
  9.3 0.9 copy-done.3
  10.2 0.1 pack.1
  10.2 0.0 collective-permute-done
  10.2 0.0 copy-start.5
  10.2 13.1 %all_to_all.5 = bf16[4,160,512]{2,1,0:T(8,128)(2,1)S(1)} all-to-all(bf16[4,160,512]{2,1,0:T(8,128)(2,1)S(1)} %pack.1), channel_id=1, replica_groups=mesh['z'=8,'y'=4,'x'=4,'core'=2,'row'=2] {'y'}, dimensions={0} | all-to-all | bytes 1310720 | tf_op jit(solution)/shard_map/all_to_all | solution.py:163
  23.3 0.9 slice.41
  24.2 0.0 all-gather.4.cloned.1.call-update
  24.2 0.0 all-gather.6.cloned.1.call-start
  24.3 0.1 copy.11
  24.5 9.1 %collective-permute-start.3 = (bf16[1,64,512]{2,1,0:T(8,128)(2,1)S(1)}, bf16[1,64,512]{2,1,0:T(8,128)(2,1)S(1)}, u32[]{:S(2)}, u32[]{:S(2)}) collective-permute-start(bf16[1,64,512]{2,1,0:T(8,128)(2,1)S(1)} %squeeze.7), channel_id=1, source_target_pairs={{0,256},{64,320},{128,384},{192,448},{256,0},{320,64},{384,128},{4... | collective-permute-start | bytes 196616 | tf_op jit(solution)/shard_map/ppermute | solution.py:145
  33.7 1.9 %collective-permute-start.1 = (bf16[1,64,512]{2,1,0:T(8,128)(2,1)S(1)}, bf16[1,64,512]{2,1,0:T(8,128)(2,1)S(1)}, u32[]{:S(2)}, u32[]{:S(2)}) collective-permute-start(bf16[1,64,512]{2,1,0:T(8,128)(2,1)S(1)} %squeeze.6), channel_id=1, source_target_pairs={{0,256},{64,320},{128,384},{192,448},{256,0},{320,64},{384,128},{4... | collective-permute-start | bytes 196616 | tf_op jit(solution)/shard_map/ppermute | solution.py:145
  35.6 0.2 collective-permute-done.3
  35.9 5.2 %collective-permute-start.4 = (bf16[2,64,512]{2,1,0:T(8,128)(2,1)S(1)}, bf16[2,64,512]{2,1,0:T(8,128)(2,1)S(1)}, u32[]{:S(2)}, u32[]{:S(2)}) collective-permute-start(bf16[2,64,512]{2,1,0:T(8,128)(2,1)S(1)} %pad_maximum_fusion.5), channel_id=1, source_target_pairs={{0,128},{64,192},{128,0},{192,64},{256,384},{320,448},{384,256},{4... | collective-permute-start | bytes 393224 | tf_op jit(solution)/shard_map/ppermute | solution.py:145
  41.1 5.4 %collective-permute-done.1 = bf16[1,64,512]{2,1,0:T(8,128)(2,1)S(1)} collective-permute-done((bf16[1,64,512]{2,1,0:T(8,128)(2,1)S(1)}, bf16[1,64,512]{2,1,0:T(8,128)(2,1)S(1)}, u32[]{:S(2)}, u32[]{:S(2)}) %collective-permute-start.1) | collective-permute-done | bytes 65568 | tf_op jit(solution)/shard_map/ppermute | solution.py:145
  46.5 4.6 %collective-permute-start.2 = (bf16[2,64,512]{2,1,0:T(8,128)(2,1)S(1)}, bf16[2,64,512]{2,1,0:T(8,128)(2,1)S(1)}, u32[]{:S(2)}, u32[]{:S(2)}) collective-permute-start(bf16[2,64,512]{2,1,0:T(8,128)(2,1)S(1)} %pad_maximum_fusion.4), channel_id=1, source_target_pairs={{0,128},{64,192},{128,0},{192,64},{256,384},{320,448},{384,256},{4... | collective-permute-start | bytes 393224 | tf_op jit(solution)/shard_map/ppermute | solution.py:145
  51.1 0.0 collective-permute-done.4
  51.1 4.5 %collective-permute-done.2 = bf16[2,64,512]{2,1,0:T(8,128)(2,1)S(1)} collective-permute-done((bf16[2,64,512]{2,1,0:T(8,128)(2,1)S(1)}, bf16[2,64,512]{2,1,0:T(8,128)(2,1)S(1)}, u32[]{:S(2)}, u32[]{:S(2)}) %collective-permute-start.2) | collective-permute-done | bytes 131104 | tf_op jit(solution)/shard_map/ppermute | solution.py:145
  55.6 0.0 copy-done.5
  55.7 0.0 all-gather.6.cloned.1.call-update
  55.7 7.5 %collective-permute-start.6 = (bf16[4,64,512]{2,1,0:T(8,128)(2,1)S(1)}, bf16[4,64,512]{2,1,0:T(8,128)(2,1)S(1)}, u32[]{:S(2)}, u32[]{:S(2)}) collective-permute-start(bf16[4,64,512]{2,1,0:T(8,128)(2,1)S(1)} %constant_dynamic-update-slice_fusion.3), channel_id=1, source_target_pairs={{0,64},{64,0},{128,192},{192,128},{256,320},{320,256},{384,448},{4... | collective-permute-start | bytes 786440 | tf_op jit(solution)/shard_map/ppermute | solution.py:145
  63.2 1.9 %collective-permute-start.5 = (bf16[4,64,512]{2,1,0:T(8,128)(2,1)S(1)}, bf16[4,64,512]{2,1,0:T(8,128)(2,1)S(1)}, u32[]{:S(2)}, u32[]{:S(2)}) collective-permute-start(bf16[4,64,512]{2,1,0:T(8,128)(2,1)S(1)} %constant_dynamic-update-slice_fusion), channel_id=1, source_target_pairs={{0,64},{64,0},{128,192},{192,128},{256,320},{320,256},{384,448},{4... | collective-permute-start | bytes 786440 | tf_op jit(solution)/shard_map/ppermute | solution.py:145
  65.1 0.0 copy-done.7
  65.1 5.3 %collective-permute-done.6 = bf16[4,64,512]{2,1,0:T(8,128)(2,1)S(1)} collective-permute-done((bf16[4,64,512]{2,1,0:T(8,128)(2,1)S(1)}, bf16[4,64,512]{2,1,0:T(8,128)(2,1)S(1)}, u32[]{:S(2)}, u32[]{:S(2)}) %collective-permute-start.6) | collective-permute-done | bytes 262176 | tf_op jit(solution)/shard_map/ppermute | solution.py:145
  70.4 0.1 pad_maximum_fusion.1.refs_1_
  70.4 2.9 %collective-permute-done.5 = bf16[4,64,512]{2,1,0:T(8,128)(2,1)S(1)} collective-permute-done((bf16[4,64,512]{2,1,0:T(8,128)(2,1)S(1)}, bf16[4,64,512]{2,1,0:T(8,128)(2,1)S(1)}, u32[]{:S(2)}, u32[]{:S(2)}) %collective-permute-start.5) | collective-permute-done | bytes 262176 | tf_op jit(solution)/shard_map/ppermute | solution.py:145
  73.3 0.1 pad_maximum_fusion.refs_0_
  73.4 0.0 all-gather.4.cloned.1.call-done.gram_ref
  73.4 0.0 copy-start.1
  73.4 2.2 %copy-done.1 = bf16[8,512,512]{2,1,0:T(8,128)(2,1)S(1)} copy-done((bf16[8,512,512]{2,1,0:T(8,128)(2,1)S(1)}, bf16[8,512,512]{2,1,0:T(8,128)(2,1)}, u32[]{:S(2)}) %copy-start.1) | copy-done | bytes 4194328
  75.6 2.0 %kernel_matrix.1 = bf16[128,512]{1,0:T(8,128)(2,1)S(1)} custom-call(s32[8]{0:T(128)S(1)} %broadcast_xor_fusion.slots, bf16[8,512,512]{2,1,0:T(8,128)(2,1)S(1)} %copy-done.1, bf16[8,64,512]{2,1,0:T(8,128)(2,1)S(1)} %pad_maximum_fusion.refs_0_, bf16[8,64,512]{2,1,0:T(8,128)(2,1)S(1)} %pad_maximum_fusion.1.refs_1_), custom_call_target="tpu_custom_call" | custom-call | flops 536870912 | bytes 5242880 | tf_op jit(solution)/shard_map/kernel_matrix/pallas_call | solution.py:51
  77.6 5.9 %collective-permute-start.7 = (bf16[1,128,512]{2,1,0:T(8,128)(2,1)S(1)}, bf16[1,128,512]{2,1,0:T(8,128)(2,1)S(1)}, u32[]{:S(2)}, u32[]{:S(2)}) collective-permute-start(bf16[1,128,512]{2,1,0:T(8,128)(2,1)S(1)} %bitcast.12), channel_id=1, source_target_pairs={{0,256},{64,320},{128,384},{192,448},{256,0},{320,64},{384,128},{4... | collective-permute-start | bytes 393224 | tf_op jit(solution)/shard_map/ppermute | solution.py:145
  83.5 12.0 %collective-permute-done.7 = bf16[1,128,512]{2,1,0:T(8,128)(2,1)S(1)} collective-permute-done((bf16[1,128,512]{2,1,0:T(8,128)(2,1)S(1)}, bf16[1,128,512]{2,1,0:T(8,128)(2,1)S(1)}, u32[]{:S(2)}, u32[]{:S(2)}) %collective-permute-start.7) | collective-permute-done | bytes 131104 | tf_op jit(solution)/shard_map/ppermute | solution.py:145
  95.5 1.9 %collective-permute-start.8 = (bf16[2,128,512]{2,1,0:T(8,128)(2,1)S(1)}, bf16[2,128,512]{2,1,0:T(8,128)(2,1)S(1)}, u32[]{:S(2)}, u32[]{:S(2)}) collective-permute-start(bf16[2,128,512]{2,1,0:T(8,128)(2,1)S(1)} %pad_maximum_fusion.3), channel_id=1, source_target_pairs={{0,128},{64,192},{128,0},{192,64},{256,384},{320,448},{384,256},{4... | collective-permute-start | bytes 786440 | tf_op jit(solution)/shard_map/ppermute | solution.py:145
  97.5 13.7 %collective-permute-done.8 = bf16[2,128,512]{2,1,0:T(8,128)(2,1)S(1)} collective-permute-done((bf16[2,128,512]{2,1,0:T(8,128)(2,1)S(1)}, bf16[2,128,512]{2,1,0:T(8,128)(2,1)S(1)}, u32[]{:S(2)}, u32[]{:S(2)}) %collective-permute-start.8) | collective-permute-done | bytes 262176 | tf_op jit(solution)/shard_map/ppermute | solution.py:145
  111.1 0.1 pad_maximum_fusion.2.refs_0_
  111.2 2.2 %all-gather.6.cloned.1.call-done = bf16[4096,512]{1,0:T(8,128)(2,1)} async-done(((bf16[512,512]{1,0:T(8,128)(2,1)}), bf16[4096,512]{1,0:T(8,128)(2,1)}) %all-gather.6.cloned.1.call-update) | async-done | bytes 4194320 | tf_op jit(solution)/shard_map/all_gather | solution.py:173
  113.3 4.6 %collective-permute-start.11 = (bf16[4,128,512]{2,1,0:T(8,128)(2,1)S(1)}, bf16[4,128,512]{2,1,0:T(8,128)(2,1)S(1)}, u32[]{:S(2)}, u32[]{:S(2)}) collective-permute-start(bf16[4,128,512]{2,1,0:T(8,128)(2,1)S(1)} %pad_maximum_fusion.2.refs_0_), channel_id=1, source_target_pairs={{0,48},{16,0},{32,16},{48,32},{1,49},{17,1},{33,17},{49,33},{2,50}... | collective-permute-start | bytes 1572872 | tf_op jit(solution)/shard_map/ppermute | solution.py:179
  118.0 1.9 %collective-permute-start.9 = (bf16[4,128,512]{2,1,0:T(8,128)(2,1)S(1)}, bf16[4,128,512]{2,1,0:T(8,128)(2,1)S(1)}, u32[]{:S(2)}, u32[]{:S(2)}) collective-permute-start(bf16[4,128,512]{2,1,0:T(8,128)(2,1)S(1)} %pad_maximum_fusion.2.refs_0_), channel_id=1, source_target_pairs={{0,16},{16,32},{32,48},{48,0},{1,17},{17,33},{33,49},{49,1},{2,18}... | collective-permute-start | bytes 1572872 | tf_op jit(solution)/shard_map/ppermute | solution.py:179
  119.9 0.0 copy-start
  119.9 2.2 %copy-done = bf16[4096,512]{1,0:T(8,128)(2,1)S(1)} copy-done((bf16[4096,512]{1,0:T(8,128)(2,1)S(1)}, bf16[4096,512]{1,0:T(8,128)(2,1)}, u32[]{:S(2)}) %copy-start) | copy-done | bytes 4194328
  122.1 1.8 %partial_scores.3 = (f32[512,128]{1,0:T(8,128)S(1)}, f32[512,128]{1,0:T(8,128)S(1)}) custom-call(s32[4]{0:T(128)S(1)} %bitcast.17, bf16[8,512,512]{2,1,0:T(8,128)(2,1)S(1)} %bitcast.9, bf16[4,128,512]{2,1,0:T(8,128)(2,1)S(1)} %pad_maximum_fusion.2.refs_0_), custom_call_target="tpu_custom_call" | custom-call | flops 536870912 | bytes 4718592 | tf_op jit(solution)/shard_map/partial_scores/pallas_call | solution.py:85
  123.9 3.5 %collective-permute-start.14 = (f32[512,128]{1,0:T(8,128)S(1)}, f32[512,128]{1,0:T(8,128)S(1)}, u32[]{:S(2)}, u32[]{:S(2)}) collective-permute-start(f32[512,128]{1,0:T(8,128)S(1)} %get-tuple-element.20), channel_id=1, source_target_pairs={{0,64},{64,0},{128,192},{192,128},{256,320},{320,256},{384,448},{4... | collective-permute-start | bytes 786440 | tf_op jit(solution)/shard_map/ppermute | solution.py:145
  127.3 6.6 %collective-permute-done.14.refs_1_ = f32[512,128]{1,0:T(8,128)S(1)} collective-permute-done((f32[512,128]{1,0:T(8,128)S(1)}, f32[512,128]{1,0:T(8,128)S(1)}, u32[]{:S(2)}, u32[]{:S(2)}) %collective-permute-start.14) | collective-permute-done | bytes 262176 | tf_op jit(solution)/shard_map/ppermute | solution.py:145
  133.9 0.0 collective-permute-done.11.refs_0_
  134.0 4.9 %collective-permute-start.12 = (bf16[2,128,512]{2,1,0:T(8,128)(2,1)S(1)}, bf16[2,128,512]{2,1,0:T(8,128)(2,1)S(1)}, u32[]{:S(2)}, u32[]{:S(2)}) collective-permute-start(bf16[2,128,512]{2,1,0:T(8,128)(2,1)S(1)} %slice.43), channel_id=1, source_target_pairs={{0,48},{16,0},{32,16},{48,32},{1,49},{17,1},{33,17},{49,33},{2,50}... | collective-permute-start | bytes 786440 | tf_op jit(solution)/shard_map/ppermute | solution.py:184
  138.8 0.0 collective-permute-done.9.refs_1_
  138.9 0.0 copy-start.6
  138.9 0.0 copy-start.4
  138.9 1.9 %collective-permute-start.10 = (bf16[2,128,512]{2,1,0:T(8,128)(2,1)S(1)}, bf16[2,128,512]{2,1,0:T(8,128)(2,1)S(1)}, u32[]{:S(2)}, u32[]{:S(2)}) collective-permute-start(bf16[2,128,512]{2,1,0:T(8,128)(2,1)S(1)} %slice.42), channel_id=1, source_target_pairs={{0,16},{16,32},{32,48},{48,0},{1,17},{17,33},{33,49},{49,1},{2,18}... | collective-permute-start | bytes 786440 | tf_op jit(solution)/shard_map/ppermute | solution.py:184
  140.8 1.8 %partial_scores.5 = (f32[512,256]{1,0:T(8,128)S(1)}, f32[512,256]{1,0:T(8,128)S(1)}) custom-call(s32[4]{0:T(128)S(1)} %bitcast.18, bf16[8,512,512]{2,1,0:T(8,128)(2,1)S(1)} %bitcast.10, bf16[4,128,512]{2,1,0:T(8,128)(2,1)S(1)} %collective-permute-done.11.refs_0_, bf16[4,128,512]{2,1,0:T(8,128)(2,1)S(1)} %collective-permute-done.9.refs_1_), custom_call_target="tpu_custom_call" | custom-call | flops 1073741824 | bytes 5242880 | tf_op jit(solution)/shard_map/partial_scores/pallas_call | solution.py:85
  142.6 3.5 %collective-permute-start.15 = (f32[512,256]{1,0:T(8,128)S(1)}, f32[512,256]{1,0:T(8,128)S(1)}, u32[]{:S(2)}, u32[]{:S(2)}) collective-permute-start(f32[512,256]{1,0:T(8,128)S(1)} %get-tuple-element.28), channel_id=1, source_target_pairs={{0,64},{64,0},{128,192},{192,128},{256,320},{320,256},{384,448},{4... | collective-permute-start | bytes 1572872 | tf_op jit(solution)/shard_map/ppermute | solution.py:145
  146.1 0.0 collective-permute-done.12.refs_1_
  146.1 2.6 %collective-permute-done.10.refs_0_ = bf16[2,128,512]{2,1,0:T(8,128)(2,1)S(1)} collective-permute-done((bf16[2,128,512]{2,1,0:T(8,128)(2,1)S(1)}, bf16[2,128,512]{2,1,0:T(8,128)(2,1)S(1)}, u32[]{:S(2)}, u32[]{:S(2)}) %collective-permute-start.10) | collective-permute-done | bytes 262176 | tf_op jit(solution)/shard_map/ppermute | solution.py:184
  148.7 1.8 %partial_scores.4 = (f32[512,128]{1,0:T(8,128)S(1)}, f32[512,128]{1,0:T(8,128)S(1)}) custom-call(s32[4]{0:T(128)S(1)} %bitcast.19, bf16[8,512,512]{2,1,0:T(8,128)(2,1)S(1)} %bitcast.11, bf16[2,128,512]{2,1,0:T(8,128)(2,1)S(1)} %collective-permute-done.10.refs_0_, bf16[2,128,512]{2,1,0:T(8,128)(2,1)S(1)} %collective-permute-done.12.refs_1_), custom_call_target="tpu_custom_call" | custom-call | flops 536870912 | bytes 4718592 | tf_op jit(solution)/shard_map/partial_scores/pallas_call | solution.py:85
  150.5 3.5 %collective-permute-start.13 = (f32[512,128]{1,0:T(8,128)S(1)}, f32[512,128]{1,0:T(8,128)S(1)}, u32[]{:S(2)}, u32[]{:S(2)}) collective-permute-start(f32[512,128]{1,0:T(8,128)S(1)} %get-tuple-element.24), channel_id=1, source_target_pairs={{0,64},{64,0},{128,192},{192,128},{256,320},{320,256},{384,448},{4... | collective-permute-start | bytes 786440 | tf_op jit(solution)/shard_map/ppermute | solution.py:145
  154.0 0.0 copy-done.6
  154.0 0.7 slice.29.places
  154.7 4.7 %collective-permute-done.15.refs_3_ = f32[512,256]{1,0:T(8,128)S(1)} collective-permute-done((f32[512,256]{1,0:T(8,128)S(1)}, f32[512,256]{1,0:T(8,128)S(1)}, u32[]{:S(2)}, u32[]{:S(2)}) %collective-permute-start.15) | collective-permute-done | bytes 524320 | tf_op jit(solution)/shard_map/ppermute | solution.py:145
  159.4 1.5 finish.2.refs_2_
  160.9 1.6 collective-permute-done.13.refs_1_
  162.5 1.4 finish.3
  (22 shorter events, 0.3 us)
Async XLA Ops:
  6.5 58.6 %copy-start.7 = (s32[8]{0:T(128)S(1)}, s32[8]{0:T(128)}, u32[]{:S(2)}) copy-start(s32[8]{0:T(128)} %constant.21.clone) | copy-start | bytes 100
  6.5 66.9 %all-gather.4.cloned.1.call-start = ((), (), s32[]{:S(2)}) async-start(), calls=%async_computation.1 | async-start | bytes 4718592 | tf_op jit(solution)/shard_map/all_gather | solution.py:168
  6.5 3.7 %collective-permute-start = (bf16[512,512]{1,0:T(8,128)(2,1)}, bf16[512,512]{1,0:T(8,128)(2,1)S(1)}, u32[]{:S(2)}, u32[]{:S(2)}) collective-permute-start(bf16[512,512]{1,0:T(8,128)(2,1)} %param.6), channel_id=1, source_target_pairs={{0,0},{2,64},{64,2},{66,66},{128,128},{130,192},{192,130},{194,194... | collective-permute-start | bytes 1572872 | tf_op jit(solution)/shard_map/ppermute | solution.py:161
  8.4 0.9 copy-start.2
  9.3 0.9 copy-start.3
  10.2 45.4 %copy-start.5 = (bf16[512,512]{1,0:T(8,128)(2,1)}, bf16[512,512]{1,0:T(8,128)(2,1)S(1)}, u32[]{:S(2)}) copy-start(bf16[512,512]{1,0:T(8,128)(2,1)S(1)} %collective-permute-done) | copy-start | bytes 1572868
  24.2 89.1 %all-gather.6.cloned.1.call-start = ((), (), s32[]{:S(2)}) async-start(), calls=%async_computation.2 | async-start | bytes 4718592 | tf_op jit(solution)/shard_map/all_gather | solution.py:173
  24.5 11.3 %collective-permute-start.3 = (bf16[1,64,512]{2,1,0:T(8,128)(2,1)S(1)}, bf16[1,64,512]{2,1,0:T(8,128)(2,1)S(1)}, u32[]{:S(2)}, u32[]{:S(2)}) collective-permute-start(bf16[1,64,512]{2,1,0:T(8,128)(2,1)S(1)} %squeeze.7), channel_id=1, source_target_pairs={{0,256},{64,320},{128,384},{192,448},{256,0},{320,64},{384,128},{4... | collective-permute-start | bytes 196616 | tf_op jit(solution)/shard_map/ppermute | solution.py:145
  33.7 12.8 %collective-permute-start.1 = (bf16[1,64,512]{2,1,0:T(8,128)(2,1)S(1)}, bf16[1,64,512]{2,1,0:T(8,128)(2,1)S(1)}, u32[]{:S(2)}, u32[]{:S(2)}) collective-permute-start(bf16[1,64,512]{2,1,0:T(8,128)(2,1)S(1)} %squeeze.6), channel_id=1, source_target_pairs={{0,256},{64,320},{128,384},{192,448},{256,0},{320,64},{384,128},{4... | collective-permute-start | bytes 196616 | tf_op jit(solution)/shard_map/ppermute | solution.py:145
  35.9 15.2 %collective-permute-start.4 = (bf16[2,64,512]{2,1,0:T(8,128)(2,1)S(1)}, bf16[2,64,512]{2,1,0:T(8,128)(2,1)S(1)}, u32[]{:S(2)}, u32[]{:S(2)}) collective-permute-start(bf16[2,64,512]{2,1,0:T(8,128)(2,1)S(1)} %pad_maximum_fusion.5), channel_id=1, source_target_pairs={{0,128},{64,192},{128,0},{192,64},{256,384},{320,448},{384,256},{4... | collective-permute-start | bytes 393224 | tf_op jit(solution)/shard_map/ppermute | solution.py:145
  46.5 9.2 %collective-permute-start.2 = (bf16[2,64,512]{2,1,0:T(8,128)(2,1)S(1)}, bf16[2,64,512]{2,1,0:T(8,128)(2,1)S(1)}, u32[]{:S(2)}, u32[]{:S(2)}) collective-permute-start(bf16[2,64,512]{2,1,0:T(8,128)(2,1)S(1)} %pad_maximum_fusion.4), channel_id=1, source_target_pairs={{0,128},{64,192},{128,0},{192,64},{256,384},{320,448},{384,256},{4... | collective-permute-start | bytes 393224 | tf_op jit(solution)/shard_map/ppermute | solution.py:145
  55.7 14.7 %collective-permute-start.6 = (bf16[4,64,512]{2,1,0:T(8,128)(2,1)S(1)}, bf16[4,64,512]{2,1,0:T(8,128)(2,1)S(1)}, u32[]{:S(2)}, u32[]{:S(2)}) collective-permute-start(bf16[4,64,512]{2,1,0:T(8,128)(2,1)S(1)} %constant_dynamic-update-slice_fusion.3), channel_id=1, source_target_pairs={{0,64},{64,0},{128,192},{192,128},{256,320},{320,256},{384,448},{4... | collective-permute-start | bytes 786440 | tf_op jit(solution)/shard_map/ppermute | solution.py:145
  63.2 10.2 %collective-permute-start.5 = (bf16[4,64,512]{2,1,0:T(8,128)(2,1)S(1)}, bf16[4,64,512]{2,1,0:T(8,128)(2,1)S(1)}, u32[]{:S(2)}, u32[]{:S(2)}) collective-permute-start(bf16[4,64,512]{2,1,0:T(8,128)(2,1)S(1)} %constant_dynamic-update-slice_fusion), channel_id=1, source_target_pairs={{0,64},{64,0},{128,192},{192,128},{256,320},{320,256},{384,448},{4... | collective-permute-start | bytes 786440 | tf_op jit(solution)/shard_map/ppermute | solution.py:145
  73.4 2.2 %copy-start.1 = (bf16[8,512,512]{2,1,0:T(8,128)(2,1)S(1)}, bf16[8,512,512]{2,1,0:T(8,128)(2,1)}, u32[]{:S(2)}) copy-start(bf16[8,512,512]{2,1,0:T(8,128)(2,1)} %all-gather.4.cloned.1.call-done.gram_ref) | copy-start | bytes 12582916
  77.6 17.9 %collective-permute-start.7 = (bf16[1,128,512]{2,1,0:T(8,128)(2,1)S(1)}, bf16[1,128,512]{2,1,0:T(8,128)(2,1)S(1)}, u32[]{:S(2)}, u32[]{:S(2)}) collective-permute-start(bf16[1,128,512]{2,1,0:T(8,128)(2,1)S(1)} %bitcast.12), channel_id=1, source_target_pairs={{0,256},{64,320},{128,384},{192,448},{256,0},{320,64},{384,128},{4... | collective-permute-start | bytes 393224 | tf_op jit(solution)/shard_map/ppermute | solution.py:145
  95.5 15.6 %collective-permute-start.8 = (bf16[2,128,512]{2,1,0:T(8,128)(2,1)S(1)}, bf16[2,128,512]{2,1,0:T(8,128)(2,1)S(1)}, u32[]{:S(2)}, u32[]{:S(2)}) collective-permute-start(bf16[2,128,512]{2,1,0:T(8,128)(2,1)S(1)} %pad_maximum_fusion.3), channel_id=1, source_target_pairs={{0,128},{64,192},{128,0},{192,64},{256,384},{320,448},{384,256},{4... | collective-permute-start | bytes 786440 | tf_op jit(solution)/shard_map/ppermute | solution.py:145
  113.3 20.6 %collective-permute-start.11 = (bf16[4,128,512]{2,1,0:T(8,128)(2,1)S(1)}, bf16[4,128,512]{2,1,0:T(8,128)(2,1)S(1)}, u32[]{:S(2)}, u32[]{:S(2)}) collective-permute-start(bf16[4,128,512]{2,1,0:T(8,128)(2,1)S(1)} %pad_maximum_fusion.2.refs_0_), channel_id=1, source_target_pairs={{0,48},{16,0},{32,16},{48,32},{1,49},{17,1},{33,17},{49,33},{2,50}... | collective-permute-start | bytes 1572872 | tf_op jit(solution)/shard_map/ppermute | solution.py:179
  118.0 20.9 %collective-permute-start.9 = (bf16[4,128,512]{2,1,0:T(8,128)(2,1)S(1)}, bf16[4,128,512]{2,1,0:T(8,128)(2,1)S(1)}, u32[]{:S(2)}, u32[]{:S(2)}) collective-permute-start(bf16[4,128,512]{2,1,0:T(8,128)(2,1)S(1)} %pad_maximum_fusion.2.refs_0_), channel_id=1, source_target_pairs={{0,16},{16,32},{32,48},{48,0},{1,17},{17,33},{33,49},{49,1},{2,18}... | collective-permute-start | bytes 1572872 | tf_op jit(solution)/shard_map/ppermute | solution.py:179
  119.9 2.2 %copy-start = (bf16[4096,512]{1,0:T(8,128)(2,1)S(1)}, bf16[4096,512]{1,0:T(8,128)(2,1)}, u32[]{:S(2)}) copy-start(bf16[4096,512]{1,0:T(8,128)(2,1)} %all-gather.6.cloned.1.call-done) | copy-start | bytes 12582916
  123.9 10.1 %collective-permute-start.14 = (f32[512,128]{1,0:T(8,128)S(1)}, f32[512,128]{1,0:T(8,128)S(1)}, u32[]{:S(2)}, u32[]{:S(2)}) collective-permute-start(f32[512,128]{1,0:T(8,128)S(1)} %get-tuple-element.20), channel_id=1, source_target_pairs={{0,64},{64,0},{128,192},{192,128},{256,320},{320,256},{384,448},{4... | collective-permute-start | bytes 786440 | tf_op jit(solution)/shard_map/ppermute | solution.py:145
  134.0 12.1 %collective-permute-start.12 = (bf16[2,128,512]{2,1,0:T(8,128)(2,1)S(1)}, bf16[2,128,512]{2,1,0:T(8,128)(2,1)S(1)}, u32[]{:S(2)}, u32[]{:S(2)}) collective-permute-start(bf16[2,128,512]{2,1,0:T(8,128)(2,1)S(1)} %slice.43), channel_id=1, source_target_pairs={{0,48},{16,0},{32,16},{48,32},{1,49},{17,1},{33,17},{49,33},{2,50}... | collective-permute-start | bytes 786440 | tf_op jit(solution)/shard_map/ppermute | solution.py:184
  138.9 15.1 %copy-start.6 = (s32[4]{0:T(128)S(1)}, s32[4]{0:T(128)}, u32[]{:S(2)}) copy-start(s32[4]{0:T(128)} %constant.22.clone) | copy-start | bytes 52
  138.9 20.5 %copy-start.4 = (f32[512]{0:T(512)S(1)}, f32[512]{0:T(512)}, u32[]{:S(2)}) copy-start(f32[512]{0:T(512)} %param.9) | copy-start | bytes 6148
  138.9 9.8 %collective-permute-start.10 = (bf16[2,128,512]{2,1,0:T(8,128)(2,1)S(1)}, bf16[2,128,512]{2,1,0:T(8,128)(2,1)S(1)}, u32[]{:S(2)}, u32[]{:S(2)}) collective-permute-start(bf16[2,128,512]{2,1,0:T(8,128)(2,1)S(1)} %slice.42), channel_id=1, source_target_pairs={{0,16},{16,32},{32,48},{48,0},{1,17},{17,33},{33,49},{49,1},{2,18}... | collective-permute-start | bytes 786440 | tf_op jit(solution)/shard_map/ppermute | solution.py:184
  142.6 16.8 %collective-permute-start.15 = (f32[512,256]{1,0:T(8,128)S(1)}, f32[512,256]{1,0:T(8,128)S(1)}, u32[]{:S(2)}, u32[]{:S(2)}) collective-permute-start(f32[512,256]{1,0:T(8,128)S(1)} %get-tuple-element.28), channel_id=1, source_target_pairs={{0,64},{64,0},{128,192},{192,128},{256,320},{320,256},{384,448},{4... | collective-permute-start | bytes 1572872 | tf_op jit(solution)/shard_map/ppermute | solution.py:145
  150.5 12.0 %collective-permute-start.13 = (f32[512,128]{1,0:T(8,128)S(1)}, f32[512,128]{1,0:T(8,128)S(1)}, u32[]{:S(2)}, u32[]{:S(2)}) collective-permute-start(f32[512,128]{1,0:T(8,128)S(1)} %get-tuple-element.24), channel_id=1, source_target_pairs={{0,64},{64,0},{128,192},{192,128},{256,320},{320,256},{384,448},{4... | collective-permute-start | bytes 786440 | tf_op jit(solution)/shard_map/ppermute | solution.py:145
Sparse Core Ops, SparseCore 0:
  24.3 46.9 all-gather.3
  73.5 39.7 all-gather.5

commit v16 on v12

--- a/solution.py
+++ b/solution.py
@@ -5,7 +5,7 @@
 from jax.experimental.pallas import tpu as pltpu
 from jax.sharding import Mesh, PartitionSpec as P
 
-NZ, NY, CHUNKS = 8, 4, 2
+NZ, NY = 8, 4
 NT_DIMS = (((1,), (1,)), ((), ()))
 RELATIVE = (0, 4, 2, 6, 1, 5, 3, 7)
 VMEM_LIMIT = 16 * 1024 * 1024
@@ -124,13 +124,13 @@
     got = lax.all_to_all(sent, "y", split_axis=0, concat_axis=0, tiled=True)
     gram_rows = got[:, :rows].reshape(NY * rows, depth)
     training = got[:, rows:].reshape(NY, t // folds, folds, lanes).transpose(2, 1, 0, 3)
-    training = training.reshape(CHUNKS, 1, t // CHUNKS, NY * lanes)
+    training = training.reshape(1, t, NY * lanes)
 
     gram = lax.all_gather(gram_rows, ("x", "core"), axis=0)
     query = lax.all_gather(after(query_features, gram_rows), ("x", "core"), axis=0)
     weight = residual_weight[None, :]
 
-    a, b = training[0], training[1]
+    a, b = training[:, : 3 * t // 8], training[:, 3 * t // 8 :]
     for distance in (4, 2, 1):
         a, b = exchange(a, distance), exchange(b, distance)
     a, b = kernel_matrix(slots, gram, a)[None], kernel_matrix(slots, gram, b)[None]

time: 163 us -> 179 us (1.098)
  the two profiles are of different devices: /device:TPU:192 before, /device:TPU:6 now
where the time goes in v16:
time: 179 us; the launch traced here: 176 us
  starting transfers between devices  76.9 us (43%)
  waiting for transfers between devices  47.4 us (26%)
  blocking collectives  15.1 us (8%)
  Pallas kernels  14.8 us (8%)
  between operations  13.8 us (8%)
  local copies, waits for them, and re-layouts  7.25 us (4%)
    ppermute x12, starting transfers between devices, exchange(): other = lax.ppermute(held, 'z', [(i, i ^ distance) for i in range(NZ)])  57.4 us
    ppermute x12, waiting for transfers between devices, exchange(): other = lax.ppermute(held, 'z', [(i, i ^ distance) for i in range(NZ)])  30.8 us
    all_to_all x1, blocking collectives, local(): got = lax.all_to_all(sent, 'y', split_axis=0, concat_axis=0, tiled=True)  15.1 us
    ppermute x2, waiting for transfers between devices, local(): below_a, above_a = (lax.ppermute(a, 'y', UP), lax.ppermute(a, 'y', DOWN))  12.2 us
    pallas_call x4, Pallas kernels, score_columns(): pl.pallas_call(kernel, out_shape=jax.ShapeDtypeStruct((rows, columns), jn...  10.9 us
    ppermute x2, starting transfers between devices, local(): below_b, above_b = (lax.ppermute(b, 'y', UP), lax.ppermute(b, 'y', DOWN))  8.04 us
    ppermute x2, starting transfers between devices, local(): far = (lax.ppermute(below_a, 'y', UP), lax.ppermute(above_b, 'y', DOWN))  7 us
    unnamed x14, local copies, waits for them, and re-layouts  6.2 us
  transfers between devices with their start and end apart: 20, of which 10 were waited for; matrix products, arithmetic and copies ran while one was open for 0% of the time, Pallas kernels for 7%

profile of v16, /device:TPU:6, one launch (start us, length us, event | category | flops | bytes accessed | tf_op | source)
XLA Modules:
  0.0 175.7 jit_solution(14007259574111918975)
XLA Ops:
  6.5 0.0 all-gather.4.cloned.1.call-start
  6.5 0.9 copy-done.3
  7.5 0.9 copy-done.4
  8.4 0.1 pack.1
  8.4 15.1 %all_to_all.5 = bf16[4,160,512]{2,1,0:T(8,128)(2,1)S(1)} all-to-all(bf16[4,160,512]{2,1,0:T(8,128)(2,1)S(1)} %pack.1), channel_id=1, replica_groups=mesh['z'=8,'y'=4,'x'=4,'core'=2,'row'=2] {'y'}, dimensions={0} | all-to-all | bytes 1310720 | tf_op jit(solution)/shard_map/all_to_all | solution.py:124
  23.6 0.8 slice.16
  24.4 0.0 all-gather.4.cloned.1.call-update
  24.4 0.0 all-gather.6.cloned.1.call-start
  24.5 0.7 all-gather.6.cloned.1.call-update
  25.2 0.1 copy.12
  25.3 0.1 reshape.8
  25.4 9.1 %collective-permute-start.8 = (bf16[1,80,512]{2,1,0:T(8,128)(2,1)S(1)}, bf16[1,80,512]{2,1,0:T(8,128)(2,1)S(1)}, u32[]{:S(2)}, u32[]{:S(2)}) collective-permute-start(bf16[1,80,512]{2,1,0:T(8,128)(2,1)S(1)} %slice.19), channel_id=1, source_target_pairs={{0,256},{64,320},{128,384},{192,448},{256,0},{320,64},{384,128},{4... | collective-permute-start | bytes 245768 | tf_op jit(solution)/shard_map/ppermute | solution.py:111
  34.5 7.0 %collective-permute-done.8 = bf16[1,80,512]{2,1,0:T(8,128)(2,1)S(1)} collective-permute-done((bf16[1,80,512]{2,1,0:T(8,128)(2,1)S(1)}, bf16[1,80,512]{2,1,0:T(8,128)(2,1)S(1)}, u32[]{:S(2)}, u32[]{:S(2)}) %collective-permute-start.8) | collective-permute-done | bytes 81952 | tf_op jit(solution)/shard_map/ppermute | solution.py:111
  41.6 1.9 %collective-permute-start.9 = (bf16[2,80,512]{2,1,0:T(8,128)(2,1)S(1)}, bf16[2,80,512]{2,1,0:T(8,128)(2,1)S(1)}, u32[]{:S(2)}, u32[]{:S(2)}) collective-permute-start(bf16[2,80,512]{2,1,0:T(8,128)(2,1)S(1)} %pad_maximum_fusion.8), channel_id=1, source_target_pairs={{0,128},{64,192},{128,0},{192,64},{256,384},{320,448},{384,256},{4... | collective-permute-start | bytes 491528 | tf_op jit(solution)/shard_map/ppermute | solution.py:111
  43.5 8.1 %collective-permute-done.9 = bf16[2,80,512]{2,1,0:T(8,128)(2,1)S(1)} collective-permute-done((bf16[2,80,512]{2,1,0:T(8,128)(2,1)S(1)}, bf16[2,80,512]{2,1,0:T(8,128)(2,1)S(1)}, u32[]{:S(2)}, u32[]{:S(2)}) %collective-permute-start.9) | collective-permute-done | bytes 163872 | tf_op jit(solution)/shard_map/ppermute | solution.py:111
  51.6 1.9 %collective-permute-start.10 = (bf16[4,80,512]{2,1,0:T(8,128)(2,1)S(1)}, bf16[4,80,512]{2,1,0:T(8,128)(2,1)S(1)}, u32[]{:S(2)}, u32[]{:S(2)}) collective-permute-start(bf16[4,80,512]{2,1,0:T(8,128)(2,1)S(1)} %pad_maximum_fusion.4), channel_id=1, source_target_pairs={{0,64},{64,0},{128,192},{192,128},{256,320},{320,256},{384,448},{4... | collective-permute-start | bytes 983048 | tf_op jit(solution)/shard_map/ppermute | solution.py:111
  53.6 0.0 copy-done.6
  53.6 7.5 %collective-permute-start = (bf16[1,48,512]{2,1,0:T(8,128)(2,1)S(1)}, bf16[1,48,512]{2,1,0:T(8,128)(2,1)S(1)}, u32[]{:S(2)}, u32[]{:S(2)}) collective-permute-start(bf16[1,48,512]{2,1,0:T(8,128)(2,1)S(1)} %slice.18), channel_id=1, source_target_pairs={{0,256},{64,320},{128,384},{192,448},{256,0},{320,64},{384,128},{4... | collective-permute-start | bytes 147464 | tf_op jit(solution)/shard_map/ppermute | solution.py:111
  61.1 0.0 collective-permute-done.10
  61.1 0.1 pad_maximum_fusion.training_ref
  61.2 3.7 %all-gather.4.cloned.1.call-done.gram_ref = bf16[8,512,512]{2,1,0:T(8,128)(2,1)} async-done(((bf16[1,512,512]{2,1,0:T(8,128)(2,1)}), bf16[8,512,512]{2,1,0:T(8,128)(2,1)}) %all-gather.4.cloned.1.call-update) | async-done | bytes 4194320 | tf_op jit(solution)/shard_map/all_gather | solution.py:129
  64.9 2.2 %copy-done.2 = bf16[8,512,512]{2,1,0:T(8,128)(2,1)S(1)} copy-done((bf16[8,512,512]{2,1,0:T(8,128)(2,1)S(1)}, bf16[8,512,512]{2,1,0:T(8,128)(2,1)}, u32[]{:S(2)}) %copy-start.2) | copy-done | bytes 4194328
  67.1 1.9 %kernel_matrix.3 = bf16[80,512]{1,0:T(8,128)(2,1)S(1)} custom-call(s32[8]{0:T(128)S(1)} %broadcast_xor_fusion.slots, bf16[8,512,512]{2,1,0:T(8,128)(2,1)S(1)} %copy-done.2, bf16[8,80,512]{2,1,0:T(8,128)(2,1)S(1)} %pad_maximum_fusion.training_ref), custom_call_target="tpu_custom_call" | custom-call | flops 335544320 | bytes 4849664 | tf_op jit(solution)/shard_map/kernel_matrix/pallas_call | solution.py:49
  69.0 7.6 %collective-permute-start.11 = (bf16[1,80,512]{2,1,0:T(8,128)(2,1)S(1)}, bf16[1,80,512]{2,1,0:T(8,128)(2,1)S(1)}, u32[]{:S(2)}, u32[]{:S(2)}) collective-permute-start(bf16[1,80,512]{2,1,0:T(8,128)(2,1)S(1)} %bitcast.16), channel_id=1, source_target_pairs={{0,256},{64,320},{128,384},{192,448},{256,0},{320,64},{384,128},{4... | collective-permute-start | bytes 245768 | tf_op jit(solution)/shard_map/ppermute | solution.py:111
  76.6 0.0 collective-permute-done
  76.7 4.5 %collective-permute-start.1 = (bf16[2,48,512]{2,1,0:T(8,128)(2,1)S(1)}, bf16[2,48,512]{2,1,0:T(8,128)(2,1)S(1)}, u32[]{:S(2)}, u32[]{:S(2)}) collective-permute-start(bf16[2,48,512]{2,1,0:T(8,128)(2,1)S(1)} %pad_maximum_fusion.10), channel_id=1, source_target_pairs={{0,128},{64,192},{128,0},{192,64},{256,384},{320,448},{384,256},{4... | collective-permute-start | bytes 294920 | tf_op jit(solution)/shard_map/ppermute | solution.py:111
  81.1 3.3 %collective-permute-done.11 = bf16[1,80,512]{2,1,0:T(8,128)(2,1)S(1)} collective-permute-done((bf16[1,80,512]{2,1,0:T(8,128)(2,1)S(1)}, bf16[1,80,512]{2,1,0:T(8,128)(2,1)S(1)}, u32[]{:S(2)}, u32[]{:S(2)}) %collective-permute-start.11) | collective-permute-done | bytes 81952 | tf_op jit(solution)/shard_map/ppermute | solution.py:111
  84.4 4.0 %collective-permute-start.12 = (bf16[2,80,512]{2,1,0:T(8,128)(2,1)S(1)}, bf16[2,80,512]{2,1,0:T(8,128)(2,1)S(1)}, u32[]{:S(2)}, u32[]{:S(2)}) collective-permute-start(bf16[2,80,512]{2,1,0:T(8,128)(2,1)S(1)} %pad_maximum_fusion.9), channel_id=1, source_target_pairs={{0,128},{64,192},{128,0},{192,64},{256,384},{320,448},{384,256},{4... | collective-permute-start | bytes 491528 | tf_op jit(solution)/shard_map/ppermute | solution.py:111
  88.5 0.0 collective-permute-done.1
  88.5 3.2 %collective-permute-start.2 = (bf16[4,48,512]{2,1,0:T(8,128)(2,1)S(1)}, bf16[4,48,512]{2,1,0:T(8,128)(2,1)S(1)}, u32[]{:S(2)}, u32[]{:S(2)}) collective-permute-start(bf16[4,48,512]{2,1,0:T(8,128)(2,1)S(1)} %pad_maximum_fusion.6), channel_id=1, source_target_pairs={{0,64},{64,0},{128,192},{192,128},{256,320},{320,256},{384,448},{4... | collective-permute-start | bytes 589832 | tf_op jit(solution)/shard_map/ppermute | solution.py:111
  91.7 4.6 %collective-permute-done.12 = bf16[2,80,512]{2,1,0:T(8,128)(2,1)S(1)} collective-permute-done((bf16[2,80,512]{2,1,0:T(8,128)(2,1)S(1)}, bf16[2,80,512]{2,1,0:T(8,128)(2,1)S(1)}, u32[]{:S(2)}, u32[]{:S(2)}) %collective-permute-start.12) | collective-permute-done | bytes 163872 | tf_op jit(solution)/shard_map/ppermute | solution.py:111
  96.3 0.0 copy-start.5
  96.3 1.9 %collective-permute-start.13 = (bf16[4,80,512]{2,1,0:T(8,128)(2,1)S(1)}, bf16[4,80,512]{2,1,0:T(8,128)(2,1)S(1)}, u32[]{:S(2)}, u32[]{:S(2)}) collective-permute-start(bf16[4,80,512]{2,1,0:T(8,128)(2,1)S(1)} %pad_maximum_fusion.5), channel_id=1, source_target_pairs={{0,64},{64,0},{128,192},{192,128},{256,320},{320,256},{384,448},{4... | collective-permute-start | bytes 983048 | tf_op jit(solution)/shard_map/ppermute | solution.py:111
  98.3 0.8 collective-permute-done.2
  99.1 1.9 %kernel_matrix.2 = bf16[48,512]{1,0:T(8,128)(2,1)S(1)} custom-call(s32[8]{0:T(128)S(1)} %broadcast_xor_fusion.slots, bf16[8,512,512]{2,1,0:T(8,128)(2,1)S(1)} %copy-done.2, bf16[8,48,512]{2,1,0:T(8,128)(2,1)S(1)} %pad_maximum_fusion.2.training_ref), custom_call_target="tpu_custom_call" | custom-call | flops 201326592 | bytes 4587520 | tf_op jit(solution)/shard_map/kernel_matrix/pallas_call | solution.py:49
  100.9 6.7 %collective-permute-start.3 = (bf16[1,48,512]{2,1,0:T(8,128)(2,1)S(1)}, bf16[1,48,512]{2,1,0:T(8,128)(2,1)S(1)}, u32[]{:S(2)}, u32[]{:S(2)}) collective-permute-start(bf16[1,48,512]{2,1,0:T(8,128)(2,1)S(1)} %bitcast.20), channel_id=1, source_target_pairs={{0,256},{64,320},{128,384},{192,448},{256,0},{320,64},{384,128},{4... | collective-permute-start | bytes 147464 | tf_op jit(solution)/shard_map/ppermute | solution.py:111
  107.7 3.3 %collective-permute-done.3 = bf16[1,48,512]{2,1,0:T(8,128)(2,1)S(1)} collective-permute-done((bf16[1,48,512]{2,1,0:T(8,128)(2,1)S(1)}, bf16[1,48,512]{2,1,0:T(8,128)(2,1)S(1)}, u32[]{:S(2)}, u32[]{:S(2)}) %collective-permute-start.3) | collective-permute-done | bytes 49184 | tf_op jit(solution)/shard_map/ppermute | solution.py:111
  111.0 4.0 %collective-permute-start.4 = (bf16[2,48,512]{2,1,0:T(8,128)(2,1)S(1)}, bf16[2,48,512]{2,1,0:T(8,128)(2,1)S(1)}, u32[]{:S(2)}, u32[]{:S(2)}) collective-permute-start(bf16[2,48,512]{2,1,0:T(8,128)(2,1)S(1)} %pad_maximum_fusion.11), channel_id=1, source_target_pairs={{0,128},{64,192},{128,0},{192,64},{256,384},{320,448},{384,256},{4... | collective-permute-start | bytes 294920 | tf_op jit(solution)/shard_map/ppermute | solution.py:111
  115.0 0.0 collective-permute-done.13
  115.1 0.1 pad_maximum_fusion.1.refs_1_
  115.1 4.7 %collective-permute-start.14 = (bf16[8,80,512]{2,1,0:T(8,128)(2,1)S(1)}, bf16[8,80,512]{2,1,0:T(8,128)(2,1)S(1)}, u32[]{:S(2)}, u32[]{:S(2)}) collective-permute-start(bf16[8,80,512]{2,1,0:T(8,128)(2,1)S(1)} %pad_maximum_fusion.1.refs_1_), channel_id=1, source_target_pairs={{0,48},{16,0},{32,16},{48,32},{1,49},{17,1},{33,17},{49,33},{2,50}... | collective-permute-start | bytes 1966088 | tf_op jit(solution)/shard_map/ppermute | solution.py:141
  119.8 0.0 collective-permute-done.4
  119.8 4.9 %collective-permute-start.5 = (bf16[4,48,512]{2,1,0:T(8,128)(2,1)S(1)}, bf16[4,48,512]{2,1,0:T(8,128)(2,1)S(1)}, u32[]{:S(2)}, u32[]{:S(2)}) collective-permute-start(bf16[4,48,512]{2,1,0:T(8,128)(2,1)S(1)} %pad_maximum_fusion.7), channel_id=1, source_target_pairs={{0,64},{64,0},{128,192},{192,128},{256,320},{320,256},{384,448},{4... | collective-permute-start | bytes 589832 | tf_op jit(solution)/shard_map/ppermute | solution.py:111
  124.8 3.7 %collective-permute-done.5 = bf16[4,48,512]{2,1,0:T(8,128)(2,1)S(1)} collective-permute-done((bf16[4,48,512]{2,1,0:T(8,128)(2,1)S(1)}, bf16[4,48,512]{2,1,0:T(8,128)(2,1)S(1)}, u32[]{:S(2)}, u32[]{:S(2)}) %collective-permute-start.5) | collective-permute-done | bytes 196640 | tf_op jit(solution)/shard_map/ppermute | solution.py:111
  128.6 2.0 %collective-permute-start.6 = (bf16[8,48,512]{2,1,0:T(8,128)(2,1)S(1)}, bf16[8,48,512]{2,1,0:T(8,128)(2,1)S(1)}, u32[]{:S(2)}, u32[]{:S(2)}) collective-permute-start(bf16[8,48,512]{2,1,0:T(8,128)(2,1)S(1)} %pad_maximum_fusion.3.refs_0_), channel_id=1, source_target_pairs={{0,16},{16,32},{32,48},{48,0},{1,17},{17,33},{33,49},{49,1},{2,18}... | collective-permute-start | bytes 1179656 | tf_op jit(solution)/shard_map/ppermute | solution.py:140
  130.6 3.4 %collective-permute-start.16 = (bf16[8,80,512]{2,1,0:T(8,128)(2,1)S(1)}, bf16[8,80,512]{2,1,0:T(8,128)(2,1)S(1)}, u32[]{:S(2)}, u32[]{:S(2)}) collective-permute-start(bf16[8,80,512]{2,1,0:T(8,128)(2,1)S(1)} %pad_maximum_fusion.1.refs_1_), channel_id=1, source_target_pairs={{0,16},{16,32},{32,48},{48,0},{1,17},{17,33},{33,49},{49,1},{2,18}... | collective-permute-start | bytes 1966088 | tf_op jit(solution)/shard_map/ppermute | solution.py:141
  134.0 0.0 collective-permute-done.14.refs_1_
  134.0 5.1 %collective-permute-start.15 = (bf16[8,80,512]{2,1,0:T(8,128)(2,1)S(1)}, bf16[8,80,512]{2,1,0:T(8,128)(2,1)S(1)}, u32[]{:S(2)}, u32[]{:S(2)}) collective-permute-start(bf16[8,80,512]{2,1,0:T(8,128)(2,1)S(1)} %collective-permute-done.14.refs_1_), channel_id=1, source_target_pairs={{0,48},{16,0},{32,16},{48,32},{1,49},{17,1},{33,17},{49,33},{2,50}... | collective-permute-start | bytes 1966088 | tf_op jit(solution)/shard_map/ppermute | solution.py:147
  139.1 2.4 %collective-permute-start.17 = (bf16[8,48,512]{2,1,0:T(8,128)(2,1)S(1)}, bf16[8,48,512]{2,1,0:T(8,128)(2,1)}, u32[]{:S(2)}, u32[]{:S(2)}) collective-permute-start(bf16[8,48,512]{2,1,0:T(8,128)(2,1)S(1)} %pad_maximum_fusion.3.refs_0_), channel_id=1, source_target_pairs={{0,48},{16,0},{32,16},{48,32},{1,49},{17,1},{33,17},{49,33},{2,50}... | collective-permute-start | bytes 1179656 | tf_op jit(solution)/shard_map/ppermute | solution.py:140
  141.5 2.2 %collective-permute-done.6.refs_0_ = bf16[8,48,512]{2,1,0:T(8,128)(2,1)S(1)} collective-permute-done((bf16[8,48,512]{2,1,0:T(8,128)(2,1)S(1)}, bf16[8,48,512]{2,1,0:T(8,128)(2,1)S(1)}, u32[]{:S(2)}, u32[]{:S(2)}) %collective-permute-start.6) | collective-permute-done | bytes 393248 | tf_op jit(solution)/shard_map/ppermute | solution.py:140
  143.7 1.9 %collective-permute-start.7 = (bf16[8,48,512]{2,1,0:T(8,128)(2,1)S(1)}, bf16[8,48,512]{2,1,0:T(8,128)(2,1)}, u32[]{:S(2)}, u32[]{:S(2)}) collective-permute-start(bf16[8,48,512]{2,1,0:T(8,128)(2,1)S(1)} %collective-permute-done.6.refs_0_), channel_id=1, source_target_pairs={{0,16},{16,32},{32,48},{48,0},{1,17},{17,33},{33,49},{49,1},{2,18}... | collective-permute-start | bytes 1179656 | tf_op jit(solution)/shard_map/ppermute | solution.py:147
  145.6 0.0 all-gather.6.cloned.1.call-done
  145.7 0.0 copy-done.5
  145.7 0.0 copy-start
  145.7 2.2 %copy-done = bf16[4096,512]{1,0:T(8,128)(2,1)S(1)} copy-done((bf16[4096,512]{1,0:T(8,128)(2,1)S(1)}, bf16[4096,512]{1,0:T(8,128)(2,1)}, u32[]{:S(2)}) %copy-start) | copy-done | bytes 4194328
  147.9 2.5 %score_columns.4.refs_2_ = f32[512,512]{1,0:T(8,128)} custom-call(s32[8]{0:T(128)S(1)} %broadcast_xor_fusion.slots, s32[1]{0:T(128)} %bitcast.9.place, bf16[8,512,512]{2,1,0:T(8,128)(2,1)S(1)} %bitcast.12, f32[1,512]{1,0:T(1,128)S(1)} %bitcast.24, bf16[8,48,512]{2,1,0:T(8,128)(2,1)S(1)} %pad_maximum_fusion.3.refs_0_, ...), custom_call_target="tpu_custom_call" | custom-call | flops 536870912 | bytes 5242880 | tf_op jit(solution)/shard_map/score_columns/pallas_call | solution.py:91
  150.4 10.0 %collective-permute-done.17.refs_0_ = bf16[8,48,512]{2,1,0:T(8,128)(2,1)} collective-permute-done((bf16[8,48,512]{2,1,0:T(8,128)(2,1)S(1)}, bf16[8,48,512]{2,1,0:T(8,128)(2,1)}, u32[]{:S(2)}, u32[]{:S(2)}) %collective-permute-start.17) | collective-permute-done | bytes 393248 | tf_op jit(solution)/shard_map/ppermute | solution.py:140
  160.3 0.0 copy-done.1
  160.4 3.0 %score_columns.5.refs_2_ = f32[512,512]{1,0:T(8,128)} custom-call(s32[8]{0:T(128)S(1)} %broadcast_xor_fusion.slots, s32[1]{0:T(128)} %bitcast.8.place, bf16[8,512,512]{2,1,0:T(8,128)(2,1)S(1)} %bitcast.13, f32[1,512]{1,0:T(1,128)S(1)} %bitcast.25, bf16[8,48,512]{2,1,0:T(8,128)(2,1)} %collective-permute-done.17.refs_0_, ...), custom_call_target="tpu_custom_call", output_to_operand_aliasing={{}: (6, {})} | custom-call | flops 536870912 | bytes 5242880 | tf_op jit(solution)/shard_map/score_columns/pallas_call | solution.py:91
  163.3 0.0 collective-permute-done.16.refs_1_
  163.3 2.5 %score_columns.6.refs_2_ = f32[512,512]{1,0:T(8,128)} custom-call(s32[8]{0:T(128)S(1)} %broadcast_xor_fusion.slots, s32[1]{0:T(128)} %bitcast.7.place, bf16[8,512,512]{2,1,0:T(8,128)(2,1)S(1)} %bitcast.14, f32[1,512]{1,0:T(1,128)S(1)} %bitcast.26, bf16[8,48,512]{2,1,0:T(8,128)(2,1)S(1)} %collective-permute-done.6.refs_0_, ...), custom_call_target="tpu_custom_call", output_to_operand_aliasing={{}: (6, {})} | custom-call | flops 536870912 | bytes 5242880 | tf_op jit(solution)/shard_map/score_columns/pallas_call | solution.py:91
  165.8 0.0 collective-permute-done.7.refs_0_
  165.9 0.0 collective-permute-done.15.refs_1_
  165.9 3.0 %score_columns.7 = f32[512,512]{1,0:T(8,128)} custom-call(s32[8]{0:T(128)S(1)} %broadcast_xor_fusion.slots, s32[1]{0:T(128)} %bitcast.place, bf16[8,512,512]{2,1,0:T(8,128)(2,1)S(1)} %bitcast.15, f32[1,512]{1,0:T(1,128)S(1)} %bitcast.27, bf16[8,48,512]{2,1,0:T(8,128)(2,1)} %collective-permute-done.7.refs_0_, ...), custom_call_target="tpu_custom_call", output_to_operand_aliasing={{}: (6, {})} | custom-call | flops 536870912 | bytes 5242880 | tf_op jit(solution)/shard_map/score_columns/pallas_call | solution.py:91
  (20 shorter events, 0.3 us)
Async XLA Ops:
  6.5 47.0 %copy-start.6 = (s32[8]{0:T(128)S(1)}, s32[8]{0:T(128)}, u32[]{:S(2)}) copy-start(s32[8]{0:T(128)} %constant.30.clone) | copy-start | bytes 100
  6.5 58.3 %all-gather.4.cloned.1.call-start = ((), (), s32[]{:S(2)}) async-start(), calls=%async_computation.1 | async-start | bytes 4718592 | tf_op jit(solution)/shard_map/all_gather | solution.py:129
  6.5 0.9 copy-start.3
  7.5 0.9 copy-start.4
  24.4 121.2 %all-gather.6.cloned.1.call-start = ((), (), s32[]{:S(2)}) async-start(), calls=%async_computation.2 | async-start | bytes 4718592 | tf_op jit(solution)/shard_map/all_gather | solution.py:130
  25.4 16.1 %collective-permute-start.8 = (bf16[1,80,512]{2,1,0:T(8,128)(2,1)S(1)}, bf16[1,80,512]{2,1,0:T(8,128)(2,1)S(1)}, u32[]{:S(2)}, u32[]{:S(2)}) collective-permute-start(bf16[1,80,512]{2,1,0:T(8,128)(2,1)S(1)} %slice.19), channel_id=1, source_target_pairs={{0,256},{64,320},{128,384},{192,448},{256,0},{320,64},{384,128},{4... | collective-permute-start | bytes 245768 | tf_op jit(solution)/shard_map/ppermute | solution.py:111
  41.6 10.0 %collective-permute-start.9 = (bf16[2,80,512]{2,1,0:T(8,128)(2,1)S(1)}, bf16[2,80,512]{2,1,0:T(8,128)(2,1)S(1)}, u32[]{:S(2)}, u32[]{:S(2)}) collective-permute-start(bf16[2,80,512]{2,1,0:T(8,128)(2,1)S(1)} %pad_maximum_fusion.8), channel_id=1, source_target_pairs={{0,128},{64,192},{128,0},{192,64},{256,384},{320,448},{384,256},{4... | collective-permute-start | bytes 491528 | tf_op jit(solution)/shard_map/ppermute | solution.py:111
  51.6 9.5 %collective-permute-start.10 = (bf16[4,80,512]{2,1,0:T(8,128)(2,1)S(1)}, bf16[4,80,512]{2,1,0:T(8,128)(2,1)S(1)}, u32[]{:S(2)}, u32[]{:S(2)}) collective-permute-start(bf16[4,80,512]{2,1,0:T(8,128)(2,1)S(1)} %pad_maximum_fusion.4), channel_id=1, source_target_pairs={{0,64},{64,0},{128,192},{192,128},{256,320},{320,256},{384,448},{4... | collective-permute-start | bytes 983048 | tf_op jit(solution)/shard_map/ppermute | solution.py:111
  53.6 23.0 %collective-permute-start = (bf16[1,48,512]{2,1,0:T(8,128)(2,1)S(1)}, bf16[1,48,512]{2,1,0:T(8,128)(2,1)S(1)}, u32[]{:S(2)}, u32[]{:S(2)}) collective-permute-start(bf16[1,48,512]{2,1,0:T(8,128)(2,1)S(1)} %slice.18), channel_id=1, source_target_pairs={{0,256},{64,320},{128,384},{192,448},{256,0},{320,64},{384,128},{4... | collective-permute-start | bytes 147464 | tf_op jit(solution)/shard_map/ppermute | solution.py:111
  64.9 2.2 %copy-start.2 = (bf16[8,512,512]{2,1,0:T(8,128)(2,1)S(1)}, bf16[8,512,512]{2,1,0:T(8,128)(2,1)}, u32[]{:S(2)}) copy-start(bf16[8,512,512]{2,1,0:T(8,128)(2,1)} %all-gather.4.cloned.1.call-done.gram_ref) | copy-start | bytes 12582916
  69.0 15.4 %collective-permute-start.11 = (bf16[1,80,512]{2,1,0:T(8,128)(2,1)S(1)}, bf16[1,80,512]{2,1,0:T(8,128)(2,1)S(1)}, u32[]{:S(2)}, u32[]{:S(2)}) collective-permute-start(bf16[1,80,512]{2,1,0:T(8,128)(2,1)S(1)} %bitcast.16), channel_id=1, source_target_pairs={{0,256},{64,320},{128,384},{192,448},{256,0},{320,64},{384,128},{4... | collective-permute-start | bytes 245768 | tf_op jit(solution)/shard_map/ppermute | solution.py:111
  76.7 11.8 %collective-permute-start.1 = (bf16[2,48,512]{2,1,0:T(8,128)(2,1)S(1)}, bf16[2,48,512]{2,1,0:T(8,128)(2,1)S(1)}, u32[]{:S(2)}, u32[]{:S(2)}) collective-permute-start(bf16[2,48,512]{2,1,0:T(8,128)(2,1)S(1)} %pad_maximum_fusion.10), channel_id=1, source_target_pairs={{0,128},{64,192},{128,0},{192,64},{256,384},{320,448},{384,256},{4... | collective-permute-start | bytes 294920 | tf_op jit(solution)/shard_map/ppermute | solution.py:111
  84.4 11.9 %collective-permute-start.12 = (bf16[2,80,512]{2,1,0:T(8,128)(2,1)S(1)}, bf16[2,80,512]{2,1,0:T(8,128)(2,1)S(1)}, u32[]{:S(2)}, u32[]{:S(2)}) collective-permute-start(bf16[2,80,512]{2,1,0:T(8,128)(2,1)S(1)} %pad_maximum_fusion.9), channel_id=1, source_target_pairs={{0,128},{64,192},{128,0},{192,64},{256,384},{320,448},{384,256},{4... | collective-permute-start | bytes 491528 | tf_op jit(solution)/shard_map/ppermute | solution.py:111
  88.5 10.5 %collective-permute-start.2 = (bf16[4,48,512]{2,1,0:T(8,128)(2,1)S(1)}, bf16[4,48,512]{2,1,0:T(8,128)(2,1)S(1)}, u32[]{:S(2)}, u32[]{:S(2)}) collective-permute-start(bf16[4,48,512]{2,1,0:T(8,128)(2,1)S(1)} %pad_maximum_fusion.6), channel_id=1, source_target_pairs={{0,64},{64,0},{128,192},{192,128},{256,320},{320,256},{384,448},{4... | collective-permute-start | bytes 589832 | tf_op jit(solution)/shard_map/ppermute | solution.py:111
  96.3 49.3 %copy-start.5 = (f32[512]{0:T(512)S(1)}, f32[512]{0:T(512)}, u32[]{:S(2)}) copy-start(f32[512]{0:T(512)} %param.8) | copy-start | bytes 6148
  96.3 18.7 %collective-permute-start.13 = (bf16[4,80,512]{2,1,0:T(8,128)(2,1)S(1)}, bf16[4,80,512]{2,1,0:T(8,128)(2,1)S(1)}, u32[]{:S(2)}, u32[]{:S(2)}) collective-permute-start(bf16[4,80,512]{2,1,0:T(8,128)(2,1)S(1)} %pad_maximum_fusion.5), channel_id=1, source_target_pairs={{0,64},{64,0},{128,192},{192,128},{256,320},{320,256},{384,448},{4... | collective-permute-start | bytes 983048 | tf_op jit(solution)/shard_map/ppermute | solution.py:111
  100.9 10.1 %collective-permute-start.3 = (bf16[1,48,512]{2,1,0:T(8,128)(2,1)S(1)}, bf16[1,48,512]{2,1,0:T(8,128)(2,1)S(1)}, u32[]{:S(2)}, u32[]{:S(2)}) collective-permute-start(bf16[1,48,512]{2,1,0:T(8,128)(2,1)S(1)} %bitcast.20), channel_id=1, source_target_pairs={{0,256},{64,320},{128,384},{192,448},{256,0},{320,64},{384,128},{4... | collective-permute-start | bytes 147464 | tf_op jit(solution)/shard_map/ppermute | solution.py:111
  111.0 8.8 %collective-permute-start.4 = (bf16[2,48,512]{2,1,0:T(8,128)(2,1)S(1)}, bf16[2,48,512]{2,1,0:T(8,128)(2,1)S(1)}, u32[]{:S(2)}, u32[]{:S(2)}) collective-permute-start(bf16[2,48,512]{2,1,0:T(8,128)(2,1)S(1)} %pad_maximum_fusion.11), channel_id=1, source_target_pairs={{0,128},{64,192},{128,0},{192,64},{256,384},{320,448},{384,256},{4... | collective-permute-start | bytes 294920 | tf_op jit(solution)/shard_map/ppermute | solution.py:111
  115.1 18.9 %collective-permute-start.14 = (bf16[8,80,512]{2,1,0:T(8,128)(2,1)S(1)}, bf16[8,80,512]{2,1,0:T(8,128)(2,1)S(1)}, u32[]{:S(2)}, u32[]{:S(2)}) collective-permute-start(bf16[8,80,512]{2,1,0:T(8,128)(2,1)S(1)} %pad_maximum_fusion.1.refs_1_), channel_id=1, source_target_pairs={{0,48},{16,0},{32,16},{48,32},{1,49},{17,1},{33,17},{49,33},{2,50}... | collective-permute-start | bytes 1966088 | tf_op jit(solution)/shard_map/ppermute | solution.py:141
  119.8 8.7 %collective-permute-start.5 = (bf16[4,48,512]{2,1,0:T(8,128)(2,1)S(1)}, bf16[4,48,512]{2,1,0:T(8,128)(2,1)S(1)}, u32[]{:S(2)}, u32[]{:S(2)}) collective-permute-start(bf16[4,48,512]{2,1,0:T(8,128)(2,1)S(1)} %pad_maximum_fusion.7), channel_id=1, source_target_pairs={{0,64},{64,0},{128,192},{192,128},{256,320},{320,256},{384,448},{4... | collective-permute-start | bytes 589832 | tf_op jit(solution)/shard_map/ppermute | solution.py:111
  128.6 15.2 %collective-permute-start.6 = (bf16[8,48,512]{2,1,0:T(8,128)(2,1)S(1)}, bf16[8,48,512]{2,1,0:T(8,128)(2,1)S(1)}, u32[]{:S(2)}, u32[]{:S(2)}) collective-permute-start(bf16[8,48,512]{2,1,0:T(8,128)(2,1)S(1)} %pad_maximum_fusion.3.refs_0_), channel_id=1, source_target_pairs={{0,16},{16,32},{32,48},{48,0},{1,17},{17,33},{33,49},{49,1},{2,18}... | collective-permute-start | bytes 1179656 | tf_op jit(solution)/shard_map/ppermute | solution.py:140
  130.6 32.7 %collective-permute-start.16 = (bf16[8,80,512]{2,1,0:T(8,128)(2,1)S(1)}, bf16[8,80,512]{2,1,0:T(8,128)(2,1)S(1)}, u32[]{:S(2)}, u32[]{:S(2)}) collective-permute-start(bf16[8,80,512]{2,1,0:T(8,128)(2,1)S(1)} %pad_maximum_fusion.1.refs_1_), channel_id=1, source_target_pairs={{0,16},{16,32},{32,48},{48,0},{1,17},{17,33},{33,49},{49,1},{2,18}... | collective-permute-start | bytes 1966088 | tf_op jit(solution)/shard_map/ppermute | solution.py:141
  134.0 31.8 %collective-permute-start.15 = (bf16[8,80,512]{2,1,0:T(8,128)(2,1)S(1)}, bf16[8,80,512]{2,1,0:T(8,128)(2,1)S(1)}, u32[]{:S(2)}, u32[]{:S(2)}) collective-permute-start(bf16[8,80,512]{2,1,0:T(8,128)(2,1)S(1)} %collective-permute-done.14.refs_1_), channel_id=1, source_target_pairs={{0,48},{16,0},{32,16},{48,32},{1,49},{17,1},{33,17},{49,33},{2,50}... | collective-permute-start | bytes 1966088 | tf_op jit(solution)/shard_map/ppermute | solution.py:147
  139.1 21.2 %collective-permute-start.17 = (bf16[8,48,512]{2,1,0:T(8,128)(2,1)S(1)}, bf16[8,48,512]{2,1,0:T(8,128)(2,1)}, u32[]{:S(2)}, u32[]{:S(2)}) collective-permute-start(bf16[8,48,512]{2,1,0:T(8,128)(2,1)S(1)} %pad_maximum_fusion.3.refs_0_), channel_id=1, source_target_pairs={{0,48},{16,0},{32,16},{48,32},{1,49},{17,1},{33,17},{49,33},{2,50}... | collective-permute-start | bytes 1179656 | tf_op jit(solution)/shard_map/ppermute | solution.py:140
  143.7 22.1 %collective-permute-start.7 = (bf16[8,48,512]{2,1,0:T(8,128)(2,1)S(1)}, bf16[8,48,512]{2,1,0:T(8,128)(2,1)}, u32[]{:S(2)}, u32[]{:S(2)}) collective-permute-start(bf16[8,48,512]{2,1,0:T(8,128)(2,1)S(1)} %collective-permute-done.6.refs_0_), channel_id=1, source_target_pairs={{0,16},{16,32},{32,48},{48,0},{1,17},{17,33},{33,49},{49,1},{2,18}... | collective-permute-start | bytes 1179656 | tf_op jit(solution)/shard_map/ppermute | solution.py:147
  145.7 2.2 %copy-start = (bf16[4096,512]{1,0:T(8,128)(2,1)S(1)}, bf16[4096,512]{1,0:T(8,128)(2,1)}, u32[]{:S(2)}) copy-start(bf16[4096,512]{1,0:T(8,128)(2,1)} %all-gather.6.cloned.1.call-done) | copy-start | bytes 12582916
  147.9 12.5 %copy-start.1 = (bf16[4096,512]{1,0:T(8,128)(2,1)S(1)}, bf16[4096,512]{1,0:T(8,128)(2,1)}, u32[]{:S(2)}) copy-start(bf16[4096,512]{1,0:T(8,128)(2,1)} %all-gather.6.cloned.1.call-done) | copy-start | bytes 12582916
Sparse Core Ops, SparseCore 0:
  24.5 40.2 all-gather.3
  67.0 39.7 all-gather.5
